TPU v7x, 32 devices: a whole 2x2x4 slice. The times are simulated.
32 devices in a mesh: groups: 2 (over y), row: 8 (over z, x), col: 2 (over core).
Axes of the slice: x: 2, y: 2, z: 4, core: 2. Of those that a mesh axis runs over, the one named last changes fastest.
Arguments:
- inductance: float32 [2048, 16384], P(('groups', 'col'), 'row'), parts along dimension 0, may hold values from -0.0625 to 0.0625
- current_rates: float32 [16384, 4096], P('row', ('groups', 'col')), parts along dimension 1, may hold values from -6 to 6
Outputs:
- induced_voltage: float32 [1024, 4096], P('row', ('groups', 'col')), parts along dimension 1
There are 2 independent parts, one for each index of `groups`. A program takes and returns all parts, laid end to end along the dimension named above; each array names one. Nothing has to cross between parts.
All inputs are finite; a program needn't handle non-finite values.
Results may differ from a plain program's by a relative error of at most 0.000071.
Values sent between devices are 32-bit elements; how exact they have to be, the bound alone decides.
No kernel may reach another device: no remote copies, remote signals or barrier semaphores. Data moves between devices by JAX's collectives and lax.ppermute only.
A program may use at most 64 MiB of HBM per device.

v0:
```python
import jax
import jax.numpy as jnp
from jax import lax
from jax.sharding import PartitionSpec as P


def product(left, right):
    return jnp.dot(left, right, precision=lax.Precision.HIGHEST, preferred_element_type=jnp.float32)


def shards(inductance, current_rates):
    rows_all = lax.all_gather(inductance, "col", axis=0, tiled=True)
    partial_value = product(rows_all, current_rates)
    return lax.psum_scatter(partial_value, "row", scatter_dimension=0, tiled=True)


def solution(mesh):
    placed = (P(("groups", "col"), "row"), P("row", ("groups", "col")))
    return jax.shard_map(
        shards, mesh=mesh, in_specs=placed, out_specs=P("row", ("groups", "col")), check_vma=False
    )
```

profile of v0, /device:TPU:0, one launch (start us, length us, event | category | flops | bytes accessed | tf_op | source)
XLA Modules:
  0.0 160.0 jit_solution(3209384312272387114)
XLA Ops:
  6.5 0.0 all-gather.2.cloned.1.call-start
  6.5 0.7 all-gather.2.cloned.1.call-update
  7.3 0.0 reduce-scatter.2.cloned.1.call-start
  7.3 24.2 %all-gather.2.cloned.1.call-done = f32[1024,2048]{1,0:T(8,128)} async-done(((f32[512,2048]{1,0:T(8,128)}), f32[1024,2048]{1,0:T(8,128)}) %all-gather.2.cloned.1.call-update) | async-done | bytes 8388624 | tf_op jit(solution)/shard_map/all_gather | solution.py:12
  31.5 31.9 %fusion = f32[1024,1024]{1,0:T(8,128)} fusion(f32[1024,2048]{1,0:T(8,128)} %all-gather.2.cloned.1.call-done, f32[2048,1024]{1,0:T(8,128)} %param.3), kind=kOutput, calls=%fused_computation | convolution fusion | flops 25769803776 | bytes 20971520 | tf_op jit(solution)/shard_map/dot_general | solution.py:8
  63.3 0.0 reduce-scatter.2.cloned.1.call-update
  63.4 89.8 %reduce-scatter.2.cloned.1.call-done = f32[128,1024]{1,0:T(8,128)} async-done(((f32[1024,1024]{1,0:T(8,128)}), f32[128,1024]{1,0:T(8,128)}) %reduce-scatter.2.cloned.1.call-update) | async-done | bytes 524304 | tf_op jit(solution)/shard_map/reduce_scatter | solution.py:14
Async XLA Ops:
  6.5 25.0 %all-gather.2.cloned.1.call-start = ((), (), s32[]{:S(2)}) async-start(), calls=%async_computation.1 | async-start | bytes 12582912 | tf_op jit(solution)/shard_map/all_gather | solution.py:12
  7.3 145.9 %reduce-scatter.2.cloned.1.call-start = ((), (), s32[]{:S(2)}) async-start(), calls=%async_computation.2 | async-start | bytes 4718592 | tf_op jit(solution)/shard_map/reduce_scatter | solution.py:14
Sparse Core Ops, SparseCore 0:
  8.9 22.5 all-gather.1
  63.5 89.6 reduce-scatter.1
where the time goes:
time: 160 us
  waiting for transfers between devices  115 us (72%)
  matrix products  31.9 us (20%)
  between operations  13.4 us (8%)
    reduce_scatter x1, waiting for transfers between devices, shards(): lax.psum_scatter(partial_value, 'row', scatter_dimension=0, tiled=True)  89.8 us
    dot_general x1, matrix products, product(): jnp.dot(left, right, precision=lax.Precision.HIGHEST, preferred_element_t...  31.9 us
    all_gather x1, waiting for transfers between devices, shards(): rows_all = lax.all_gather(inductance, 'col', axis=0, tiled=True)  24.2 us
  transfers between devices with their start and end apart: 2, of which 2 were waited for; matrix products, arithmetic and copies ran while one was open for 0% of the time, Pallas kernels for 0%

commit v1 on v0

v1 whole, which is shorter than its diff:
```python
import jax
import jax.numpy as jnp
import numpy as np
from jax import lax
from jax.sharding import PartitionSpec as P


def product(left, right):
    return jnp.dot(left, right, precision=lax.Precision.HIGH, preferred_element_type=jnp.float32)


def ring_order(mesh):
    count = mesh.shape["row"]
    axes = list(mesh.axis_names)
    line = np.moveaxis(mesh.devices, axes.index("row"), 0).reshape(count, -1)[:, 0]
    spots = [tuple(device.coords) for device in line]
    moving = [axis for axis in range(3) if len({spot[axis] for spot in spots}) > 1]
    plain = list(range(count))
    if len(moving) != 2:
        return plain
    for outer, inner in (moving, moving[::-1]):
        across = sorted({spot[outer] for spot in spots})
        along = sorted({spot[inner] for spot in spots})
        if len(across) % 2 or len(across) * len(along) != count:
            continue
        at = {(spot[outer], spot[inner]): index for index, spot in enumerate(spots)}
        walk = [at[across[0], along[0]]]
        for turn, a in enumerate(across):
            rest = along[1:]
            walk += [at[a, b] for b in (rest if turn % 2 == 0 else rest[::-1])]
        walk += [at[a, along[0]] for a in across[:0:-1]]
        return walk
    return plain


def solution(mesh):
    rows = mesh.shape["row"]
    cols = mesh.shape["col"]
    order = ring_order(mesh)
    place = np.zeros(rows, np.int32)
    place[order] = np.arange(rows)
    swap = [(core, cols - 1 - core) for core in range(cols)]
    ahead = [(order[i], order[(i + 1) % rows]) for i in range(rows)]
    behind = [(order[i], order[(i - 1) % rows]) for i in range(rows)]

    def shards(inductance, current_rates):
        held = inductance.shape[0]
        size = held * cols // rows
        half = size // 2
        mine = lax.axis_index("col")
        spot = jnp.asarray(place)[lax.axis_index("row")]
        walk = jnp.asarray(np.array(order, np.int32))
        other = lax.ppermute(inductance, "col", swap)
        partial = jnp.concatenate([product(inductance, current_rates), product(other, current_rates)])

        def block(step, side):
            target = walk[(spot + step + rows) % rows]
            start = (target * size + mine * held) % (cols * held) + side * half
            return lax.dynamic_slice_in_dim(partial, start, half)

        up, down = block(-1, 0), block(1, 1)
        for step in range(1, rows):
            up = lax.ppermute(up, "row", ahead) + block(-1 - step, 0)
            down = lax.ppermute(down, "row", behind) + block(1 + step, 1)
        return jnp.concatenate([up, down])

    placed = (P(("groups", "col"), "row"), P("row", ("groups", "col")))
    return jax.shard_map(
        shards, mesh=mesh, in_specs=placed, out_specs=P("row", ("groups", "col")), check_vma=False
    )
```

time: 160 us -> 164 us (1.025); the launches traced: 160 us -> 162 us
  waiting for transfers between devices: 115 us -> 66.8 us
  starting transfers between devices: 0.04 us -> 35.8 us
  other arithmetic: 0 us -> 10.6 us
  matrix products: 31.9 us -> 21.6 us
  between operations: 13.4 us -> 22.5 us
  local copies, waits for them, and re-layouts: 0 us -> 4.59 us
    reduce_scatter x1 -> x0, waiting for transfers between devices: 89.8 us -> none  [shards(): lax.psum_scatter(partial_value, 'row', scatter_dimension=0, tiled=True)]
    ppermute x0 -> x15, waiting for transfers between devices: none -> 66.8 us  [the longest x7 34.1 us: shards(): up = lax.ppermute(up, 'row', ahead) + block(-1 - step, 0)]
    ppermute x0 -> x15, starting transfers between devices: none -> 35.8 us  [the longest x7 17.9 us: shards(): down = lax.ppermute(down, 'row', behind) + block(1 + step, 1)]
    all_gather x1 -> x0, waiting for transfers between devices: 24.2 us -> none  [shards(): rows_all = lax.all_gather(inductance, 'col', axis=0, tiled=True)]
    dot_general x1 -> x2, matrix products: 31.9 us -> 21.6 us  [product(): jnp.dot(left, right, precision=lax.Precision.HIGH, preferred_element_type...]
    add x0 -> x14, other arithmetic: none -> 9.73 us  [the longest x7 5.19 us: shards(): down = lax.ppermute(down, 'row', behind) + block(1 + step, 1)]
    dynamic_slice x0 -> x2, local copies, waits for them, and re-layouts: none -> 3.26 us  [the longest x1 2.02 us: block(): target = walk[(spot + step + rows) % rows]]
  transfers between devices with their start and end apart: 2 -> 15, of which waited for: 2 -> 14; matrix products, arithmetic and copies ran while one was open for 0% -> 9% of each run, Pallas kernels for 0% -> 0%
where the time goes in v1:
time: 164 us; the launch traced here: 162 us
  waiting for transfers between devices  66.8 us (41%)
  starting transfers between devices  35.8 us (22%)
  between operations  22.5 us (14%)
  matrix products  21.6 us (13%)
  other arithmetic  10.6 us (6%)
  local copies, waits for them, and re-layouts  4.59 us (3%)
    ppermute x7, waiting for transfers between devices, shards(): up = lax.ppermute(up, 'row', ahead) + block(-1 - step, 0)  34.1 us
    ppermute x7, waiting for transfers between devices, shards(): down = lax.ppermute(down, 'row', behind) + block(1 + step, 1)  32.7 us
    dot_general x2, matrix products, product(): jnp.dot(left, right, precision=lax.Precision.HIGH, preferred_element_type...  21.6 us
    ppermute x7, starting transfers between devices, shards(): down = lax.ppermute(down, 'row', behind) + block(1 + step, 1)  17.9 us
    ppermute x7, starting transfers between devices, shards(): up = lax.ppermute(up, 'row', ahead) + block(-1 - step, 0)  17.4 us
    add x7, other arithmetic, shards(): down = lax.ppermute(down, 'row', behind) + block(1 + step, 1)  5.19 us
    add x7, other arithmetic, shards(): up = lax.ppermute(up, 'row', ahead) + block(-1 - step, 0)  4.54 us
  transfers between devices with their start and end apart: 15, of which 14 were waited for; matrix products, arithmetic and copies ran while one was open for 9% of the time, Pallas kernels for 0%

profile of v1, /device:TPU:0, one launch (start us, length us, event | category | flops | bytes accessed | tf_op | source)
XLA Modules:
  0.0 162.0 jit_solution(13325480028816051303)
XLA Ops:
  0.0 0.5 collective-permute-start
  0.5 1.2 dynamic_slice.99
  13.6 2.0 %fusion.30 = (s32[1]{0:T(128)}, s32[1]{0:T(128)}, s32[1]{0:T(128)}, s32[1]{0:T(128)}, s32[1]{0:T(128)}, /*index=5*/s32[1]{0:T(128)}, s32[1]{0:T(128)}, s32[1]{0:...) fusion(s32[8]{0:T(128)} %constant.233.clone, ...), kind=kLoop, calls=%fused_computation.63 | loop fusion | bytes 192 | tf_op jit(solution)/shard_map/dynamic_slice | solution.py:57
  16.2 10.8 %fusion.31 = f32[512,1024]{1,0:T(8,128)S(1)} fusion(f32[512,2048]{1,0:T(8,128)} %param.4, f32[2048,1024]{1,0:T(8,128)} %param.5), kind=kOutput, calls=%fused_computation.64 | convolution fusion | flops 6442450944 | bytes 14680064 | tf_op jit(solution)/shard_map/dot_general | solution.py:9
  27.0 0.0 collective-permute-done
  27.0 10.8 %fusion.32 = f32[512,1024]{1,0:T(8,128)S(1)} fusion(f32[512,2048]{1,0:T(8,128)} %collective-permute-done, f32[2048,1024]{1,0:T(8,128)} %param.5), kind=kOutput, calls=%fused_computation.65 | convolution fusion | flops 6442450944 | bytes 14680064 | tf_op jit(solution)/shard_map/dot_general | solution.py:9
  37.9 0.0 copy-start
  37.9 1.3 copy-done
  39.2 0.1 fusion.1
  39.3 2.6 %collective-permute-start.1 = (f32[64,1024]{1,0:T(8,128)S(1)}, f32[64,1024]{1,0:T(8,128)S(1)}, u32[]{:S(2)}, u32[]{:S(2)}) collective-permute-start(f32[64,1024]{1,0:T(8,128)S(1)} %fusion.1), channel_id=1, source_target_pairs={{0,4},{4,8},{8,12},{12,14},{14,10},{10,6},{6,2},{2,0},{1,5},{5,9},... | collective-permute-start | bytes 786440 | tf_op jit(solution)/shard_map/ppermute | solution.py:63
  42.5 6.3 %collective-permute-done.1 = f32[64,1024]{1,0:T(8,128)S(1)} collective-permute-done((f32[64,1024]{1,0:T(8,128)S(1)}, f32[64,1024]{1,0:T(8,128)S(1)}, u32[]{:S(2)}, u32[]{:S(2)}) %collective-permute-start.1) | collective-permute-done | bytes 262176 | tf_op jit(solution)/shard_map/ppermute | solution.py:63
  48.8 0.1 fusion.28
  48.9 1.9 %collective-permute-start.2 = (f32[64,1024]{1,0:T(8,128)S(1)}, f32[64,1024]{1,0:T(8,128)S(1)}, u32[]{:S(2)}, u32[]{:S(2)}) collective-permute-start(f32[64,1024]{1,0:T(8,128)S(1)} %fusion.28), channel_id=1, source_target_pairs={{0,4},{4,8},{8,12},{12,14},{14,10},{10,6},{6,2},{2,0},{1,5},{5,9},... | collective-permute-start | bytes 786440 | tf_op jit(solution)/shard_map/ppermute | solution.py:63
  51.5 6.6 %collective-permute-done.2 = f32[64,1024]{1,0:T(8,128)S(1)} collective-permute-done((f32[64,1024]{1,0:T(8,128)S(1)}, f32[64,1024]{1,0:T(8,128)S(1)}, u32[]{:S(2)}, u32[]{:S(2)}) %collective-permute-start.2) | collective-permute-done | bytes 262176 | tf_op jit(solution)/shard_map/ppermute | solution.py:63
  58.1 1.0 fusion.27
  59.1 0.7 collective-permute-start.3
  60.5 5.9 %collective-permute-done.3 = f32[64,1024]{1,0:T(8,128)S(1)} collective-permute-done((f32[64,1024]{1,0:T(8,128)S(1)}, f32[64,1024]{1,0:T(8,128)S(1)}, u32[]{:S(2)}, u32[]{:S(2)}) %collective-permute-start.3) | collective-permute-done | bytes 262176 | tf_op jit(solution)/shard_map/ppermute | solution.py:63
  66.4 1.0 fusion.26
  67.4 2.5 %collective-permute-start.4 = (f32[64,1024]{1,0:T(8,128)S(1)}, f32[64,1024]{1,0:T(8,128)S(1)}, u32[]{:S(2)}, u32[]{:S(2)}) collective-permute-start(f32[64,1024]{1,0:T(8,128)S(1)} %fusion.26), channel_id=1, source_target_pairs={{0,4},{4,8},{8,12},{12,14},{14,10},{10,6},{6,2},{2,0},{1,5},{5,9},... | collective-permute-start | bytes 786440 | tf_op jit(solution)/shard_map/ppermute | solution.py:63
  70.6 4.0 %collective-permute-done.4 = f32[64,1024]{1,0:T(8,128)S(1)} collective-permute-done((f32[64,1024]{1,0:T(8,128)S(1)}, f32[64,1024]{1,0:T(8,128)S(1)}, u32[]{:S(2)}, u32[]{:S(2)}) %collective-permute-start.4) | collective-permute-done | bytes 262176 | tf_op jit(solution)/shard_map/ppermute | solution.py:63
  74.6 1.0 fusion.25
  75.7 2.6 %collective-permute-start.5 = (f32[64,1024]{1,0:T(8,128)S(1)}, f32[64,1024]{1,0:T(8,128)S(1)}, u32[]{:S(2)}, u32[]{:S(2)}) collective-permute-start(f32[64,1024]{1,0:T(8,128)S(1)} %fusion.25), channel_id=1, source_target_pairs={{0,4},{4,8},{8,12},{12,14},{14,10},{10,6},{6,2},{2,0},{1,5},{5,9},... | collective-permute-start | bytes 786440 | tf_op jit(solution)/shard_map/ppermute | solution.py:63
  78.9 4.1 %collective-permute-done.5 = f32[64,1024]{1,0:T(8,128)S(1)} collective-permute-done((f32[64,1024]{1,0:T(8,128)S(1)}, f32[64,1024]{1,0:T(8,128)S(1)}, u32[]{:S(2)}, u32[]{:S(2)}) %collective-permute-start.5) | collective-permute-done | bytes 262176 | tf_op jit(solution)/shard_map/ppermute | solution.py:63
  83.0 1.0 fusion.24
  84.1 2.5 %collective-permute-start.6 = (f32[64,1024]{1,0:T(8,128)S(1)}, f32[64,1024]{1,0:T(8,128)S(1)}, u32[]{:S(2)}, u32[]{:S(2)}) collective-permute-start(f32[64,1024]{1,0:T(8,128)S(1)} %fusion.24), channel_id=1, source_target_pairs={{0,4},{4,8},{8,12},{12,14},{14,10},{10,6},{6,2},{2,0},{1,5},{5,9},... | collective-permute-start | bytes 786440 | tf_op jit(solution)/shard_map/ppermute | solution.py:63
  87.3 3.2 %collective-permute-done.6 = f32[64,1024]{1,0:T(8,128)S(1)} collective-permute-done((f32[64,1024]{1,0:T(8,128)S(1)}, f32[64,1024]{1,0:T(8,128)S(1)}, u32[]{:S(2)}, u32[]{:S(2)}) %collective-permute-start.6) | collective-permute-done | bytes 262176 | tf_op jit(solution)/shard_map/ppermute | solution.py:63
  90.5 0.1 fusion.23
  90.6 4.6 %collective-permute-start.7 = (f32[64,1024]{1,0:T(8,128)S(1)}, f32[64,1024]{1,0:T(8,128)S(1)}, u32[]{:S(2)}, u32[]{:S(2)}) collective-permute-start(f32[64,1024]{1,0:T(8,128)S(1)} %fusion.23), channel_id=1, source_target_pairs={{0,4},{4,8},{8,12},{12,14},{14,10},{10,6},{6,2},{2,0},{1,5},{5,9},... | collective-permute-start | bytes 786440 | tf_op jit(solution)/shard_map/ppermute | solution.py:63
  96.5 4.0 %collective-permute-done.7 = f32[64,1024]{1,0:T(8,128)S(1)} collective-permute-done((f32[64,1024]{1,0:T(8,128)S(1)}, f32[64,1024]{1,0:T(8,128)S(1)}, u32[]{:S(2)}, u32[]{:S(2)}) %collective-permute-start.7) | collective-permute-done | bytes 262176 | tf_op jit(solution)/shard_map/ppermute | solution.py:63
  100.6 0.2 fusion.22
  100.7 2.1 %collective-permute-start.8 = (f32[64,1024]{1,0:T(8,128)S(1)}, f32[64,1024]{1,0:T(8,128)S(1)}, u32[]{:S(2)}, u32[]{:S(2)}) collective-permute-start(f32[64,1024]{1,0:T(8,128)S(1)} %get-tuple-element.6), channel_id=1, source_target_pairs={{0,2},{4,0},{8,4},{12,8},{14,12},{10,14},{6,10},{2,6},{1,3},{5,1},... | collective-permute-start | bytes 786440 | tf_op jit(solution)/shard_map/ppermute | solution.py:64
  103.6 6.2 %collective-permute-done.8 = f32[64,1024]{1,0:T(8,128)S(1)} collective-permute-done((f32[64,1024]{1,0:T(8,128)S(1)}, f32[64,1024]{1,0:T(8,128)S(1)}, u32[]{:S(2)}, u32[]{:S(2)}) %collective-permute-start.8) | collective-permute-done | bytes 262176 | tf_op jit(solution)/shard_map/ppermute | solution.py:64
  109.8 1.0 fusion.21
  110.8 1.2 collective-permute-start.9
  112.7 5.9 %collective-permute-done.9 = f32[64,1024]{1,0:T(8,128)S(1)} collective-permute-done((f32[64,1024]{1,0:T(8,128)S(1)}, f32[64,1024]{1,0:T(8,128)S(1)}, u32[]{:S(2)}, u32[]{:S(2)}) %collective-permute-start.9) | collective-permute-done | bytes 262176 | tf_op jit(solution)/shard_map/ppermute | solution.py:64
  118.6 1.0 fusion.20
  119.6 2.5 %collective-permute-start.10 = (f32[64,1024]{1,0:T(8,128)S(1)}, f32[64,1024]{1,0:T(8,128)S(1)}, u32[]{:S(2)}, u32[]{:S(2)}) collective-permute-start(f32[64,1024]{1,0:T(8,128)S(1)} %fusion.20), channel_id=1, source_target_pairs={{0,2},{4,0},{8,4},{12,8},{14,12},{10,14},{6,10},{2,6},{1,3},{5,1},... | collective-permute-start | bytes 786440 | tf_op jit(solution)/shard_map/ppermute | solution.py:64
  122.8 4.4 %collective-permute-done.10 = f32[64,1024]{1,0:T(8,128)S(1)} collective-permute-done((f32[64,1024]{1,0:T(8,128)S(1)}, f32[64,1024]{1,0:T(8,128)S(1)}, u32[]{:S(2)}, u32[]{:S(2)}) %collective-permute-start.10) | collective-permute-done | bytes 262176 | tf_op jit(solution)/shard_map/ppermute | solution.py:64
  127.3 1.0 fusion.19
  128.3 2.8 %collective-permute-start.11 = (f32[64,1024]{1,0:T(8,128)S(1)}, f32[64,1024]{1,0:T(8,128)S(1)}, u32[]{:S(2)}, u32[]{:S(2)}) collective-permute-start(f32[64,1024]{1,0:T(8,128)S(1)} %fusion.19), channel_id=1, source_target_pairs={{0,2},{4,0},{8,4},{12,8},{14,12},{10,14},{6,10},{2,6},{1,3},{5,1},... | collective-permute-start | bytes 786440 | tf_op jit(solution)/shard_map/ppermute | solution.py:64
  131.8 4.4 %collective-permute-done.11 = f32[64,1024]{1,0:T(8,128)S(1)} collective-permute-done((f32[64,1024]{1,0:T(8,128)S(1)}, f32[64,1024]{1,0:T(8,128)S(1)}, u32[]{:S(2)}, u32[]{:S(2)}) %collective-permute-start.11) | collective-permute-done | bytes 262176 | tf_op jit(solution)/shard_map/ppermute | solution.py:64
  136.2 1.0 fusion.18
  137.2 2.5 %collective-permute-start.12 = (f32[64,1024]{1,0:T(8,128)S(1)}, f32[64,1024]{1,0:T(8,128)S(1)}, u32[]{:S(2)}, u32[]{:S(2)}) collective-permute-start(f32[64,1024]{1,0:T(8,128)S(1)} %fusion.18), channel_id=1, source_target_pairs={{0,2},{4,0},{8,4},{12,8},{14,12},{10,14},{6,10},{2,6},{1,3},{5,1},... | collective-permute-start | bytes 786440 | tf_op jit(solution)/shard_map/ppermute | solution.py:64
  140.4 3.3 %collective-permute-done.12 = f32[64,1024]{1,0:T(8,128)S(1)} collective-permute-done((f32[64,1024]{1,0:T(8,128)S(1)}, f32[64,1024]{1,0:T(8,128)S(1)}, u32[]{:S(2)}, u32[]{:S(2)}) %collective-permute-start.12) | collective-permute-done | bytes 262176 | tf_op jit(solution)/shard_map/ppermute | solution.py:64
  143.7 0.8 fusion.17
  144.6 2.7 %collective-permute-start.13 = (f32[64,1024]{1,0:T(8,128)S(1)}, f32[64,1024]{1,0:T(8,128)S(1)}, u32[]{:S(2)}, u32[]{:S(2)}) collective-permute-start(f32[64,1024]{1,0:T(8,128)S(1)} %fusion.17), channel_id=1, source_target_pairs={{0,2},{4,0},{8,4},{12,8},{14,12},{10,14},{6,10},{2,6},{1,3},{5,1},... | collective-permute-start | bytes 786440 | tf_op jit(solution)/shard_map/ppermute | solution.py:64
  147.9 3.6 %collective-permute-done.13 = f32[64,1024]{1,0:T(8,128)S(1)} collective-permute-done((f32[64,1024]{1,0:T(8,128)S(1)}, f32[64,1024]{1,0:T(8,128)S(1)}, u32[]{:S(2)}, u32[]{:S(2)}) %collective-permute-start.13) | collective-permute-done | bytes 262176 | tf_op jit(solution)/shard_map/ppermute | solution.py:64
  151.5 0.1 fusion.16
  151.6 4.0 %collective-permute-start.14 = (f32[64,1024]{1,0:T(8,128)S(1)}, f32[64,1024]{1,0:T(8,128)S(1)}, u32[]{:S(2)}, u32[]{:S(2)}) collective-permute-start(f32[64,1024]{1,0:T(8,128)S(1)} %fusion.16), channel_id=1, source_target_pairs={{0,2},{4,0},{8,4},{12,8},{14,12},{10,14},{6,10},{2,6},{1,3},{5,1},... | collective-permute-start | bytes 786440 | tf_op jit(solution)/shard_map/ppermute | solution.py:64
  156.3 4.8 %collective-permute-done.14 = f32[64,1024]{1,0:T(8,128)S(1)} collective-permute-done((f32[64,1024]{1,0:T(8,128)S(1)}, f32[64,1024]{1,0:T(8,128)S(1)}, u32[]{:S(2)}, u32[]{:S(2)}) %collective-permute-start.14) | collective-permute-done | bytes 262176 | tf_op jit(solution)/shard_map/ppermute | solution.py:64
  161.0 0.1 fusion.29
  161.1 0.8 pad_maximum_fusion
Async XLA Ops:
  0.0 27.0 %collective-permute-start = (f32[512,2048]{1,0:T(8,128)}, f32[512,2048]{1,0:T(8,128)}, u32[]{:S(2)}, u32[]{:S(2)}) collective-permute-start(f32[512,2048]{1,0:T(8,128)} %param.4), channel_id=1, source_target_pairs={{0,1},{1,0},{2,3},{3,2},{4,5},{5,4},{6,7},{7,6},{8,9},{9,8},{10,11... | collective-permute-start | bytes 12582920 | tf_op jit(solution)/shard_map/ppermute | solution.py:53
  37.9 1.3 copy-start
  39.3 9.5 %collective-permute-start.1 = (f32[64,1024]{1,0:T(8,128)S(1)}, f32[64,1024]{1,0:T(8,128)S(1)}, u32[]{:S(2)}, u32[]{:S(2)}) collective-permute-start(f32[64,1024]{1,0:T(8,128)S(1)} %fusion.1), channel_id=1, source_target_pairs={{0,4},{4,8},{8,12},{12,14},{14,10},{10,6},{6,2},{2,0},{1,5},{5,9},... | collective-permute-start | bytes 786440 | tf_op jit(solution)/shard_map/ppermute | solution.py:63
  48.9 9.2 %collective-permute-start.2 = (f32[64,1024]{1,0:T(8,128)S(1)}, f32[64,1024]{1,0:T(8,128)S(1)}, u32[]{:S(2)}, u32[]{:S(2)}) collective-permute-start(f32[64,1024]{1,0:T(8,128)S(1)} %fusion.28), channel_id=1, source_target_pairs={{0,4},{4,8},{8,12},{12,14},{14,10},{10,6},{6,2},{2,0},{1,5},{5,9},... | collective-permute-start | bytes 786440 | tf_op jit(solution)/shard_map/ppermute | solution.py:63
  59.1 7.2 %collective-permute-start.3 = (f32[64,1024]{1,0:T(8,128)S(1)}, f32[64,1024]{1,0:T(8,128)S(1)}, u32[]{:S(2)}, u32[]{:S(2)}) collective-permute-start(f32[64,1024]{1,0:T(8,128)S(1)} %fusion.27), channel_id=1, source_target_pairs={{0,4},{4,8},{8,12},{12,14},{14,10},{10,6},{6,2},{2,0},{1,5},{5,9},... | collective-permute-start | bytes 786440 | tf_op jit(solution)/shard_map/ppermute | solution.py:63
  67.4 7.2 %collective-permute-start.4 = (f32[64,1024]{1,0:T(8,128)S(1)}, f32[64,1024]{1,0:T(8,128)S(1)}, u32[]{:S(2)}, u32[]{:S(2)}) collective-permute-start(f32[64,1024]{1,0:T(8,128)S(1)} %fusion.26), channel_id=1, source_target_pairs={{0,4},{4,8},{8,12},{12,14},{14,10},{10,6},{6,2},{2,0},{1,5},{5,9},... | collective-permute-start | bytes 786440 | tf_op jit(solution)/shard_map/ppermute | solution.py:63
  75.7 7.4 %collective-permute-start.5 = (f32[64,1024]{1,0:T(8,128)S(1)}, f32[64,1024]{1,0:T(8,128)S(1)}, u32[]{:S(2)}, u32[]{:S(2)}) collective-permute-start(f32[64,1024]{1,0:T(8,128)S(1)} %fusion.25), channel_id=1, source_target_pairs={{0,4},{4,8},{8,12},{12,14},{14,10},{10,6},{6,2},{2,0},{1,5},{5,9},... | collective-permute-start | bytes 786440 | tf_op jit(solution)/shard_map/ppermute | solution.py:63
  84.1 6.4 %collective-permute-start.6 = (f32[64,1024]{1,0:T(8,128)S(1)}, f32[64,1024]{1,0:T(8,128)S(1)}, u32[]{:S(2)}, u32[]{:S(2)}) collective-permute-start(f32[64,1024]{1,0:T(8,128)S(1)} %fusion.24), channel_id=1, source_target_pairs={{0,4},{4,8},{8,12},{12,14},{14,10},{10,6},{6,2},{2,0},{1,5},{5,9},... | collective-permute-start | bytes 786440 | tf_op jit(solution)/shard_map/ppermute | solution.py:63
  90.6 9.9 %collective-permute-start.7 = (f32[64,1024]{1,0:T(8,128)S(1)}, f32[64,1024]{1,0:T(8,128)S(1)}, u32[]{:S(2)}, u32[]{:S(2)}) collective-permute-start(f32[64,1024]{1,0:T(8,128)S(1)} %fusion.23), channel_id=1, source_target_pairs={{0,4},{4,8},{8,12},{12,14},{14,10},{10,6},{6,2},{2,0},{1,5},{5,9},... | collective-permute-start | bytes 786440 | tf_op jit(solution)/shard_map/ppermute | solution.py:63
  100.7 9.0 %collective-permute-start.8 = (f32[64,1024]{1,0:T(8,128)S(1)}, f32[64,1024]{1,0:T(8,128)S(1)}, u32[]{:S(2)}, u32[]{:S(2)}) collective-permute-start(f32[64,1024]{1,0:T(8,128)S(1)} %get-tuple-element.6), channel_id=1, source_target_pairs={{0,2},{4,0},{8,4},{12,8},{14,12},{10,14},{6,10},{2,6},{1,3},{5,1},... | collective-permute-start | bytes 786440 | tf_op jit(solution)/shard_map/ppermute | solution.py:64
  110.8 7.8 %collective-permute-start.9 = (f32[64,1024]{1,0:T(8,128)S(1)}, f32[64,1024]{1,0:T(8,128)S(1)}, u32[]{:S(2)}, u32[]{:S(2)}) collective-permute-start(f32[64,1024]{1,0:T(8,128)S(1)} %fusion.21), channel_id=1, source_target_pairs={{0,2},{4,0},{8,4},{12,8},{14,12},{10,14},{6,10},{2,6},{1,3},{5,1},... | collective-permute-start | bytes 786440 | tf_op jit(solution)/shard_map/ppermute | solution.py:64
  119.6 7.6 %collective-permute-start.10 = (f32[64,1024]{1,0:T(8,128)S(1)}, f32[64,1024]{1,0:T(8,128)S(1)}, u32[]{:S(2)}, u32[]{:S(2)}) collective-permute-start(f32[64,1024]{1,0:T(8,128)S(1)} %fusion.20), channel_id=1, source_target_pairs={{0,2},{4,0},{8,4},{12,8},{14,12},{10,14},{6,10},{2,6},{1,3},{5,1},... | collective-permute-start | bytes 786440 | tf_op jit(solution)/shard_map/ppermute | solution.py:64
  128.3 7.9 %collective-permute-start.11 = (f32[64,1024]{1,0:T(8,128)S(1)}, f32[64,1024]{1,0:T(8,128)S(1)}, u32[]{:S(2)}, u32[]{:S(2)}) collective-permute-start(f32[64,1024]{1,0:T(8,128)S(1)} %fusion.19), channel_id=1, source_target_pairs={{0,2},{4,0},{8,4},{12,8},{14,12},{10,14},{6,10},{2,6},{1,3},{5,1},... | collective-permute-start | bytes 786440 | tf_op jit(solution)/shard_map/ppermute | solution.py:64
  137.2 6.5 %collective-permute-start.12 = (f32[64,1024]{1,0:T(8,128)S(1)}, f32[64,1024]{1,0:T(8,128)S(1)}, u32[]{:S(2)}, u32[]{:S(2)}) collective-permute-start(f32[64,1024]{1,0:T(8,128)S(1)} %fusion.18), channel_id=1, source_target_pairs={{0,2},{4,0},{8,4},{12,8},{14,12},{10,14},{6,10},{2,6},{1,3},{5,1},... | collective-permute-start | bytes 786440 | tf_op jit(solution)/shard_map/ppermute | solution.py:64
  144.6 6.9 %collective-permute-start.13 = (f32[64,1024]{1,0:T(8,128)S(1)}, f32[64,1024]{1,0:T(8,128)S(1)}, u32[]{:S(2)}, u32[]{:S(2)}) collective-permute-start(f32[64,1024]{1,0:T(8,128)S(1)} %fusion.17), channel_id=1, source_target_pairs={{0,2},{4,0},{8,4},{12,8},{14,12},{10,14},{6,10},{2,6},{1,3},{5,1},... | collective-permute-start | bytes 786440 | tf_op jit(solution)/shard_map/ppermute | solution.py:64
  151.6 9.4 %collective-permute-start.14 = (f32[64,1024]{1,0:T(8,128)S(1)}, f32[64,1024]{1,0:T(8,128)S(1)}, u32[]{:S(2)}, u32[]{:S(2)}) collective-permute-start(f32[64,1024]{1,0:T(8,128)S(1)} %fusion.16), channel_id=1, source_target_pairs={{0,2},{4,0},{8,4},{12,8},{14,12},{10,14},{6,10},{2,6},{1,3},{5,1},... | collective-permute-start | bytes 786440 | tf_op jit(solution)/shard_map/ppermute | solution.py:64

commit v2 on v1

v2 whole, which is shorter than its diff:
```python
import functools

import jax
import jax.numpy as jnp
import numpy as np
from jax import lax
from jax.experimental import pallas as pl
from jax.experimental.pallas import tpu as pltpu
from jax.sharding import PartitionSpec as P

CALLS = 8
LANES = 256


def ring_order(mesh):
    count = mesh.shape["row"]
    axes = list(mesh.axis_names)
    line = np.moveaxis(mesh.devices, axes.index("row"), 0).reshape(count, -1)[:, 0]
    spots = [tuple(device.coords) for device in line]
    moving = [axis for axis in range(3) if len({spot[axis] for spot in spots}) > 1]
    plain = list(range(count))
    if len(moving) != 2:
        return plain
    for outer, inner in (moving, moving[::-1]):
        across = sorted({spot[outer] for spot in spots})
        along = sorted({spot[inner] for spot in spots})
        if len(across) % 2 or len(across) * len(along) != count:
            continue
        at = {(spot[outer], spot[inner]): index for index, spot in enumerate(spots)}
        walk = [at[across[0], along[0]]]
        for turn, a in enumerate(across):
            rest = along[1:]
            walk += [at[a, b] for b in (rest if turn % 2 == 0 else rest[::-1])]
        walk += [at[a, along[0]] for a in across[:0:-1]]
        return walk
    return plain


def looked_up(table):
    row, col = lax.axis_index("row"), lax.axis_index("col")
    found = jnp.int32(0)
    for r in range(table.shape[0]):
        for c in range(table.shape[1]):
            found = jnp.where((row == r) & (col == c), jnp.int32(table[r, c]), found)
    return found


def pick_kernel(starts, size, a_ref, out_ref, sems):
    copies = []
    for index in range(starts.shape[-1]):
        start = pl.multiple_of(looked_up(starts[..., index]), size)
        copies.append(
            pltpu.make_async_copy(
                a_ref.at[pl.ds(start, size)], out_ref.at[pl.ds(index * size, size)], sems.at[index]
            )
        )
    for copy in copies:
        copy.start()
    for copy in copies:
        copy.wait()


def pick(inductance, starts, size):
    count = starts.shape[-1]
    width = inductance.shape[1]
    return pl.pallas_call(
        functools.partial(pick_kernel, starts, size),
        out_shape=jax.ShapeDtypeStruct((count * size, width), jnp.float32),
        in_specs=[pl.BlockSpec(memory_space=pl.ANY)],
        out_specs=pl.BlockSpec(memory_space=pl.ANY),
        scratch_shapes=[pltpu.SemaphoreType.DMA((count,))],
        cost_estimate=pl.CostEstimate(flops=0, bytes_accessed=8 * count * size * width, transcendentals=0),
        name="pick",
    )(inductance)


def halves(value):
    high = value.astype(jnp.bfloat16)
    return high, (value - high.astype(jnp.float32)).astype(jnp.bfloat16)


def split_kernel(value_ref, high_ref, low_ref):
    high_ref[...], low_ref[...] = halves(value_ref[...])


def split(current_rates, part, parts):
    depth, width = current_rates.shape
    width //= parts
    tile = 256
    out = jax.ShapeDtypeStruct((depth, width), jnp.bfloat16)
    return pl.pallas_call(
        split_kernel,
        grid=(depth // tile,),
        out_shape=(out, out),
        in_specs=[pl.BlockSpec((tile, width), lambda k: (k, part))],
        out_specs=[pl.BlockSpec((tile, width), lambda k: (k, 0))] * 2,
        cost_estimate=pl.CostEstimate(flops=4 * depth * width, bytes_accessed=8 * depth * width, transcendentals=0),
        name="split",
    )(current_rates)


def product_kernel(starts, size, bounds, *refs):
    count = len(bounds)
    sources, (high_ref, low_ref, out_ref, raw, stack, sems) = refs[:count], refs[count:]
    depth = raw.shape[0]

    @pl.when(pl.program_id(0) == 0)
    def _():
        for index in range(starts.shape[-1]):
            start = looked_up(starts[..., index])
            first = 0
            for source, last in zip(sources, bounds):

                @pl.when((start >= first) & (start < last))
                def _(source=source, first=first, start=start, index=index):
                    pltpu.make_async_copy(
                        source.at[pl.ds(pl.multiple_of(start - first, size), size)],
                        raw.at[pl.ds(index * size, size)],
                        sems.at[index],
                    ).start()

                first = last
        for index in range(starts.shape[-1]):
            pltpu.make_async_copy(
                sources[0].at[pl.ds(0, size)], raw.at[pl.ds(index * size, size)], sems.at[index]
            ).wait()
        stack[:depth], stack[depth:] = halves(raw[...])

    both = jnp.dot(stack[...], high_ref[...], preferred_element_type=jnp.float32)
    rest = jnp.dot(stack[:depth], low_ref[...], preferred_element_type=jnp.float32)
    out_ref[...] = both[:depth] + (both[depth:] + rest)


def product(sources, starts, size, high, low):
    depth = starts.shape[-1] * size
    inner, width = high.shape
    tile = min(LANES, width)
    return pl.pallas_call(
        functools.partial(product_kernel, starts, size, list(np.cumsum([s.shape[0] for s in sources]))),
        grid=(width // tile,),
        out_shape=jax.ShapeDtypeStruct((depth, width), jnp.float32),
        in_specs=[pl.BlockSpec(memory_space=pl.ANY)] * len(sources)
        + [pl.BlockSpec((inner, tile), lambda j: (0, j))] * 2,
        out_specs=pl.BlockSpec((depth, tile), lambda j: (0, j)),
        scratch_shapes=[
            pltpu.VMEM((depth, inner), jnp.float32),
            pltpu.VMEM((2 * depth, inner), jnp.bfloat16),
            pltpu.SemaphoreType.DMA((starts.shape[-1],)),
        ],
        compiler_params=pltpu.CompilerParams(vmem_limit_bytes=16 * 2**20),
        cost_estimate=pl.CostEstimate(
            flops=6 * depth * inner * width,
            bytes_accessed=4 * depth * inner + 4 * inner * width + 4 * depth * width,
            transcendentals=0,
        ),
        name="product",
    )(*sources, high, low)


def plan(order, rows, cols, size):
    place = np.zeros(rows, np.int64)
    place[order] = np.arange(rows)
    each = rows // cols
    needs = np.zeros((rows, cols, rows), np.int64)
    for row in range(rows):
        for core in range(cols):
            way = -1 if core == 0 else 1
            needs[row, core] = [order[(place[row] + way * (k + 1)) % rows] for k in range(rows)]
    taken = np.zeros((rows, cols, rows), np.int64)
    given = np.zeros((rows, cols, each), np.int64)
    for row in range(rows):
        for core in range(cols):
            arrived = 0
            for k, block in enumerate(needs[row, core]):
                if block // each == core:
                    taken[row, core, k] = (block - core * each) * size
                else:
                    taken[row, core, k] = (each + arrived) * size
                    arrived += 1
            wanted = [block for block in needs[row, 1 - core] if block // each == core]
            given[row, core] = [(block - core * each) * size for block in wanted]
    return taken, given


def solution(mesh):
    rows, cols = mesh.shape["row"], mesh.shape["col"]
    order = ring_order(mesh)
    group = max(rows // CALLS, 1)
    swap = [(core, cols - 1 - core) for core in range(cols)]
    around = [
        (order[i] * cols + core, order[(i + (1 if core == 0 else -1)) % rows] * cols + core)
        for i in range(rows)
        for core in range(cols)
    ]

    def shards(inductance, current_rates):
        size = inductance.shape[0] * cols // rows
        taken, given = plan(order, rows, cols, size)
        soon = lax.ppermute(pick(inductance, given[..., :group], size), "col", swap)
        late = lax.ppermute(pick(inductance, given[..., group:], size), "col", swap)
        rates = [split(current_rates, part, 2) for part in range(2)]
        first = [product([inductance, soon], taken[..., :group], size, *pair) for pair in rates]
        sums = [part[:size] for part in first]
        for step in range(1, rows):
            passed = [lax.ppermute(part, ("row", "col"), around) for part in sums]
            if step % group == 0:
                starts = taken[..., step : step + group]
                first = [product([inductance, soon, late], starts, size, *pair) for pair in rates]
            at = step % group * size
            sums = [got + part[at : at + size] for got, part in zip(passed, first)]
        return jnp.concatenate(sums, axis=1)

    placed = (P(("groups", "col"), "row"), P("row", ("groups", "col")))
    return jax.shard_map(
        shards, mesh=mesh, in_specs=placed, out_specs=P("row", ("groups", "col")), check_vma=False
    )
```

time: 164 us -> 210 us (1.28)
  Pallas kernels: 0 us -> 173 us
  waiting for transfers between devices: 66.8 us -> 10.8 us
  between operations: 22.5 us -> 0.3 us
  matrix products: 21.6 us -> 0 us
  starting transfers between devices: 35.8 us -> 18.5 us
  other arithmetic: 10.6 us -> 1.34 us
    pallas_call x0 -> x20, Pallas kernels: none -> 173 us  [the longest x2 129 us: pick(): pl.pallas_call(functools.partial(pick_kernel, starts, size), out_shape=ja...]
    ppermute x15 -> x16, waiting for transfers between devices: 66.8 us -> 10.8 us  [the longest x14 10.7 us: shards(): passed = [lax.ppermute(part, ('row', 'col'), around) for part in sums]]
    dot_general x2 -> x0, matrix products: 21.6 us -> none  [product(): jnp.dot(left, right, precision=lax.Precision.HIGH, preferred_element_type...]
    ppermute x15 -> x16, starting transfers between devices: 35.8 us -> 18.5 us  [the longest x14 17.9 us: shards(): passed = [lax.ppermute(part, ('row', 'col'), around) for part in sums]]
    add x14, other arithmetic: 9.73 us -> 0.51 us  [shards(): sums = [got + part[at:at + size] for got, part in zip(passed, first)]]
    unnamed x2 -> x12, local copies, waits for them, and re-layouts: 1.34 us -> 5.38 us
    dynamic_slice x2 -> x0, local copies, waits for them, and re-layouts: 3.26 us -> none  [the longest x1 2.02 us: block(): target = walk[(spot + step + rows) % rows]]
  transfers between devices with their start and end apart: 15 -> 16, of which waited for: 14 -> 6; matrix products, arithmetic and copies ran while one was open for 9% -> 0% of each run, Pallas kernels for 0% -> 37%
where the time goes in v2:
time: 210 us; the launch traced here: 209 us
  Pallas kernels  173 us (82%)
  starting transfers between devices  18.5 us (9%)
  waiting for transfers between devices  10.8 us (5%)
  local copies, waits for them, and re-layouts  5.38 us (3%)
    pallas_call x2, Pallas kernels, pick(): pl.pallas_call(functools.partial(pick_kernel, starts, size), out_shape=ja...  129 us
    pallas_call x16, Pallas kernels, product(): pl.pallas_call(functools.partial(product_kernel, starts, size, list(np.cu...  30.3 us
    ppermute x14, starting transfers between devices, shards(): passed = [lax.ppermute(part, ('row', 'col'), around) for part in sums]  17.9 us
    pallas_call x2, Pallas kernels, split(): pl.pallas_call(split_kernel, grid=(depth // tile,), out_shape=(out, out),...  13.3 us
    ppermute x14, waiting for transfers between devices, shards(): passed = [lax.ppermute(part, ('row', 'col'), around) for part in sums]  10.7 us
    unnamed x12, local copies, waits for them, and re-layouts  5.38 us
  transfers between devices with their start and end apart: 16, of which 6 were waited for; matrix products, arithmetic and copies ran while one was open for 0% of the time, Pallas kernels for 37%

profile of v2, /device:TPU:0, one launch (start us, length us, event | category | flops | bytes accessed | tf_op | source)
XLA Modules:
  0.0 209.2 jit_solution(11903283445044157553)
XLA Ops:
  0.0 96.4 %pick.3 = f32[384,2048]{1,0:T(8,128)} custom-call(f32[512,2048]{1,0:T(8,128)} %refs_0_.31), custom_call_target="tpu_custom_call" | custom-call | bytes 6291456 | tf_op jit(solution)/shard_map/pick/pallas_call | solution.py:66
  96.4 0.5 collective-permute-start.2
  96.9 32.9 %pick.2 = f32[128,2048]{1,0:T(8,128)} custom-call(f32[512,2048]{1,0:T(8,128)} %refs_0_.31), custom_call_target="tpu_custom_call" | custom-call | bytes 2097152 | tf_op jit(solution)/shard_map/pick/pallas_call | solution.py:66
  129.8 0.1 collective-permute-start
  129.9 6.6 %split.2 = (bf16[2048,512]{1,0:T(8,128)(2,1)}, bf16[2048,512]{1,0:T(8,128)(2,1)}) custom-call(f32[2048,1024]{1,0:T(8,128)} %value_ref.3), custom_call_target="tpu_custom_call" | custom-call | flops 4194304 | bytes 8388608 | tf_op jit(solution)/shard_map/split/pallas_call | solution.py:91
  136.6 6.7 %split.3 = (bf16[2048,512]{1,0:T(8,128)(2,1)}, bf16[2048,512]{1,0:T(8,128)(2,1)}) custom-call(f32[2048,1024]{1,0:T(8,128)} %value_ref.3), custom_call_target="tpu_custom_call" | custom-call | flops 4194304 | bytes 8388608 | tf_op jit(solution)/shard_map/split/pallas_call | solution.py:91
  143.3 0.0 collective-permute-done.refs_1_
  143.3 0.0 copy-start
  143.3 2.2 %copy-done = f32[512,2048]{1,0:T(8,128)S(1)} copy-done((f32[512,2048]{1,0:T(8,128)S(1)}, f32[512,2048]{1,0:T(8,128)}, u32[]{:S(2)}) %copy-start) | copy-done | bytes 4194328
  145.5 0.0 copy-start.3
  145.5 1.6 copy-done.3
  147.1 0.0 copy-start.4
  147.1 1.6 copy-done.4
  148.6 0.0 copy-start.1
  148.6 0.0 copy-start.2
  148.6 1.7 product.16
  150.4 3.1 %collective-permute-start.1 = (f32[128,512]{1,0:T(8,128)S(1)}, f32[128,512]{1,0:T(8,128)S(1)}, u32[]{:S(2)}, u32[]{:S(2)}) collective-permute-start(f32[128,512]{1,0:T(8,128)S(1)} %product.16), channel_id=1, source_target_pairs={{0,4},{1,3},{4,8},{5,1},{8,12},{9,5},{12,14},{13,9},{14,10},{15,13... | collective-permute-start | bytes 786440 | tf_op jit(solution)/shard_map/ppermute | solution.py:205
  153.5 0.0 copy-done.1
  153.5 0.0 copy-done.2
  153.5 1.7 product.24
  155.2 1.6 collective-permute-start.9
  156.9 0.0 collective-permute-done.2.refs_2_
  156.9 0.0 copy-done.5
  156.9 1.7 product.17
  158.6 0.0 collective-permute-done.1
  158.7 2.9 %collective-permute-start.3 = (f32[128,512]{1,0:T(8,128)S(1)}, f32[128,512]{1,0:T(8,128)S(1)}, u32[]{:S(2)}, u32[]{:S(2)}) collective-permute-start(f32[128,512]{1,0:T(8,128)S(1)} %add.42), channel_id=1, source_target_pairs={{0,4},{1,3},{4,8},{5,1},{8,12},{9,5},{12,14},{13,9},{14,10},{15,13... | collective-permute-start | bytes 786440 | tf_op jit(solution)/shard_map/ppermute | solution.py:205
  161.6 1.7 product.25
  163.4 0.0 collective-permute-done.9
  163.4 2.9 %collective-permute-start.10 = (f32[128,512]{1,0:T(8,128)S(1)}, f32[128,512]{1,0:T(8,128)S(1)}, u32[]{:S(2)}, u32[]{:S(2)}) collective-permute-start(f32[128,512]{1,0:T(8,128)S(1)} %add.49), channel_id=1, source_target_pairs={{0,4},{1,3},{4,8},{5,1},{8,12},{9,5},{12,14},{13,9},{14,10},{15,13... | collective-permute-start | bytes 786440 | tf_op jit(solution)/shard_map/ppermute | solution.py:205
  166.3 2.9 %product.18 = f32[128,512]{1,0:T(8,128)S(1)} custom-call(f32[512,2048]{1,0:T(8,128)S(1)} %copy-done, f32[128,2048]{1,0:T(8,128)} %collective-permute-done.refs_1_, f32[384,2048]{1,0:T(8,128)S(1)} %collective-permute-done.2.refs_2_, bf16[2048,512]{1,0:T(8,128)(2,1)S(1)} %copy-done.3, bf16[2048,512]{1,0:T(8,128)(2,1)S(1)} %copy-done.5), custom_call_target="tpu_custom_call" | custom-call | flops 805306368 | bytes 5505024 | tf_op jit(solution)/shard_map/product/pallas_call | solution.py:138
  169.2 2.9 %product.26 = f32[128,512]{1,0:T(8,128)S(1)} custom-call(f32[512,2048]{1,0:T(8,128)S(1)} %copy-done, f32[128,2048]{1,0:T(8,128)} %collective-permute-done.refs_1_, f32[384,2048]{1,0:T(8,128)S(1)} %collective-permute-done.2.refs_2_, bf16[2048,512]{1,0:T(8,128)(2,1)S(1)} %copy-done.1, bf16[2048,512]{1,0:T(8,128)(2,1)S(1)} %copy-done.2), custom_call_target="tpu_custom_call" | custom-call | flops 805306368 | bytes 5505024 | tf_op jit(solution)/shard_map/product/pallas_call | solution.py:138
  172.1 0.0 collective-permute-done.3
  172.2 0.1 collective-permute-start.4
  172.2 0.0 collective-permute-done.10
  172.3 0.5 collective-permute-start.11
  172.7 1.7 product.19
  174.5 1.8 product.27
  176.3 2.3 %collective-permute-done.4 = f32[128,512]{1,0:T(8,128)S(1)} collective-permute-done((f32[128,512]{1,0:T(8,128)S(1)}, f32[128,512]{1,0:T(8,128)S(1)}, u32[]{:S(2)}, u32[]{:S(2)}) %collective-permute-start.4) | collective-permute-done | bytes 262176 | tf_op jit(solution)/shard_map/ppermute | solution.py:205
  178.6 1.0 collective-permute-start.5
  179.6 1.8 collective-permute-done.11
  181.4 0.1 collective-permute-start.12
  181.5 1.8 product.20
  183.3 1.8 product.28
  185.0 0.0 collective-permute-done.5
  185.1 1.0 collective-permute-start.6
  186.1 1.8 collective-permute-done.12
  187.9 1.0 collective-permute-start.13
  188.9 1.7 product.21
  190.7 1.8 product.29
  192.4 0.0 collective-permute-done.6
  192.5 0.1 collective-permute-start.7
  192.6 1.8 collective-permute-done.13
  194.4 1.2 collective-permute-start.14
  195.5 1.7 product.22
  197.3 1.8 product.30
  199.1 0.0 collective-permute-done.7
  199.1 2.3 %collective-permute-start.8 = (f32[128,512]{1,0:T(8,128)S(1)}, f32[128,512]{1,0:T(8,128)S(1)}, u32[]{:S(2)}, u32[]{:S(2)}) collective-permute-start(f32[128,512]{1,0:T(8,128)S(1)} %add.47), channel_id=1, source_target_pairs={{0,4},{1,3},{4,8},{5,1},{8,12},{9,5},{12,14},{13,9},{14,10},{15,13... | collective-permute-start | bytes 786440 | tf_op jit(solution)/shard_map/ppermute | solution.py:205
  201.4 0.3 collective-permute-done.14
  201.8 0.3 collective-permute-start.15
  202.0 1.7 product.23
  203.8 1.8 product.31
  205.5 0.0 collective-permute-done.8
  205.6 2.8 %collective-permute-done.15 = f32[128,512]{1,0:T(8,128)S(1)} collective-permute-done((f32[128,512]{1,0:T(8,128)S(1)}, f32[128,512]{1,0:T(8,128)S(1)}, u32[]{:S(2)}, u32[]{:S(2)}) %collective-permute-start.15) | collective-permute-done | bytes 262176 | tf_op jit(solution)/shard_map/ppermute | solution.py:205
  208.4 0.8 pad_maximum_fusion
  (15 shorter events, 0.5 us)
Async XLA Ops:
  96.4 60.4 %collective-permute-start.2 = (f32[384,2048]{1,0:T(8,128)}, f32[384,2048]{1,0:T(8,128)S(1)}, u32[]{:S(2)}, u32[]{:S(2)}) collective-permute-start(f32[384,2048]{1,0:T(8,128)} %pick.3), channel_id=1, source_target_pairs={{0,1},{1,0},{2,3},{3,2},{4,5},{5,4},{6,7},{7,6},{8,9},{9,8},{10,11... | collective-permute-start | bytes 9437192 | tf_op jit(solution)/shard_map/ppermute | solution.py:200
  129.8 13.4 %collective-permute-start = (f32[128,2048]{1,0:T(8,128)}, f32[128,2048]{1,0:T(8,128)}, u32[]{:S(2)}, u32[]{:S(2)}) collective-permute-start(f32[128,2048]{1,0:T(8,128)} %pick.2), channel_id=1, source_target_pairs={{0,1},{1,0},{2,3},{3,2},{4,5},{5,4},{6,7},{7,6},{8,9},{9,8},{10,11... | collective-permute-start | bytes 3145736 | tf_op jit(solution)/shard_map/ppermute | solution.py:199
  143.3 2.2 %copy-start = (f32[512,2048]{1,0:T(8,128)S(1)}, f32[512,2048]{1,0:T(8,128)}, u32[]{:S(2)}) copy-start(f32[512,2048]{1,0:T(8,128)} %refs_0_.31) | copy-start | bytes 12582916
  145.5 1.6 copy-start.3
  147.1 1.6 copy-start.4
  148.6 4.8 %copy-start.1 = (bf16[2048,512]{1,0:T(8,128)(2,1)S(1)}, bf16[2048,512]{1,0:T(8,128)(2,1)}, u32[]{:S(2)}) copy-start(bf16[2048,512]{1,0:T(8,128)(2,1)} %get-tuple-element.11.refs_2_.refs_3_) | copy-start | bytes 6291460
  148.6 4.8 %copy-start.2 = (bf16[2048,512]{1,0:T(8,128)(2,1)S(1)}, bf16[2048,512]{1,0:T(8,128)(2,1)}, u32[]{:S(2)}) copy-start(bf16[2048,512]{1,0:T(8,128)(2,1)} %get-tuple-element.12.refs_3_.refs_4_) | copy-start | bytes 6291460
  150.4 8.2 %collective-permute-start.1 = (f32[128,512]{1,0:T(8,128)S(1)}, f32[128,512]{1,0:T(8,128)S(1)}, u32[]{:S(2)}, u32[]{:S(2)}) collective-permute-start(f32[128,512]{1,0:T(8,128)S(1)} %product.16), channel_id=1, source_target_pairs={{0,4},{1,3},{4,8},{5,1},{8,12},{9,5},{12,14},{13,9},{14,10},{15,13... | collective-permute-start | bytes 786440 | tf_op jit(solution)/shard_map/ppermute | solution.py:205
  153.5 3.4 %copy-start.5 = (bf16[2048,512]{1,0:T(8,128)(2,1)S(1)}, bf16[2048,512]{1,0:T(8,128)(2,1)}, u32[]{:S(2)}) copy-start(bf16[2048,512]{1,0:T(8,128)(2,1)} %get-tuple-element.10.refs_3_.refs_4_) | copy-start | bytes 6291460
  155.2 8.1 %collective-permute-start.9 = (f32[128,512]{1,0:T(8,128)S(1)}, f32[128,512]{1,0:T(8,128)S(1)}, u32[]{:S(2)}, u32[]{:S(2)}) collective-permute-start(f32[128,512]{1,0:T(8,128)S(1)} %product.24), channel_id=1, source_target_pairs={{0,4},{1,3},{4,8},{5,1},{8,12},{9,5},{12,14},{13,9},{14,10},{15,13... | collective-permute-start | bytes 786440 | tf_op jit(solution)/shard_map/ppermute | solution.py:205
  158.7 13.4 %collective-permute-start.3 = (f32[128,512]{1,0:T(8,128)S(1)}, f32[128,512]{1,0:T(8,128)S(1)}, u32[]{:S(2)}, u32[]{:S(2)}) collective-permute-start(f32[128,512]{1,0:T(8,128)S(1)} %add.42), channel_id=1, source_target_pairs={{0,4},{1,3},{4,8},{5,1},{8,12},{9,5},{12,14},{13,9},{14,10},{15,13... | collective-permute-start | bytes 786440 | tf_op jit(solution)/shard_map/ppermute | solution.py:205
  163.4 8.8 %collective-permute-start.10 = (f32[128,512]{1,0:T(8,128)S(1)}, f32[128,512]{1,0:T(8,128)S(1)}, u32[]{:S(2)}, u32[]{:S(2)}) collective-permute-start(f32[128,512]{1,0:T(8,128)S(1)} %add.49), channel_id=1, source_target_pairs={{0,4},{1,3},{4,8},{5,1},{8,12},{9,5},{12,14},{13,9},{14,10},{15,13... | collective-permute-start | bytes 786440 | tf_op jit(solution)/shard_map/ppermute | solution.py:205
  172.2 6.4 %collective-permute-start.4 = (f32[128,512]{1,0:T(8,128)S(1)}, f32[128,512]{1,0:T(8,128)S(1)}, u32[]{:S(2)}, u32[]{:S(2)}) collective-permute-start(f32[128,512]{1,0:T(8,128)S(1)} %add.43), channel_id=1, source_target_pairs={{0,4},{1,3},{4,8},{5,1},{8,12},{9,5},{12,14},{13,9},{14,10},{15,13... | collective-permute-start | bytes 786440 | tf_op jit(solution)/shard_map/ppermute | solution.py:205
  172.3 9.1 %collective-permute-start.11 = (f32[128,512]{1,0:T(8,128)S(1)}, f32[128,512]{1,0:T(8,128)S(1)}, u32[]{:S(2)}, u32[]{:S(2)}) collective-permute-start(f32[128,512]{1,0:T(8,128)S(1)} %add.50), channel_id=1, source_target_pairs={{0,4},{1,3},{4,8},{5,1},{8,12},{9,5},{12,14},{13,9},{14,10},{15,13... | collective-permute-start | bytes 786440 | tf_op jit(solution)/shard_map/ppermute | solution.py:205
  178.6 6.4 %collective-permute-start.5 = (f32[128,512]{1,0:T(8,128)S(1)}, f32[128,512]{1,0:T(8,128)S(1)}, u32[]{:S(2)}, u32[]{:S(2)}) collective-permute-start(f32[128,512]{1,0:T(8,128)S(1)} %add.44), channel_id=1, source_target_pairs={{0,4},{1,3},{4,8},{5,1},{8,12},{9,5},{12,14},{13,9},{14,10},{15,13... | collective-permute-start | bytes 786440 | tf_op jit(solution)/shard_map/ppermute | solution.py:205
  181.4 6.4 %collective-permute-start.12 = (f32[128,512]{1,0:T(8,128)S(1)}, f32[128,512]{1,0:T(8,128)S(1)}, u32[]{:S(2)}, u32[]{:S(2)}) collective-permute-start(f32[128,512]{1,0:T(8,128)S(1)} %add.51), channel_id=1, source_target_pairs={{0,4},{1,3},{4,8},{5,1},{8,12},{9,5},{12,14},{13,9},{14,10},{15,13... | collective-permute-start | bytes 786440 | tf_op jit(solution)/shard_map/ppermute | solution.py:205
  185.1 7.3 %collective-permute-start.6 = (f32[128,512]{1,0:T(8,128)S(1)}, f32[128,512]{1,0:T(8,128)S(1)}, u32[]{:S(2)}, u32[]{:S(2)}) collective-permute-start(f32[128,512]{1,0:T(8,128)S(1)} %add.45), channel_id=1, source_target_pairs={{0,4},{1,3},{4,8},{5,1},{8,12},{9,5},{12,14},{13,9},{14,10},{15,13... | collective-permute-start | bytes 786440 | tf_op jit(solution)/shard_map/ppermute | solution.py:205
  187.9 6.4 %collective-permute-start.13 = (f32[128,512]{1,0:T(8,128)S(1)}, f32[128,512]{1,0:T(8,128)S(1)}, u32[]{:S(2)}, u32[]{:S(2)}) collective-permute-start(f32[128,512]{1,0:T(8,128)S(1)} %add.52), channel_id=1, source_target_pairs={{0,4},{1,3},{4,8},{5,1},{8,12},{9,5},{12,14},{13,9},{14,10},{15,13... | collective-permute-start | bytes 786440 | tf_op jit(solution)/shard_map/ppermute | solution.py:205
  192.5 6.6 %collective-permute-start.7 = (f32[128,512]{1,0:T(8,128)S(1)}, f32[128,512]{1,0:T(8,128)S(1)}, u32[]{:S(2)}, u32[]{:S(2)}) collective-permute-start(f32[128,512]{1,0:T(8,128)S(1)} %add.46), channel_id=1, source_target_pairs={{0,4},{1,3},{4,8},{5,1},{8,12},{9,5},{12,14},{13,9},{14,10},{15,13... | collective-permute-start | bytes 786440 | tf_op jit(solution)/shard_map/ppermute | solution.py:205
  194.4 7.3 %collective-permute-start.14 = (f32[128,512]{1,0:T(8,128)S(1)}, f32[128,512]{1,0:T(8,128)S(1)}, u32[]{:S(2)}, u32[]{:S(2)}) collective-permute-start(f32[128,512]{1,0:T(8,128)S(1)} %add.53), channel_id=1, source_target_pairs={{0,4},{1,3},{4,8},{5,1},{8,12},{9,5},{12,14},{13,9},{14,10},{15,13... | collective-permute-start | bytes 786440 | tf_op jit(solution)/shard_map/ppermute | solution.py:205
  199.1 6.4 %collective-permute-start.8 = (f32[128,512]{1,0:T(8,128)S(1)}, f32[128,512]{1,0:T(8,128)S(1)}, u32[]{:S(2)}, u32[]{:S(2)}) collective-permute-start(f32[128,512]{1,0:T(8,128)S(1)} %add.47), channel_id=1, source_target_pairs={{0,4},{1,3},{4,8},{5,1},{8,12},{9,5},{12,14},{13,9},{14,10},{15,13... | collective-permute-start | bytes 786440 | tf_op jit(solution)/shard_map/ppermute | solution.py:205
  201.8 6.6 %collective-permute-start.15 = (f32[128,512]{1,0:T(8,128)S(1)}, f32[128,512]{1,0:T(8,128)S(1)}, u32[]{:S(2)}, u32[]{:S(2)}) collective-permute-start(f32[128,512]{1,0:T(8,128)S(1)} %add.54), channel_id=1, source_target_pairs={{0,4},{1,3},{4,8},{5,1},{8,12},{9,5},{12,14},{13,9},{14,10},{15,13... | collective-permute-start | bytes 786440 | tf_op jit(solution)/shard_map/ppermute | solution.py:205

commit v3 on v2

--- a/solution.py
+++ b/solution.py
@@ -45,7 +45,8 @@
     return found
 
 
-def pick_kernel(starts, size, a_ref, out_ref, sems):
+def pick_kernel(starts, size, a_ref, *refs):
+    out_ref, sems = refs[-2:]
     copies = []
     for index in range(starts.shape[-1]):
         start = pl.multiple_of(looked_up(starts[..., index]), size)
@@ -60,18 +61,19 @@
         copy.wait()
 
 
-def pick(inductance, starts, size):
+def pick(inductance, starts, size, *after):
     count = starts.shape[-1]
     width = inductance.shape[1]
     return pl.pallas_call(
         functools.partial(pick_kernel, starts, size),
         out_shape=jax.ShapeDtypeStruct((count * size, width), jnp.float32),
-        in_specs=[pl.BlockSpec(memory_space=pl.ANY)],
-        out_specs=pl.BlockSpec(memory_space=pl.ANY),
+        in_specs=[pl.BlockSpec(memory_space=pl.ANY)] * (1 + len(after)),
+        out_specs=pl.BlockSpec(memory_space=pltpu.VMEM),
         scratch_shapes=[pltpu.SemaphoreType.DMA((count,))],
+        compiler_params=pltpu.CompilerParams(vmem_limit_bytes=8 * 2**20),
         cost_estimate=pl.CostEstimate(flops=0, bytes_accessed=8 * count * size * width, transcendentals=0),
         name="pick",
-    )(inductance)
+    )(inductance, *after)
 
 
 def halves(value):
@@ -86,7 +88,7 @@
 def split(current_rates, part, parts):
     depth, width = current_rates.shape
     width //= parts
-    tile = 256
+    tile = min(512, depth)
     out = jax.ShapeDtypeStruct((depth, width), jnp.bfloat16)
     return pl.pallas_call(
         split_kernel,
@@ -94,54 +96,56 @@
         out_shape=(out, out),
         in_specs=[pl.BlockSpec((tile, width), lambda k: (k, part))],
         out_specs=[pl.BlockSpec((tile, width), lambda k: (k, 0))] * 2,
+        compiler_params=pltpu.CompilerParams(vmem_limit_bytes=8 * 2**20),
         cost_estimate=pl.CostEstimate(flops=4 * depth * width, bytes_accessed=8 * depth * width, transcendentals=0),
         name="split",
     )(current_rates)
 
 
-def product_kernel(starts, size, bounds, *refs):
+def product_kernel(starts, size, bounds, parts, *refs):
     count = len(bounds)
-    sources, (high_ref, low_ref, out_ref, raw, stack, sems) = refs[:count], refs[count:]
+    sources, pairs, outs = refs[:count], refs[count : count + 2 * parts], refs[count + 2 * parts : -3]
+    raw, stack, sems = refs[-3:]
     depth = raw.shape[0]
-
-    @pl.when(pl.program_id(0) == 0)
-    def _():
-        for index in range(starts.shape[-1]):
-            start = looked_up(starts[..., index])
-            first = 0
-            for source, last in zip(sources, bounds):
-
-                @pl.when((start >= first) & (start < last))
-                def _(source=source, first=first, start=start, index=index):
-                    pltpu.make_async_copy(
-                        source.at[pl.ds(pl.multiple_of(start - first, size), size)],
-                        raw.at[pl.ds(index * size, size)],
-                        sems.at[index],
-                    ).start()
-
-                first = last
-        for index in range(starts.shape[-1]):
-            pltpu.make_async_copy(
-                sources[0].at[pl.ds(0, size)], raw.at[pl.ds(index * size, size)], sems.at[index]
-            ).wait()
-        stack[:depth], stack[depth:] = halves(raw[...])
-
-    both = jnp.dot(stack[...], high_ref[...], preferred_element_type=jnp.float32)
-    rest = jnp.dot(stack[:depth], low_ref[...], preferred_element_type=jnp.float32)
-    out_ref[...] = both[:depth] + (both[depth:] + rest)
-
-
-def product(sources, starts, size, high, low):
+    for index in range(starts.shape[-1]):
+        start = looked_up(starts[..., index])
+        first = 0
+        for source, last in zip(sources, bounds):
+
+            @pl.when((start >= first) & (start < last))
+            def _(source=source, first=first, start=start, index=index):
+                pltpu.make_async_copy(
+                    source.at[pl.ds(pl.multiple_of(start - first, size), size)],
+                    raw.at[pl.ds(index * size, size)],
+                    sems.at[index],
+                ).start()
+
+            first = last
+    for index in range(starts.shape[-1]):
+        pltpu.make_async_copy(
+            sources[0].at[pl.ds(0, size)], raw.at[pl.ds(index * size, size)], sems.at[index]
+        ).wait()
+    stack[:depth], stack[depth:] = halves(raw[...])
+    for part in range(parts):
+        high_ref, low_ref, out_ref = pairs[2 * part], pairs[2 * part + 1], outs[part]
+        width = out_ref.shape[1]
+        tile = min(LANES, width)
+        for at in range(0, width, tile):
+            both = jnp.dot(stack[...], high_ref[:, at : at + tile], preferred_element_type=jnp.float32)
+            rest = jnp.dot(stack[:depth], low_ref[:, at : at + tile], preferred_element_type=jnp.float32)
+            out_ref[:, at : at + tile] = both[:depth] + (both[depth:] + rest)
+
+
+def product(sources, starts, size, pairs):
     depth = starts.shape[-1] * size
-    inner, width = high.shape
-    tile = min(LANES, width)
+    inner, width = pairs[0].shape
+    parts = len(pairs) // 2
     return pl.pallas_call(
-        functools.partial(product_kernel, starts, size, list(np.cumsum([s.shape[0] for s in sources]))),
-        grid=(width // tile,),
-        out_shape=jax.ShapeDtypeStruct((depth, width), jnp.float32),
+        functools.partial(product_kernel, starts, size, list(np.cumsum([s.shape[0] for s in sources])), parts),
+        out_shape=[jax.ShapeDtypeStruct((depth, width), jnp.float32)] * parts,
         in_specs=[pl.BlockSpec(memory_space=pl.ANY)] * len(sources)
-        + [pl.BlockSpec((inner, tile), lambda j: (0, j))] * 2,
-        out_specs=pl.BlockSpec((depth, tile), lambda j: (0, j)),
+        + [pl.BlockSpec(memory_space=pltpu.VMEM)] * len(pairs),
+        out_specs=[pl.BlockSpec(memory_space=pltpu.VMEM)] * parts,
         scratch_shapes=[
             pltpu.VMEM((depth, inner), jnp.float32),
             pltpu.VMEM((2 * depth, inner), jnp.bfloat16),
@@ -149,12 +153,12 @@
         ],
         compiler_params=pltpu.CompilerParams(vmem_limit_bytes=16 * 2**20),
         cost_estimate=pl.CostEstimate(
-            flops=6 * depth * inner * width,
-            bytes_accessed=4 * depth * inner + 4 * inner * width + 4 * depth * width,
+            flops=6 * depth * inner * width * parts,
+            bytes_accessed=4 * depth * inner + 4 * inner * width * parts + 4 * depth * width * parts,
             transcendentals=0,
         ),
         name="product",
-    )(*sources, high, low)
+    )(*sources, *pairs)
 
 
 def plan(order, rows, cols, size):
@@ -196,18 +200,19 @@
     def shards(inductance, current_rates):
         size = inductance.shape[0] * cols // rows
         taken, given = plan(order, rows, cols, size)
-        soon = lax.ppermute(pick(inductance, given[..., :group], size), "col", swap)
-        late = lax.ppermute(pick(inductance, given[..., group:], size), "col", swap)
+        picked = pick(inductance, given[..., :group], size)
+        soon = lax.ppermute(picked, "col", swap)
+        late = lax.ppermute(pick(inductance, given[..., group:], size, picked), "col", swap)
         rates = [split(current_rates, part, 2) for part in range(2)]
-        first = [product([inductance, soon], taken[..., :group], size, *pair) for pair in rates]
-        sums = [part[:size] for part in first]
+        terms = [product([inductance, soon], taken[..., :group], size, pair)[0] for pair in rates]
+        sums = [term[:size] for term in terms]
         for step in range(1, rows):
             passed = [lax.ppermute(part, ("row", "col"), around) for part in sums]
             if step % group == 0:
                 starts = taken[..., step : step + group]
-                first = [product([inductance, soon, late], starts, size, *pair) for pair in rates]
+                terms = product([inductance, soon, late], starts, size, rates[0] + rates[1])
             at = step % group * size
-            sums = [got + part[at : at + size] for got, part in zip(passed, first)]
+            sums = [got + term[at : at + size] for got, term in zip(passed, terms)]
         return jnp.concatenate(sums, axis=1)
 
     placed = (P(("groups", "col"), "row"), P("row", ("groups", "col")))

time: 210 us -> 61.5 us (0.29)
  Pallas kernels: 173 us -> 17.6 us
  starting transfers between devices: 18.5 us -> 26 us
    pallas_call x2, Pallas kernels: 129 us -> 0.36 us  [pick(): pl.pallas_call(functools.partial(pick_kernel, starts, size), out_shape=ja...]
    pallas_call x16 -> x9, Pallas kernels: 30.3 us -> 15.4 us  [product(): pl.pallas_call(functools.partial(product_kernel, starts, size, list(np.cu...]
    pallas_call x2, Pallas kernels: 13.3 us -> 1.82 us  [split(): pl.pallas_call(split_kernel, grid=(depth // tile,), out_shape=(out, out),...]
    ppermute x14, starting transfers between devices: 17.9 us -> 25.4 us  [shards(): passed = [lax.ppermute(part, ('row', 'col'), around) for part in sums]]
    ppermute x2, waiting for transfers between devices: 0.01 us -> 2.38 us  [the longest x1 2.38 us: shards(): soon = lax.ppermute(picked, 'col', swap)]
    unnamed x12 -> x6, local copies, waits for them, and re-layouts: 5.38 us -> 4.68 us
  transfers between devices with their start and end apart: 16 -> 16, of which waited for: 6 -> 9; matrix products, arithmetic and copies ran while one was open for 0% -> 1% of each run, Pallas kernels for 37% -> 28%
where the time goes in v3:
time: 61.5 us; the launch traced here: 61.3 us
  starting transfers between devices  26 us (42%)
  Pallas kernels  17.6 us (29%)
  waiting for transfers between devices  11.6 us (19%)
  local copies, waits for them, and re-layouts  4.68 us (8%)
  other arithmetic  1.34 us (2%)
    ppermute x14, starting transfers between devices, shards(): passed = [lax.ppermute(part, ('row', 'col'), around) for part in sums]  25.4 us
    pallas_call x9, Pallas kernels, product(): pl.pallas_call(functools.partial(product_kernel, starts, size, list(np.cu...  15.4 us
    ppermute x14, waiting for transfers between devices, shards(): passed = [lax.ppermute(part, ('row', 'col'), around) for part in sums]  9.17 us
    unnamed x6, local copies, waits for them, and re-layouts  4.68 us
    ppermute x1, waiting for transfers between devices, shards(): soon = lax.ppermute(picked, 'col', swap)  2.38 us
    pallas_call x2, Pallas kernels, split(): pl.pallas_call(split_kernel, grid=(depth // tile,), out_shape=(out, out),...  1.82 us
  transfers between devices with their start and end apart: 16, of which 9 were waited for; matrix products, arithmetic and copies ran while one was open for 1% of the time, Pallas kernels for 28%

profile of v3, /device:TPU:0, one launch (start us, length us, event | category | flops | bytes accessed | tf_op | source)
XLA Modules:
  0.0 61.3 jit_solution(6656892670065117886)
XLA Ops:
  0.0 0.0 copy-start
  0.0 2.2 %copy-done = f32[512,2048]{1,0:T(8,128)S(1)} copy-done((f32[512,2048]{1,0:T(8,128)S(1)}, f32[512,2048]{1,0:T(8,128)}, u32[]{:S(2)}) %copy-start) | copy-done | bytes 4194328
  2.2 0.1 pick.2.refs_0_
  2.3 0.0 copy-start.2
  2.3 0.3 pick.3
  2.6 0.5 collective-permute-start.2
  3.1 0.1 collective-permute-start
  3.2 2.5 %copy-done.2 = f32[2048,1024]{1,0:T(8,128)S(1)} copy-done((f32[2048,1024]{1,0:T(8,128)S(1)}, f32[2048,1024]{1,0:T(8,128)}, u32[]{:S(2)}) %copy-start.2) | copy-done | bytes 8388632
  5.7 0.9 %split.3 = (bf16[2048,512]{1,0:T(8,128)(2,1)S(1)}, bf16[2048,512]{1,0:T(8,128)(2,1)S(1)}) custom-call(f32[2048,1024]{1,0:T(8,128)S(1)} %copy-done.2), custom_call_target="tpu_custom_call" | custom-call | flops 4194304 | bytes 8388608 | tf_op jit(solution)/shard_map/split/pallas_call | solution.py:93
  6.6 0.0 copy-start.1
  6.6 0.9 %split.2 = (bf16[2048,512]{1,0:T(8,128)(2,1)S(1)}, bf16[2048,512]{1,0:T(8,128)(2,1)S(1)}) custom-call(f32[2048,1024]{1,0:T(8,128)S(1)} %copy-done.2), custom_call_target="tpu_custom_call" | custom-call | flops 4194304 | bytes 8388608 | tf_op jit(solution)/shard_map/split/pallas_call | solution.py:93
  7.5 2.4 %collective-permute-done.refs_1_ = f32[128,2048]{1,0:T(8,128)S(1)} collective-permute-done((f32[128,2048]{1,0:T(8,128)S(1)}, f32[128,2048]{1,0:T(8,128)S(1)}, u32[]{:S(2)}, u32[]{:S(2)}) %collective-permute-start) | collective-permute-done | bytes 1048608 | tf_op jit(solution)/shard_map/ppermute | solution.py:204
  9.9 0.0 copy-done.1
  9.9 1.1 %product.17 = f32[128,512]{1,0:T(8,128)S(1)} custom-call(f32[512,2048]{1,0:T(8,128)S(1)} %copy-done.1, f32[128,2048]{1,0:T(8,128)S(1)} %collective-permute-done.refs_1_, bf16[2048,512]{1,0:T(8,128)(2,1)S(1)} %get-tuple-element.25.refs_5_.refs_2_, bf16[2048,512]{1,0:T(8,128)(2,1)S(1)} %get-tuple-element.26.refs_6_.refs_3_), custom_call_target="tpu_custom_call" | custom-call | flops 805306368 | bytes 5505024 | tf_op jit(solution)/shard_map/product/pallas_call | solution.py:143
  11.0 3.0 %collective-permute-start.9 = (f32[128,512]{1,0:T(8,128)S(1)}, f32[128,512]{1,0:T(8,128)S(1)}, u32[]{:S(2)}, u32[]{:S(2)}) collective-permute-start(f32[128,512]{1,0:T(8,128)S(1)} %product.17), channel_id=1, source_target_pairs={{0,4},{1,3},{4,8},{5,1},{8,12},{9,5},{12,14},{13,9},{14,10},{15,13... | collective-permute-start | bytes 786440 | tf_op jit(solution)/shard_map/ppermute | solution.py:210
  13.9 1.1 %product.9 = f32[128,512]{1,0:T(8,128)S(1)} custom-call(f32[512,2048]{1,0:T(8,128)S(1)} %copy-done.1, f32[128,2048]{1,0:T(8,128)S(1)} %collective-permute-done.refs_1_, bf16[2048,512]{1,0:T(8,128)(2,1)S(1)} %get-tuple-element.23.refs_2_.refs_3_, bf16[2048,512]{1,0:T(8,128)(2,1)S(1)} %get-tuple-element.24.refs_3_.refs_4_), custom_call_target="tpu_custom_call" | custom-call | flops 805306368 | bytes 5505024 | tf_op jit(solution)/shard_map/product/pallas_call | solution.py:143
  15.0 1.6 %collective-permute-start.1 = (f32[128,512]{1,0:T(8,128)S(1)}, f32[128,512]{1,0:T(8,128)S(1)}, u32[]{:S(2)}, u32[]{:S(2)}) collective-permute-start(f32[128,512]{1,0:T(8,128)S(1)} %product.9), channel_id=1, source_target_pairs={{0,4},{1,3},{4,8},{5,1},{8,12},{9,5},{12,14},{13,9},{14,10},{15,13... | collective-permute-start | bytes 786440 | tf_op jit(solution)/shard_map/ppermute | solution.py:210
  16.6 0.0 collective-permute-done.2.refs_2_
  16.6 1.9 %product.10 = (f32[128,512]{1,0:T(8,128)S(1)}, f32[128,512]{1,0:T(8,128)S(1)}) custom-call(f32[512,2048]{1,0:T(8,128)S(1)} %copy-done.1, f32[128,2048]{1,0:T(8,128)S(1)} %collective-permute-done.refs_1_, f32[384,2048]{1,0:T(8,128)S(1)} %collective-permute-done.2.refs_2_, bf16[2048,512]{1,0:T(8,128)(2,1)S(1)} %get-tuple-element.23.refs_2_.refs_3_, ...), custom_call_target="tpu_custom_call" | custom-call | flops 1610612736 | bytes 9961472 | tf_op jit(solution)/shard_map/product/pallas_call | solution.py:143
  18.5 0.0 collective-permute-done.9
  18.6 1.8 %collective-permute-start.10 = (f32[128,512]{1,0:T(8,128)S(1)}, f32[128,512]{1,0:T(8,128)S(1)}, u32[]{:S(2)}, u32[]{:S(2)}) collective-permute-start(f32[128,512]{1,0:T(8,128)S(1)} %add.49), channel_id=1, source_target_pairs={{0,4},{1,3},{4,8},{5,1},{8,12},{9,5},{12,14},{13,9},{14,10},{15,13... | collective-permute-start | bytes 786440 | tf_op jit(solution)/shard_map/ppermute | solution.py:210
  20.4 1.0 %collective-permute-done.1 = f32[128,512]{1,0:T(8,128)S(1)} collective-permute-done((f32[128,512]{1,0:T(8,128)S(1)}, f32[128,512]{1,0:T(8,128)S(1)}, u32[]{:S(2)}, u32[]{:S(2)}) %collective-permute-start.1) | collective-permute-done | bytes 262176 | tf_op jit(solution)/shard_map/ppermute | solution.py:210
  21.5 1.7 %collective-permute-start.3 = (f32[128,512]{1,0:T(8,128)S(1)}, f32[128,512]{1,0:T(8,128)S(1)}, u32[]{:S(2)}, u32[]{:S(2)}) collective-permute-start(f32[128,512]{1,0:T(8,128)S(1)} %add.42), channel_id=1, source_target_pairs={{0,4},{1,3},{4,8},{5,1},{8,12},{9,5},{12,14},{13,9},{14,10},{15,13... | collective-permute-start | bytes 786440 | tf_op jit(solution)/shard_map/ppermute | solution.py:210
  23.2 1.9 %product.11 = (f32[128,512]{1,0:T(8,128)S(1)}, f32[128,512]{1,0:T(8,128)S(1)}) custom-call(f32[512,2048]{1,0:T(8,128)S(1)} %copy-done.1, f32[128,2048]{1,0:T(8,128)S(1)} %collective-permute-done.refs_1_, f32[384,2048]{1,0:T(8,128)S(1)} %collective-permute-done.2.refs_2_, bf16[2048,512]{1,0:T(8,128)(2,1)S(1)} %get-tuple-element.23.refs_2_.refs_3_, ...), custom_call_target="tpu_custom_call" | custom-call | flops 1610612736 | bytes 9961472 | tf_op jit(solution)/shard_map/product/pallas_call | solution.py:143
  25.1 0.0 collective-permute-done.10
  25.2 1.7 %collective-permute-start.11 = (f32[128,512]{1,0:T(8,128)S(1)}, f32[128,512]{1,0:T(8,128)S(1)}, u32[]{:S(2)}, u32[]{:S(2)}) collective-permute-start(f32[128,512]{1,0:T(8,128)S(1)} %add.50), channel_id=1, source_target_pairs={{0,4},{1,3},{4,8},{5,1},{8,12},{9,5},{12,14},{13,9},{14,10},{15,13... | collective-permute-start | bytes 786440 | tf_op jit(solution)/shard_map/ppermute | solution.py:210
  26.9 1.0 %collective-permute-done.3 = f32[128,512]{1,0:T(8,128)S(1)} collective-permute-done((f32[128,512]{1,0:T(8,128)S(1)}, f32[128,512]{1,0:T(8,128)S(1)}, u32[]{:S(2)}, u32[]{:S(2)}) %collective-permute-start.3) | collective-permute-done | bytes 262176 | tf_op jit(solution)/shard_map/ppermute | solution.py:210
  27.9 1.7 %collective-permute-start.4 = (f32[128,512]{1,0:T(8,128)S(1)}, f32[128,512]{1,0:T(8,128)S(1)}, u32[]{:S(2)}, u32[]{:S(2)}) collective-permute-start(f32[128,512]{1,0:T(8,128)S(1)} %add.43), channel_id=1, source_target_pairs={{0,4},{1,3},{4,8},{5,1},{8,12},{9,5},{12,14},{13,9},{14,10},{15,13... | collective-permute-start | bytes 786440 | tf_op jit(solution)/shard_map/ppermute | solution.py:210
  29.7 1.9 %product.12 = (f32[128,512]{1,0:T(8,128)S(1)}, f32[128,512]{1,0:T(8,128)S(1)}) custom-call(f32[512,2048]{1,0:T(8,128)S(1)} %copy-done.1, f32[128,2048]{1,0:T(8,128)S(1)} %collective-permute-done.refs_1_, f32[384,2048]{1,0:T(8,128)S(1)} %collective-permute-done.2.refs_2_, bf16[2048,512]{1,0:T(8,128)(2,1)S(1)} %get-tuple-element.23.refs_2_.refs_3_, ...), custom_call_target="tpu_custom_call" | custom-call | flops 1610612736 | bytes 9961472 | tf_op jit(solution)/shard_map/product/pallas_call | solution.py:143
  31.6 0.0 collective-permute-done.11
  31.6 1.7 %collective-permute-start.12 = (f32[128,512]{1,0:T(8,128)S(1)}, f32[128,512]{1,0:T(8,128)S(1)}, u32[]{:S(2)}, u32[]{:S(2)}) collective-permute-start(f32[128,512]{1,0:T(8,128)S(1)} %add.51), channel_id=1, source_target_pairs={{0,4},{1,3},{4,8},{5,1},{8,12},{9,5},{12,14},{13,9},{14,10},{15,13... | collective-permute-start | bytes 786440 | tf_op jit(solution)/shard_map/ppermute | solution.py:210
  33.3 1.0 %collective-permute-done.4 = f32[128,512]{1,0:T(8,128)S(1)} collective-permute-done((f32[128,512]{1,0:T(8,128)S(1)}, f32[128,512]{1,0:T(8,128)S(1)}, u32[]{:S(2)}, u32[]{:S(2)}) %collective-permute-start.4) | collective-permute-done | bytes 262176 | tf_op jit(solution)/shard_map/ppermute | solution.py:210
  34.4 1.7 %collective-permute-start.5 = (f32[128,512]{1,0:T(8,128)S(1)}, f32[128,512]{1,0:T(8,128)S(1)}, u32[]{:S(2)}, u32[]{:S(2)}) collective-permute-start(f32[128,512]{1,0:T(8,128)S(1)} %add.44), channel_id=1, source_target_pairs={{0,4},{1,3},{4,8},{5,1},{8,12},{9,5},{12,14},{13,9},{14,10},{15,13... | collective-permute-start | bytes 786440 | tf_op jit(solution)/shard_map/ppermute | solution.py:210
  36.1 1.9 %product.13 = (f32[128,512]{1,0:T(8,128)S(1)}, f32[128,512]{1,0:T(8,128)S(1)}) custom-call(f32[512,2048]{1,0:T(8,128)S(1)} %copy-done.1, f32[128,2048]{1,0:T(8,128)S(1)} %collective-permute-done.refs_1_, f32[384,2048]{1,0:T(8,128)S(1)} %collective-permute-done.2.refs_2_, bf16[2048,512]{1,0:T(8,128)(2,1)S(1)} %get-tuple-element.23.refs_2_.refs_3_, ...), custom_call_target="tpu_custom_call" | custom-call | flops 1610612736 | bytes 9961472 | tf_op jit(solution)/shard_map/product/pallas_call | solution.py:143
  38.0 0.0 collective-permute-done.12
  38.1 1.7 %collective-permute-start.13 = (f32[128,512]{1,0:T(8,128)S(1)}, f32[128,512]{1,0:T(8,128)S(1)}, u32[]{:S(2)}, u32[]{:S(2)}) collective-permute-start(f32[128,512]{1,0:T(8,128)S(1)} %add.52), channel_id=1, source_target_pairs={{0,4},{1,3},{4,8},{5,1},{8,12},{9,5},{12,14},{13,9},{14,10},{15,13... | collective-permute-start | bytes 786440 | tf_op jit(solution)/shard_map/ppermute | solution.py:210
  39.8 1.0 %collective-permute-done.5 = f32[128,512]{1,0:T(8,128)S(1)} collective-permute-done((f32[128,512]{1,0:T(8,128)S(1)}, f32[128,512]{1,0:T(8,128)S(1)}, u32[]{:S(2)}, u32[]{:S(2)}) %collective-permute-start.5) | collective-permute-done | bytes 262176 | tf_op jit(solution)/shard_map/ppermute | solution.py:210
  40.9 1.7 %collective-permute-start.6 = (f32[128,512]{1,0:T(8,128)S(1)}, f32[128,512]{1,0:T(8,128)S(1)}, u32[]{:S(2)}, u32[]{:S(2)}) collective-permute-start(f32[128,512]{1,0:T(8,128)S(1)} %add.45), channel_id=1, source_target_pairs={{0,4},{1,3},{4,8},{5,1},{8,12},{9,5},{12,14},{13,9},{14,10},{15,13... | collective-permute-start | bytes 786440 | tf_op jit(solution)/shard_map/ppermute | solution.py:210
  42.6 1.9 %product.14 = (f32[128,512]{1,0:T(8,128)S(1)}, f32[128,512]{1,0:T(8,128)S(1)}) custom-call(f32[512,2048]{1,0:T(8,128)S(1)} %copy-done.1, f32[128,2048]{1,0:T(8,128)S(1)} %collective-permute-done.refs_1_, f32[384,2048]{1,0:T(8,128)S(1)} %collective-permute-done.2.refs_2_, bf16[2048,512]{1,0:T(8,128)(2,1)S(1)} %get-tuple-element.23.refs_2_.refs_3_, ...), custom_call_target="tpu_custom_call" | custom-call | flops 1610612736 | bytes 9961472 | tf_op jit(solution)/shard_map/product/pallas_call | solution.py:143
  44.5 0.0 collective-permute-done.13
  44.5 1.7 %collective-permute-start.14 = (f32[128,512]{1,0:T(8,128)S(1)}, f32[128,512]{1,0:T(8,128)S(1)}, u32[]{:S(2)}, u32[]{:S(2)}) collective-permute-start(f32[128,512]{1,0:T(8,128)S(1)} %add.53), channel_id=1, source_target_pairs={{0,4},{1,3},{4,8},{5,1},{8,12},{9,5},{12,14},{13,9},{14,10},{15,13... | collective-permute-start | bytes 786440 | tf_op jit(solution)/shard_map/ppermute | solution.py:210
  46.3 1.0 %collective-permute-done.6 = f32[128,512]{1,0:T(8,128)S(1)} collective-permute-done((f32[128,512]{1,0:T(8,128)S(1)}, f32[128,512]{1,0:T(8,128)S(1)}, u32[]{:S(2)}, u32[]{:S(2)}) %collective-permute-start.6) | collective-permute-done | bytes 262176 | tf_op jit(solution)/shard_map/ppermute | solution.py:210
  47.4 1.7 %collective-permute-start.7 = (f32[128,512]{1,0:T(8,128)S(1)}, f32[128,512]{1,0:T(8,128)S(1)}, u32[]{:S(2)}, u32[]{:S(2)}) collective-permute-start(f32[128,512]{1,0:T(8,128)S(1)} %add.46), channel_id=1, source_target_pairs={{0,4},{1,3},{4,8},{5,1},{8,12},{9,5},{12,14},{13,9},{14,10},{15,13... | collective-permute-start | bytes 786440 | tf_op jit(solution)/shard_map/ppermute | solution.py:210
  49.1 2.1 %product.15 = (f32[128,512]{1,0:T(8,128)S(1)}, f32[128,512]{1,0:T(8,128)S(1)}) custom-call(f32[512,2048]{1,0:T(8,128)S(1)} %copy-done.1, f32[128,2048]{1,0:T(8,128)S(1)} %collective-permute-done.refs_1_, f32[384,2048]{1,0:T(8,128)S(1)} %collective-permute-done.2.refs_2_, bf16[2048,512]{1,0:T(8,128)(2,1)S(1)} %get-tuple-element.23.refs_2_.refs_3_, ...), custom_call_target="tpu_custom_call" | custom-call | flops 1610612736 | bytes 9961472 | tf_op jit(solution)/shard_map/product/pallas_call | solution.py:143
  51.1 0.0 collective-permute-done.14
  51.2 1.6 %collective-permute-start.15 = (f32[128,512]{1,0:T(8,128)S(1)}, f32[128,512]{1,0:T(8,128)S(1)}, u32[]{:S(2)}, u32[]{:S(2)}) collective-permute-start(f32[128,512]{1,0:T(8,128)S(1)} %add.54), channel_id=1, source_target_pairs={{0,4},{1,3},{4,8},{5,1},{8,12},{9,5},{12,14},{13,9},{14,10},{15,13... | collective-permute-start | bytes 786440 | tf_op jit(solution)/shard_map/ppermute | solution.py:210
  52.8 1.0 %collective-permute-done.7 = f32[128,512]{1,0:T(8,128)S(1)} collective-permute-done((f32[128,512]{1,0:T(8,128)S(1)}, f32[128,512]{1,0:T(8,128)S(1)}, u32[]{:S(2)}, u32[]{:S(2)}) %collective-permute-start.7) | collective-permute-done | bytes 262176 | tf_op jit(solution)/shard_map/ppermute | solution.py:210
  53.8 1.7 %collective-permute-start.8 = (f32[128,512]{1,0:T(8,128)S(1)}, f32[128,512]{1,0:T(8,128)S(1)}, u32[]{:S(2)}, u32[]{:S(2)}) collective-permute-start(f32[128,512]{1,0:T(8,128)S(1)} %add.47), channel_id=1, source_target_pairs={{0,4},{1,3},{4,8},{5,1},{8,12},{9,5},{12,14},{13,9},{14,10},{15,13... | collective-permute-start | bytes 786440 | tf_op jit(solution)/shard_map/ppermute | solution.py:210
  55.5 1.9 %product.16 = (f32[128,512]{1,0:T(8,128)S(1)}, f32[128,512]{1,0:T(8,128)S(1)}) custom-call(f32[512,2048]{1,0:T(8,128)S(1)} %copy-done.1, f32[128,2048]{1,0:T(8,128)S(1)} %collective-permute-done.refs_1_, f32[384,2048]{1,0:T(8,128)S(1)} %collective-permute-done.2.refs_2_, bf16[2048,512]{1,0:T(8,128)(2,1)S(1)} %get-tuple-element.23.refs_2_.refs_3_, ...), custom_call_target="tpu_custom_call" | custom-call | flops 1610612736 | bytes 9961472 | tf_op jit(solution)/shard_map/product/pallas_call | solution.py:143
  57.4 0.2 collective-permute-done.15
  57.7 2.8 %collective-permute-done.8 = f32[128,512]{1,0:T(8,128)S(1)} collective-permute-done((f32[128,512]{1,0:T(8,128)S(1)}, f32[128,512]{1,0:T(8,128)S(1)}, u32[]{:S(2)}, u32[]{:S(2)}) %collective-permute-start.8) | collective-permute-done | bytes 262176 | tf_op jit(solution)/shard_map/ppermute | solution.py:210
  60.5 0.8 %pad_maximum_fusion = f32[128,1024]{1,0:T(8,128)} fusion(f32[128,512]{1,0:T(8,128)S(1)} %add.55, f32[128,512]{1,0:T(8,128)S(1)} %add.48), kind=kLoop, calls=%fused_computation | loop fusion | flops 131072 | bytes 1048576 | tf_op jit(solution)/shard_map/concatenate | solution.py:216
  (14 shorter events, 0.5 us)
Async XLA Ops:
  0.0 2.2 %copy-start = (f32[512,2048]{1,0:T(8,128)S(1)}, f32[512,2048]{1,0:T(8,128)}, u32[]{:S(2)}) copy-start(f32[512,2048]{1,0:T(8,128)} %refs_0_.17) | copy-start | bytes 12582916
  2.3 3.4 %copy-start.2 = (f32[2048,1024]{1,0:T(8,128)S(1)}, f32[2048,1024]{1,0:T(8,128)}, u32[]{:S(2)}) copy-start(f32[2048,1024]{1,0:T(8,128)} %value_ref.3) | copy-start | bytes 25165828
  2.6 14.1 %collective-permute-start.2 = (f32[384,2048]{1,0:T(8,128)S(1)}, f32[384,2048]{1,0:T(8,128)S(1)}, u32[]{:S(2)}, u32[]{:S(2)}) collective-permute-start(f32[384,2048]{1,0:T(8,128)S(1)} %pick.3), channel_id=1, source_target_pairs={{0,1},{1,0},{2,3},{3,2},{4,5},{5,4},{6,7},{7,6},{8,9},{9,8},{10,11... | collective-permute-start | bytes 9437192 | tf_op jit(solution)/shard_map/ppermute | solution.py:205
  3.1 6.8 %collective-permute-start = (f32[128,2048]{1,0:T(8,128)S(1)}, f32[128,2048]{1,0:T(8,128)S(1)}, u32[]{:S(2)}, u32[]{:S(2)}) collective-permute-start(f32[128,2048]{1,0:T(8,128)S(1)} %pick.2.refs_0_), channel_id=1, source_target_pairs={{0,1},{1,0},{2,3},{3,2},{4,5},{5,4},{6,7},{7,6},{8,9},{9,8},{10,11... | collective-permute-start | bytes 3145736 | tf_op jit(solution)/shard_map/ppermute | solution.py:204
  6.6 3.3 %copy-start.1 = (f32[512,2048]{1,0:T(8,128)S(1)}, f32[512,2048]{1,0:T(8,128)}, u32[]{:S(2)}) copy-start(f32[512,2048]{1,0:T(8,128)} %refs_0_.17) | copy-start | bytes 12582916
  11.0 7.6 %collective-permute-start.9 = (f32[128,512]{1,0:T(8,128)S(1)}, f32[128,512]{1,0:T(8,128)S(1)}, u32[]{:S(2)}, u32[]{:S(2)}) collective-permute-start(f32[128,512]{1,0:T(8,128)S(1)} %product.17), channel_id=1, source_target_pairs={{0,4},{1,3},{4,8},{5,1},{8,12},{9,5},{12,14},{13,9},{14,10},{15,13... | collective-permute-start | bytes 786440 | tf_op jit(solution)/shard_map/ppermute | solution.py:210
  15.0 6.4 %collective-permute-start.1 = (f32[128,512]{1,0:T(8,128)S(1)}, f32[128,512]{1,0:T(8,128)S(1)}, u32[]{:S(2)}, u32[]{:S(2)}) collective-permute-start(f32[128,512]{1,0:T(8,128)S(1)} %product.9), channel_id=1, source_target_pairs={{0,4},{1,3},{4,8},{5,1},{8,12},{9,5},{12,14},{13,9},{14,10},{15,13... | collective-permute-start | bytes 786440 | tf_op jit(solution)/shard_map/ppermute | solution.py:210
  18.6 6.5 %collective-permute-start.10 = (f32[128,512]{1,0:T(8,128)S(1)}, f32[128,512]{1,0:T(8,128)S(1)}, u32[]{:S(2)}, u32[]{:S(2)}) collective-permute-start(f32[128,512]{1,0:T(8,128)S(1)} %add.49), channel_id=1, source_target_pairs={{0,4},{1,3},{4,8},{5,1},{8,12},{9,5},{12,14},{13,9},{14,10},{15,13... | collective-permute-start | bytes 786440 | tf_op jit(solution)/shard_map/ppermute | solution.py:210
  21.5 6.4 %collective-permute-start.3 = (f32[128,512]{1,0:T(8,128)S(1)}, f32[128,512]{1,0:T(8,128)S(1)}, u32[]{:S(2)}, u32[]{:S(2)}) collective-permute-start(f32[128,512]{1,0:T(8,128)S(1)} %add.42), channel_id=1, source_target_pairs={{0,4},{1,3},{4,8},{5,1},{8,12},{9,5},{12,14},{13,9},{14,10},{15,13... | collective-permute-start | bytes 786440 | tf_op jit(solution)/shard_map/ppermute | solution.py:210
  25.2 6.4 %collective-permute-start.11 = (f32[128,512]{1,0:T(8,128)S(1)}, f32[128,512]{1,0:T(8,128)S(1)}, u32[]{:S(2)}, u32[]{:S(2)}) collective-permute-start(f32[128,512]{1,0:T(8,128)S(1)} %add.50), channel_id=1, source_target_pairs={{0,4},{1,3},{4,8},{5,1},{8,12},{9,5},{12,14},{13,9},{14,10},{15,13... | collective-permute-start | bytes 786440 | tf_op jit(solution)/shard_map/ppermute | solution.py:210
  27.9 6.4 %collective-permute-start.4 = (f32[128,512]{1,0:T(8,128)S(1)}, f32[128,512]{1,0:T(8,128)S(1)}, u32[]{:S(2)}, u32[]{:S(2)}) collective-permute-start(f32[128,512]{1,0:T(8,128)S(1)} %add.43), channel_id=1, source_target_pairs={{0,4},{1,3},{4,8},{5,1},{8,12},{9,5},{12,14},{13,9},{14,10},{15,13... | collective-permute-start | bytes 786440 | tf_op jit(solution)/shard_map/ppermute | solution.py:210
  31.6 6.4 %collective-permute-start.12 = (f32[128,512]{1,0:T(8,128)S(1)}, f32[128,512]{1,0:T(8,128)S(1)}, u32[]{:S(2)}, u32[]{:S(2)}) collective-permute-start(f32[128,512]{1,0:T(8,128)S(1)} %add.51), channel_id=1, source_target_pairs={{0,4},{1,3},{4,8},{5,1},{8,12},{9,5},{12,14},{13,9},{14,10},{15,13... | collective-permute-start | bytes 786440 | tf_op jit(solution)/shard_map/ppermute | solution.py:210
  34.4 6.4 %collective-permute-start.5 = (f32[128,512]{1,0:T(8,128)S(1)}, f32[128,512]{1,0:T(8,128)S(1)}, u32[]{:S(2)}, u32[]{:S(2)}) collective-permute-start(f32[128,512]{1,0:T(8,128)S(1)} %add.44), channel_id=1, source_target_pairs={{0,4},{1,3},{4,8},{5,1},{8,12},{9,5},{12,14},{13,9},{14,10},{15,13... | collective-permute-start | bytes 786440 | tf_op jit(solution)/shard_map/ppermute | solution.py:210
  38.1 6.4 %collective-permute-start.13 = (f32[128,512]{1,0:T(8,128)S(1)}, f32[128,512]{1,0:T(8,128)S(1)}, u32[]{:S(2)}, u32[]{:S(2)}) collective-permute-start(f32[128,512]{1,0:T(8,128)S(1)} %add.52), channel_id=1, source_target_pairs={{0,4},{1,3},{4,8},{5,1},{8,12},{9,5},{12,14},{13,9},{14,10},{15,13... | collective-permute-start | bytes 786440 | tf_op jit(solution)/shard_map/ppermute | solution.py:210
  40.9 6.4 %collective-permute-start.6 = (f32[128,512]{1,0:T(8,128)S(1)}, f32[128,512]{1,0:T(8,128)S(1)}, u32[]{:S(2)}, u32[]{:S(2)}) collective-permute-start(f32[128,512]{1,0:T(8,128)S(1)} %add.45), channel_id=1, source_target_pairs={{0,4},{1,3},{4,8},{5,1},{8,12},{9,5},{12,14},{13,9},{14,10},{15,13... | collective-permute-start | bytes 786440 | tf_op jit(solution)/shard_map/ppermute | solution.py:210
  44.5 6.6 %collective-permute-start.14 = (f32[128,512]{1,0:T(8,128)S(1)}, f32[128,512]{1,0:T(8,128)S(1)}, u32[]{:S(2)}, u32[]{:S(2)}) collective-permute-start(f32[128,512]{1,0:T(8,128)S(1)} %add.53), channel_id=1, source_target_pairs={{0,4},{1,3},{4,8},{5,1},{8,12},{9,5},{12,14},{13,9},{14,10},{15,13... | collective-permute-start | bytes 786440 | tf_op jit(solution)/shard_map/ppermute | solution.py:210
  47.4 6.4 %collective-permute-start.7 = (f32[128,512]{1,0:T(8,128)S(1)}, f32[128,512]{1,0:T(8,128)S(1)}, u32[]{:S(2)}, u32[]{:S(2)}) collective-permute-start(f32[128,512]{1,0:T(8,128)S(1)} %add.46), channel_id=1, source_target_pairs={{0,4},{1,3},{4,8},{5,1},{8,12},{9,5},{12,14},{13,9},{14,10},{15,13... | collective-permute-start | bytes 786440 | tf_op jit(solution)/shard_map/ppermute | solution.py:210
  51.2 6.4 %collective-permute-start.15 = (f32[128,512]{1,0:T(8,128)S(1)}, f32[128,512]{1,0:T(8,128)S(1)}, u32[]{:S(2)}, u32[]{:S(2)}) collective-permute-start(f32[128,512]{1,0:T(8,128)S(1)} %add.54), channel_id=1, source_target_pairs={{0,4},{1,3},{4,8},{5,1},{8,12},{9,5},{12,14},{13,9},{14,10},{15,13... | collective-permute-start | bytes 786440 | tf_op jit(solution)/shard_map/ppermute | solution.py:210
  53.8 6.6 %collective-permute-start.8 = (f32[128,512]{1,0:T(8,128)S(1)}, f32[128,512]{1,0:T(8,128)S(1)}, u32[]{:S(2)}, u32[]{:S(2)}) collective-permute-start(f32[128,512]{1,0:T(8,128)S(1)} %add.47), channel_id=1, source_target_pairs={{0,4},{1,3},{4,8},{5,1},{8,12},{9,5},{12,14},{13,9},{14,10},{15,13... | collective-permute-start | bytes 786440 | tf_op jit(solution)/shard_map/ppermute | solution.py:210

commit v4 on v3

--- a/solution.py
+++ b/solution.py
@@ -85,26 +85,25 @@
     high_ref[...], low_ref[...] = halves(value_ref[...])
 
 
-def split(current_rates, part, parts):
+def split(current_rates):
     depth, width = current_rates.shape
-    width //= parts
     tile = min(512, depth)
     out = jax.ShapeDtypeStruct((depth, width), jnp.bfloat16)
     return pl.pallas_call(
         split_kernel,
         grid=(depth // tile,),
         out_shape=(out, out),
-        in_specs=[pl.BlockSpec((tile, width), lambda k: (k, part))],
+        in_specs=[pl.BlockSpec((tile, width), lambda k: (k, 0))],
         out_specs=[pl.BlockSpec((tile, width), lambda k: (k, 0))] * 2,
-        compiler_params=pltpu.CompilerParams(vmem_limit_bytes=8 * 2**20),
+        compiler_params=pltpu.CompilerParams(vmem_limit_bytes=12 * 2**20),
         cost_estimate=pl.CostEstimate(flops=4 * depth * width, bytes_accessed=8 * depth * width, transcendentals=0),
         name="split",
     )(current_rates)
 
 
-def product_kernel(starts, size, bounds, parts, *refs):
+def product_kernel(starts, size, bounds, cuts, *refs):
     count = len(bounds)
-    sources, pairs, outs = refs[:count], refs[count : count + 2 * parts], refs[count + 2 * parts : -3]
+    sources, (high_ref, low_ref), outs = refs[:count], refs[count : count + 2], refs[count + 2 : -3]
     raw, stack, sems = refs[-3:]
     depth = raw.shape[0]
     for index in range(starts.shape[-1]):
@@ -126,26 +125,26 @@
             sources[0].at[pl.ds(0, size)], raw.at[pl.ds(index * size, size)], sems.at[index]
         ).wait()
     stack[:depth], stack[depth:] = halves(raw[...])
-    for part in range(parts):
-        high_ref, low_ref, out_ref = pairs[2 * part], pairs[2 * part + 1], outs[part]
-        width = out_ref.shape[1]
-        tile = min(LANES, width)
-        for at in range(0, width, tile):
-            both = jnp.dot(stack[...], high_ref[:, at : at + tile], preferred_element_type=jnp.float32)
-            rest = jnp.dot(stack[:depth], low_ref[:, at : at + tile], preferred_element_type=jnp.float32)
-            out_ref[:, at : at + tile] = both[:depth] + (both[depth:] + rest)
-
-
-def product(sources, starts, size, pairs):
+    for at in range(cuts[0], cuts[-1], LANES):
+        upto = min(at + LANES, cuts[-1])
+        both = jnp.dot(stack[...], high_ref[:, at:upto], preferred_element_type=jnp.float32)
+        rest = jnp.dot(stack[:depth], low_ref[:, at:upto], preferred_element_type=jnp.float32)
+        total = both[:depth] + (both[depth:] + rest)
+        for out_ref, left, right in zip(outs, cuts, cuts[1:]):
+            first, last = max(at, left), min(upto, right)
+            if first < last:
+                out_ref[:, first - left : last - left] = total[:, first - at : last - at]
+
+
+def product(sources, starts, size, pair, cuts):
     depth = starts.shape[-1] * size
-    inner, width = pairs[0].shape
-    parts = len(pairs) // 2
-    return pl.pallas_call(
-        functools.partial(product_kernel, starts, size, list(np.cumsum([s.shape[0] for s in sources])), parts),
-        out_shape=[jax.ShapeDtypeStruct((depth, width), jnp.float32)] * parts,
-        in_specs=[pl.BlockSpec(memory_space=pl.ANY)] * len(sources)
-        + [pl.BlockSpec(memory_space=pltpu.VMEM)] * len(pairs),
-        out_specs=[pl.BlockSpec(memory_space=pltpu.VMEM)] * parts,
+    inner = pair[0].shape[0]
+    width = cuts[-1] - cuts[0]
+    return pl.pallas_call(
+        functools.partial(product_kernel, starts, size, list(np.cumsum([s.shape[0] for s in sources])), cuts),
+        out_shape=[jax.ShapeDtypeStruct((depth, right - left), jnp.float32) for left, right in zip(cuts, cuts[1:])],
+        in_specs=[pl.BlockSpec(memory_space=pl.ANY)] * len(sources) + [pl.BlockSpec(memory_space=pltpu.VMEM)] * 2,
+        out_specs=[pl.BlockSpec(memory_space=pltpu.VMEM)] * (len(cuts) - 1),
         scratch_shapes=[
             pltpu.VMEM((depth, inner), jnp.float32),
             pltpu.VMEM((2 * depth, inner), jnp.bfloat16),
@@ -153,36 +152,52 @@
         ],
         compiler_params=pltpu.CompilerParams(vmem_limit_bytes=16 * 2**20),
         cost_estimate=pl.CostEstimate(
-            flops=6 * depth * inner * width * parts,
-            bytes_accessed=4 * depth * inner + 4 * inner * width * parts + 4 * depth * width * parts,
+            flops=6 * depth * inner * width,
+            bytes_accessed=4 * depth * inner + 4 * inner * width + 4 * depth * width,
             transcendentals=0,
         ),
         name="product",
-    )(*sources, *pairs)
+    )(*sources, *pair)
+
+
+def finish_kernel(*refs):
+    out_ref = refs[-1]
+    for part in range(2):
+        above, below, own = refs[3 * part : 3 * part + 3]
+        width = own.shape[1]
+        out_ref[:, part * width : (part + 1) * width] = (above[...] + below[...]) + own[...]
+
+
+def finish(*values):
+    depth, width = values[0].shape
+    return pl.pallas_call(
+        finish_kernel,
+        out_shape=jax.ShapeDtypeStruct((depth, 2 * width), jnp.float32),
+        in_specs=[pl.BlockSpec(memory_space=pltpu.VMEM)] * 6,
+        out_specs=pl.BlockSpec(memory_space=pltpu.VMEM),
+        compiler_params=pltpu.CompilerParams(vmem_limit_bytes=8 * 2**20),
+        name="finish",
+    )(*values)
 
 
 def plan(order, rows, cols, size):
     place = np.zeros(rows, np.int64)
     place[order] = np.arange(rows)
-    each = rows // cols
-    needs = np.zeros((rows, cols, rows), np.int64)
-    for row in range(rows):
-        for core in range(cols):
-            way = -1 if core == 0 else 1
-            needs[row, core] = [order[(place[row] + way * (k + 1)) % rows] for k in range(rows)]
+    each, half = rows // cols, rows // 2
+    steps = [half] + [way * (half - step) for step in range(1, half) for way in (1, -1)] + [0]
     taken = np.zeros((rows, cols, rows), np.int64)
     given = np.zeros((rows, cols, each), np.int64)
     for row in range(rows):
+        needs = [order[(place[row] + step) % rows] for step in steps]
         for core in range(cols):
             arrived = 0
-            for k, block in enumerate(needs[row, core]):
+            for k, block in enumerate(needs):
                 if block // each == core:
                     taken[row, core, k] = (block - core * each) * size
                 else:
                     taken[row, core, k] = (each + arrived) * size
                     arrived += 1
-            wanted = [block for block in needs[row, 1 - core] if block // each == core]
-            given[row, core] = [(block - core * each) * size for block in wanted]
+            given[row, core] = [(block - core * each) * size for block in needs if block // each == core]
     return taken, given
 
 
@@ -190,30 +205,47 @@
     rows, cols = mesh.shape["row"], mesh.shape["col"]
     order = ring_order(mesh)
     group = max(rows // CALLS, 1)
+    half = rows // 2
     swap = [(core, cols - 1 - core) for core in range(cols)]
-    around = [
-        (order[i] * cols + core, order[(i + (1 if core == 0 else -1)) % rows] * cols + core)
-        for i in range(rows)
-        for core in range(cols)
-    ]
+    ways = [[(order[i], order[(i + way) % rows]) for i in range(rows)] for way in (1, -1)]
 
     def shards(inductance, current_rates):
         size = inductance.shape[0] * cols // rows
         taken, given = plan(order, rows, cols, size)
-        picked = pick(inductance, given[..., :group], size)
-        soon = lax.ppermute(picked, "col", swap)
-        late = lax.ppermute(pick(inductance, given[..., group:], size, picked), "col", swap)
-        rates = [split(current_rates, part, 2) for part in range(2)]
-        terms = [product([inductance, soon], taken[..., :group], size, pair)[0] for pair in rates]
-        sums = [term[:size] for term in terms]
-        for step in range(1, rows):
-            passed = [lax.ppermute(part, ("row", "col"), around) for part in sums]
-            if step % group == 0:
-                starts = taken[..., step : step + group]
-                terms = product([inductance, soon, late], starts, size, rates[0] + rates[1])
-            at = step % group * size
-            sums = [got + term[at : at + size] for got, term in zip(passed, terms)]
-        return jnp.concatenate(sums, axis=1)
+        width = current_rates.shape[1]
+        cuts = [0, width // 2, width]
+        held = given.shape[-1]
+
+        def swapped(first, *after):
+            return lax.ppermute(pick(inductance, given[..., first : first + group], size, *after), "col", swap)
+
+        sources = [inductance, swapped(0)]
+        pair = split(current_rates)
+        for first in range(group, held, group):
+            sources.append(swapped(first, pair[0]))
+        starts = taken[..., :group]
+        calls = [[product(sources[:2], starts, size, pair, cuts[part : part + 2])[0] for part in range(2)]]
+
+        def term(index, part):
+            call, at = divmod(index, group)
+            while len(calls) <= call:
+                first = len(calls) * group
+                have = sources[: 2 + len(calls)]
+                calls.append(product(have, taken[..., first : first + group], size, pair, cuts))
+            return calls[call][part][at * size : (at + 1) * size]
+
+        sums = [[None, None], [None, None]]
+        for step in range(half):
+            for late in (1, 0):
+                for way in range(2):
+                    part = (way + late) % 2
+                    if step == 0 and late:
+                        continue
+                    value = term(2 * step - 1 + way if step else 0, part)
+                    if sums[way][part] is not None:
+                        value = sums[way][part] + value
+                    sums[way][part] = lax.ppermute(value, "row", ways[way])
+        return finish(*(each for part in range(2) for each in (sums[0][part], sums[1][part], term(rows - 1, part))))
 
     placed = (P(("groups", "col"), "row"), P("row", ("groups", "col")))
     return jax.shard_map(

time: 61.5 us -> 56.7 us (0.922)
  starting transfers between devices: 26 us -> 17.3 us
  waiting for transfers between devices: 11.6 us -> 14.9 us
  local copies, waits for them, and re-layouts: 4.68 us -> 5.83 us
  other arithmetic: 1.34 us -> 0.36 us
    ppermute x16 -> x18, starting transfers between devices: 26 us -> 17.3 us  [the longest x14 16 us: shards(): sums[way][part] = lax.ppermute(value, 'row', ways[way])]
    ppermute x16 -> x18, waiting for transfers between devices: 11.6 us -> 14.9 us  [the longest x14 14.9 us: shards(): sums[way][part] = lax.ppermute(value, 'row', ways[way])]
    unnamed x6, local copies, waits for them, and re-layouts: 4.68 us -> 5.83 us
    pallas_call x0 -> x1, Pallas kernels: none -> 0.87 us  [finish(): pl.pallas_call(finish_kernel, out_shape=jax.ShapeDtypeStruct((depth, 2 *...]
    concatenate x1 -> x0, other arithmetic: 0.83 us -> none  [shards(): return jnp.concatenate(sums, axis=1)]
    pallas_call x2 -> x1, Pallas kernels: 1.82 us -> 1.22 us  [split(): pl.pallas_call(split_kernel, grid=(depth // tile,), out_shape=(out, out),...]
  transfers between devices with their start and end apart: 16 -> 18, of which waited for: 9 -> 8; matrix products, arithmetic and copies ran while one was open for 1% -> 1% of each run, Pallas kernels for 28% -> 30%
where the time goes in v4:
time: 56.7 us; the launch traced here: 56.6 us
  Pallas kernels  18 us (32%)
  starting transfers between devices  17.3 us (31%)
  waiting for transfers between devices  14.9 us (26%)
  local copies, waits for them, and re-layouts  5.83 us (10%)
    ppermute x14, starting transfers between devices, shards(): sums[way][part] = lax.ppermute(value, 'row', ways[way])  16 us
    pallas_call x9, Pallas kernels, product(): pl.pallas_call(functools.partial(product_kernel, starts, size, list(np.cu...  15.5 us
    ppermute x14, waiting for transfers between devices, shards(): sums[way][part] = lax.ppermute(value, 'row', ways[way])  14.9 us
    unnamed x6, local copies, waits for them, and re-layouts  5.83 us
    ppermute x4, starting transfers between devices, swapped(): lax.ppermute(pick(inductance, given[..., first:first + group], size, *aft...  1.23 us
    pallas_call x1, Pallas kernels, split(): pl.pallas_call(split_kernel, grid=(depth // tile,), out_shape=(out, out),...  1.22 us
  transfers between devices with their start and end apart: 18, of which 8 were waited for; matrix products, arithmetic and copies ran while one was open for 1% of the time, Pallas kernels for 30%

profile of v4, /device:TPU:0, one launch (start us, length us, event | category | flops | bytes accessed | tf_op | source)
XLA Modules:
  0.0 56.6 jit_solution(14946102763172840682)
XLA Ops:
  0.0 0.0 copy-start
  0.0 2.2 %copy-done = f32[512,2048]{1,0:T(8,128)S(1)} copy-done((f32[512,2048]{1,0:T(8,128)S(1)}, f32[512,2048]{1,0:T(8,128)}, u32[]{:S(2)}) %copy-start) | copy-done | bytes 4194328
  2.2 0.1 pick.4
  2.3 0.0 copy-start.1
  2.3 0.5 collective-permute-start
  2.8 0.0 copy-start.2
  2.8 3.6 %copy-done.2 = f32[2048,1024]{1,0:T(8,128)S(1)} copy-done((f32[2048,1024]{1,0:T(8,128)S(1)}, f32[2048,1024]{1,0:T(8,128)}, u32[]{:S(2)}) %copy-start.2) | copy-done | bytes 8388632
  6.4 1.2 %split.1 = (bf16[2048,1024]{1,0:T(8,128)(2,1)S(1)}, bf16[2048,1024]{1,0:T(8,128)(2,1)S(1)}) custom-call(f32[2048,1024]{1,0:T(8,128)S(1)} %copy-done.2), custom_call_target="tpu_custom_call" | custom-call | flops 8388608 | bytes 16777216 | tf_op jit(solution)/shard_map/split/pallas_call | solution.py:92
  7.7 0.0 copy-done.1
  7.7 0.1 pick.5
  7.8 0.1 collective-permute-start.2
  7.9 0.1 pick.6
  8.0 0.5 collective-permute-start.4
  8.5 0.1 pick.7
  8.6 0.1 collective-permute-start.5
  8.7 0.0 collective-permute-done.refs_1_
  8.7 1.1 %product.17 = f32[128,512]{1,0:T(8,128)S(1)} custom-call(f32[512,2048]{1,0:T(8,128)S(1)} %copy-done.1, f32[128,2048]{1,0:T(8,128)S(1)} %collective-permute-done.refs_1_, bf16[2048,1024]{1,0:T(8,128)(2,1)S(1)} %get-tuple-element.21.refs_2_.refs_0_.refs_3_.refs_5_.refs_4_, bf16[2048,1024]{1,0:T(8,128)(2,1)S(1)} %get-tuple-element.22.refs_3_.refs_4_.refs_6_.refs_5_), custom_call_target="tpu_custom_call" | custom-call | flops 805306368 | bytes 5505024 | tf_op jit(solution)/shard_map/product/pallas_call | solution.py:143
  9.8 3.1 %collective-permute-start.14 = (f32[128,512]{1,0:T(8,128)S(1)}, f32[128,512]{1,0:T(8,128)S(1)}, u32[]{:S(2)}, u32[]{:S(2)}) collective-permute-start(f32[128,512]{1,0:T(8,128)S(1)} %product.17), channel_id=1, source_target_pairs={{0,2},{4,0},{8,4},{12,8},{14,12},{10,14},{6,10},{2,6},{1,3},{5,1},... | collective-permute-start | bytes 786440 | tf_op jit(solution)/shard_map/ppermute | solution.py:247
  12.9 1.1 %product.9 = f32[128,512]{1,0:T(8,128)S(1)} custom-call(f32[512,2048]{1,0:T(8,128)S(1)} %copy-done.1, f32[128,2048]{1,0:T(8,128)S(1)} %collective-permute-done.refs_1_, bf16[2048,1024]{1,0:T(8,128)(2,1)S(1)} %get-tuple-element.21.refs_2_.refs_0_.refs_3_.refs_5_.refs_4_, bf16[2048,1024]{1,0:T(8,128)(2,1)S(1)} %get-tuple-element.22.refs_3_.refs_4_.refs_6_.refs_5_), custom_call_target="tpu_custom_call" | custom-call | flops 805306368 | bytes 5505024 | tf_op jit(solution)/shard_map/product/pallas_call | solution.py:143
  14.0 0.2 collective-permute-start.1
  14.2 0.0 collective-permute-done.2.refs_2_
  14.2 1.9 %product.10 = (f32[128,512]{1,0:T(8,128)S(1)}, f32[128,512]{1,0:T(8,128)S(1)}) custom-call(f32[512,2048]{1,0:T(8,128)S(1)} %copy-done.1, f32[128,2048]{1,0:T(8,128)S(1)} %collective-permute-done.refs_1_, f32[128,2048]{1,0:T(8,128)S(1)} %collective-permute-done.2.refs_2_, bf16[2048,1024]{1,0:T(8,128)(2,1)S(1)} %get-tuple-element.21.refs_2_.refs_0_.refs_3_.refs_5_.refs_4_, ...), custom_call_target="tpu_custom_call" | custom-call | flops 1610612736 | bytes 9961472 | tf_op jit(solution)/shard_map/product/pallas_call | solution.py:143
  16.0 2.0 %collective-permute-start.11 = (f32[128,512]{1,0:T(8,128)S(1)}, f32[128,512]{1,0:T(8,128)S(1)}, u32[]{:S(2)}, u32[]{:S(2)}) collective-permute-start(f32[128,512]{1,0:T(8,128)S(1)} %get-tuple-element.30), channel_id=1, source_target_pairs={{0,4},{4,8},{8,12},{12,14},{14,10},{10,6},{6,2},{2,0},{1,5},{5,9},... | collective-permute-start | bytes 786440 | tf_op jit(solution)/shard_map/ppermute | solution.py:247
  18.1 0.0 collective-permute-done.4.refs_3_
  18.1 1.9 %product.13 = (f32[128,512]{1,0:T(8,128)S(1)}, f32[128,512]{1,0:T(8,128)S(1)}) custom-call(f32[512,2048]{1,0:T(8,128)S(1)} %copy-done.1, f32[128,2048]{1,0:T(8,128)S(1)} %collective-permute-done.refs_1_, f32[128,2048]{1,0:T(8,128)S(1)} %collective-permute-done.2.refs_2_, f32[128,2048]{1,0:T(8,128)S(1)} %collective-permute-done.4.refs_3_, ...), custom_call_target="tpu_custom_call" | custom-call | flops 1610612736 | bytes 9961472 | tf_op jit(solution)/shard_map/product/pallas_call | solution.py:143
  20.0 0.1 collective-permute-start.8
  20.1 0.0 collective-permute-done.14
  20.1 1.9 %collective-permute-start.15 = (f32[128,512]{1,0:T(8,128)S(1)}, f32[128,512]{1,0:T(8,128)S(1)}, u32[]{:S(2)}, u32[]{:S(2)}) collective-permute-start(f32[128,512]{1,0:T(8,128)S(1)} %add.37), channel_id=1, source_target_pairs={{0,2},{4,0},{8,4},{12,8},{14,12},{10,14},{6,10},{2,6},{1,3},{5,1},... | collective-permute-start | bytes 786440 | tf_op jit(solution)/shard_map/ppermute | solution.py:247
  22.1 1.2 %collective-permute-done.1 = f32[128,512]{1,0:T(8,128)S(1)} collective-permute-done((f32[128,512]{1,0:T(8,128)S(1)}, f32[128,512]{1,0:T(8,128)S(1)}, u32[]{:S(2)}, u32[]{:S(2)}) %collective-permute-start.1) | collective-permute-done | bytes 262176 | tf_op jit(solution)/shard_map/ppermute | solution.py:247
  23.3 0.1 collective-permute-start.3
  23.4 0.0 collective-permute-done.5.refs_4_
  23.4 1.9 %product.14 = (f32[128,512]{1,0:T(8,128)S(1)}, f32[128,512]{1,0:T(8,128)S(1)}) custom-call(f32[512,2048]{1,0:T(8,128)S(1)} %copy-done.1, f32[128,2048]{1,0:T(8,128)S(1)} %collective-permute-done.refs_1_, f32[128,2048]{1,0:T(8,128)S(1)} %collective-permute-done.2.refs_2_, f32[128,2048]{1,0:T(8,128)S(1)} %collective-permute-done.4.refs_3_, ...), custom_call_target="tpu_custom_call" | custom-call | flops 1610612736 | bytes 9961472 | tf_op jit(solution)/shard_map/product/pallas_call | solution.py:143
  25.3 1.9 %product.11 = (f32[128,512]{1,0:T(8,128)S(1)}, f32[128,512]{1,0:T(8,128)S(1)}) custom-call(f32[512,2048]{1,0:T(8,128)S(1)} %copy-done.1, f32[128,2048]{1,0:T(8,128)S(1)} %collective-permute-done.refs_1_, f32[128,2048]{1,0:T(8,128)S(1)} %collective-permute-done.2.refs_2_, f32[128,2048]{1,0:T(8,128)S(1)} %collective-permute-done.4.refs_3_, ...), custom_call_target="tpu_custom_call" | custom-call | flops 1610612736 | bytes 9961472 | tf_op jit(solution)/shard_map/product/pallas_call | solution.py:143
  27.2 1.6 %collective-permute-done.11 = f32[128,512]{1,0:T(8,128)S(1)} collective-permute-done((f32[128,512]{1,0:T(8,128)S(1)}, f32[128,512]{1,0:T(8,128)S(1)}, u32[]{:S(2)}, u32[]{:S(2)}) %collective-permute-start.11) | collective-permute-done | bytes 262176 | tf_op jit(solution)/shard_map/ppermute | solution.py:247
  28.9 0.5 collective-permute-start.12
  29.4 0.0 collective-permute-done.8
  29.4 1.6 %collective-permute-start.9 = (f32[128,512]{1,0:T(8,128)S(1)}, f32[128,512]{1,0:T(8,128)S(1)}, u32[]{:S(2)}, u32[]{:S(2)}) collective-permute-start(f32[128,512]{1,0:T(8,128)S(1)} %add.33), channel_id=1, source_target_pairs={{0,2},{4,0},{8,4},{12,8},{14,12},{10,14},{6,10},{2,6},{1,3},{5,1},... | collective-permute-start | bytes 786440 | tf_op jit(solution)/shard_map/ppermute | solution.py:247
  31.1 3.8 %collective-permute-done.15 = f32[128,512]{1,0:T(8,128)S(1)} collective-permute-done((f32[128,512]{1,0:T(8,128)S(1)}, f32[128,512]{1,0:T(8,128)S(1)}, u32[]{:S(2)}, u32[]{:S(2)}) %collective-permute-start.15) | collective-permute-done | bytes 262176 | tf_op jit(solution)/shard_map/ppermute | solution.py:247
  34.9 0.1 collective-permute-start.16
  35.0 0.0 collective-permute-done.3
  35.1 2.0 %collective-permute-start.6 = (f32[128,512]{1,0:T(8,128)S(1)}, f32[128,512]{1,0:T(8,128)S(1)}, u32[]{:S(2)}, u32[]{:S(2)}) collective-permute-start(f32[128,512]{1,0:T(8,128)S(1)} %add.31), channel_id=1, source_target_pairs={{0,4},{4,8},{8,12},{12,14},{14,10},{10,6},{6,2},{2,0},{1,5},{5,9},... | collective-permute-start | bytes 786440 | tf_op jit(solution)/shard_map/ppermute | solution.py:247
  37.1 1.9 %product.15 = (f32[128,512]{1,0:T(8,128)S(1)}, f32[128,512]{1,0:T(8,128)S(1)}) custom-call(f32[512,2048]{1,0:T(8,128)S(1)} %copy-done.1, f32[128,2048]{1,0:T(8,128)S(1)} %collective-permute-done.refs_1_, f32[128,2048]{1,0:T(8,128)S(1)} %collective-permute-done.2.refs_2_, f32[128,2048]{1,0:T(8,128)S(1)} %collective-permute-done.4.refs_3_, ...), custom_call_target="tpu_custom_call" | custom-call | flops 1610612736 | bytes 9961472 | tf_op jit(solution)/shard_map/product/pallas_call | solution.py:143
  39.0 2.1 %product.12 = (f32[128,512]{1,0:T(8,128)S(1)}, f32[128,512]{1,0:T(8,128)S(1)}) custom-call(f32[512,2048]{1,0:T(8,128)S(1)} %copy-done.1, f32[128,2048]{1,0:T(8,128)S(1)} %collective-permute-done.refs_1_, f32[128,2048]{1,0:T(8,128)S(1)} %collective-permute-done.2.refs_2_, f32[128,2048]{1,0:T(8,128)S(1)} %collective-permute-done.4.refs_3_, ...), custom_call_target="tpu_custom_call" | custom-call | flops 1610612736 | bytes 9961472 | tf_op jit(solution)/shard_map/product/pallas_call | solution.py:143
  41.1 0.0 collective-permute-done.12
  41.1 1.7 %collective-permute-start.13 = (f32[128,512]{1,0:T(8,128)S(1)}, f32[128,512]{1,0:T(8,128)S(1)}, u32[]{:S(2)}, u32[]{:S(2)}) collective-permute-start(f32[128,512]{1,0:T(8,128)S(1)} %add.36), channel_id=1, source_target_pairs={{0,4},{4,8},{8,12},{12,14},{14,10},{10,6},{6,2},{2,0},{1,5},{5,9},... | collective-permute-start | bytes 786440 | tf_op jit(solution)/shard_map/ppermute | solution.py:247
  42.8 0.0 collective-permute-done.9
  42.8 0.5 collective-permute-start.10
  43.3 2.8 %collective-permute-done.16 = f32[128,512]{1,0:T(8,128)S(1)} collective-permute-done((f32[128,512]{1,0:T(8,128)S(1)}, f32[128,512]{1,0:T(8,128)S(1)}, u32[]{:S(2)}, u32[]{:S(2)}) %collective-permute-start.16) | collective-permute-done | bytes 262176 | tf_op jit(solution)/shard_map/ppermute | solution.py:247
  46.1 0.1 collective-permute-start.17
  46.2 0.0 collective-permute-done.6
  46.3 2.0 %collective-permute-start.7 = (f32[128,512]{1,0:T(8,128)S(1)}, f32[128,512]{1,0:T(8,128)S(1)}, u32[]{:S(2)}, u32[]{:S(2)}) collective-permute-start(f32[128,512]{1,0:T(8,128)S(1)} %add.32), channel_id=1, source_target_pairs={{0,4},{4,8},{8,12},{12,14},{14,10},{10,6},{6,2},{2,0},{1,5},{5,9},... | collective-permute-start | bytes 786440 | tf_op jit(solution)/shard_map/ppermute | solution.py:247
  48.3 1.9 %product.16 = (f32[128,512]{1,0:T(8,128)S(1)}, f32[128,512]{1,0:T(8,128)S(1)}) custom-call(f32[512,2048]{1,0:T(8,128)S(1)} %copy-done.1, f32[128,2048]{1,0:T(8,128)S(1)} %collective-permute-done.refs_1_, f32[128,2048]{1,0:T(8,128)S(1)} %collective-permute-done.2.refs_2_, f32[128,2048]{1,0:T(8,128)S(1)} %collective-permute-done.4.refs_3_, ...), custom_call_target="tpu_custom_call" | custom-call | flops 1610612736 | bytes 9961472 | tf_op jit(solution)/shard_map/product/pallas_call | solution.py:143
  50.2 1.1 %collective-permute-done.13.refs_3_ = f32[128,512]{1,0:T(8,128)S(1)} collective-permute-done((f32[128,512]{1,0:T(8,128)S(1)}, f32[128,512]{1,0:T(8,128)S(1)}, u32[]{:S(2)}, u32[]{:S(2)}) %collective-permute-start.13) | collective-permute-done | bytes 262176 | tf_op jit(solution)/shard_map/ppermute | solution.py:247
  51.3 0.8 %collective-permute-done.10.refs_1_ = f32[128,512]{1,0:T(8,128)S(1)} collective-permute-done((f32[128,512]{1,0:T(8,128)S(1)}, f32[128,512]{1,0:T(8,128)S(1)}, u32[]{:S(2)}, u32[]{:S(2)}) %collective-permute-start.10) | collective-permute-done | bytes 262176 | tf_op jit(solution)/shard_map/ppermute | solution.py:247
  52.1 3.4 %collective-permute-done.17.refs_4_ = f32[128,512]{1,0:T(8,128)S(1)} collective-permute-done((f32[128,512]{1,0:T(8,128)S(1)}, f32[128,512]{1,0:T(8,128)S(1)}, u32[]{:S(2)}, u32[]{:S(2)}) %collective-permute-start.17) | collective-permute-done | bytes 262176 | tf_op jit(solution)/shard_map/ppermute | solution.py:247
  55.5 0.2 collective-permute-done.7.refs_0_
  55.7 0.9 %finish.1 = f32[128,1024]{1,0:T(8,128)} custom-call(f32[128,512]{1,0:T(8,128)S(1)} %collective-permute-done.7.refs_0_, f32[128,512]{1,0:T(8,128)S(1)} %collective-permute-done.10.refs_1_, f32[128,512]{1,0:T(8,128)S(1)} %get-tuple-element.29.refs_2_, f32[128,512]{1,0:T(8,128)S(1)} %collective-permute-done.13.refs_3_, ...), custom_call_target="tpu_custom_call" | custom-call | tf_op jit(solution)/shard_map/finish/pallas_call | solution.py:173
  (10 shorter events, 0.4 us)
Async XLA Ops:
  0.0 2.2 %copy-start = (f32[512,2048]{1,0:T(8,128)S(1)}, f32[512,2048]{1,0:T(8,128)}, u32[]{:S(2)}) copy-start(f32[512,2048]{1,0:T(8,128)} %refs_0_.17) | copy-start | bytes 12582916
  2.3 5.4 %copy-start.1 = (f32[512,2048]{1,0:T(8,128)S(1)}, f32[512,2048]{1,0:T(8,128)}, u32[]{:S(2)}) copy-start(f32[512,2048]{1,0:T(8,128)} %refs_0_.17) | copy-start | bytes 12582916
  2.3 6.4 %collective-permute-start = (f32[128,2048]{1,0:T(8,128)S(1)}, f32[128,2048]{1,0:T(8,128)S(1)}, u32[]{:S(2)}, u32[]{:S(2)}) collective-permute-start(f32[128,2048]{1,0:T(8,128)S(1)} %pick.4), channel_id=1, source_target_pairs={{0,1},{1,0},{2,3},{3,2},{4,5},{5,4},{6,7},{7,6},{8,9},{9,8},{10,11... | collective-permute-start | bytes 3145736 | tf_op jit(solution)/shard_map/ppermute | solution.py:220
  2.8 3.6 %copy-start.2 = (f32[2048,1024]{1,0:T(8,128)S(1)}, f32[2048,1024]{1,0:T(8,128)}, u32[]{:S(2)}) copy-start(f32[2048,1024]{1,0:T(8,128)} %value_ref.1) | copy-start | bytes 25165828
  7.8 6.4 %collective-permute-start.2 = (f32[128,2048]{1,0:T(8,128)S(1)}, f32[128,2048]{1,0:T(8,128)S(1)}, u32[]{:S(2)}, u32[]{:S(2)}) collective-permute-start(f32[128,2048]{1,0:T(8,128)S(1)} %pick.5), channel_id=1, source_target_pairs={{0,1},{1,0},{2,3},{3,2},{4,5},{5,4},{6,7},{7,6},{8,9},{9,8},{10,11... | collective-permute-start | bytes 3145736 | tf_op jit(solution)/shard_map/ppermute | solution.py:220
  8.0 10.1 %collective-permute-start.4 = (f32[128,2048]{1,0:T(8,128)S(1)}, f32[128,2048]{1,0:T(8,128)S(1)}, u32[]{:S(2)}, u32[]{:S(2)}) collective-permute-start(f32[128,2048]{1,0:T(8,128)S(1)} %pick.6), channel_id=1, source_target_pairs={{0,1},{1,0},{2,3},{3,2},{4,5},{5,4},{6,7},{7,6},{8,9},{9,8},{10,11... | collective-permute-start | bytes 3145736 | tf_op jit(solution)/shard_map/ppermute | solution.py:220
  8.6 14.8 %collective-permute-start.5 = (f32[128,2048]{1,0:T(8,128)S(1)}, f32[128,2048]{1,0:T(8,128)S(1)}, u32[]{:S(2)}, u32[]{:S(2)}) collective-permute-start(f32[128,2048]{1,0:T(8,128)S(1)} %pick.7), channel_id=1, source_target_pairs={{0,1},{1,0},{2,3},{3,2},{4,5},{5,4},{6,7},{7,6},{8,9},{9,8},{10,11... | collective-permute-start | bytes 3145736 | tf_op jit(solution)/shard_map/ppermute | solution.py:220
  9.8 10.3 %collective-permute-start.14 = (f32[128,512]{1,0:T(8,128)S(1)}, f32[128,512]{1,0:T(8,128)S(1)}, u32[]{:S(2)}, u32[]{:S(2)}) collective-permute-start(f32[128,512]{1,0:T(8,128)S(1)} %product.17), channel_id=1, source_target_pairs={{0,2},{4,0},{8,4},{12,8},{14,12},{10,14},{6,10},{2,6},{1,3},{5,1},... | collective-permute-start | bytes 786440 | tf_op jit(solution)/shard_map/ppermute | solution.py:247
  14.0 9.3 %collective-permute-start.1 = (f32[128,512]{1,0:T(8,128)S(1)}, f32[128,512]{1,0:T(8,128)S(1)}, u32[]{:S(2)}, u32[]{:S(2)}) collective-permute-start(f32[128,512]{1,0:T(8,128)S(1)} %product.9), channel_id=1, source_target_pairs={{0,4},{4,8},{8,12},{12,14},{14,10},{10,6},{6,2},{2,0},{1,5},{5,9},... | collective-permute-start | bytes 786440 | tf_op jit(solution)/shard_map/ppermute | solution.py:247
  16.0 12.8 %collective-permute-start.11 = (f32[128,512]{1,0:T(8,128)S(1)}, f32[128,512]{1,0:T(8,128)S(1)}, u32[]{:S(2)}, u32[]{:S(2)}) collective-permute-start(f32[128,512]{1,0:T(8,128)S(1)} %get-tuple-element.30), channel_id=1, source_target_pairs={{0,4},{4,8},{8,12},{12,14},{14,10},{10,6},{6,2},{2,0},{1,5},{5,9},... | collective-permute-start | bytes 786440 | tf_op jit(solution)/shard_map/ppermute | solution.py:247
  20.0 9.4 %collective-permute-start.8 = (f32[128,512]{1,0:T(8,128)S(1)}, f32[128,512]{1,0:T(8,128)S(1)}, u32[]{:S(2)}, u32[]{:S(2)}) collective-permute-start(f32[128,512]{1,0:T(8,128)S(1)} %get-tuple-element.26), channel_id=1, source_target_pairs={{0,2},{4,0},{8,4},{12,8},{14,12},{10,14},{6,10},{2,6},{1,3},{5,1},... | collective-permute-start | bytes 786440 | tf_op jit(solution)/shard_map/ppermute | solution.py:247
  20.1 14.8 %collective-permute-start.15 = (f32[128,512]{1,0:T(8,128)S(1)}, f32[128,512]{1,0:T(8,128)S(1)}, u32[]{:S(2)}, u32[]{:S(2)}) collective-permute-start(f32[128,512]{1,0:T(8,128)S(1)} %add.37), channel_id=1, source_target_pairs={{0,2},{4,0},{8,4},{12,8},{14,12},{10,14},{6,10},{2,6},{1,3},{5,1},... | collective-permute-start | bytes 786440 | tf_op jit(solution)/shard_map/ppermute | solution.py:247
  23.3 11.7 %collective-permute-start.3 = (f32[128,512]{1,0:T(8,128)S(1)}, f32[128,512]{1,0:T(8,128)S(1)}, u32[]{:S(2)}, u32[]{:S(2)}) collective-permute-start(f32[128,512]{1,0:T(8,128)S(1)} %add.30), channel_id=1, source_target_pairs={{0,4},{4,8},{8,12},{12,14},{14,10},{10,6},{6,2},{2,0},{1,5},{5,9},... | collective-permute-start | bytes 786440 | tf_op jit(solution)/shard_map/ppermute | solution.py:247
  28.9 12.2 %collective-permute-start.12 = (f32[128,512]{1,0:T(8,128)S(1)}, f32[128,512]{1,0:T(8,128)S(1)}, u32[]{:S(2)}, u32[]{:S(2)}) collective-permute-start(f32[128,512]{1,0:T(8,128)S(1)} %add.35), channel_id=1, source_target_pairs={{0,4},{4,8},{8,12},{12,14},{14,10},{10,6},{6,2},{2,0},{1,5},{5,9},... | collective-permute-start | bytes 786440 | tf_op jit(solution)/shard_map/ppermute | solution.py:247
  29.4 13.4 %collective-permute-start.9 = (f32[128,512]{1,0:T(8,128)S(1)}, f32[128,512]{1,0:T(8,128)S(1)}, u32[]{:S(2)}, u32[]{:S(2)}) collective-permute-start(f32[128,512]{1,0:T(8,128)S(1)} %add.33), channel_id=1, source_target_pairs={{0,2},{4,0},{8,4},{12,8},{14,12},{10,14},{6,10},{2,6},{1,3},{5,1},... | collective-permute-start | bytes 786440 | tf_op jit(solution)/shard_map/ppermute | solution.py:247
  34.9 11.2 %collective-permute-start.16 = (f32[128,512]{1,0:T(8,128)S(1)}, f32[128,512]{1,0:T(8,128)S(1)}, u32[]{:S(2)}, u32[]{:S(2)}) collective-permute-start(f32[128,512]{1,0:T(8,128)S(1)} %add.38), channel_id=1, source_target_pairs={{0,2},{4,0},{8,4},{12,8},{14,12},{10,14},{6,10},{2,6},{1,3},{5,1},... | collective-permute-start | bytes 786440 | tf_op jit(solution)/shard_map/ppermute | solution.py:247
  35.1 11.2 %collective-permute-start.6 = (f32[128,512]{1,0:T(8,128)S(1)}, f32[128,512]{1,0:T(8,128)S(1)}, u32[]{:S(2)}, u32[]{:S(2)}) collective-permute-start(f32[128,512]{1,0:T(8,128)S(1)} %add.31), channel_id=1, source_target_pairs={{0,4},{4,8},{8,12},{12,14},{14,10},{10,6},{6,2},{2,0},{1,5},{5,9},... | collective-permute-start | bytes 786440 | tf_op jit(solution)/shard_map/ppermute | solution.py:247
  41.1 10.2 %collective-permute-start.13 = (f32[128,512]{1,0:T(8,128)S(1)}, f32[128,512]{1,0:T(8,128)S(1)}, u32[]{:S(2)}, u32[]{:S(2)}) collective-permute-start(f32[128,512]{1,0:T(8,128)S(1)} %add.36), channel_id=1, source_target_pairs={{0,4},{4,8},{8,12},{12,14},{14,10},{10,6},{6,2},{2,0},{1,5},{5,9},... | collective-permute-start | bytes 786440 | tf_op jit(solution)/shard_map/ppermute | solution.py:247
  42.8 9.3 %collective-permute-start.10 = (f32[128,512]{1,0:T(8,128)S(1)}, f32[128,512]{1,0:T(8,128)S(1)}, u32[]{:S(2)}, u32[]{:S(2)}) collective-permute-start(f32[128,512]{1,0:T(8,128)S(1)} %add.34), channel_id=1, source_target_pairs={{0,2},{4,0},{8,4},{12,8},{14,12},{10,14},{6,10},{2,6},{1,3},{5,1},... | collective-permute-start | bytes 786440 | tf_op jit(solution)/shard_map/ppermute | solution.py:247
  46.1 9.4 %collective-permute-start.17 = (f32[128,512]{1,0:T(8,128)S(1)}, f32[128,512]{1,0:T(8,128)S(1)}, u32[]{:S(2)}, u32[]{:S(2)}) collective-permute-start(f32[128,512]{1,0:T(8,128)S(1)} %add.39), channel_id=1, source_target_pairs={{0,2},{4,0},{8,4},{12,8},{14,12},{10,14},{6,10},{2,6},{1,3},{5,1},... | collective-permute-start | bytes 786440 | tf_op jit(solution)/shard_map/ppermute | solution.py:247
  46.3 9.4 %collective-permute-start.7 = (f32[128,512]{1,0:T(8,128)S(1)}, f32[128,512]{1,0:T(8,128)S(1)}, u32[]{:S(2)}, u32[]{:S(2)}) collective-permute-start(f32[128,512]{1,0:T(8,128)S(1)} %add.32), channel_id=1, source_target_pairs={{0,4},{4,8},{8,12},{12,14},{14,10},{10,6},{6,2},{2,0},{1,5},{5,9},... | collective-permute-start | bytes 786440 | tf_op jit(solution)/shard_map/ppermute | solution.py:247

commit v5 on v4

--- a/solution.py
+++ b/solution.py
@@ -10,6 +10,7 @@
 
 CALLS = 8
 LANES = 256
+MIB = 2**20
 
 
 def ring_order(mesh):
@@ -45,14 +46,16 @@
     return found
 
 
-def pick_kernel(starts, size, a_ref, *refs):
-    out_ref, sems = refs[-2:]
+def pick_kernel(starts, size, group, a_ref, *refs):
+    count = starts.shape[-1]
+    outs, sems = refs[-1 - count // group : -1], refs[-1]
     copies = []
-    for index in range(starts.shape[-1]):
+    for index in range(count):
         start = pl.multiple_of(looked_up(starts[..., index]), size)
+        out_ref, at = outs[index // group], index % group * size
         copies.append(
             pltpu.make_async_copy(
-                a_ref.at[pl.ds(start, size)], out_ref.at[pl.ds(index * size, size)], sems.at[index]
+                a_ref.at[pl.ds(start, size)], out_ref.at[pl.ds(at, size)], sems.at[index]
             )
         )
     for copy in copies:
@@ -61,16 +64,16 @@
         copy.wait()
 
 
-def pick(inductance, starts, size, *after):
+def pick(inductance, starts, size, group, room, *after):
     count = starts.shape[-1]
     width = inductance.shape[1]
     return pl.pallas_call(
-        functools.partial(pick_kernel, starts, size),
-        out_shape=jax.ShapeDtypeStruct((count * size, width), jnp.float32),
+        functools.partial(pick_kernel, starts, size, group),
+        out_shape=[jax.ShapeDtypeStruct((group * size, width), jnp.float32)] * (count // group),
         in_specs=[pl.BlockSpec(memory_space=pl.ANY)] * (1 + len(after)),
-        out_specs=pl.BlockSpec(memory_space=pltpu.VMEM),
+        out_specs=[pl.BlockSpec(memory_space=pltpu.VMEM)] * (count // group),
         scratch_shapes=[pltpu.SemaphoreType.DMA((count,))],
-        compiler_params=pltpu.CompilerParams(vmem_limit_bytes=8 * 2**20),
+        compiler_params=pltpu.CompilerParams(vmem_limit_bytes=room * MIB),
         cost_estimate=pl.CostEstimate(flops=0, bytes_accessed=8 * count * size * width, transcendentals=0),
         name="pick",
     )(inductance, *after)
@@ -87,7 +90,7 @@
 
 def split(current_rates):
     depth, width = current_rates.shape
-    tile = min(512, depth)
+    tile = min(256, depth)
     out = jax.ShapeDtypeStruct((depth, width), jnp.bfloat16)
     return pl.pallas_call(
         split_kernel,
@@ -95,7 +98,7 @@
         out_shape=(out, out),
         in_specs=[pl.BlockSpec((tile, width), lambda k: (k, 0))],
         out_specs=[pl.BlockSpec((tile, width), lambda k: (k, 0))] * 2,
-        compiler_params=pltpu.CompilerParams(vmem_limit_bytes=12 * 2**20),
+        compiler_params=pltpu.CompilerParams(vmem_limit_bytes=8 * MIB),
         cost_estimate=pl.CostEstimate(flops=4 * depth * width, bytes_accessed=8 * depth * width, transcendentals=0),
         name="split",
     )(current_rates)
@@ -150,7 +153,7 @@
             pltpu.VMEM((2 * depth, inner), jnp.bfloat16),
             pltpu.SemaphoreType.DMA((starts.shape[-1],)),
         ],
-        compiler_params=pltpu.CompilerParams(vmem_limit_bytes=16 * 2**20),
+        compiler_params=pltpu.CompilerParams(vmem_limit_bytes=16 * MIB),
         cost_estimate=pl.CostEstimate(
             flops=6 * depth * inner * width,
             bytes_accessed=4 * depth * inner + 4 * inner * width + 4 * depth * width,
@@ -175,12 +178,12 @@
         out_shape=jax.ShapeDtypeStruct((depth, 2 * width), jnp.float32),
         in_specs=[pl.BlockSpec(memory_space=pltpu.VMEM)] * 6,
         out_specs=pl.BlockSpec(memory_space=pltpu.VMEM),
-        compiler_params=pltpu.CompilerParams(vmem_limit_bytes=8 * 2**20),
+        compiler_params=pltpu.CompilerParams(vmem_limit_bytes=8 * MIB),
         name="finish",
     )(*values)
 
 
-def plan(order, rows, cols, size):
+def plan(order, rows, cols, size, group):
     place = np.zeros(rows, np.int64)
     place[order] = np.arange(rows)
     each, half = rows // cols, rows // 2
@@ -190,13 +193,12 @@
     for row in range(rows):
         needs = [order[(place[row] + step) % rows] for step in steps]
         for core in range(cols):
-            arrived = 0
+            seen = [0, 0]
             for k, block in enumerate(needs):
-                if block // each == core:
-                    taken[row, core, k] = (block - core * each) * size
-                else:
-                    taken[row, core, k] = (each + arrived) * size
-                    arrived += 1
+                received = int(block // each != core)
+                chunk, at = divmod(seen[received], group)
+                taken[row, core, k] = ((2 * chunk + received) * group + at) * size
+                seen[received] += 1
             given[row, core] = [(block - core * each) * size for block in needs if block // each == core]
     return taken, given
 
@@ -211,29 +213,25 @@
 
     def shards(inductance, current_rates):
         size = inductance.shape[0] * cols // rows
-        taken, given = plan(order, rows, cols, size)
+        taken, given = plan(order, rows, cols, size, group)
         width = current_rates.shape[1]
         cuts = [0, width // 2, width]
-        held = given.shape[-1]
-
-        def swapped(first, *after):
-            return lax.ppermute(pick(inductance, given[..., first : first + group], size, *after), "col", swap)
-
-        sources = [inductance, swapped(0)]
-        pair = split(current_rates)
-        for first in range(group, held, group):
-            sources.append(swapped(first, pair[0]))
-        starts = taken[..., :group]
-        calls = [[product(sources[:2], starts, size, pair, cuts[part : part + 2])[0] for part in range(2)]]
+        calls = {}
 
         def term(index, part):
             call, at = divmod(index, group)
-            while len(calls) <= call:
-                first = len(calls) * group
-                have = sources[: 2 + len(calls)]
-                calls.append(product(have, taken[..., first : first + group], size, pair, cuts))
-            return calls[call][part][at * size : (at + 1) * size]
-
+            if (call, part) not in calls:
+                parts = [part] if call < 3 else [0, 1]
+                starts = taken[..., call * group : (call + 1) * group]
+                edges = cuts[parts[0] : parts[-1] + 2]
+                got = product(sources[: 2 * call + 2], starts, size, pair, edges)
+                calls.update({(call, each): value for each, value in zip(parts, got)})
+            return calls[call, part][at * size : (at + 1) * size]
+
+        own = pick(inductance, given[..., :group], size, group, 52)
+        own += pick(inductance, given[..., group:], size, group, 48, *own)
+        sources = [rows for each in own for rows in (each, lax.ppermute(each, "col", swap))]
+        pair = split(current_rates)
         sums = [[None, None], [None, None]]
         for step in range(half):
             for late in (1, 0):

time: 56.7 us -> 54.1 us (0.954)
  local copies, waits for them, and re-layouts: 5.83 us -> 0.01 us
  Pallas kernels: 18 us -> 21.9 us
  starting transfers between devices: 17.3 us -> 15.4 us
  waiting for transfers between devices: 14.9 us -> 16.1 us
    unnamed x6 -> x2, local copies, waits for them, and re-layouts: 5.83 us -> 0.01 us
    pallas_call x4 -> x2, Pallas kernels: 0.37 us -> 3.7 us  [pick(): pl.pallas_call(functools.partial(pick_kernel, starts, size, group), out_s...]
    ppermute x14, starting transfers between devices: 16 us -> 14.2 us  [shards(): sums[way][part] = lax.ppermute(value, 'row', ways[way])]
    ppermute x14, waiting for transfers between devices: 14.9 us -> 16.1 us  [shards(): sums[way][part] = lax.ppermute(value, 'row', ways[way])]
    pallas_call x9 -> x11, Pallas kernels: 15.5 us -> 16.2 us  [product(): pl.pallas_call(functools.partial(product_kernel, starts, size, list(np.cu...]
  transfers between devices with their start and end apart: 18 -> 18, of which waited for: 8 -> 10; matrix products, arithmetic and copies ran while one was open for 1% -> 1% of each run, Pallas kernels for 30% -> 36%
where the time goes in v5:
time: 54.1 us; the launch traced here: 54 us
  Pallas kernels  21.9 us (40%)
  waiting for transfers between devices  16.1 us (30%)
  starting transfers between devices  15.4 us (28%)
    pallas_call x11, Pallas kernels, product(): pl.pallas_call(functools.partial(product_kernel, starts, size, list(np.cu...  16.2 us
    ppermute x14, waiting for transfers between devices, shards(): sums[way][part] = lax.ppermute(value, 'row', ways[way])  16.1 us
    ppermute x14, starting transfers between devices, shards(): sums[way][part] = lax.ppermute(value, 'row', ways[way])  14.2 us
    pallas_call x2, Pallas kernels, pick(): pl.pallas_call(functools.partial(pick_kernel, starts, size, group), out_s...  3.7 us
    pallas_call x1, Pallas kernels, split(): pl.pallas_call(split_kernel, grid=(depth // tile,), out_shape=(out, out),...  1.21 us
    ppermute x4, starting transfers between devices, shards(): lax.ppermute(each, 'col', swap)  1.16 us
  transfers between devices with their start and end apart: 18, of which 10 were waited for; matrix products, arithmetic and copies ran while one was open for 1% of the time, Pallas kernels for 36%

profile of v5, /device:TPU:0, one launch (start us, length us, event | category | flops | bytes accessed | tf_op | source)
XLA Modules:
  0.0 54.0 jit_solution(4218963030575259508)
XLA Ops:
  0.0 0.0 copy-start
  0.0 1.4 %pick.2.refs_0_ = f32[128,2048]{1,0:T(8,128)S(1)} custom-call(f32[512,2048]{1,0:T(8,128)} %a_ref.3), custom_call_target="tpu_custom_call" | custom-call | bytes 2097152 | tf_op jit(solution)/shard_map/pick/pallas_call | solution.py:70
  1.4 0.5 collective-permute-start
  1.9 2.3 %pick.3 = (f32[128,2048]{1,0:T(8,128)S(1)}, f32[128,2048]{1,0:T(8,128)S(1)}, f32[128,2048]{1,0:T(8,128)S(1)}) custom-call(f32[512,2048]{1,0:T(8,128)} %a_ref.3, f32[128,2048]{1,0:T(8,128)S(1)} %pick.2.refs_0_), custom_call_target="tpu_custom_call" | custom-call | bytes 6291456 | tf_op jit(solution)/shard_map/pick/pallas_call | solution.py:70
  4.2 0.1 collective-permute-start.2
  4.3 0.5 collective-permute-start.4
  4.8 0.1 collective-permute-start.5
  4.9 0.0 copy-done
  4.9 1.2 %split.1 = (bf16[2048,1024]{1,0:T(8,128)(2,1)S(1)}, bf16[2048,1024]{1,0:T(8,128)(2,1)S(1)}) custom-call(f32[2048,1024]{1,0:T(8,128)S(1)} %copy-done), custom_call_target="tpu_custom_call" | custom-call | flops 8388608 | bytes 16777216 | tf_op jit(solution)/shard_map/split/pallas_call | solution.py:95
  6.1 0.0 collective-permute-done.refs_1_
  6.1 1.1 %product.20 = f32[128,512]{1,0:T(8,128)S(1)} custom-call(f32[128,2048]{1,0:T(8,128)S(1)} %pick.2.refs_0_, f32[128,2048]{1,0:T(8,128)S(1)} %collective-permute-done.refs_1_, bf16[2048,1024]{1,0:T(8,128)(2,1)S(1)} %get-tuple-element.20.refs_2_.refs_4_.refs_8_.refs_6_, bf16[2048,1024]{1,0:T(8,128)(2,1)S(1)} %get-tuple-element.21.refs_3_.refs_5_.refs_9_.refs_7_), custom_call_target="tpu_custom_call" | custom-call | flops 805306368 | bytes 5505024 | tf_op jit(solution)/shard_map/product/pallas_call | solution.py:146
  7.2 3.1 %collective-permute-start.14 = (f32[128,512]{1,0:T(8,128)S(1)}, f32[128,512]{1,0:T(8,128)S(1)}, u32[]{:S(2)}, u32[]{:S(2)}) collective-permute-start(f32[128,512]{1,0:T(8,128)S(1)} %product.20), channel_id=1, source_target_pairs={{0,2},{4,0},{8,4},{12,8},{14,12},{10,14},{6,10},{2,6},{1,3},{5,1},... | collective-permute-start | bytes 786440 | tf_op jit(solution)/shard_map/ppermute | solution.py:245
  10.3 1.1 %product.11 = f32[128,512]{1,0:T(8,128)S(1)} custom-call(f32[128,2048]{1,0:T(8,128)S(1)} %pick.2.refs_0_, f32[128,2048]{1,0:T(8,128)S(1)} %collective-permute-done.refs_1_, bf16[2048,1024]{1,0:T(8,128)(2,1)S(1)} %get-tuple-element.20.refs_2_.refs_4_.refs_8_.refs_6_, bf16[2048,1024]{1,0:T(8,128)(2,1)S(1)} %get-tuple-element.21.refs_3_.refs_5_.refs_9_.refs_7_), custom_call_target="tpu_custom_call" | custom-call | flops 805306368 | bytes 5505024 | tf_op jit(solution)/shard_map/product/pallas_call | solution.py:146
  11.3 0.2 collective-permute-start.1
  11.5 0.0 collective-permute-done.2.refs_3_
  11.5 1.1 %product.19 = f32[128,512]{1,0:T(8,128)S(1)} custom-call(f32[128,2048]{1,0:T(8,128)S(1)} %pick.2.refs_0_, f32[128,2048]{1,0:T(8,128)S(1)} %collective-permute-done.refs_1_, f32[128,2048]{1,0:T(8,128)S(1)} %get-tuple-element.22.refs_2_, f32[128,2048]{1,0:T(8,128)S(1)} %collective-permute-done.2.refs_3_, ...), custom_call_target="tpu_custom_call" | custom-call | flops 805306368 | bytes 5505024 | tf_op jit(solution)/shard_map/product/pallas_call | solution.py:146
  12.6 2.0 %collective-permute-start.11 = (f32[128,512]{1,0:T(8,128)S(1)}, f32[128,512]{1,0:T(8,128)S(1)}, u32[]{:S(2)}, u32[]{:S(2)}) collective-permute-start(f32[128,512]{1,0:T(8,128)S(1)} %product.19), channel_id=1, source_target_pairs={{0,4},{4,8},{8,12},{12,14},{14,10},{10,6},{6,2},{2,0},{1,5},{5,9},... | collective-permute-start | bytes 786440 | tf_op jit(solution)/shard_map/ppermute | solution.py:245
  14.6 0.0 collective-permute-done.4.refs_5_
  14.6 1.1 %product.15 = f32[128,512]{1,0:T(8,128)S(1)} custom-call(f32[128,2048]{1,0:T(8,128)S(1)} %pick.2.refs_0_, f32[128,2048]{1,0:T(8,128)S(1)} %collective-permute-done.refs_1_, f32[128,2048]{1,0:T(8,128)S(1)} %get-tuple-element.22.refs_2_, f32[128,2048]{1,0:T(8,128)S(1)} %collective-permute-done.2.refs_3_, f32[128,2048]{1,0:T(8,128)S(1)} %get-tuple-element.23.refs_4_, ...), custom_call_target="tpu_custom_call" | custom-call | flops 805306368 | bytes 5505024 | tf_op jit(solution)/shard_map/product/pallas_call | solution.py:146
  15.7 0.1 collective-permute-start.8
  15.8 1.1 %product.21 = f32[128,512]{1,0:T(8,128)S(1)} custom-call(f32[128,2048]{1,0:T(8,128)S(1)} %pick.2.refs_0_, f32[128,2048]{1,0:T(8,128)S(1)} %collective-permute-done.refs_1_, f32[128,2048]{1,0:T(8,128)S(1)} %get-tuple-element.22.refs_2_, f32[128,2048]{1,0:T(8,128)S(1)} %collective-permute-done.2.refs_3_, f32[128,2048]{1,0:T(8,128)S(1)} %get-tuple-element.23.refs_4_, ...), custom_call_target="tpu_custom_call" | custom-call | flops 805306368 | bytes 5505024 | tf_op jit(solution)/shard_map/product/pallas_call | solution.py:146
  16.9 1.1 %product.12 = f32[128,512]{1,0:T(8,128)S(1)} custom-call(f32[128,2048]{1,0:T(8,128)S(1)} %pick.2.refs_0_, f32[128,2048]{1,0:T(8,128)S(1)} %collective-permute-done.refs_1_, f32[128,2048]{1,0:T(8,128)S(1)} %get-tuple-element.22.refs_2_, f32[128,2048]{1,0:T(8,128)S(1)} %collective-permute-done.2.refs_3_, ...), custom_call_target="tpu_custom_call" | custom-call | flops 805306368 | bytes 5505024 | tf_op jit(solution)/shard_map/product/pallas_call | solution.py:146
  18.0 0.0 collective-permute-done.14
  18.1 1.9 %collective-permute-start.15 = (f32[128,512]{1,0:T(8,128)S(1)}, f32[128,512]{1,0:T(8,128)S(1)}, u32[]{:S(2)}, u32[]{:S(2)}) collective-permute-start(f32[128,512]{1,0:T(8,128)S(1)} %add.37), channel_id=1, source_target_pairs={{0,2},{4,0},{8,4},{12,8},{14,12},{10,14},{6,10},{2,6},{1,3},{5,1},... | collective-permute-start | bytes 786440 | tf_op jit(solution)/shard_map/ppermute | solution.py:245
  20.0 0.6 %collective-permute-done.1 = f32[128,512]{1,0:T(8,128)S(1)} collective-permute-done((f32[128,512]{1,0:T(8,128)S(1)}, f32[128,512]{1,0:T(8,128)S(1)}, u32[]{:S(2)}, u32[]{:S(2)}) %collective-permute-start.1) | collective-permute-done | bytes 262176 | tf_op jit(solution)/shard_map/ppermute | solution.py:245
  20.6 0.1 collective-permute-start.3
  20.8 0.0 collective-permute-done.5.refs_7_
  20.8 1.9 %product.16 = (f32[128,512]{1,0:T(8,128)S(1)}, f32[128,512]{1,0:T(8,128)S(1)}) custom-call(f32[128,2048]{1,0:T(8,128)S(1)} %pick.2.refs_0_, f32[128,2048]{1,0:T(8,128)S(1)} %collective-permute-done.refs_1_, f32[128,2048]{1,0:T(8,128)S(1)} %get-tuple-element.22.refs_2_, f32[128,2048]{1,0:T(8,128)S(1)} %collective-permute-done.2.refs_3_, ...), custom_call_target="tpu_custom_call" | custom-call | flops 1610612736 | bytes 9961472 | tf_op jit(solution)/shard_map/product/pallas_call | solution.py:146
  22.7 1.9 %product.13 = (f32[128,512]{1,0:T(8,128)S(1)}, f32[128,512]{1,0:T(8,128)S(1)}) custom-call(f32[128,2048]{1,0:T(8,128)S(1)} %pick.2.refs_0_, f32[128,2048]{1,0:T(8,128)S(1)} %collective-permute-done.refs_1_, f32[128,2048]{1,0:T(8,128)S(1)} %get-tuple-element.22.refs_2_, f32[128,2048]{1,0:T(8,128)S(1)} %collective-permute-done.2.refs_3_, ...), custom_call_target="tpu_custom_call" | custom-call | flops 1610612736 | bytes 9961472 | tf_op jit(solution)/shard_map/product/pallas_call | solution.py:146
  24.6 1.6 %collective-permute-done.11 = f32[128,512]{1,0:T(8,128)S(1)} collective-permute-done((f32[128,512]{1,0:T(8,128)S(1)}, f32[128,512]{1,0:T(8,128)S(1)}, u32[]{:S(2)}, u32[]{:S(2)}) %collective-permute-start.11) | collective-permute-done | bytes 262176 | tf_op jit(solution)/shard_map/ppermute | solution.py:245
  26.3 0.5 collective-permute-start.12
  26.8 0.0 collective-permute-done.8
  26.8 1.6 %collective-permute-start.9 = (f32[128,512]{1,0:T(8,128)S(1)}, f32[128,512]{1,0:T(8,128)S(1)}, u32[]{:S(2)}, u32[]{:S(2)}) collective-permute-start(f32[128,512]{1,0:T(8,128)S(1)} %add.33), channel_id=1, source_target_pairs={{0,2},{4,0},{8,4},{12,8},{14,12},{10,14},{6,10},{2,6},{1,3},{5,1},... | collective-permute-start | bytes 786440 | tf_op jit(solution)/shard_map/ppermute | solution.py:245
  28.4 2.0 %collective-permute-done.15 = f32[128,512]{1,0:T(8,128)S(1)} collective-permute-done((f32[128,512]{1,0:T(8,128)S(1)}, f32[128,512]{1,0:T(8,128)S(1)}, u32[]{:S(2)}, u32[]{:S(2)}) %collective-permute-start.15) | collective-permute-done | bytes 262176 | tf_op jit(solution)/shard_map/ppermute | solution.py:245
  30.5 0.3 collective-permute-start.16
  30.7 1.1 %collective-permute-done.3 = f32[128,512]{1,0:T(8,128)S(1)} collective-permute-done((f32[128,512]{1,0:T(8,128)S(1)}, f32[128,512]{1,0:T(8,128)S(1)}, u32[]{:S(2)}, u32[]{:S(2)}) %collective-permute-start.3) | collective-permute-done | bytes 262176 | tf_op jit(solution)/shard_map/ppermute | solution.py:245
  31.9 0.8 %collective-permute-start.6 = (f32[128,512]{1,0:T(8,128)S(1)}, f32[128,512]{1,0:T(8,128)S(1)}, u32[]{:S(2)}, u32[]{:S(2)}) collective-permute-start(f32[128,512]{1,0:T(8,128)S(1)} %add.31), channel_id=1, source_target_pairs={{0,4},{4,8},{8,12},{12,14},{14,10},{10,6},{6,2},{2,0},{1,5},{5,9},... | collective-permute-start | bytes 786440 | tf_op jit(solution)/shard_map/ppermute | solution.py:245
  32.6 1.9 %product.17 = (f32[128,512]{1,0:T(8,128)S(1)}, f32[128,512]{1,0:T(8,128)S(1)}) custom-call(f32[128,2048]{1,0:T(8,128)S(1)} %pick.2.refs_0_, f32[128,2048]{1,0:T(8,128)S(1)} %collective-permute-done.refs_1_, f32[128,2048]{1,0:T(8,128)S(1)} %get-tuple-element.22.refs_2_, f32[128,2048]{1,0:T(8,128)S(1)} %collective-permute-done.2.refs_3_, ...), custom_call_target="tpu_custom_call" | custom-call | flops 1610612736 | bytes 9961472 | tf_op jit(solution)/shard_map/product/pallas_call | solution.py:146
  34.5 2.1 %product.14 = (f32[128,512]{1,0:T(8,128)S(1)}, f32[128,512]{1,0:T(8,128)S(1)}) custom-call(f32[128,2048]{1,0:T(8,128)S(1)} %pick.2.refs_0_, f32[128,2048]{1,0:T(8,128)S(1)} %collective-permute-done.refs_1_, f32[128,2048]{1,0:T(8,128)S(1)} %get-tuple-element.22.refs_2_, f32[128,2048]{1,0:T(8,128)S(1)} %collective-permute-done.2.refs_3_, ...), custom_call_target="tpu_custom_call" | custom-call | flops 1610612736 | bytes 9961472 | tf_op jit(solution)/shard_map/product/pallas_call | solution.py:146
  36.6 0.8 %collective-permute-done.12 = f32[128,512]{1,0:T(8,128)S(1)} collective-permute-done((f32[128,512]{1,0:T(8,128)S(1)}, f32[128,512]{1,0:T(8,128)S(1)}, u32[]{:S(2)}, u32[]{:S(2)}) %collective-permute-start.12) | collective-permute-done | bytes 262176 | tf_op jit(solution)/shard_map/ppermute | solution.py:245
  37.5 1.1 %collective-permute-start.13 = (f32[128,512]{1,0:T(8,128)S(1)}, f32[128,512]{1,0:T(8,128)S(1)}, u32[]{:S(2)}, u32[]{:S(2)}) collective-permute-start(f32[128,512]{1,0:T(8,128)S(1)} %add.36), channel_id=1, source_target_pairs={{0,4},{4,8},{8,12},{12,14},{14,10},{10,6},{6,2},{2,0},{1,5},{5,9},... | collective-permute-start | bytes 786440 | tf_op jit(solution)/shard_map/ppermute | solution.py:245
  38.6 0.0 collective-permute-done.9
  38.6 1.1 %collective-permute-start.10 = (f32[128,512]{1,0:T(8,128)S(1)}, f32[128,512]{1,0:T(8,128)S(1)}, u32[]{:S(2)}, u32[]{:S(2)}) collective-permute-start(f32[128,512]{1,0:T(8,128)S(1)} %add.34), channel_id=1, source_target_pairs={{0,2},{4,0},{8,4},{12,8},{14,12},{10,14},{6,10},{2,6},{1,3},{5,1},... | collective-permute-start | bytes 786440 | tf_op jit(solution)/shard_map/ppermute | solution.py:245
  39.7 2.0 %collective-permute-done.16 = f32[128,512]{1,0:T(8,128)S(1)} collective-permute-done((f32[128,512]{1,0:T(8,128)S(1)}, f32[128,512]{1,0:T(8,128)S(1)}, u32[]{:S(2)}, u32[]{:S(2)}) %collective-permute-start.16) | collective-permute-done | bytes 262176 | tf_op jit(solution)/shard_map/ppermute | solution.py:245
  41.7 0.7 %collective-permute-start.17 = (f32[128,512]{1,0:T(8,128)S(1)}, f32[128,512]{1,0:T(8,128)S(1)}, u32[]{:S(2)}, u32[]{:S(2)}) collective-permute-start(f32[128,512]{1,0:T(8,128)S(1)} %add.39), channel_id=1, source_target_pairs={{0,2},{4,0},{8,4},{12,8},{14,12},{10,14},{6,10},{2,6},{1,3},{5,1},... | collective-permute-start | bytes 786440 | tf_op jit(solution)/shard_map/ppermute | solution.py:245
  42.4 0.7 %collective-permute-done.6 = f32[128,512]{1,0:T(8,128)S(1)} collective-permute-done((f32[128,512]{1,0:T(8,128)S(1)}, f32[128,512]{1,0:T(8,128)S(1)}, u32[]{:S(2)}, u32[]{:S(2)}) %collective-permute-start.6) | collective-permute-done | bytes 262176 | tf_op jit(solution)/shard_map/ppermute | solution.py:245
  43.1 0.8 %collective-permute-start.7 = (f32[128,512]{1,0:T(8,128)S(1)}, f32[128,512]{1,0:T(8,128)S(1)}, u32[]{:S(2)}, u32[]{:S(2)}) collective-permute-start(f32[128,512]{1,0:T(8,128)S(1)} %add.32), channel_id=1, source_target_pairs={{0,4},{4,8},{8,12},{12,14},{14,10},{10,6},{6,2},{2,0},{1,5},{5,9},... | collective-permute-start | bytes 786440 | tf_op jit(solution)/shard_map/ppermute | solution.py:245
  43.9 1.9 %product.18 = (f32[128,512]{1,0:T(8,128)S(1)}, f32[128,512]{1,0:T(8,128)S(1)}) custom-call(f32[128,2048]{1,0:T(8,128)S(1)} %pick.2.refs_0_, f32[128,2048]{1,0:T(8,128)S(1)} %collective-permute-done.refs_1_, f32[128,2048]{1,0:T(8,128)S(1)} %get-tuple-element.22.refs_2_, f32[128,2048]{1,0:T(8,128)S(1)} %collective-permute-done.2.refs_3_, ...), custom_call_target="tpu_custom_call" | custom-call | flops 1610612736 | bytes 9961472 | tf_op jit(solution)/shard_map/product/pallas_call | solution.py:146
  45.7 2.9 %collective-permute-done.13.refs_3_ = f32[128,512]{1,0:T(8,128)S(1)} collective-permute-done((f32[128,512]{1,0:T(8,128)S(1)}, f32[128,512]{1,0:T(8,128)S(1)}, u32[]{:S(2)}, u32[]{:S(2)}) %collective-permute-start.13) | collective-permute-done | bytes 262176 | tf_op jit(solution)/shard_map/ppermute | solution.py:245
  48.7 0.0 collective-permute-done.10.refs_1_
  48.7 2.6 %collective-permute-done.17.refs_4_ = f32[128,512]{1,0:T(8,128)S(1)} collective-permute-done((f32[128,512]{1,0:T(8,128)S(1)}, f32[128,512]{1,0:T(8,128)S(1)}, u32[]{:S(2)}, u32[]{:S(2)}) %collective-permute-start.17) | collective-permute-done | bytes 262176 | tf_op jit(solution)/shard_map/ppermute | solution.py:245
  51.3 1.8 %collective-permute-done.7.refs_0_ = f32[128,512]{1,0:T(8,128)S(1)} collective-permute-done((f32[128,512]{1,0:T(8,128)S(1)}, f32[128,512]{1,0:T(8,128)S(1)}, u32[]{:S(2)}, u32[]{:S(2)}) %collective-permute-start.7) | collective-permute-done | bytes 262176 | tf_op jit(solution)/shard_map/ppermute | solution.py:245
  53.1 0.9 %finish.1 = f32[128,1024]{1,0:T(8,128)} custom-call(f32[128,512]{1,0:T(8,128)S(1)} %collective-permute-done.7.refs_0_, f32[128,512]{1,0:T(8,128)S(1)} %collective-permute-done.10.refs_1_, f32[128,512]{1,0:T(8,128)S(1)} %get-tuple-element.29.refs_2_, f32[128,512]{1,0:T(8,128)S(1)} %collective-permute-done.13.refs_3_, ...), custom_call_target="tpu_custom_call" | custom-call | tf_op jit(solution)/shard_map/finish/pallas_call | solution.py:176
  (10 shorter events, 0.4 us)
Async XLA Ops:
  0.0 4.9 %copy-start = (f32[2048,1024]{1,0:T(8,128)S(1)}, f32[2048,1024]{1,0:T(8,128)}, u32[]{:S(2)}) copy-start(f32[2048,1024]{1,0:T(8,128)} %value_ref.1) | copy-start | bytes 25165828
  1.4 4.7 %collective-permute-start = (f32[128,2048]{1,0:T(8,128)S(1)}, f32[128,2048]{1,0:T(8,128)S(1)}, u32[]{:S(2)}, u32[]{:S(2)}) collective-permute-start(f32[128,2048]{1,0:T(8,128)S(1)} %pick.2.refs_0_), channel_id=1, source_target_pairs={{0,1},{1,0},{2,3},{3,2},{4,5},{5,4},{6,7},{7,6},{8,9},{9,8},{10,11... | collective-permute-start | bytes 3145736 | tf_op jit(solution)/shard_map/ppermute | solution.py:233
  4.2 7.3 %collective-permute-start.2 = (f32[128,2048]{1,0:T(8,128)S(1)}, f32[128,2048]{1,0:T(8,128)S(1)}, u32[]{:S(2)}, u32[]{:S(2)}) collective-permute-start(f32[128,2048]{1,0:T(8,128)S(1)} %get-tuple-element.22.refs_2_), channel_id=1, source_target_pairs={{0,1},{1,0},{2,3},{3,2},{4,5},{5,4},{6,7},{7,6},{8,9},{9,8},{10,11... | collective-permute-start | bytes 3145736 | tf_op jit(solution)/shard_map/ppermute | solution.py:233
  4.3 10.3 %collective-permute-start.4 = (f32[128,2048]{1,0:T(8,128)S(1)}, f32[128,2048]{1,0:T(8,128)S(1)}, u32[]{:S(2)}, u32[]{:S(2)}) collective-permute-start(f32[128,2048]{1,0:T(8,128)S(1)} %get-tuple-element.23.refs_4_), channel_id=1, source_target_pairs={{0,1},{1,0},{2,3},{3,2},{4,5},{5,4},{6,7},{7,6},{8,9},{9,8},{10,11... | collective-permute-start | bytes 3145736 | tf_op jit(solution)/shard_map/ppermute | solution.py:233
  4.8 16.0 %collective-permute-start.5 = (f32[128,2048]{1,0:T(8,128)S(1)}, f32[128,2048]{1,0:T(8,128)S(1)}, u32[]{:S(2)}, u32[]{:S(2)}) collective-permute-start(f32[128,2048]{1,0:T(8,128)S(1)} %get-tuple-element.24.refs_6_), channel_id=1, source_target_pairs={{0,1},{1,0},{2,3},{3,2},{4,5},{5,4},{6,7},{7,6},{8,9},{9,8},{10,11... | collective-permute-start | bytes 3145736 | tf_op jit(solution)/shard_map/ppermute | solution.py:233
  7.2 10.8 %collective-permute-start.14 = (f32[128,512]{1,0:T(8,128)S(1)}, f32[128,512]{1,0:T(8,128)S(1)}, u32[]{:S(2)}, u32[]{:S(2)}) collective-permute-start(f32[128,512]{1,0:T(8,128)S(1)} %product.20), channel_id=1, source_target_pairs={{0,2},{4,0},{8,4},{12,8},{14,12},{10,14},{6,10},{2,6},{1,3},{5,1},... | collective-permute-start | bytes 786440 | tf_op jit(solution)/shard_map/ppermute | solution.py:245
  11.3 9.3 %collective-permute-start.1 = (f32[128,512]{1,0:T(8,128)S(1)}, f32[128,512]{1,0:T(8,128)S(1)}, u32[]{:S(2)}, u32[]{:S(2)}) collective-permute-start(f32[128,512]{1,0:T(8,128)S(1)} %product.11), channel_id=1, source_target_pairs={{0,4},{4,8},{8,12},{12,14},{14,10},{10,6},{6,2},{2,0},{1,5},{5,9},... | collective-permute-start | bytes 786440 | tf_op jit(solution)/shard_map/ppermute | solution.py:245
  12.6 13.6 %collective-permute-start.11 = (f32[128,512]{1,0:T(8,128)S(1)}, f32[128,512]{1,0:T(8,128)S(1)}, u32[]{:S(2)}, u32[]{:S(2)}) collective-permute-start(f32[128,512]{1,0:T(8,128)S(1)} %product.19), channel_id=1, source_target_pairs={{0,4},{4,8},{8,12},{12,14},{14,10},{10,6},{6,2},{2,0},{1,5},{5,9},... | collective-permute-start | bytes 786440 | tf_op jit(solution)/shard_map/ppermute | solution.py:245
  15.7 11.1 %collective-permute-start.8 = (f32[128,512]{1,0:T(8,128)S(1)}, f32[128,512]{1,0:T(8,128)S(1)}, u32[]{:S(2)}, u32[]{:S(2)}) collective-permute-start(f32[128,512]{1,0:T(8,128)S(1)} %product.15), channel_id=1, source_target_pairs={{0,2},{4,0},{8,4},{12,8},{14,12},{10,14},{6,10},{2,6},{1,3},{5,1},... | collective-permute-start | bytes 786440 | tf_op jit(solution)/shard_map/ppermute | solution.py:245
  18.1 12.4 %collective-permute-start.15 = (f32[128,512]{1,0:T(8,128)S(1)}, f32[128,512]{1,0:T(8,128)S(1)}, u32[]{:S(2)}, u32[]{:S(2)}) collective-permute-start(f32[128,512]{1,0:T(8,128)S(1)} %add.37), channel_id=1, source_target_pairs={{0,2},{4,0},{8,4},{12,8},{14,12},{10,14},{6,10},{2,6},{1,3},{5,1},... | collective-permute-start | bytes 786440 | tf_op jit(solution)/shard_map/ppermute | solution.py:245
  20.6 11.2 %collective-permute-start.3 = (f32[128,512]{1,0:T(8,128)S(1)}, f32[128,512]{1,0:T(8,128)S(1)}, u32[]{:S(2)}, u32[]{:S(2)}) collective-permute-start(f32[128,512]{1,0:T(8,128)S(1)} %add.30), channel_id=1, source_target_pairs={{0,4},{4,8},{8,12},{12,14},{14,10},{10,6},{6,2},{2,0},{1,5},{5,9},... | collective-permute-start | bytes 786440 | tf_op jit(solution)/shard_map/ppermute | solution.py:245
  26.3 11.2 %collective-permute-start.12 = (f32[128,512]{1,0:T(8,128)S(1)}, f32[128,512]{1,0:T(8,128)S(1)}, u32[]{:S(2)}, u32[]{:S(2)}) collective-permute-start(f32[128,512]{1,0:T(8,128)S(1)} %add.35), channel_id=1, source_target_pairs={{0,4},{4,8},{8,12},{12,14},{14,10},{10,6},{6,2},{2,0},{1,5},{5,9},... | collective-permute-start | bytes 786440 | tf_op jit(solution)/shard_map/ppermute | solution.py:245
  26.8 11.8 %collective-permute-start.9 = (f32[128,512]{1,0:T(8,128)S(1)}, f32[128,512]{1,0:T(8,128)S(1)}, u32[]{:S(2)}, u32[]{:S(2)}) collective-permute-start(f32[128,512]{1,0:T(8,128)S(1)} %add.33), channel_id=1, source_target_pairs={{0,2},{4,0},{8,4},{12,8},{14,12},{10,14},{6,10},{2,6},{1,3},{5,1},... | collective-permute-start | bytes 786440 | tf_op jit(solution)/shard_map/ppermute | solution.py:245
  30.5 11.2 %collective-permute-start.16 = (f32[128,512]{1,0:T(8,128)S(1)}, f32[128,512]{1,0:T(8,128)S(1)}, u32[]{:S(2)}, u32[]{:S(2)}) collective-permute-start(f32[128,512]{1,0:T(8,128)S(1)} %add.38), channel_id=1, source_target_pairs={{0,2},{4,0},{8,4},{12,8},{14,12},{10,14},{6,10},{2,6},{1,3},{5,1},... | collective-permute-start | bytes 786440 | tf_op jit(solution)/shard_map/ppermute | solution.py:245
  31.9 11.2 %collective-permute-start.6 = (f32[128,512]{1,0:T(8,128)S(1)}, f32[128,512]{1,0:T(8,128)S(1)}, u32[]{:S(2)}, u32[]{:S(2)}) collective-permute-start(f32[128,512]{1,0:T(8,128)S(1)} %add.31), channel_id=1, source_target_pairs={{0,4},{4,8},{8,12},{12,14},{14,10},{10,6},{6,2},{2,0},{1,5},{5,9},... | collective-permute-start | bytes 786440 | tf_op jit(solution)/shard_map/ppermute | solution.py:245
  37.5 11.2 %collective-permute-start.13 = (f32[128,512]{1,0:T(8,128)S(1)}, f32[128,512]{1,0:T(8,128)S(1)}, u32[]{:S(2)}, u32[]{:S(2)}) collective-permute-start(f32[128,512]{1,0:T(8,128)S(1)} %add.36), channel_id=1, source_target_pairs={{0,4},{4,8},{8,12},{12,14},{14,10},{10,6},{6,2},{2,0},{1,5},{5,9},... | collective-permute-start | bytes 786440 | tf_op jit(solution)/shard_map/ppermute | solution.py:245
  38.6 10.1 %collective-permute-start.10 = (f32[128,512]{1,0:T(8,128)S(1)}, f32[128,512]{1,0:T(8,128)S(1)}, u32[]{:S(2)}, u32[]{:S(2)}) collective-permute-start(f32[128,512]{1,0:T(8,128)S(1)} %add.34), channel_id=1, source_target_pairs={{0,2},{4,0},{8,4},{12,8},{14,12},{10,14},{6,10},{2,6},{1,3},{5,1},... | collective-permute-start | bytes 786440 | tf_op jit(solution)/shard_map/ppermute | solution.py:245
  41.7 9.6 %collective-permute-start.17 = (f32[128,512]{1,0:T(8,128)S(1)}, f32[128,512]{1,0:T(8,128)S(1)}, u32[]{:S(2)}, u32[]{:S(2)}) collective-permute-start(f32[128,512]{1,0:T(8,128)S(1)} %add.39), channel_id=1, source_target_pairs={{0,2},{4,0},{8,4},{12,8},{14,12},{10,14},{6,10},{2,6},{1,3},{5,1},... | collective-permute-start | bytes 786440 | tf_op jit(solution)/shard_map/ppermute | solution.py:245
  43.1 10.0 %collective-permute-start.7 = (f32[128,512]{1,0:T(8,128)S(1)}, f32[128,512]{1,0:T(8,128)S(1)}, u32[]{:S(2)}, u32[]{:S(2)}) collective-permute-start(f32[128,512]{1,0:T(8,128)S(1)} %add.32), channel_id=1, source_target_pairs={{0,4},{4,8},{8,12},{12,14},{14,10},{10,6},{6,2},{2,0},{1,5},{5,9},... | collective-permute-start | bytes 786440 | tf_op jit(solution)/shard_map/ppermute | solution.py:245

commit v6 on v5

v6 whole, which is shorter than its diff:
```python
import functools

import jax
import jax.numpy as jnp
import numpy as np
from jax import lax
from jax.experimental import pallas as pl
from jax.experimental.pallas import tpu as pltpu
from jax.sharding import PartitionSpec as P

CALLS = 8
LANES = 256
MIB = 2**20


def ring_order(mesh):
    count = mesh.shape["row"]
    axes = list(mesh.axis_names)
    line = np.moveaxis(mesh.devices, axes.index("row"), 0).reshape(count, -1)[:, 0]
    spots = [tuple(device.coords) for device in line]
    moving = [axis for axis in range(3) if len({spot[axis] for spot in spots}) > 1]
    plain = list(range(count))
    if len(moving) != 2:
        return plain
    for outer, inner in (moving, moving[::-1]):
        across = sorted({spot[outer] for spot in spots})
        along = sorted({spot[inner] for spot in spots})
        if len(across) % 2 or len(across) * len(along) != count:
            continue
        at = {(spot[outer], spot[inner]): index for index, spot in enumerate(spots)}
        walk = [at[across[0], along[0]]]
        for turn, a in enumerate(across):
            rest = along[1:]
            walk += [at[a, b] for b in (rest if turn % 2 == 0 else rest[::-1])]
        walk += [at[a, along[0]] for a in across[:0:-1]]
        return walk
    return plain


def looked_up(table):
    row, col = lax.axis_index("row"), lax.axis_index("col")
    found = jnp.int32(0)
    for r in range(table.shape[0]):
        for c in range(table.shape[1]):
            found = jnp.where((row == r) & (col == c), jnp.int32(table[r, c]), found)
    return found


def block_copies(starts, size, chunks, a_ref, outs, sems):
    spots = [(out_ref, at * size) for out_ref, count in zip(outs, chunks) for at in range(count)]
    return [
        pltpu.make_async_copy(
            a_ref.at[pl.ds(pl.multiple_of(looked_up(starts[..., index]), size), size)],
            out_ref.at[pl.ds(at, size)],
            sems.at[index],
        )
        for index, (out_ref, at) in enumerate(spots)
    ]


def pick_kernel(starts, size, chunks, a_ref, out_ref, sems):
    copies = block_copies(starts, size, chunks, a_ref, [out_ref], sems)
    for copy in copies:
        copy.start()
    for copy in copies:
        copy.wait()


def pick(inductance, starts, size):
    count = starts.shape[-1]
    width = inductance.shape[1]
    return pl.pallas_call(
        functools.partial(pick_kernel, starts, size, [count]),
        out_shape=jax.ShapeDtypeStruct((count * size, width), jnp.float32),
        in_specs=[pl.BlockSpec(memory_space=pl.ANY)],
        out_specs=pl.BlockSpec(memory_space=pltpu.VMEM),
        scratch_shapes=[pltpu.SemaphoreType.DMA((count,))],
        compiler_params=pltpu.CompilerParams(vmem_limit_bytes=50 * MIB),
        cost_estimate=pl.CostEstimate(flops=0, bytes_accessed=8 * count * size * width, transcendentals=0),
        name="pick",
    )(inductance)


def first_column(part, width):
    return jnp.where((lax.axis_index("col") == 0) == (part == 0), width, 0)


def halves(value):
    high = value.astype(jnp.bfloat16)
    return high, (value - high.astype(jnp.float32)).astype(jnp.bfloat16)


def split_kernel(value_ref, high_ref, low_ref):
    high_ref[...], low_ref[...] = halves(value_ref[...])


def split(current_rates):
    depth, width = current_rates.shape
    tile = min(256, depth)
    tiled = pl.BlockSpec((tile, width), lambda k: (k, 0))
    return pl.pallas_call(
        split_kernel,
        grid=(depth // tile,),
        out_shape=[jax.ShapeDtypeStruct((depth, width), jnp.bfloat16)] * 2,
        in_specs=[tiled],
        out_specs=[tiled] * 2,
        compiler_params=pltpu.CompilerParams(vmem_limit_bytes=40 * MIB),
        cost_estimate=pl.CostEstimate(flops=4 * depth * width, bytes_accessed=8 * depth * width, transcendentals=0),
        name="split",
    )(current_rates)


def product_kernel(starts, size, bounds, parts, given, chunks, *refs):
    count = len(bounds)
    sources, (high_ref, low_ref), refs = refs[:count], refs[count : count + 2], refs[count + 2 :]
    *outs, raw, stack, sems, late_sems = refs
    depth = raw.shape[0]
    late = []
    if chunks:
        a_ref, *outs = outs
        late = block_copies(given, size, chunks, a_ref, outs[len(parts) :], late_sems)
    for copy in late:
        copy.start()
    for index in range(starts.shape[-1]):
        start = looked_up(starts[..., index])
        first = 0
        for source, last in zip(sources, bounds):

            @pl.when((start >= first) & (start < last))
            def _(source=source, first=first, start=start, index=index):
                pltpu.make_async_copy(
                    source.at[pl.ds(pl.multiple_of(start - first, size), size)],
                    raw.at[pl.ds(index * size, size)],
                    sems.at[index],
                ).start()

            first = last
    for index in range(starts.shape[-1]):
        pltpu.make_async_copy(
            sources[0].at[pl.ds(0, size)], raw.at[pl.ds(index * size, size)], sems.at[index]
        ).wait()
    stack[:depth], stack[depth:] = halves(raw[...])
    for part, out_ref in zip(parts, outs):
        width = out_ref.shape[1]
        tile = min(LANES, width)
        for at in range(0, width, tile):
            columns = pl.ds(pl.multiple_of(first_column(part, width) + at, tile), tile)
            both = jnp.dot(stack[...], high_ref[:, columns], preferred_element_type=jnp.float32)
            rest = jnp.dot(stack[:depth], low_ref[:, columns], preferred_element_type=jnp.float32)
            out_ref[:, at : at + tile] = both[:depth] + (both[depth:] + rest)
    for copy in late:
        copy.wait()


def product(sources, starts, size, pair, parts, inductance=None, given=np.zeros(0), chunks=()):
    depth = starts.shape[-1] * size
    inner, width = pair[0].shape
    wanted = [inductance] if chunks else []
    half = jax.ShapeDtypeStruct((depth, width // 2), jnp.float32)
    return pl.pallas_call(
        functools.partial(
            product_kernel, starts, size, list(np.cumsum([s.shape[0] for s in sources])), parts, given, chunks
        ),
        out_shape=[half] * len(parts) + [jax.ShapeDtypeStruct((chunk * size, inner), jnp.float32) for chunk in chunks],
        in_specs=[pl.BlockSpec(memory_space=pl.ANY)] * len(sources) + [pl.BlockSpec(memory_space=pltpu.VMEM)] * 2
        + [pl.BlockSpec(memory_space=pl.ANY)] * len(wanted),
        out_specs=[pl.BlockSpec(memory_space=pltpu.VMEM)] * len(parts)
        + [pl.BlockSpec(memory_space=pl.ANY)] * len(chunks),
        scratch_shapes=[
            pltpu.VMEM((depth, inner), jnp.float32),
            pltpu.VMEM((2 * depth, inner), jnp.bfloat16),
            pltpu.SemaphoreType.DMA((starts.shape[-1],)),
            pltpu.SemaphoreType.DMA((max(given.shape[-1], 1),)),
        ],
        compiler_params=pltpu.CompilerParams(vmem_limit_bytes=(40 if chunks else 16) * MIB),
        cost_estimate=pl.CostEstimate(
            flops=3 * depth * inner * width * len(parts),
            bytes_accessed=4 * depth * inner + (2 * inner + 2 * depth) * width * len(parts),
            transcendentals=0,
        ),
        name="product",
    )(*sources, *pair, *wanted)


def finish_kernel(*refs):
    out_ref = refs[-1]
    for part in range(2):
        above, below, own = refs[3 * part : 3 * part + 3]
        width = own.shape[1]
        columns = pl.ds(pl.multiple_of(first_column(part, width), width), width)
        out_ref[:, columns] = (above[...] + below[...]) + own[...]


def finish(*values):
    depth, width = values[0].shape
    return pl.pallas_call(
        finish_kernel,
        out_shape=jax.ShapeDtypeStruct((depth, 2 * width), jnp.float32),
        in_specs=[pl.BlockSpec(memory_space=pltpu.VMEM)] * 6,
        out_specs=pl.BlockSpec(memory_space=pltpu.VMEM),
        compiler_params=pltpu.CompilerParams(vmem_limit_bytes=8 * MIB),
        name="finish",
    )(*values)


def plan(order, rows, cols, size, chunks):
    place = np.zeros(rows, np.int64)
    place[order] = np.arange(rows)
    each, half = rows // cols, rows // 2
    needs = np.zeros((rows, cols, rows), np.int64)
    for core in range(cols):
        ways = (-1, 1) if core == 0 else (1, -1)
        steps = [half] + [way * (half - step) for step in range(1, half) for way in ways] + [0]
        for row in range(rows):
            needs[row, core] = [order[(place[row] + step) % rows] for step in steps]
    spots = [(2 * sum(chunks[:chunk]) + at, count) for chunk, count in enumerate(chunks) for at in range(count)]
    taken = np.zeros((rows, cols, rows), np.int64)
    given = np.zeros((rows, cols, each), np.int64)
    for row in range(rows):
        for core in range(cols):
            sent = [block for block in needs[row, cols - 1 - core] if block // each == core]
            given[row, core] = [(block - core * each) * size for block in sent]
            arrived = 0
            for k, block in enumerate(needs[row, core]):
                if block // each == core:
                    taken[row, core, k] = spots[sent.index(block)][0] * size
                else:
                    taken[row, core, k] = sum(spots[arrived]) * size
                    arrived += 1
    return taken, given


def solution(mesh):
    rows, cols = mesh.shape["row"], mesh.shape["col"]
    order = ring_order(mesh)
    group = max(rows // CALLS, 1)
    half = rows // 2
    swap = [(core, cols - 1 - core) for core in range(cols)]
    ways = [
        [
            (order[i] * cols + core, order[(i + (way if core else -way)) % rows] * cols + core)
            for i in range(rows)
            for core in range(cols)
        ]
        for way in (1, -1)
    ]

    def shards(inductance, current_rates):
        size = inductance.shape[0] * cols // rows
        spare = int(group > 1)
        chunks = [group + spare] + [group] * (rows // cols // group - 2) + [group - spare]
        taken, given = plan(order, rows, cols, size, chunks)
        own = [pick(inductance, given[..., : chunks[0]], size)]
        received = [lax.ppermute(own[0], "col", swap)]
        pair = split(current_rates)
        early, *later = product(
            [own[0], received[0]], taken[..., :group], size, pair, [0], inductance, given[..., chunks[0] :], chunks[1:]
        )
        own += later
        received += [lax.ppermute(each, "col", swap) for each in later]
        sources = [rows for pair_of in zip(own, received) for rows in pair_of]
        firsts = np.cumsum([0] + [each.shape[0] for each in sources])
        calls = {(0, 0): early}

        def term(index, part):
            call, at = divmod(index, group)
            if (call, part) not in calls:
                parts = [part] if call < 3 else [0, 1]
                starts = taken[..., call * group : (call + 1) * group]
                have = sources[: int(np.searchsorted(firsts, starts.max(), "right"))]
                got = product(have, starts, size, pair, parts)
                calls.update({(call, each): value for each, value in zip(parts, got)})
            return calls[call, part][at * size : (at + 1) * size]

        sums = [[None, None], [None, None]]
        for step in range(half):
            for late in (1, 0):
                for way in range(2):
                    part = (way + late) % 2
                    if step == 0 and late:
                        continue
                    value = term(2 * step - 1 + way if step else 0, part)
                    if sums[way][part] is not None:
                        value = sums[way][part] + value
                    sums[way][part] = lax.ppermute(value, ("row", "col"), ways[way])
        return finish(*(each for part in range(2) for each in (sums[0][part], sums[1][part], term(rows - 1, part))))

    placed = (P(("groups", "col"), "row"), P("row", ("groups", "col")))
    return jax.shard_map(
        shards, mesh=mesh, in_specs=placed, out_specs=P("row", ("groups", "col")), check_vma=False
    )
```

time: 54.1 us -> 58.1 us (1.074)
  Pallas kernels: 21.9 us -> 25.9 us
  waiting for transfers between devices: 16.1 us -> 14.6 us
  starting transfers between devices: 15.4 us -> 16.8 us
    pallas_call x3 -> x2, Pallas kernels: 4.91 us -> 7.26 us  [the longest x1 6.02 us: split(): pl.pallas_call(split_kernel, grid=(depth // tile,), out_shape=[jax.ShapeD...]
    pallas_call x11, Pallas kernels: 16.2 us -> 17.8 us  [product(): pl.pallas_call(functools.partial(product_kernel, starts, size, list(np.cu...]
    ppermute x18, waiting for transfers between devices: 16.1 us -> 14.6 us  [the longest x14 14.6 us: shards(): sums[way][part] = lax.ppermute(value, ('row', 'col'), ways[way])]
    ppermute x18, starting transfers between devices: 15.4 us -> 16.8 us  [the longest x14 15.6 us: shards(): sums[way][part] = lax.ppermute(value, ('row', 'col'), ways[way])]
  transfers between devices with their start and end apart: 18 -> 18, of which waited for: 10 -> 8; matrix products, arithmetic and copies ran while one was open for 1% -> 1% of each run, Pallas kernels for 36% -> 38%
where the time goes in v6:
time: 58.1 us; the launch traced here: 57.8 us
  Pallas kernels  25.9 us (45%)
  starting transfers between devices  16.8 us (29%)
  waiting for transfers between devices  14.6 us (25%)
    pallas_call x11, Pallas kernels, product(): pl.pallas_call(functools.partial(product_kernel, starts, size, list(np.cu...  17.8 us
    ppermute x14, starting transfers between devices, shards(): sums[way][part] = lax.ppermute(value, ('row', 'col'), ways[way])  15.6 us
    ppermute x14, waiting for transfers between devices, shards(): sums[way][part] = lax.ppermute(value, ('row', 'col'), ways[way])  14.6 us
    pallas_call x1, Pallas kernels, split(): pl.pallas_call(split_kernel, grid=(depth // tile,), out_shape=[jax.ShapeD...  6.02 us
    pallas_call x1, Pallas kernels, pick(): pl.pallas_call(functools.partial(pick_kernel, starts, size, [count]), out...  1.23 us
  transfers between devices with their start and end apart: 18, of which 8 were waited for; matrix products, arithmetic and copies ran while one was open for 1% of the time, Pallas kernels for 38%

profile of v6, /device:TPU:0, one launch (start us, length us, event | category | flops | bytes accessed | tf_op | source)
XLA Modules:
  0.0 57.8 jit_solution(4365923706547322617)
XLA Ops:
  0.0 1.2 %pick.1.refs_0_ = f32[128,2048]{1,0:T(8,128)S(1)} custom-call(f32[512,2048]{1,0:T(8,128)} %refs_4_.1), custom_call_target="tpu_custom_call" | custom-call | bytes 2097152 | tf_op jit(solution)/shard_map/pick/pallas_call | solution.py:72
  1.2 0.5 collective-permute-start
  1.8 6.0 %split.1 = (bf16[2048,1024]{1,0:T(8,128)(2,1)S(1)}, bf16[2048,1024]{1,0:T(8,128)(2,1)S(1)}) custom-call(f32[2048,1024]{1,0:T(8,128)} %value_ref.1), custom_call_target="tpu_custom_call" | custom-call | flops 8388608 | bytes 16777216 | tf_op jit(solution)/shard_map/split/pallas_call | solution.py:101
  7.8 0.0 collective-permute-done.refs_1_
  7.8 1.9 %product.11 = (f32[128,512]{1,0:T(8,128)S(1)}, f32[128,2048]{1,0:T(8,128)S(1)}, f32[128,2048]{1,0:T(8,128)S(1)}, f32[128,2048]{1,0:T(8,128)S(1)}) custom-call(f32[128,2048]{1,0:T(8,128)S(1)} %pick.1.refs_0_, f32[128,2048]{1,0:T(8,128)S(1)} %collective-permute-done.refs_1_, bf16[2048,1024]{1,0:T(8,128)(2,1)S(1)} %get-tuple-element.21.refs_2_.refs_5_.refs_8_.refs_6_, ...), custom_call_target="tpu_custom_call" | custom-call | flops 805306368 | bytes 5505024 | tf_op jit(solution)/shard_map/product/pallas_call | solution.py:160
  9.7 0.1 collective-permute-start.2
  9.9 0.5 collective-permute-start.4
  10.3 0.1 collective-permute-start.5
  10.4 2.9 %collective-permute-start.1 = (f32[128,512]{1,0:T(8,128)S(1)}, f32[128,512]{1,0:T(8,128)S(1)}, u32[]{:S(2)}, u32[]{:S(2)}) collective-permute-start(f32[128,512]{1,0:T(8,128)S(1)} %get-tuple-element.23), channel_id=1, source_target_pairs={{0,2},{1,5},{4,0},{5,9},{8,4},{9,13},{12,8},{13,15},{14,12},{15,11... | collective-permute-start | bytes 786440 | tf_op jit(solution)/shard_map/ppermute | solution.py:285
  13.3 1.1 %product.20 = f32[128,512]{1,0:T(8,128)S(1)} custom-call(f32[128,2048]{1,0:T(8,128)S(1)} %pick.1.refs_0_, f32[128,2048]{1,0:T(8,128)S(1)} %collective-permute-done.refs_1_, bf16[2048,1024]{1,0:T(8,128)(2,1)S(1)} %get-tuple-element.21.refs_2_.refs_5_.refs_8_.refs_6_, bf16[2048,1024]{1,0:T(8,128)(2,1)S(1)} %get-tuple-element.22.refs_3_.refs_6_.refs_9_.refs_7_), custom_call_target="tpu_custom_call" | custom-call | flops 805306368 | bytes 5505024 | tf_op jit(solution)/shard_map/product/pallas_call | solution.py:160
  14.4 0.1 collective-permute-start.14
  14.6 0.0 collective-permute-done.2.refs_3_
  14.6 1.1 %product.12 = f32[128,512]{1,0:T(8,128)S(1)} custom-call(f32[128,2048]{1,0:T(8,128)S(1)} %pick.1.refs_0_, f32[128,2048]{1,0:T(8,128)S(1)} %collective-permute-done.refs_1_, f32[128,2048]{1,0:T(8,128)S(1)} %get-tuple-element.24.refs_2_, f32[128,2048]{1,0:T(8,128)S(1)} %collective-permute-done.2.refs_3_, f32[128,2048]{1,0:T(8,128)S(1)} %get-tuple-element.25.refs_4_, ...), custom_call_target="tpu_custom_call" | custom-call | flops 805306368 | bytes 5505024 | tf_op jit(solution)/shard_map/product/pallas_call | solution.py:160
  15.7 4.0 %collective-permute-done.1 = f32[128,512]{1,0:T(8,128)S(1)} collective-permute-done((f32[128,512]{1,0:T(8,128)S(1)}, f32[128,512]{1,0:T(8,128)S(1)}, u32[]{:S(2)}, u32[]{:S(2)}) %collective-permute-start.1) | collective-permute-done | bytes 262176 | tf_op jit(solution)/shard_map/ppermute | solution.py:285
  19.7 2.5 %collective-permute-start.3 = (f32[128,512]{1,0:T(8,128)S(1)}, f32[128,512]{1,0:T(8,128)S(1)}, u32[]{:S(2)}, u32[]{:S(2)}) collective-permute-start(f32[128,512]{1,0:T(8,128)S(1)} %add.30), channel_id=1, source_target_pairs={{0,2},{1,5},{4,0},{5,9},{8,4},{9,13},{12,8},{13,15},{14,12},{15,11... | collective-permute-start | bytes 786440 | tf_op jit(solution)/shard_map/ppermute | solution.py:285
  22.3 0.0 collective-permute-done.4.refs_5_
  22.3 1.1 %product.15 = f32[128,512]{1,0:T(8,128)S(1)} custom-call(f32[128,2048]{1,0:T(8,128)S(1)} %pick.1.refs_0_, f32[128,2048]{1,0:T(8,128)S(1)} %collective-permute-done.refs_1_, f32[128,2048]{1,0:T(8,128)S(1)} %get-tuple-element.24.refs_2_, f32[128,2048]{1,0:T(8,128)S(1)} %collective-permute-done.2.refs_3_, f32[128,2048]{1,0:T(8,128)S(1)} %get-tuple-element.25.refs_4_, ...), custom_call_target="tpu_custom_call" | custom-call | flops 805306368 | bytes 5505024 | tf_op jit(solution)/shard_map/product/pallas_call | solution.py:160
  23.4 0.1 collective-permute-start.8
  23.5 1.2 %product.19 = f32[128,512]{1,0:T(8,128)S(1)} custom-call(f32[128,2048]{1,0:T(8,128)S(1)} %pick.1.refs_0_, f32[128,2048]{1,0:T(8,128)S(1)} %collective-permute-done.refs_1_, f32[128,2048]{1,0:T(8,128)S(1)} %get-tuple-element.24.refs_2_, f32[128,2048]{1,0:T(8,128)S(1)} %collective-permute-done.2.refs_3_, f32[128,2048]{1,0:T(8,128)S(1)} %get-tuple-element.25.refs_4_, ...), custom_call_target="tpu_custom_call" | custom-call | flops 805306368 | bytes 5505024 | tf_op jit(solution)/shard_map/product/pallas_call | solution.py:160
  24.7 2.0 %collective-permute-start.11 = (f32[128,512]{1,0:T(8,128)S(1)}, f32[128,512]{1,0:T(8,128)S(1)}, u32[]{:S(2)}, u32[]{:S(2)}) collective-permute-start(f32[128,512]{1,0:T(8,128)S(1)} %product.19), channel_id=1, source_target_pairs={{0,2},{1,5},{4,0},{5,9},{8,4},{9,13},{12,8},{13,15},{14,12},{15,11... | collective-permute-start | bytes 786440 | tf_op jit(solution)/shard_map/ppermute | solution.py:285
  26.7 1.1 %product.21 = f32[128,512]{1,0:T(8,128)S(1)} custom-call(f32[128,2048]{1,0:T(8,128)S(1)} %pick.1.refs_0_, f32[128,2048]{1,0:T(8,128)S(1)} %collective-permute-done.refs_1_, f32[128,2048]{1,0:T(8,128)S(1)} %get-tuple-element.24.refs_2_, f32[128,2048]{1,0:T(8,128)S(1)} %collective-permute-done.2.refs_3_, f32[128,2048]{1,0:T(8,128)S(1)} %get-tuple-element.25.refs_4_, ...), custom_call_target="tpu_custom_call" | custom-call | flops 805306368 | bytes 5505024 | tf_op jit(solution)/shard_map/product/pallas_call | solution.py:160
  27.8 0.0 collective-permute-done.14
  27.8 0.1 collective-permute-start.15
  28.0 0.0 collective-permute-done.5.refs_7_
  28.0 2.0 %product.13 = (f32[128,512]{1,0:T(8,128)S(1)}, f32[128,512]{1,0:T(8,128)S(1)}) custom-call(f32[128,2048]{1,0:T(8,128)S(1)} %pick.1.refs_0_, f32[128,2048]{1,0:T(8,128)S(1)} %collective-permute-done.refs_1_, f32[128,2048]{1,0:T(8,128)S(1)} %get-tuple-element.24.refs_2_, f32[128,2048]{1,0:T(8,128)S(1)} %collective-permute-done.2.refs_3_, ...), custom_call_target="tpu_custom_call" | custom-call | flops 1610612736 | bytes 9961472 | tf_op jit(solution)/shard_map/product/pallas_call | solution.py:160
  30.0 2.0 %product.16 = (f32[128,512]{1,0:T(8,128)S(1)}, f32[128,512]{1,0:T(8,128)S(1)}) custom-call(f32[128,2048]{1,0:T(8,128)S(1)} %pick.1.refs_0_, f32[128,2048]{1,0:T(8,128)S(1)} %collective-permute-done.refs_1_, f32[128,2048]{1,0:T(8,128)S(1)} %get-tuple-element.24.refs_2_, f32[128,2048]{1,0:T(8,128)S(1)} %collective-permute-done.2.refs_3_, ...), custom_call_target="tpu_custom_call" | custom-call | flops 1610612736 | bytes 9961472 | tf_op jit(solution)/shard_map/product/pallas_call | solution.py:160
  32.0 0.0 collective-permute-done.3
  32.1 2.0 %collective-permute-start.6 = (f32[128,512]{1,0:T(8,128)S(1)}, f32[128,512]{1,0:T(8,128)S(1)}, u32[]{:S(2)}, u32[]{:S(2)}) collective-permute-start(f32[128,512]{1,0:T(8,128)S(1)} %add.31), channel_id=1, source_target_pairs={{0,2},{1,5},{4,0},{5,9},{8,4},{9,13},{12,8},{13,15},{14,12},{15,11... | collective-permute-start | bytes 786440 | tf_op jit(solution)/shard_map/ppermute | solution.py:285
  34.0 0.0 collective-permute-done.8
  34.1 0.2 collective-permute-start.9
  34.2 0.4 collective-permute-done.11
  34.6 1.7 %collective-permute-start.12 = (f32[128,512]{1,0:T(8,128)S(1)}, f32[128,512]{1,0:T(8,128)S(1)}, u32[]{:S(2)}, u32[]{:S(2)}) collective-permute-start(f32[128,512]{1,0:T(8,128)S(1)} %add.35), channel_id=1, source_target_pairs={{0,2},{1,5},{4,0},{5,9},{8,4},{9,13},{12,8},{13,15},{14,12},{15,11... | collective-permute-start | bytes 786440 | tf_op jit(solution)/shard_map/ppermute | solution.py:285
  36.4 0.7 %collective-permute-done.15 = f32[128,512]{1,0:T(8,128)S(1)} collective-permute-done((f32[128,512]{1,0:T(8,128)S(1)}, f32[128,512]{1,0:T(8,128)S(1)}, u32[]{:S(2)}, u32[]{:S(2)}) %collective-permute-start.15) | collective-permute-done | bytes 262176 | tf_op jit(solution)/shard_map/ppermute | solution.py:285
  37.1 0.1 collective-permute-start.16
  37.2 2.2 %product.14 = (f32[128,512]{1,0:T(8,128)S(1)}, f32[128,512]{1,0:T(8,128)S(1)}) custom-call(f32[128,2048]{1,0:T(8,128)S(1)} %pick.1.refs_0_, f32[128,2048]{1,0:T(8,128)S(1)} %collective-permute-done.refs_1_, f32[128,2048]{1,0:T(8,128)S(1)} %get-tuple-element.24.refs_2_, f32[128,2048]{1,0:T(8,128)S(1)} %collective-permute-done.2.refs_3_, ...), custom_call_target="tpu_custom_call" | custom-call | flops 1610612736 | bytes 9961472 | tf_op jit(solution)/shard_map/product/pallas_call | solution.py:160
  39.4 2.0 %product.17 = (f32[128,512]{1,0:T(8,128)S(1)}, f32[128,512]{1,0:T(8,128)S(1)}) custom-call(f32[128,2048]{1,0:T(8,128)S(1)} %pick.1.refs_0_, f32[128,2048]{1,0:T(8,128)S(1)} %collective-permute-done.refs_1_, f32[128,2048]{1,0:T(8,128)S(1)} %get-tuple-element.24.refs_2_, f32[128,2048]{1,0:T(8,128)S(1)} %collective-permute-done.2.refs_3_, ...), custom_call_target="tpu_custom_call" | custom-call | flops 1610612736 | bytes 9961472 | tf_op jit(solution)/shard_map/product/pallas_call | solution.py:160
  41.4 0.0 collective-permute-done.6
  41.5 2.0 %collective-permute-start.7 = (f32[128,512]{1,0:T(8,128)S(1)}, f32[128,512]{1,0:T(8,128)S(1)}, u32[]{:S(2)}, u32[]{:S(2)}) collective-permute-start(f32[128,512]{1,0:T(8,128)S(1)} %add.32), channel_id=1, source_target_pairs={{0,2},{1,5},{4,0},{5,9},{8,4},{9,13},{12,8},{13,15},{14,12},{15,11... | collective-permute-start | bytes 786440 | tf_op jit(solution)/shard_map/ppermute | solution.py:285
  43.5 0.0 collective-permute-done.9
  43.5 0.1 collective-permute-start.10
  43.7 3.3 %collective-permute-done.12 = f32[128,512]{1,0:T(8,128)S(1)} collective-permute-done((f32[128,512]{1,0:T(8,128)S(1)}, f32[128,512]{1,0:T(8,128)S(1)}, u32[]{:S(2)}, u32[]{:S(2)}) %collective-permute-start.12) | collective-permute-done | bytes 262176 | tf_op jit(solution)/shard_map/ppermute | solution.py:285
  47.0 1.6 %collective-permute-start.13 = (f32[128,512]{1,0:T(8,128)S(1)}, f32[128,512]{1,0:T(8,128)S(1)}, u32[]{:S(2)}, u32[]{:S(2)}) collective-permute-start(f32[128,512]{1,0:T(8,128)S(1)} %add.36), channel_id=1, source_target_pairs={{0,2},{1,5},{4,0},{5,9},{8,4},{9,13},{12,8},{13,15},{14,12},{15,11... | collective-permute-start | bytes 786440 | tf_op jit(solution)/shard_map/ppermute | solution.py:285
  48.6 0.4 collective-permute-done.16
  49.0 0.2 collective-permute-start.17
  49.2 2.0 %product.18 = (f32[128,512]{1,0:T(8,128)S(1)}, f32[128,512]{1,0:T(8,128)S(1)}) custom-call(f32[128,2048]{1,0:T(8,128)S(1)} %pick.1.refs_0_, f32[128,2048]{1,0:T(8,128)S(1)} %collective-permute-done.refs_1_, f32[128,2048]{1,0:T(8,128)S(1)} %get-tuple-element.24.refs_2_, f32[128,2048]{1,0:T(8,128)S(1)} %collective-permute-done.2.refs_3_, ...), custom_call_target="tpu_custom_call" | custom-call | flops 1610612736 | bytes 9961472 | tf_op jit(solution)/shard_map/product/pallas_call | solution.py:160
  51.2 1.4 %collective-permute-done.7.refs_0_ = f32[128,512]{1,0:T(8,128)S(1)} collective-permute-done((f32[128,512]{1,0:T(8,128)S(1)}, f32[128,512]{1,0:T(8,128)S(1)}, u32[]{:S(2)}, u32[]{:S(2)}) %collective-permute-start.7) | collective-permute-done | bytes 262176 | tf_op jit(solution)/shard_map/ppermute | solution.py:285
  52.6 1.3 %collective-permute-done.10.refs_1_ = f32[128,512]{1,0:T(8,128)S(1)} collective-permute-done((f32[128,512]{1,0:T(8,128)S(1)}, f32[128,512]{1,0:T(8,128)S(1)}, u32[]{:S(2)}, u32[]{:S(2)}) %collective-permute-start.10) | collective-permute-done | bytes 262176 | tf_op jit(solution)/shard_map/ppermute | solution.py:285
  53.9 3.1 %collective-permute-done.13.refs_3_ = f32[128,512]{1,0:T(8,128)S(1)} collective-permute-done((f32[128,512]{1,0:T(8,128)S(1)}, f32[128,512]{1,0:T(8,128)S(1)}, u32[]{:S(2)}, u32[]{:S(2)}) %collective-permute-start.13) | collective-permute-done | bytes 262176 | tf_op jit(solution)/shard_map/ppermute | solution.py:285
  57.0 0.0 collective-permute-done.17.refs_4_
  57.0 0.9 %finish.1 = f32[128,1024]{1,0:T(8,128)} custom-call(f32[128,512]{1,0:T(8,128)S(1)} %collective-permute-done.7.refs_0_, f32[128,512]{1,0:T(8,128)S(1)} %collective-permute-done.10.refs_1_, f32[128,512]{1,0:T(8,128)S(1)} %get-tuple-element.31.refs_2_, f32[128,512]{1,0:T(8,128)S(1)} %collective-permute-done.13.refs_3_, ...), custom_call_target="tpu_custom_call" | custom-call | tf_op jit(solution)/shard_map/finish/pallas_call | solution.py:196
  (10 shorter events, 0.4 us)
Async XLA Ops:
  1.2 6.6 %collective-permute-start = (f32[128,2048]{1,0:T(8,128)S(1)}, f32[128,2048]{1,0:T(8,128)S(1)}, u32[]{:S(2)}, u32[]{:S(2)}) collective-permute-start(f32[128,2048]{1,0:T(8,128)S(1)} %pick.1.refs_0_), channel_id=1, source_target_pairs={{0,1},{1,0},{2,3},{3,2},{4,5},{5,4},{6,7},{7,6},{8,9},{9,8},{10,11... | collective-permute-start | bytes 3145736 | tf_op jit(solution)/shard_map/ppermute | solution.py:254
  9.7 4.8 %collective-permute-start.2 = (f32[128,2048]{1,0:T(8,128)S(1)}, f32[128,2048]{1,0:T(8,128)S(1)}, u32[]{:S(2)}, u32[]{:S(2)}) collective-permute-start(f32[128,2048]{1,0:T(8,128)S(1)} %get-tuple-element.24.refs_2_), channel_id=1, source_target_pairs={{0,1},{1,0},{2,3},{3,2},{4,5},{5,4},{6,7},{7,6},{8,9},{9,8},{10,11... | collective-permute-start | bytes 3145736 | tf_op jit(solution)/shard_map/ppermute | solution.py:260
  9.9 12.4 %collective-permute-start.4 = (f32[128,2048]{1,0:T(8,128)S(1)}, f32[128,2048]{1,0:T(8,128)S(1)}, u32[]{:S(2)}, u32[]{:S(2)}) collective-permute-start(f32[128,2048]{1,0:T(8,128)S(1)} %get-tuple-element.25.refs_4_), channel_id=1, source_target_pairs={{0,1},{1,0},{2,3},{3,2},{4,5},{5,4},{6,7},{7,6},{8,9},{9,8},{10,11... | collective-permute-start | bytes 3145736 | tf_op jit(solution)/shard_map/ppermute | solution.py:260
  10.3 17.7 %collective-permute-start.5 = (f32[128,2048]{1,0:T(8,128)S(1)}, f32[128,2048]{1,0:T(8,128)S(1)}, u32[]{:S(2)}, u32[]{:S(2)}) collective-permute-start(f32[128,2048]{1,0:T(8,128)S(1)} %get-tuple-element.26.refs_6_), channel_id=1, source_target_pairs={{0,1},{1,0},{2,3},{3,2},{4,5},{5,4},{6,7},{7,6},{8,9},{9,8},{10,11... | collective-permute-start | bytes 3145736 | tf_op jit(solution)/shard_map/ppermute | solution.py:260
  10.4 9.3 %collective-permute-start.1 = (f32[128,512]{1,0:T(8,128)S(1)}, f32[128,512]{1,0:T(8,128)S(1)}, u32[]{:S(2)}, u32[]{:S(2)}) collective-permute-start(f32[128,512]{1,0:T(8,128)S(1)} %get-tuple-element.23), channel_id=1, source_target_pairs={{0,2},{1,5},{4,0},{5,9},{8,4},{9,13},{12,8},{13,15},{14,12},{15,11... | collective-permute-start | bytes 786440 | tf_op jit(solution)/shard_map/ppermute | solution.py:285
  14.4 13.4 %collective-permute-start.14 = (f32[128,512]{1,0:T(8,128)S(1)}, f32[128,512]{1,0:T(8,128)S(1)}, u32[]{:S(2)}, u32[]{:S(2)}) collective-permute-start(f32[128,512]{1,0:T(8,128)S(1)} %product.20), channel_id=1, source_target_pairs={{0,4},{1,3},{4,8},{5,1},{8,12},{9,5},{12,14},{13,9},{14,10},{15,13... | collective-permute-start | bytes 786440 | tf_op jit(solution)/shard_map/ppermute | solution.py:285
  19.7 12.3 %collective-permute-start.3 = (f32[128,512]{1,0:T(8,128)S(1)}, f32[128,512]{1,0:T(8,128)S(1)}, u32[]{:S(2)}, u32[]{:S(2)}) collective-permute-start(f32[128,512]{1,0:T(8,128)S(1)} %add.30), channel_id=1, source_target_pairs={{0,2},{1,5},{4,0},{5,9},{8,4},{9,13},{12,8},{13,15},{14,12},{15,11... | collective-permute-start | bytes 786440 | tf_op jit(solution)/shard_map/ppermute | solution.py:285
  23.4 10.6 %collective-permute-start.8 = (f32[128,512]{1,0:T(8,128)S(1)}, f32[128,512]{1,0:T(8,128)S(1)}, u32[]{:S(2)}, u32[]{:S(2)}) collective-permute-start(f32[128,512]{1,0:T(8,128)S(1)} %product.15), channel_id=1, source_target_pairs={{0,4},{1,3},{4,8},{5,1},{8,12},{9,5},{12,14},{13,9},{14,10},{15,13... | collective-permute-start | bytes 786440 | tf_op jit(solution)/shard_map/ppermute | solution.py:285
  24.7 9.9 %collective-permute-start.11 = (f32[128,512]{1,0:T(8,128)S(1)}, f32[128,512]{1,0:T(8,128)S(1)}, u32[]{:S(2)}, u32[]{:S(2)}) collective-permute-start(f32[128,512]{1,0:T(8,128)S(1)} %product.19), channel_id=1, source_target_pairs={{0,2},{1,5},{4,0},{5,9},{8,4},{9,13},{12,8},{13,15},{14,12},{15,11... | collective-permute-start | bytes 786440 | tf_op jit(solution)/shard_map/ppermute | solution.py:285
  27.8 9.2 %collective-permute-start.15 = (f32[128,512]{1,0:T(8,128)S(1)}, f32[128,512]{1,0:T(8,128)S(1)}, u32[]{:S(2)}, u32[]{:S(2)}) collective-permute-start(f32[128,512]{1,0:T(8,128)S(1)} %add.37), channel_id=1, source_target_pairs={{0,4},{1,3},{4,8},{5,1},{8,12},{9,5},{12,14},{13,9},{14,10},{15,13... | collective-permute-start | bytes 786440 | tf_op jit(solution)/shard_map/ppermute | solution.py:285
  32.1 9.4 %collective-permute-start.6 = (f32[128,512]{1,0:T(8,128)S(1)}, f32[128,512]{1,0:T(8,128)S(1)}, u32[]{:S(2)}, u32[]{:S(2)}) collective-permute-start(f32[128,512]{1,0:T(8,128)S(1)} %add.31), channel_id=1, source_target_pairs={{0,2},{1,5},{4,0},{5,9},{8,4},{9,13},{12,8},{13,15},{14,12},{15,11... | collective-permute-start | bytes 786440 | tf_op jit(solution)/shard_map/ppermute | solution.py:285
  34.1 9.4 %collective-permute-start.9 = (f32[128,512]{1,0:T(8,128)S(1)}, f32[128,512]{1,0:T(8,128)S(1)}, u32[]{:S(2)}, u32[]{:S(2)}) collective-permute-start(f32[128,512]{1,0:T(8,128)S(1)} %add.33), channel_id=1, source_target_pairs={{0,4},{1,3},{4,8},{5,1},{8,12},{9,5},{12,14},{13,9},{14,10},{15,13... | collective-permute-start | bytes 786440 | tf_op jit(solution)/shard_map/ppermute | solution.py:285
  34.6 12.3 %collective-permute-start.12 = (f32[128,512]{1,0:T(8,128)S(1)}, f32[128,512]{1,0:T(8,128)S(1)}, u32[]{:S(2)}, u32[]{:S(2)}) collective-permute-start(f32[128,512]{1,0:T(8,128)S(1)} %add.35), channel_id=1, source_target_pairs={{0,2},{1,5},{4,0},{5,9},{8,4},{9,13},{12,8},{13,15},{14,12},{15,11... | collective-permute-start | bytes 786440 | tf_op jit(solution)/shard_map/ppermute | solution.py:285
  37.1 11.9 %collective-permute-start.16 = (f32[128,512]{1,0:T(8,128)S(1)}, f32[128,512]{1,0:T(8,128)S(1)}, u32[]{:S(2)}, u32[]{:S(2)}) collective-permute-start(f32[128,512]{1,0:T(8,128)S(1)} %add.38), channel_id=1, source_target_pairs={{0,4},{1,3},{4,8},{5,1},{8,12},{9,5},{12,14},{13,9},{14,10},{15,13... | collective-permute-start | bytes 786440 | tf_op jit(solution)/shard_map/ppermute | solution.py:285
  41.5 11.1 %collective-permute-start.7 = (f32[128,512]{1,0:T(8,128)S(1)}, f32[128,512]{1,0:T(8,128)S(1)}, u32[]{:S(2)}, u32[]{:S(2)}) collective-permute-start(f32[128,512]{1,0:T(8,128)S(1)} %add.32), channel_id=1, source_target_pairs={{0,2},{1,5},{4,0},{5,9},{8,4},{9,13},{12,8},{13,15},{14,12},{15,11... | collective-permute-start | bytes 786440 | tf_op jit(solution)/shard_map/ppermute | solution.py:285
  43.5 10.3 %collective-permute-start.10 = (f32[128,512]{1,0:T(8,128)S(1)}, f32[128,512]{1,0:T(8,128)S(1)}, u32[]{:S(2)}, u32[]{:S(2)}) collective-permute-start(f32[128,512]{1,0:T(8,128)S(1)} %add.34), channel_id=1, source_target_pairs={{0,4},{1,3},{4,8},{5,1},{8,12},{9,5},{12,14},{13,9},{14,10},{15,13... | collective-permute-start | bytes 786440 | tf_op jit(solution)/shard_map/ppermute | solution.py:285
  47.0 9.9 %collective-permute-start.13 = (f32[128,512]{1,0:T(8,128)S(1)}, f32[128,512]{1,0:T(8,128)S(1)}, u32[]{:S(2)}, u32[]{:S(2)}) collective-permute-start(f32[128,512]{1,0:T(8,128)S(1)} %add.36), channel_id=1, source_target_pairs={{0,2},{1,5},{4,0},{5,9},{8,4},{9,13},{12,8},{13,15},{14,12},{15,11... | collective-permute-start | bytes 786440 | tf_op jit(solution)/shard_map/ppermute | solution.py:285
  49.0 7.9 %collective-permute-start.17 = (f32[128,512]{1,0:T(8,128)S(1)}, f32[128,512]{1,0:T(8,128)S(1)}, u32[]{:S(2)}, u32[]{:S(2)}) collective-permute-start(f32[128,512]{1,0:T(8,128)S(1)} %add.39), channel_id=1, source_target_pairs={{0,4},{1,3},{4,8},{5,1},{8,12},{9,5},{12,14},{13,9},{14,10},{15,13... | collective-permute-start | bytes 786440 | tf_op jit(solution)/shard_map/ppermute | solution.py:285

commit v7 on v6

--- a/solution.py
+++ b/solution.py
@@ -10,6 +10,7 @@
 
 CALLS = 8
 LANES = 256
+PIECE = 16
 MIB = 2**20
 
 
@@ -46,43 +47,39 @@
     return found
 
 
-def block_copies(starts, size, chunks, a_ref, outs, sems):
-    spots = [(out_ref, at * size) for out_ref, count in zip(outs, chunks) for at in range(count)]
-    return [
-        pltpu.make_async_copy(
-            a_ref.at[pl.ds(pl.multiple_of(looked_up(starts[..., index]), size), size)],
-            out_ref.at[pl.ds(at, size)],
-            sems.at[index],
-        )
-        for index, (out_ref, at) in enumerate(spots)
-    ]
-
-
-def pick_kernel(starts, size, chunks, a_ref, out_ref, sems):
-    copies = block_copies(starts, size, chunks, a_ref, [out_ref], sems)
-    for copy in copies:
-        copy.start()
-    for copy in copies:
-        copy.wait()
-
-
-def pick(inductance, starts, size):
-    count = starts.shape[-1]
+def pick_kernel(starts, size, chunks, a_ref, *refs):
+    outs, sems = refs[-1 - len(chunks) : -1], refs[-1]
+    spots = [(chunk, at * size) for chunk, count in enumerate(chunks) for at in range(count)]
+    piece = min(size, PIECE)
+    for index, (chunk, first) in enumerate(spots):
+        start = looked_up(starts[..., index])
+        for at in range(0, size, piece):
+            pltpu.make_async_copy(
+                a_ref.at[pl.ds(pl.multiple_of(start + at, piece), piece)],
+                outs[chunk].at[pl.ds(first + at, piece)],
+                sems.at[chunk],
+            ).start()
+    for chunk, out_ref in enumerate(outs):
+        pltpu.make_async_copy(a_ref.at[pl.ds(0, out_ref.shape[0])], out_ref, sems.at[chunk]).wait()
+
+
+def pick(inductance, starts, size, chunks, room, *after):
     width = inductance.shape[1]
-    return pl.pallas_call(
-        functools.partial(pick_kernel, starts, size, [count]),
-        out_shape=jax.ShapeDtypeStruct((count * size, width), jnp.float32),
-        in_specs=[pl.BlockSpec(memory_space=pl.ANY)],
-        out_specs=pl.BlockSpec(memory_space=pltpu.VMEM),
-        scratch_shapes=[pltpu.SemaphoreType.DMA((count,))],
-        compiler_params=pltpu.CompilerParams(vmem_limit_bytes=50 * MIB),
-        cost_estimate=pl.CostEstimate(flops=0, bytes_accessed=8 * count * size * width, transcendentals=0),
+    moved = 8 * sum(chunks) * size * width
+    return pl.pallas_call(
+        functools.partial(pick_kernel, starts, size, chunks),
+        out_shape=[jax.ShapeDtypeStruct((count * size, width), jnp.float32) for count in chunks],
+        in_specs=[pl.BlockSpec(memory_space=pl.ANY)] * (1 + len(after)),
+        out_specs=[pl.BlockSpec(memory_space=pltpu.VMEM)] * len(chunks),
+        scratch_shapes=[pltpu.SemaphoreType.DMA((len(chunks),))],
+        compiler_params=pltpu.CompilerParams(vmem_limit_bytes=room * MIB),
+        cost_estimate=pl.CostEstimate(flops=0, bytes_accessed=moved, transcendentals=0),
         name="pick",
-    )(inductance)
-
-
-def first_column(part, width):
-    return jnp.where((lax.axis_index("col") == 0) == (part == 0), width, 0)
+    )(inductance, *after)
+
+
+def side(part):
+    return jnp.where((lax.axis_index("col") == 0) == (part == 0), 1, 0)
 
 
 def halves(value):
@@ -90,37 +87,33 @@
     return high, (value - high.astype(jnp.float32)).astype(jnp.bfloat16)
 
 
-def split_kernel(value_ref, high_ref, low_ref):
+def split_kernel(value_ref, *refs):
+    high_ref, low_ref = refs[-2:]
     high_ref[...], low_ref[...] = halves(value_ref[...])
 
 
-def split(current_rates):
+def split(current_rates, part, *after):
     depth, width = current_rates.shape
-    tile = min(256, depth)
-    tiled = pl.BlockSpec((tile, width), lambda k: (k, 0))
+    width //= 2
+    tile = min(512, depth)
     return pl.pallas_call(
         split_kernel,
         grid=(depth // tile,),
         out_shape=[jax.ShapeDtypeStruct((depth, width), jnp.bfloat16)] * 2,
-        in_specs=[tiled],
-        out_specs=[tiled] * 2,
-        compiler_params=pltpu.CompilerParams(vmem_limit_bytes=40 * MIB),
+        in_specs=[pl.BlockSpec((tile, width), lambda k: (k, side(part)))]
+        + [pl.BlockSpec(memory_space=pl.ANY)] * len(after),
+        out_specs=[pl.BlockSpec((tile, width), lambda k: (k, 0))] * 2,
+        compiler_params=pltpu.CompilerParams(vmem_limit_bytes=8 * MIB),
         cost_estimate=pl.CostEstimate(flops=4 * depth * width, bytes_accessed=8 * depth * width, transcendentals=0),
         name="split",
-    )(current_rates)
-
-
-def product_kernel(starts, size, bounds, parts, given, chunks, *refs):
+    )(current_rates, *after)
+
+
+def product_kernel(starts, size, bounds, parts, *refs):
     count = len(bounds)
-    sources, (high_ref, low_ref), refs = refs[:count], refs[count : count + 2], refs[count + 2 :]
-    *outs, raw, stack, sems, late_sems = refs
+    sources, pairs = refs[:count], refs[count : count + 2 * parts]
+    outs, (raw, stack, sems) = refs[-3 - parts : -3], refs[-3:]
     depth = raw.shape[0]
-    late = []
-    if chunks:
-        a_ref, *outs = outs
-        late = block_copies(given, size, chunks, a_ref, outs[len(parts) :], late_sems)
-    for copy in late:
-        copy.start()
     for index in range(starts.shape[-1]):
         start = looked_up(starts[..., index])
         first = 0
@@ -140,46 +133,39 @@
             sources[0].at[pl.ds(0, size)], raw.at[pl.ds(index * size, size)], sems.at[index]
         ).wait()
     stack[:depth], stack[depth:] = halves(raw[...])
-    for part, out_ref in zip(parts, outs):
+    for part, out_ref in enumerate(outs):
+        high_ref, low_ref = pairs[2 * part : 2 * part + 2]
         width = out_ref.shape[1]
         tile = min(LANES, width)
         for at in range(0, width, tile):
-            columns = pl.ds(pl.multiple_of(first_column(part, width) + at, tile), tile)
-            both = jnp.dot(stack[...], high_ref[:, columns], preferred_element_type=jnp.float32)
-            rest = jnp.dot(stack[:depth], low_ref[:, columns], preferred_element_type=jnp.float32)
+            both = jnp.dot(stack[...], high_ref[:, at : at + tile], preferred_element_type=jnp.float32)
+            rest = jnp.dot(stack[:depth], low_ref[:, at : at + tile], preferred_element_type=jnp.float32)
             out_ref[:, at : at + tile] = both[:depth] + (both[depth:] + rest)
-    for copy in late:
-        copy.wait()
-
-
-def product(sources, starts, size, pair, parts, inductance=None, given=np.zeros(0), chunks=()):
+
+
+def product(sources, starts, size, pairs, *after):
     depth = starts.shape[-1] * size
-    inner, width = pair[0].shape
-    wanted = [inductance] if chunks else []
-    half = jax.ShapeDtypeStruct((depth, width // 2), jnp.float32)
-    return pl.pallas_call(
-        functools.partial(
-            product_kernel, starts, size, list(np.cumsum([s.shape[0] for s in sources])), parts, given, chunks
-        ),
-        out_shape=[half] * len(parts) + [jax.ShapeDtypeStruct((chunk * size, inner), jnp.float32) for chunk in chunks],
-        in_specs=[pl.BlockSpec(memory_space=pl.ANY)] * len(sources) + [pl.BlockSpec(memory_space=pltpu.VMEM)] * 2
-        + [pl.BlockSpec(memory_space=pl.ANY)] * len(wanted),
-        out_specs=[pl.BlockSpec(memory_space=pltpu.VMEM)] * len(parts)
-        + [pl.BlockSpec(memory_space=pl.ANY)] * len(chunks),
+    inner, width = pairs[0].shape
+    parts = len(pairs) // 2
+    anywhere, whole = pl.BlockSpec(memory_space=pl.ANY), pl.BlockSpec(memory_space=pltpu.VMEM)
+    return pl.pallas_call(
+        functools.partial(product_kernel, starts, size, list(np.cumsum([s.shape[0] for s in sources])), parts),
+        out_shape=[jax.ShapeDtypeStruct((depth, width), jnp.float32)] * parts,
+        in_specs=[anywhere] * len(sources) + [whole] * len(pairs) + [anywhere] * len(after),
+        out_specs=[whole] * parts,
         scratch_shapes=[
             pltpu.VMEM((depth, inner), jnp.float32),
             pltpu.VMEM((2 * depth, inner), jnp.bfloat16),
             pltpu.SemaphoreType.DMA((starts.shape[-1],)),
-            pltpu.SemaphoreType.DMA((max(given.shape[-1], 1),)),
         ],
-        compiler_params=pltpu.CompilerParams(vmem_limit_bytes=(40 if chunks else 16) * MIB),
+        compiler_params=pltpu.CompilerParams(vmem_limit_bytes=16 * MIB),
         cost_estimate=pl.CostEstimate(
-            flops=3 * depth * inner * width * len(parts),
-            bytes_accessed=4 * depth * inner + (2 * inner + 2 * depth) * width * len(parts),
+            flops=6 * depth * inner * width * parts,
+            bytes_accessed=4 * depth * inner + 4 * (inner + depth) * width * parts,
             transcendentals=0,
         ),
         name="product",
-    )(*sources, *pair, *wanted)
+    )(*sources, *pairs, *after)
 
 
 def finish_kernel(*refs):
@@ -187,7 +173,7 @@
     for part in range(2):
         above, below, own = refs[3 * part : 3 * part + 3]
         width = own.shape[1]
-        columns = pl.ds(pl.multiple_of(first_column(part, width), width), width)
+        columns = pl.ds(pl.multiple_of(side(part) * width, width), width)
         out_ref[:, columns] = (above[...] + below[...]) + own[...]
 
 
@@ -250,26 +236,25 @@
         spare = int(group > 1)
         chunks = [group + spare] + [group] * (rows // cols // group - 2) + [group - spare]
         taken, given = plan(order, rows, cols, size, chunks)
-        own = [pick(inductance, given[..., : chunks[0]], size)]
-        received = [lax.ppermute(own[0], "col", swap)]
-        pair = split(current_rates)
-        early, *later = product(
-            [own[0], received[0]], taken[..., :group], size, pair, [0], inductance, given[..., chunks[0] :], chunks[1:]
-        )
-        own += later
-        received += [lax.ppermute(each, "col", swap) for each in later]
-        sources = [rows for pair_of in zip(own, received) for rows in pair_of]
+        own = pick(inductance, given[..., : chunks[0]], size, chunks[:1], 52)
+        own += pick(inductance, given[..., chunks[0] :], size, chunks[1:], 48, *own)
+        received = [lax.ppermute(each, "col", swap) for each in own]
+        sources = [rows for pair in zip(own, received) for rows in pair]
         firsts = np.cumsum([0] + [each.shape[0] for each in sources])
-        calls = {(0, 0): early}
+        pairs, calls, made = {}, {}, []
 
         def term(index, part):
             call, at = divmod(index, group)
             if (call, part) not in calls:
                 parts = [part] if call < 3 else [0, 1]
+                for each in parts:
+                    if each not in pairs:
+                        pairs[each] = split(current_rates, each, *made)
                 starts = taken[..., call * group : (call + 1) * group]
                 have = sources[: int(np.searchsorted(firsts, starts.max(), "right"))]
-                got = product(have, starts, size, pair, parts)
+                got = product(have, starts, size, [half for each in parts for half in pairs[each]], *made[-1:])
                 calls.update({(call, each): value for each, value in zip(parts, got)})
+                made.append(got[0])
             return calls[call, part][at * size : (at + 1) * size]
 
         sums = [[None, None], [None, None]]

time: 58.1 us -> 53.2 us (0.916)
  Pallas kernels: 25.9 us -> 22.8 us
  waiting for transfers between devices: 14.6 us -> 13.1 us
    pallas_call x1 -> x2, Pallas kernels: 6.02 us -> 1.87 us  [split(): pl.pallas_call(split_kernel, grid=(depth // tile,), out_shape=[jax.ShapeD...]
    pallas_call x1 -> x2, Pallas kernels: 1.23 us -> 3.77 us  [pick(): pl.pallas_call(functools.partial(pick_kernel, starts, size, chunks), out_...]
    pallas_call x11, Pallas kernels: 17.8 us -> 16.3 us  [product(): pl.pallas_call(functools.partial(product_kernel, starts, size, list(np.cu...]
    ppermute x14, waiting for transfers between devices: 14.6 us -> 13.1 us  [shards(): sums[way][part] = lax.ppermute(value, ('row', 'col'), ways[way])]
  transfers between devices with their start and end apart: 18 -> 18, of which waited for: 8 -> 8; matrix products, arithmetic and copies ran while one was open for 1% -> 1% of each run, Pallas kernels for 38% -> 39%
where the time goes in v7:
time: 53.2 us; the launch traced here: 53.1 us
  Pallas kernels  22.8 us (43%)
  starting transfers between devices  16.6 us (31%)
  waiting for transfers between devices  13.1 us (25%)
    pallas_call x11, Pallas kernels, product(): pl.pallas_call(functools.partial(product_kernel, starts, size, list(np.cu...  16.3 us
    ppermute x14, starting transfers between devices, shards(): sums[way][part] = lax.ppermute(value, ('row', 'col'), ways[way])  15.4 us
    ppermute x14, waiting for transfers between devices, shards(): sums[way][part] = lax.ppermute(value, ('row', 'col'), ways[way])  13.1 us
    pallas_call x2, Pallas kernels, pick(): pl.pallas_call(functools.partial(pick_kernel, starts, size, chunks), out_...  3.77 us
    pallas_call x2, Pallas kernels, split(): pl.pallas_call(split_kernel, grid=(depth // tile,), out_shape=[jax.ShapeD...  1.87 us
    ppermute x4, starting transfers between devices, shards(): received = [lax.ppermute(each, 'col', swap) for each in own]  1.16 us
  transfers between devices with their start and end apart: 18, of which 8 were waited for; matrix products, arithmetic and copies ran while one was open for 1% of the time, Pallas kernels for 39%

profile of v7, /device:TPU:0, one launch (start us, length us, event | category | flops | bytes accessed | tf_op | source)
XLA Modules:
  0.0 53.1 jit_solution(7722764508838150651)
XLA Ops:
  0.0 0.0 copy-start
  0.0 1.4 %pick.2.refs_0_ = f32[128,2048]{1,0:T(8,128)S(1)} custom-call(f32[512,2048]{1,0:T(8,128)} %a_ref.3), custom_call_target="tpu_custom_call" | custom-call | bytes 2097152 | tf_op jit(solution)/shard_map/pick/pallas_call | solution.py:69
  1.4 0.5 collective-permute-start
  2.0 2.3 %pick.3 = (f32[128,2048]{1,0:T(8,128)S(1)}, f32[128,2048]{1,0:T(8,128)S(1)}, f32[128,2048]{1,0:T(8,128)S(1)}) custom-call(f32[512,2048]{1,0:T(8,128)} %a_ref.3, f32[128,2048]{1,0:T(8,128)S(1)} %pick.2.refs_0_), custom_call_target="tpu_custom_call" | custom-call | bytes 6291456 | tf_op jit(solution)/shard_map/pick/pallas_call | solution.py:69
  4.3 0.1 collective-permute-start.2
  4.4 0.5 collective-permute-start.3
  4.9 0.1 collective-permute-start.5
  5.0 0.0 copy-done
  5.0 0.9 %split.2 = (bf16[2048,512]{1,0:T(8,128)(2,1)S(1)}, bf16[2048,512]{1,0:T(8,128)(2,1)S(1)}) custom-call(f32[2048,1024]{1,0:T(8,128)S(1)} %copy-done), custom_call_target="tpu_custom_call" | custom-call | flops 4194304 | bytes 8388608 | tf_op jit(solution)/shard_map/split/pallas_call | solution.py:99
  5.9 0.0 collective-permute-done.refs_1_
  5.9 1.1 %product.11.refs_0_.refs_4_ = f32[128,512]{1,0:T(8,128)S(1)} custom-call(f32[128,2048]{1,0:T(8,128)S(1)} %pick.2.refs_0_, f32[128,2048]{1,0:T(8,128)S(1)} %collective-permute-done.refs_1_, bf16[2048,512]{1,0:T(8,128)(2,1)S(1)} %get-tuple-element.22.refs_2_.refs_6_.refs_5_.refs_8_, bf16[2048,512]{1,0:T(8,128)(2,1)S(1)} %get-tuple-element.23.refs_3_.refs_7_.refs_6_.refs_9_), custom_call_target="tpu_custom_call" | custom-call | flops 805306368 | bytes 5505024 | tf_op jit(solution)/shard_map/product/pallas_call | solution.py:151
  7.0 3.1 %collective-permute-start.1 = (f32[128,512]{1,0:T(8,128)S(1)}, f32[128,512]{1,0:T(8,128)S(1)}, u32[]{:S(2)}, u32[]{:S(2)}) collective-permute-start(f32[128,512]{1,0:T(8,128)S(1)} %product.11.refs_0_.refs_4_), channel_id=1, source_target_pairs={{0,2},{1,5},{4,0},{5,9},{8,4},{9,13},{12,8},{13,15},{14,12},{15,11... | collective-permute-start | bytes 786440 | tf_op jit(solution)/shard_map/ppermute | solution.py:270
  10.1 0.9 %split.3 = (bf16[2048,512]{1,0:T(8,128)(2,1)S(1)}, bf16[2048,512]{1,0:T(8,128)(2,1)S(1)}) custom-call(f32[2048,1024]{1,0:T(8,128)S(1)} %copy-done, f32[128,512]{1,0:T(8,128)S(1)} %product.11.refs_0_.refs_4_), custom_call_target="tpu_custom_call" | custom-call | flops 4194304 | bytes 8388608 | tf_op jit(solution)/shard_map/split/pallas_call | solution.py:99
  11.0 1.1 %product.12.refs_7_ = f32[128,512]{1,0:T(8,128)S(1)} custom-call(f32[128,2048]{1,0:T(8,128)S(1)} %pick.2.refs_0_, f32[128,2048]{1,0:T(8,128)S(1)} %collective-permute-done.refs_1_, bf16[2048,512]{1,0:T(8,128)(2,1)S(1)} %get-tuple-element.26.refs_2_.refs_5_.refs_6_.refs_10_, bf16[2048,512]{1,0:T(8,128)(2,1)S(1)} %get-tuple-element.27.refs_3_.refs_6_.refs_7_.refs_11_, ...), custom_call_target="tpu_custom_call" | custom-call | flops 805306368 | bytes 5505024 | tf_op jit(solution)/shard_map/product/pallas_call | solution.py:151
  12.1 0.2 collective-permute-start.14
  12.3 0.0 collective-permute-done.2.refs_3_
  12.3 1.1 %product.13.refs_8_ = f32[128,512]{1,0:T(8,128)S(1)} custom-call(f32[128,2048]{1,0:T(8,128)S(1)} %pick.2.refs_0_, f32[128,2048]{1,0:T(8,128)S(1)} %collective-permute-done.refs_1_, f32[128,2048]{1,0:T(8,128)S(1)} %get-tuple-element.24.refs_2_, f32[128,2048]{1,0:T(8,128)S(1)} %collective-permute-done.2.refs_3_, f32[128,2048]{1,0:T(8,128)S(1)} %get-tuple-element.25.refs_4_, ...), custom_call_target="tpu_custom_call" | custom-call | flops 805306368 | bytes 5505024 | tf_op jit(solution)/shard_map/product/pallas_call | solution.py:151
  13.4 2.0 %collective-permute-start.11 = (f32[128,512]{1,0:T(8,128)S(1)}, f32[128,512]{1,0:T(8,128)S(1)}, u32[]{:S(2)}, u32[]{:S(2)}) collective-permute-start(f32[128,512]{1,0:T(8,128)S(1)} %product.13.refs_8_), channel_id=1, source_target_pairs={{0,2},{1,5},{4,0},{5,9},{8,4},{9,13},{12,8},{13,15},{14,12},{15,11... | collective-permute-start | bytes 786440 | tf_op jit(solution)/shard_map/ppermute | solution.py:270
  15.3 0.0 collective-permute-done.3.refs_5_
  15.3 1.1 %product.14.refs_7_ = f32[128,512]{1,0:T(8,128)S(1)} custom-call(f32[128,2048]{1,0:T(8,128)S(1)} %pick.2.refs_0_, f32[128,2048]{1,0:T(8,128)S(1)} %collective-permute-done.refs_1_, f32[128,2048]{1,0:T(8,128)S(1)} %get-tuple-element.24.refs_2_, f32[128,2048]{1,0:T(8,128)S(1)} %collective-permute-done.2.refs_3_, f32[128,2048]{1,0:T(8,128)S(1)} %get-tuple-element.25.refs_4_, ...), custom_call_target="tpu_custom_call" | custom-call | flops 805306368 | bytes 5505024 | tf_op jit(solution)/shard_map/product/pallas_call | solution.py:151
  16.4 0.2 collective-permute-start.8
  16.6 1.1 %product.15.refs_8_ = f32[128,512]{1,0:T(8,128)S(1)} custom-call(f32[128,2048]{1,0:T(8,128)S(1)} %pick.2.refs_0_, f32[128,2048]{1,0:T(8,128)S(1)} %collective-permute-done.refs_1_, f32[128,2048]{1,0:T(8,128)S(1)} %get-tuple-element.24.refs_2_, f32[128,2048]{1,0:T(8,128)S(1)} %collective-permute-done.2.refs_3_, f32[128,2048]{1,0:T(8,128)S(1)} %get-tuple-element.25.refs_4_, ...), custom_call_target="tpu_custom_call" | custom-call | flops 805306368 | bytes 5505024 | tf_op jit(solution)/shard_map/product/pallas_call | solution.py:151
  17.7 1.1 %product.16.refs_12_ = f32[128,512]{1,0:T(8,128)S(1)} custom-call(f32[128,2048]{1,0:T(8,128)S(1)} %pick.2.refs_0_, f32[128,2048]{1,0:T(8,128)S(1)} %collective-permute-done.refs_1_, f32[128,2048]{1,0:T(8,128)S(1)} %get-tuple-element.24.refs_2_, f32[128,2048]{1,0:T(8,128)S(1)} %collective-permute-done.2.refs_3_, f32[128,2048]{1,0:T(8,128)S(1)} %get-tuple-element.25.refs_4_, ...), custom_call_target="tpu_custom_call" | custom-call | flops 805306368 | bytes 5505024 | tf_op jit(solution)/shard_map/product/pallas_call | solution.py:151
  18.8 0.0 collective-permute-done.1
  18.8 1.9 %collective-permute-start.4 = (f32[128,512]{1,0:T(8,128)S(1)}, f32[128,512]{1,0:T(8,128)S(1)}, u32[]{:S(2)}, u32[]{:S(2)}) collective-permute-start(f32[128,512]{1,0:T(8,128)S(1)} %add.30), channel_id=1, source_target_pairs={{0,2},{1,5},{4,0},{5,9},{8,4},{9,13},{12,8},{13,15},{14,12},{15,11... | collective-permute-start | bytes 786440 | tf_op jit(solution)/shard_map/ppermute | solution.py:270
  20.7 0.5 collective-permute-done.14
  21.3 0.1 collective-permute-start.15
  21.3 0.0 collective-permute-done.5.refs_7_
  21.4 1.9 %product.17 = (f32[128,512]{1,0:T(8,128)S(1)}, f32[128,512]{1,0:T(8,128)S(1)}) custom-call(f32[128,2048]{1,0:T(8,128)S(1)} %pick.2.refs_0_, f32[128,2048]{1,0:T(8,128)S(1)} %collective-permute-done.refs_1_, f32[128,2048]{1,0:T(8,128)S(1)} %get-tuple-element.24.refs_2_, f32[128,2048]{1,0:T(8,128)S(1)} %collective-permute-done.2.refs_3_, ...), custom_call_target="tpu_custom_call" | custom-call | flops 1610612736 | bytes 9961472 | tf_op jit(solution)/shard_map/product/pallas_call | solution.py:151
  23.3 1.9 %product.18 = (f32[128,512]{1,0:T(8,128)S(1)}, f32[128,512]{1,0:T(8,128)S(1)}) custom-call(f32[128,2048]{1,0:T(8,128)S(1)} %pick.2.refs_0_, f32[128,2048]{1,0:T(8,128)S(1)} %collective-permute-done.refs_1_, f32[128,2048]{1,0:T(8,128)S(1)} %get-tuple-element.24.refs_2_, f32[128,2048]{1,0:T(8,128)S(1)} %collective-permute-done.2.refs_3_, ...), custom_call_target="tpu_custom_call" | custom-call | flops 1610612736 | bytes 9961472 | tf_op jit(solution)/shard_map/product/pallas_call | solution.py:151
  25.2 1.6 %collective-permute-done.8 = f32[128,512]{1,0:T(8,128)S(1)} collective-permute-done((f32[128,512]{1,0:T(8,128)S(1)}, f32[128,512]{1,0:T(8,128)S(1)}, u32[]{:S(2)}, u32[]{:S(2)}) %collective-permute-start.8) | collective-permute-done | bytes 262176 | tf_op jit(solution)/shard_map/ppermute | solution.py:270
  26.9 0.1 collective-permute-start.9
  27.0 0.0 collective-permute-done.11
  27.0 2.1 %collective-permute-start.12 = (f32[128,512]{1,0:T(8,128)S(1)}, f32[128,512]{1,0:T(8,128)S(1)}, u32[]{:S(2)}, u32[]{:S(2)}) collective-permute-start(f32[128,512]{1,0:T(8,128)S(1)} %add.35), channel_id=1, source_target_pairs={{0,2},{1,5},{4,0},{5,9},{8,4},{9,13},{12,8},{13,15},{14,12},{15,11... | collective-permute-start | bytes 786440 | tf_op jit(solution)/shard_map/ppermute | solution.py:270
  29.1 0.0 collective-permute-done.4
  29.1 1.6 %collective-permute-start.6 = (f32[128,512]{1,0:T(8,128)S(1)}, f32[128,512]{1,0:T(8,128)S(1)}, u32[]{:S(2)}, u32[]{:S(2)}) collective-permute-start(f32[128,512]{1,0:T(8,128)S(1)} %add.31), channel_id=1, source_target_pairs={{0,2},{1,5},{4,0},{5,9},{8,4},{9,13},{12,8},{13,15},{14,12},{15,11... | collective-permute-start | bytes 786440 | tf_op jit(solution)/shard_map/ppermute | solution.py:270
  30.7 0.9 %collective-permute-done.15 = f32[128,512]{1,0:T(8,128)S(1)} collective-permute-done((f32[128,512]{1,0:T(8,128)S(1)}, f32[128,512]{1,0:T(8,128)S(1)}, u32[]{:S(2)}, u32[]{:S(2)}) %collective-permute-start.15) | collective-permute-done | bytes 262176 | tf_op jit(solution)/shard_map/ppermute | solution.py:270
  31.7 0.1 collective-permute-start.16
  31.8 1.9 %product.19 = (f32[128,512]{1,0:T(8,128)S(1)}, f32[128,512]{1,0:T(8,128)S(1)}) custom-call(f32[128,2048]{1,0:T(8,128)S(1)} %pick.2.refs_0_, f32[128,2048]{1,0:T(8,128)S(1)} %collective-permute-done.refs_1_, f32[128,2048]{1,0:T(8,128)S(1)} %get-tuple-element.24.refs_2_, f32[128,2048]{1,0:T(8,128)S(1)} %collective-permute-done.2.refs_3_, ...), custom_call_target="tpu_custom_call" | custom-call | flops 1610612736 | bytes 9961472 | tf_op jit(solution)/shard_map/product/pallas_call | solution.py:151
  33.7 2.1 %product.20 = (f32[128,512]{1,0:T(8,128)S(1)}, f32[128,512]{1,0:T(8,128)S(1)}) custom-call(f32[128,2048]{1,0:T(8,128)S(1)} %pick.2.refs_0_, f32[128,2048]{1,0:T(8,128)S(1)} %collective-permute-done.refs_1_, f32[128,2048]{1,0:T(8,128)S(1)} %get-tuple-element.24.refs_2_, f32[128,2048]{1,0:T(8,128)S(1)} %collective-permute-done.2.refs_3_, ...), custom_call_target="tpu_custom_call" | custom-call | flops 1610612736 | bytes 9961472 | tf_op jit(solution)/shard_map/product/pallas_call | solution.py:151
  35.8 1.4 %collective-permute-done.9 = f32[128,512]{1,0:T(8,128)S(1)} collective-permute-done((f32[128,512]{1,0:T(8,128)S(1)}, f32[128,512]{1,0:T(8,128)S(1)}, u32[]{:S(2)}, u32[]{:S(2)}) %collective-permute-start.9) | collective-permute-done | bytes 262176 | tf_op jit(solution)/shard_map/ppermute | solution.py:270
  37.3 0.3 collective-permute-start.10
  37.6 0.0 collective-permute-done.12
  37.6 1.9 %collective-permute-start.13 = (f32[128,512]{1,0:T(8,128)S(1)}, f32[128,512]{1,0:T(8,128)S(1)}, u32[]{:S(2)}, u32[]{:S(2)}) collective-permute-start(f32[128,512]{1,0:T(8,128)S(1)} %add.36), channel_id=1, source_target_pairs={{0,2},{1,5},{4,0},{5,9},{8,4},{9,13},{12,8},{13,15},{14,12},{15,11... | collective-permute-start | bytes 786440 | tf_op jit(solution)/shard_map/ppermute | solution.py:270
  39.5 2.4 %collective-permute-done.6 = f32[128,512]{1,0:T(8,128)S(1)} collective-permute-done((f32[128,512]{1,0:T(8,128)S(1)}, f32[128,512]{1,0:T(8,128)S(1)}, u32[]{:S(2)}, u32[]{:S(2)}) %collective-permute-start.6) | collective-permute-done | bytes 262176 | tf_op jit(solution)/shard_map/ppermute | solution.py:270
  42.0 2.1 %collective-permute-start.7 = (f32[128,512]{1,0:T(8,128)S(1)}, f32[128,512]{1,0:T(8,128)S(1)}, u32[]{:S(2)}, u32[]{:S(2)}) collective-permute-start(f32[128,512]{1,0:T(8,128)S(1)} %add.32), channel_id=1, source_target_pairs={{0,2},{1,5},{4,0},{5,9},{8,4},{9,13},{12,8},{13,15},{14,12},{15,11... | collective-permute-start | bytes 786440 | tf_op jit(solution)/shard_map/ppermute | solution.py:270
  44.0 0.0 collective-permute-done.16
  44.1 0.1 collective-permute-start.17
  44.1 1.9 %product.21 = (f32[128,512]{1,0:T(8,128)S(1)}, f32[128,512]{1,0:T(8,128)S(1)}) custom-call(f32[128,2048]{1,0:T(8,128)S(1)} %pick.2.refs_0_, f32[128,2048]{1,0:T(8,128)S(1)} %collective-permute-done.refs_1_, f32[128,2048]{1,0:T(8,128)S(1)} %get-tuple-element.24.refs_2_, f32[128,2048]{1,0:T(8,128)S(1)} %collective-permute-done.2.refs_3_, ...), custom_call_target="tpu_custom_call" | custom-call | flops 1610612736 | bytes 9961472 | tf_op jit(solution)/shard_map/product/pallas_call | solution.py:151
  46.1 2.5 %collective-permute-done.10.refs_1_ = f32[128,512]{1,0:T(8,128)S(1)} collective-permute-done((f32[128,512]{1,0:T(8,128)S(1)}, f32[128,512]{1,0:T(8,128)S(1)}, u32[]{:S(2)}, u32[]{:S(2)}) %collective-permute-start.10) | collective-permute-done | bytes 262176 | tf_op jit(solution)/shard_map/ppermute | solution.py:270
  48.5 0.0 collective-permute-done.13.refs_3_
  48.5 2.6 %collective-permute-done.7.refs_0_ = f32[128,512]{1,0:T(8,128)S(1)} collective-permute-done((f32[128,512]{1,0:T(8,128)S(1)}, f32[128,512]{1,0:T(8,128)S(1)}, u32[]{:S(2)}, u32[]{:S(2)}) %collective-permute-start.7) | collective-permute-done | bytes 262176 | tf_op jit(solution)/shard_map/ppermute | solution.py:270
  51.2 1.1 %collective-permute-done.17.refs_4_ = f32[128,512]{1,0:T(8,128)S(1)} collective-permute-done((f32[128,512]{1,0:T(8,128)S(1)}, f32[128,512]{1,0:T(8,128)S(1)}, u32[]{:S(2)}, u32[]{:S(2)}) %collective-permute-start.17) | collective-permute-done | bytes 262176 | tf_op jit(solution)/shard_map/ppermute | solution.py:270
  52.2 0.9 %finish.1 = f32[128,1024]{1,0:T(8,128)} custom-call(f32[128,512]{1,0:T(8,128)S(1)} %collective-permute-done.7.refs_0_, f32[128,512]{1,0:T(8,128)S(1)} %collective-permute-done.10.refs_1_, f32[128,512]{1,0:T(8,128)S(1)} %get-tuple-element.33.refs_2_, f32[128,512]{1,0:T(8,128)S(1)} %collective-permute-done.13.refs_3_, ...), custom_call_target="tpu_custom_call" | custom-call | tf_op jit(solution)/shard_map/finish/pallas_call | solution.py:182
  (10 shorter events, 0.4 us)
Async XLA Ops:
  0.0 5.0 %copy-start = (f32[2048,1024]{1,0:T(8,128)S(1)}, f32[2048,1024]{1,0:T(8,128)}, u32[]{:S(2)}) copy-start(f32[2048,1024]{1,0:T(8,128)} %value_ref.3) | copy-start | bytes 25165828
  1.4 4.5 %collective-permute-start = (f32[128,2048]{1,0:T(8,128)S(1)}, f32[128,2048]{1,0:T(8,128)S(1)}, u32[]{:S(2)}, u32[]{:S(2)}) collective-permute-start(f32[128,2048]{1,0:T(8,128)S(1)} %pick.2.refs_0_), channel_id=1, source_target_pairs={{0,1},{1,0},{2,3},{3,2},{4,5},{5,4},{6,7},{7,6},{8,9},{9,8},{10,11... | collective-permute-start | bytes 3145736 | tf_op jit(solution)/shard_map/ppermute | solution.py:241
  4.3 8.0 %collective-permute-start.2 = (f32[128,2048]{1,0:T(8,128)S(1)}, f32[128,2048]{1,0:T(8,128)S(1)}, u32[]{:S(2)}, u32[]{:S(2)}) collective-permute-start(f32[128,2048]{1,0:T(8,128)S(1)} %get-tuple-element.24.refs_2_), channel_id=1, source_target_pairs={{0,1},{1,0},{2,3},{3,2},{4,5},{5,4},{6,7},{7,6},{8,9},{9,8},{10,11... | collective-permute-start | bytes 3145736 | tf_op jit(solution)/shard_map/ppermute | solution.py:241
  4.4 10.9 %collective-permute-start.3 = (f32[128,2048]{1,0:T(8,128)S(1)}, f32[128,2048]{1,0:T(8,128)S(1)}, u32[]{:S(2)}, u32[]{:S(2)}) collective-permute-start(f32[128,2048]{1,0:T(8,128)S(1)} %get-tuple-element.25.refs_4_), channel_id=1, source_target_pairs={{0,1},{1,0},{2,3},{3,2},{4,5},{5,4},{6,7},{7,6},{8,9},{9,8},{10,11... | collective-permute-start | bytes 3145736 | tf_op jit(solution)/shard_map/ppermute | solution.py:241
  4.9 16.5 %collective-permute-start.5 = (f32[128,2048]{1,0:T(8,128)S(1)}, f32[128,2048]{1,0:T(8,128)S(1)}, u32[]{:S(2)}, u32[]{:S(2)}) collective-permute-start(f32[128,2048]{1,0:T(8,128)S(1)} %get-tuple-element.28.refs_6_), channel_id=1, source_target_pairs={{0,1},{1,0},{2,3},{3,2},{4,5},{5,4},{6,7},{7,6},{8,9},{9,8},{10,11... | collective-permute-start | bytes 3145736 | tf_op jit(solution)/shard_map/ppermute | solution.py:241
  7.0 11.8 %collective-permute-start.1 = (f32[128,512]{1,0:T(8,128)S(1)}, f32[128,512]{1,0:T(8,128)S(1)}, u32[]{:S(2)}, u32[]{:S(2)}) collective-permute-start(f32[128,512]{1,0:T(8,128)S(1)} %product.11.refs_0_.refs_4_), channel_id=1, source_target_pairs={{0,2},{1,5},{4,0},{5,9},{8,4},{9,13},{12,8},{13,15},{14,12},{15,11... | collective-permute-start | bytes 786440 | tf_op jit(solution)/shard_map/ppermute | solution.py:270
  12.1 9.1 %collective-permute-start.14 = (f32[128,512]{1,0:T(8,128)S(1)}, f32[128,512]{1,0:T(8,128)S(1)}, u32[]{:S(2)}, u32[]{:S(2)}) collective-permute-start(f32[128,512]{1,0:T(8,128)S(1)} %product.12.refs_7_), channel_id=1, source_target_pairs={{0,4},{1,3},{4,8},{5,1},{8,12},{9,5},{12,14},{13,9},{14,10},{15,13... | collective-permute-start | bytes 786440 | tf_op jit(solution)/shard_map/ppermute | solution.py:270
  13.4 13.6 %collective-permute-start.11 = (f32[128,512]{1,0:T(8,128)S(1)}, f32[128,512]{1,0:T(8,128)S(1)}, u32[]{:S(2)}, u32[]{:S(2)}) collective-permute-start(f32[128,512]{1,0:T(8,128)S(1)} %product.13.refs_8_), channel_id=1, source_target_pairs={{0,2},{1,5},{4,0},{5,9},{8,4},{9,13},{12,8},{13,15},{14,12},{15,11... | collective-permute-start | bytes 786440 | tf_op jit(solution)/shard_map/ppermute | solution.py:270
  16.4 10.5 %collective-permute-start.8 = (f32[128,512]{1,0:T(8,128)S(1)}, f32[128,512]{1,0:T(8,128)S(1)}, u32[]{:S(2)}, u32[]{:S(2)}) collective-permute-start(f32[128,512]{1,0:T(8,128)S(1)} %product.14.refs_7_), channel_id=1, source_target_pairs={{0,4},{1,3},{4,8},{5,1},{8,12},{9,5},{12,14},{13,9},{14,10},{15,13... | collective-permute-start | bytes 786440 | tf_op jit(solution)/shard_map/ppermute | solution.py:270
  18.8 10.2 %collective-permute-start.4 = (f32[128,512]{1,0:T(8,128)S(1)}, f32[128,512]{1,0:T(8,128)S(1)}, u32[]{:S(2)}, u32[]{:S(2)}) collective-permute-start(f32[128,512]{1,0:T(8,128)S(1)} %add.30), channel_id=1, source_target_pairs={{0,2},{1,5},{4,0},{5,9},{8,4},{9,13},{12,8},{13,15},{14,12},{15,11... | collective-permute-start | bytes 786440 | tf_op jit(solution)/shard_map/ppermute | solution.py:270
  21.3 10.4 %collective-permute-start.15 = (f32[128,512]{1,0:T(8,128)S(1)}, f32[128,512]{1,0:T(8,128)S(1)}, u32[]{:S(2)}, u32[]{:S(2)}) collective-permute-start(f32[128,512]{1,0:T(8,128)S(1)} %add.37), channel_id=1, source_target_pairs={{0,4},{1,3},{4,8},{5,1},{8,12},{9,5},{12,14},{13,9},{14,10},{15,13... | collective-permute-start | bytes 786440 | tf_op jit(solution)/shard_map/ppermute | solution.py:270
  26.9 10.4 %collective-permute-start.9 = (f32[128,512]{1,0:T(8,128)S(1)}, f32[128,512]{1,0:T(8,128)S(1)}, u32[]{:S(2)}, u32[]{:S(2)}) collective-permute-start(f32[128,512]{1,0:T(8,128)S(1)} %add.33), channel_id=1, source_target_pairs={{0,4},{1,3},{4,8},{5,1},{8,12},{9,5},{12,14},{13,9},{14,10},{15,13... | collective-permute-start | bytes 786440 | tf_op jit(solution)/shard_map/ppermute | solution.py:270
  27.0 10.6 %collective-permute-start.12 = (f32[128,512]{1,0:T(8,128)S(1)}, f32[128,512]{1,0:T(8,128)S(1)}, u32[]{:S(2)}, u32[]{:S(2)}) collective-permute-start(f32[128,512]{1,0:T(8,128)S(1)} %add.35), channel_id=1, source_target_pairs={{0,2},{1,5},{4,0},{5,9},{8,4},{9,13},{12,8},{13,15},{14,12},{15,11... | collective-permute-start | bytes 786440 | tf_op jit(solution)/shard_map/ppermute | solution.py:270
  29.1 12.8 %collective-permute-start.6 = (f32[128,512]{1,0:T(8,128)S(1)}, f32[128,512]{1,0:T(8,128)S(1)}, u32[]{:S(2)}, u32[]{:S(2)}) collective-permute-start(f32[128,512]{1,0:T(8,128)S(1)} %add.31), channel_id=1, source_target_pairs={{0,2},{1,5},{4,0},{5,9},{8,4},{9,13},{12,8},{13,15},{14,12},{15,11... | collective-permute-start | bytes 786440 | tf_op jit(solution)/shard_map/ppermute | solution.py:270
  31.7 12.3 %collective-permute-start.16 = (f32[128,512]{1,0:T(8,128)S(1)}, f32[128,512]{1,0:T(8,128)S(1)}, u32[]{:S(2)}, u32[]{:S(2)}) collective-permute-start(f32[128,512]{1,0:T(8,128)S(1)} %add.38), channel_id=1, source_target_pairs={{0,4},{1,3},{4,8},{5,1},{8,12},{9,5},{12,14},{13,9},{14,10},{15,13... | collective-permute-start | bytes 786440 | tf_op jit(solution)/shard_map/ppermute | solution.py:270
  37.3 11.2 %collective-permute-start.10 = (f32[128,512]{1,0:T(8,128)S(1)}, f32[128,512]{1,0:T(8,128)S(1)}, u32[]{:S(2)}, u32[]{:S(2)}) collective-permute-start(f32[128,512]{1,0:T(8,128)S(1)} %add.34), channel_id=1, source_target_pairs={{0,4},{1,3},{4,8},{5,1},{8,12},{9,5},{12,14},{13,9},{14,10},{15,13... | collective-permute-start | bytes 786440 | tf_op jit(solution)/shard_map/ppermute | solution.py:270
  37.6 10.9 %collective-permute-start.13 = (f32[128,512]{1,0:T(8,128)S(1)}, f32[128,512]{1,0:T(8,128)S(1)}, u32[]{:S(2)}, u32[]{:S(2)}) collective-permute-start(f32[128,512]{1,0:T(8,128)S(1)} %add.36), channel_id=1, source_target_pairs={{0,2},{1,5},{4,0},{5,9},{8,4},{9,13},{12,8},{13,15},{14,12},{15,11... | collective-permute-start | bytes 786440 | tf_op jit(solution)/shard_map/ppermute | solution.py:270
  42.0 9.2 %collective-permute-start.7 = (f32[128,512]{1,0:T(8,128)S(1)}, f32[128,512]{1,0:T(8,128)S(1)}, u32[]{:S(2)}, u32[]{:S(2)}) collective-permute-start(f32[128,512]{1,0:T(8,128)S(1)} %add.32), channel_id=1, source_target_pairs={{0,2},{1,5},{4,0},{5,9},{8,4},{9,13},{12,8},{13,15},{14,12},{15,11... | collective-permute-start | bytes 786440 | tf_op jit(solution)/shard_map/ppermute | solution.py:270
  44.1 8.2 %collective-permute-start.17 = (f32[128,512]{1,0:T(8,128)S(1)}, f32[128,512]{1,0:T(8,128)S(1)}, u32[]{:S(2)}, u32[]{:S(2)}) collective-permute-start(f32[128,512]{1,0:T(8,128)S(1)} %add.39), channel_id=1, source_target_pairs={{0,4},{1,3},{4,8},{5,1},{8,12},{9,5},{12,14},{13,9},{14,10},{15,13... | collective-permute-start | bytes 786440 | tf_op jit(solution)/shard_map/ppermute | solution.py:270

commit v8 on v7

--- a/solution.py
+++ b/solution.py
@@ -112,27 +112,31 @@
 def product_kernel(starts, size, bounds, parts, *refs):
     count = len(bounds)
     sources, pairs = refs[:count], refs[count : count + 2 * parts]
-    outs, (raw, stack, sems) = refs[-3 - parts : -3], refs[-3:]
-    depth = raw.shape[0]
-    for index in range(starts.shape[-1]):
-        start = looked_up(starts[..., index])
-        first = 0
-        for source, last in zip(sources, bounds):
-
-            @pl.when((start >= first) & (start < last))
-            def _(source=source, first=first, start=start, index=index):
-                pltpu.make_async_copy(
-                    source.at[pl.ds(pl.multiple_of(start - first, size), size)],
-                    raw.at[pl.ds(index * size, size)],
-                    sems.at[index],
-                ).start()
-
-            first = last
-    for index in range(starts.shape[-1]):
-        pltpu.make_async_copy(
-            sources[0].at[pl.ds(0, size)], raw.at[pl.ds(index * size, size)], sems.at[index]
-        ).wait()
-    stack[:depth], stack[depth:] = halves(raw[...])
+    if starts is None:
+        (stack,), outs = sources, refs[-parts:]
+        depth = stack.shape[0] // 2
+    else:
+        outs, (stack, raw, sems) = refs[-3 - parts : -3], refs[-3:]
+        depth = raw.shape[0]
+        for index in range(starts.shape[-1]):
+            start = looked_up(starts[..., index])
+            first = 0
+            for source, last in zip(sources, bounds):
+
+                @pl.when((start >= first) & (start < last))
+                def _(source=source, first=first, start=start, index=index):
+                    pltpu.make_async_copy(
+                        source.at[pl.ds(pl.multiple_of(start - first, size), size)],
+                        raw.at[pl.ds(index * size, size)],
+                        sems.at[index],
+                    ).start()
+
+                first = last
+        for index in range(starts.shape[-1]):
+            pltpu.make_async_copy(
+                sources[0].at[pl.ds(0, size)], raw.at[pl.ds(index * size, size)], sems.at[index]
+            ).wait()
+        stack[:depth], stack[depth:] = halves(raw[...])
     for part, out_ref in enumerate(outs):
         high_ref, low_ref = pairs[2 * part : 2 * part + 2]
         width = out_ref.shape[1]
@@ -144,20 +148,20 @@
 
 
 def product(sources, starts, size, pairs, *after):
-    depth = starts.shape[-1] * size
+    again = starts is None
+    depth = sources[0].shape[0] // 2 if again else starts.shape[-1] * size
     inner, width = pairs[0].shape
     parts = len(pairs) // 2
     anywhere, whole = pl.BlockSpec(memory_space=pl.ANY), pl.BlockSpec(memory_space=pltpu.VMEM)
-    return pl.pallas_call(
+    fetch = [pltpu.VMEM((depth, inner), jnp.float32)]
+    fetch += [] if again else [pltpu.SemaphoreType.DMA((starts.shape[-1],))]
+    got = pl.pallas_call(
         functools.partial(product_kernel, starts, size, list(np.cumsum([s.shape[0] for s in sources])), parts),
-        out_shape=[jax.ShapeDtypeStruct((depth, width), jnp.float32)] * parts,
-        in_specs=[anywhere] * len(sources) + [whole] * len(pairs) + [anywhere] * len(after),
-        out_specs=[whole] * parts,
-        scratch_shapes=[
-            pltpu.VMEM((depth, inner), jnp.float32),
-            pltpu.VMEM((2 * depth, inner), jnp.bfloat16),
-            pltpu.SemaphoreType.DMA((starts.shape[-1],)),
-        ],
+        out_shape=[jax.ShapeDtypeStruct((depth, width), jnp.float32)] * parts
+        + [jax.ShapeDtypeStruct((2 * depth, inner), jnp.bfloat16)] * (not again),
+        in_specs=[whole if again else anywhere] * len(sources) + [whole] * len(pairs) + [anywhere] * len(after),
+        out_specs=[whole] * (parts + (not again)),
+        scratch_shapes=[] if again else fetch,
         compiler_params=pltpu.CompilerParams(vmem_limit_bytes=16 * MIB),
         cost_estimate=pl.CostEstimate(
             flops=6 * depth * inner * width * parts,
@@ -166,15 +170,24 @@
         ),
         name="product",
     )(*sources, *pairs, *after)
+    return [*got, sources[0]] if again else got
 
 
 def finish_kernel(*refs):
-    out_ref = refs[-1]
-    for part in range(2):
-        above, below, own = refs[3 * part : 3 * part + 3]
-        width = own.shape[1]
-        columns = pl.ds(pl.multiple_of(side(part) * width, width), width)
-        out_ref[:, columns] = (above[...] + below[...]) + own[...]
+    out_ref, total, sems = refs[-3:]
+    rows = total.shape[0] // sems.shape[0]
+    copies = []
+    for index in range(sems.shape[0]):
+        at = slice(index * rows, (index + 1) * rows)
+        for part in range(2):
+            above, below, own = refs[3 * part : 3 * part + 3]
+            width = own.shape[1]
+            columns = pl.ds(pl.multiple_of(side(part) * width, width), width)
+            total[at, columns] = (above[at] + below[at]) + own[at]
+        copies.append(pltpu.make_async_copy(total.at[at], out_ref.at[at], sems.at[index]))
+        copies[-1].start()
+    for copy in copies:
+        copy.wait()
 
 
 def finish(*values):
@@ -183,7 +196,11 @@
         finish_kernel,
         out_shape=jax.ShapeDtypeStruct((depth, 2 * width), jnp.float32),
         in_specs=[pl.BlockSpec(memory_space=pltpu.VMEM)] * 6,
-        out_specs=pl.BlockSpec(memory_space=pltpu.VMEM),
+        out_specs=pl.BlockSpec(memory_space=pl.ANY),
+        scratch_shapes=[
+            pltpu.VMEM((depth, 2 * width), jnp.float32),
+            pltpu.SemaphoreType.DMA((max(depth // PIECE, 1),)),
+        ],
         compiler_params=pltpu.CompilerParams(vmem_limit_bytes=8 * MIB),
         name="finish",
     )(*values)
@@ -236,12 +253,12 @@
         spare = int(group > 1)
         chunks = [group + spare] + [group] * (rows // cols // group - 2) + [group - spare]
         taken, given = plan(order, rows, cols, size, chunks)
-        own = pick(inductance, given[..., : chunks[0]], size, chunks[:1], 52)
-        own += pick(inductance, given[..., chunks[0] :], size, chunks[1:], 48, *own)
-        received = [lax.ppermute(each, "col", swap) for each in own]
-        sources = [rows for pair in zip(own, received) for rows in pair]
-        firsts = np.cumsum([0] + [each.shape[0] for each in sources])
-        pairs, calls, made = {}, {}, []
+        sources, pairs, calls, stacks, made = [], {}, {}, {}, []
+
+        def fetch(first, last, room, *after):
+            wanted = slice(sum(chunks[:first]), sum(chunks[:last]))
+            for own in pick(inductance, given[..., wanted], size, chunks[first:last], room, *after):
+                sources.extend([own, lax.ppermute(own, "col", swap)])
 
         def term(index, part):
             call, at = divmod(index, group)
@@ -251,11 +268,19 @@
                     if each not in pairs:
                         pairs[each] = split(current_rates, each, *made)
                 starts = taken[..., call * group : (call + 1) * group]
+                firsts = np.cumsum([0] + [each.shape[0] for each in sources])
                 have = sources[: int(np.searchsorted(firsts, starts.max(), "right"))]
-                got = product(have, starts, size, [half for each in parts for half in pairs[each]], *made[-1:])
+                if call in stacks:
+                    have, starts = [stacks[call]], None
+                *got, stacks[call] = product(
+                    have, starts, size, [half for each in parts for half in pairs[each]], *made[-1:]
+                )
                 calls.update({(call, each): value for each, value in zip(parts, got)})
                 made.append(got[0])
             return calls[call, part][at * size : (at + 1) * size]
+
+        fetch(0, 1, 52)
+        fetch(1, len(chunks), 48, sources[0])
 
         sums = [[None, None], [None, None]]
         for step in range(half):

time: 53.2 us -> 53.3 us (level)
  waiting for transfers between devices: 13.1 us -> 8.75 us
  Pallas kernels: 22.8 us -> 26.5 us
  starting transfers between devices: 16.6 us -> 17.2 us
    ppermute x14, waiting for transfers between devices: 13.1 us -> 8.74 us  [shards(): sums[way][part] = lax.ppermute(value, ('row', 'col'), ways[way])]
    pallas_call x11, Pallas kernels: 16.3 us -> 20 us  [product(): pl.pallas_call(functools.partial(product_kernel, starts, size, list(np.cu...]
    ppermute x14, starting transfers between devices: 15.4 us -> 16 us  [shards(): sums[way][part] = lax.ppermute(value, ('row', 'col'), ways[way])]
  transfers between devices with their start and end apart: 18 -> 18, of which waited for: 8 -> 7; matrix products, arithmetic and copies ran while one was open for 1% -> 1% of each run, Pallas kernels for 39% -> 46%
where the time goes in v8:
time: 53.3 us; the launch traced here: 53.1 us
  Pallas kernels  26.5 us (50%)
  starting transfers between devices  17.2 us (32%)
  waiting for transfers between devices  8.75 us (16%)
    pallas_call x11, Pallas kernels, product(): pl.pallas_call(functools.partial(product_kernel, starts, size, list(np.cu...  20 us
    ppermute x14, starting transfers between devices, shards(): sums[way][part] = lax.ppermute(value, ('row', 'col'), ways[way])  16 us
    ppermute x14, waiting for transfers between devices, shards(): sums[way][part] = lax.ppermute(value, ('row', 'col'), ways[way])  8.74 us
    pallas_call x2, Pallas kernels, pick(): pl.pallas_call(functools.partial(pick_kernel, starts, size, chunks), out_...  3.77 us
    pallas_call x2, Pallas kernels, split(): pl.pallas_call(split_kernel, grid=(depth // tile,), out_shape=[jax.ShapeD...  1.87 us
    ppermute x4, starting transfers between devices, fetch(): sources.extend([own, lax.ppermute(own, 'col', swap)])  1.16 us
  transfers between devices with their start and end apart: 18, of which 7 were waited for; matrix products, arithmetic and copies ran while one was open for 1% of the time, Pallas kernels for 46%

profile of v8, /device:TPU:0, one launch (start us, length us, event | category | flops | bytes accessed | tf_op | source)
XLA Modules:
  0.0 53.1 jit_solution(12483182554770796668)
XLA Ops:
  0.0 0.0 copy-start
  0.0 1.4 %pick.2.refs_0_ = f32[128,2048]{1,0:T(8,128)S(1)} custom-call(f32[512,2048]{1,0:T(8,128)} %a_ref.3), custom_call_target="tpu_custom_call" | custom-call | bytes 2097152 | tf_op jit(solution)/shard_map/pick/pallas_call | solution.py:69
  1.4 0.5 collective-permute-start
  2.0 2.3 %pick.3 = (f32[128,2048]{1,0:T(8,128)S(1)}, f32[128,2048]{1,0:T(8,128)S(1)}, f32[128,2048]{1,0:T(8,128)S(1)}) custom-call(f32[512,2048]{1,0:T(8,128)} %a_ref.3, f32[128,2048]{1,0:T(8,128)S(1)} %pick.2.refs_0_), custom_call_target="tpu_custom_call" | custom-call | bytes 6291456 | tf_op jit(solution)/shard_map/pick/pallas_call | solution.py:69
  4.3 0.1 collective-permute-start.2
  4.4 0.5 collective-permute-start.3
  4.9 0.1 collective-permute-start.5
  5.0 0.0 copy-done
  5.0 0.9 %split.2 = (bf16[2048,512]{1,0:T(8,128)(2,1)S(1)}, bf16[2048,512]{1,0:T(8,128)(2,1)S(1)}) custom-call(f32[2048,1024]{1,0:T(8,128)S(1)} %copy-done), custom_call_target="tpu_custom_call" | custom-call | flops 4194304 | bytes 8388608 | tf_op jit(solution)/shard_map/split/pallas_call | solution.py:99
  5.9 0.0 collective-permute-done.refs_1_
  5.9 1.1 %product.11 = (f32[128,512]{1,0:T(8,128)S(1)}, bf16[256,2048]{1,0:T(8,128)(2,1)S(1)}) custom-call(f32[128,2048]{1,0:T(8,128)S(1)} %pick.2.refs_0_, f32[128,2048]{1,0:T(8,128)S(1)} %collective-permute-done.refs_1_, bf16[2048,512]{1,0:T(8,128)(2,1)S(1)} %get-tuple-element.28.refs_2_.refs_6_.refs_1_.refs_8_, ...), custom_call_target="tpu_custom_call" | custom-call | flops 805306368 | bytes 5505024 | tf_op jit(solution)/shard_map/product/pallas_call | solution.py:158
  7.0 3.1 %collective-permute-start.1 = (f32[128,512]{1,0:T(8,128)S(1)}, f32[128,512]{1,0:T(8,128)S(1)}, u32[]{:S(2)}, u32[]{:S(2)}) collective-permute-start(f32[128,512]{1,0:T(8,128)S(1)} %get-tuple-element.30.refs_0_.refs_3_), channel_id=1, source_target_pairs={{0,2},{1,5},{4,0},{5,9},{8,4},{9,13},{12,8},{13,15},{14,12},{15,11... | collective-permute-start | bytes 786440 | tf_op jit(solution)/shard_map/ppermute | solution.py:295
  10.1 0.9 %split.3 = (bf16[2048,512]{1,0:T(8,128)(2,1)S(1)}, bf16[2048,512]{1,0:T(8,128)(2,1)S(1)}) custom-call(f32[2048,1024]{1,0:T(8,128)S(1)} %copy-done, f32[128,512]{1,0:T(8,128)S(1)} %get-tuple-element.30.refs_0_.refs_3_), custom_call_target="tpu_custom_call" | custom-call | flops 4194304 | bytes 8388608 | tf_op jit(solution)/shard_map/split/pallas_call | solution.py:99
  11.0 1.0 %product.12.refs_7_ = f32[128,512]{1,0:T(8,128)S(1)} custom-call(bf16[256,2048]{1,0:T(8,128)(2,1)S(1)} %get-tuple-element.35.refs_0_, bf16[2048,512]{1,0:T(8,128)(2,1)S(1)} %get-tuple-element.33.refs_1_.refs_5_.refs_10_, bf16[2048,512]{1,0:T(8,128)(2,1)S(1)} %get-tuple-element.34.refs_2_.refs_6_.refs_11_, f32[128,512]{1,0:T(8,128)S(1)} %get-tuple-element.30.refs_0_.refs_3_), custom_call_target="tpu_custom_call" | custom-call | flops 805306368 | bytes 5505024 | tf_op jit(solution)/shard_map/product/pallas_call | solution.py:158
  12.0 0.2 collective-permute-start.14
  12.2 0.0 collective-permute-done.2.refs_3_
  12.2 1.1 %product.13 = (f32[128,512]{1,0:T(8,128)S(1)}, bf16[256,2048]{1,0:T(8,128)(2,1)S(1)}) custom-call(f32[128,2048]{1,0:T(8,128)S(1)} %pick.2.refs_0_, f32[128,2048]{1,0:T(8,128)S(1)} %collective-permute-done.refs_1_, f32[128,2048]{1,0:T(8,128)S(1)} %get-tuple-element.31.refs_2_, f32[128,2048]{1,0:T(8,128)S(1)} %collective-permute-done.2.refs_3_, ...), custom_call_target="tpu_custom_call" | custom-call | flops 805306368 | bytes 5505024 | tf_op jit(solution)/shard_map/product/pallas_call | solution.py:158
  13.2 2.0 %collective-permute-start.11 = (f32[128,512]{1,0:T(8,128)S(1)}, f32[128,512]{1,0:T(8,128)S(1)}, u32[]{:S(2)}, u32[]{:S(2)}) collective-permute-start(f32[128,512]{1,0:T(8,128)S(1)} %get-tuple-element.37.refs_8_), channel_id=1, source_target_pairs={{0,2},{1,5},{4,0},{5,9},{8,4},{9,13},{12,8},{13,15},{14,12},{15,11... | collective-permute-start | bytes 786440 | tf_op jit(solution)/shard_map/ppermute | solution.py:295
  15.2 0.0 collective-permute-done.3.refs_5_
  15.2 1.1 %product.14 = (f32[128,512]{1,0:T(8,128)S(1)}, bf16[256,2048]{1,0:T(8,128)(2,1)S(1)}) custom-call(f32[128,2048]{1,0:T(8,128)S(1)} %pick.2.refs_0_, f32[128,2048]{1,0:T(8,128)S(1)} %collective-permute-done.refs_1_, f32[128,2048]{1,0:T(8,128)S(1)} %get-tuple-element.31.refs_2_, f32[128,2048]{1,0:T(8,128)S(1)} %collective-permute-done.2.refs_3_, ...), custom_call_target="tpu_custom_call" | custom-call | flops 805306368 | bytes 5505024 | tf_op jit(solution)/shard_map/product/pallas_call | solution.py:158
  16.3 0.2 collective-permute-start.8
  16.5 1.0 %product.15.refs_3_ = f32[128,512]{1,0:T(8,128)S(1)} custom-call(bf16[256,2048]{1,0:T(8,128)(2,1)S(1)} %get-tuple-element.36.refs_0_, bf16[2048,512]{1,0:T(8,128)(2,1)S(1)} %get-tuple-element.28.refs_2_.refs_6_.refs_1_.refs_8_, bf16[2048,512]{1,0:T(8,128)(2,1)S(1)} %get-tuple-element.29.refs_3_.refs_7_.refs_2_.refs_9_, f32[128,512]{1,0:T(8,128)S(1)} %get-tuple-element.38.refs_3_), custom_call_target="tpu_custom_call" | custom-call | flops 805306368 | bytes 5505024 | tf_op jit(solution)/shard_map/product/pallas_call | solution.py:158
  17.5 1.0 %product.16.refs_12_ = f32[128,512]{1,0:T(8,128)S(1)} custom-call(bf16[256,2048]{1,0:T(8,128)(2,1)S(1)} %get-tuple-element.40.refs_0_, bf16[2048,512]{1,0:T(8,128)(2,1)S(1)} %get-tuple-element.33.refs_1_.refs_5_.refs_10_, bf16[2048,512]{1,0:T(8,128)(2,1)S(1)} %get-tuple-element.34.refs_2_.refs_6_.refs_11_, f32[128,512]{1,0:T(8,128)S(1)} %product.15.refs_3_), custom_call_target="tpu_custom_call" | custom-call | flops 805306368 | bytes 5505024 | tf_op jit(solution)/shard_map/product/pallas_call | solution.py:158
  18.4 2.7 %collective-permute-done.14 = f32[128,512]{1,0:T(8,128)S(1)} collective-permute-done((f32[128,512]{1,0:T(8,128)S(1)}, f32[128,512]{1,0:T(8,128)S(1)}, u32[]{:S(2)}, u32[]{:S(2)}) %collective-permute-start.14) | collective-permute-done | bytes 262176 | tf_op jit(solution)/shard_map/ppermute | solution.py:295
  21.2 0.1 collective-permute-start.15
  21.2 0.0 collective-permute-done.1
  21.3 2.1 %collective-permute-start.4 = (f32[128,512]{1,0:T(8,128)S(1)}, f32[128,512]{1,0:T(8,128)S(1)}, u32[]{:S(2)}, u32[]{:S(2)}) collective-permute-start(f32[128,512]{1,0:T(8,128)S(1)} %add.30), channel_id=1, source_target_pairs={{0,2},{1,5},{4,0},{5,9},{8,4},{9,13},{12,8},{13,15},{14,12},{15,11... | collective-permute-start | bytes 786440 | tf_op jit(solution)/shard_map/ppermute | solution.py:295
  23.3 0.0 collective-permute-done.5.refs_7_
  23.3 2.7 %product.17 = (f32[128,512]{1,0:T(8,128)S(1)}, f32[128,512]{1,0:T(8,128)S(1)}, bf16[256,2048]{1,0:T(8,128)(2,1)}) custom-call(f32[128,2048]{1,0:T(8,128)S(1)} %pick.2.refs_0_, f32[128,2048]{1,0:T(8,128)S(1)} %collective-permute-done.refs_1_, f32[128,2048]{1,0:T(8,128)S(1)} %get-tuple-element.31.refs_2_, f32[128,2048]{1,0:T(8,128)S(1)} %collective-permute-done.2.refs_3_, ...), custom_call_target="tpu_custom_call" | custom-call | flops 1610612736 | bytes 9961472 | tf_op jit(solution)/shard_map/product/pallas_call | solution.py:158
  26.1 2.8 %product.18 = (f32[128,512]{1,0:T(8,128)S(1)}, f32[128,512]{1,0:T(8,128)S(1)}, bf16[256,2048]{1,0:T(8,128)(2,1)}) custom-call(f32[128,2048]{1,0:T(8,128)S(1)} %pick.2.refs_0_, f32[128,2048]{1,0:T(8,128)S(1)} %collective-permute-done.refs_1_, f32[128,2048]{1,0:T(8,128)S(1)} %get-tuple-element.31.refs_2_, f32[128,2048]{1,0:T(8,128)S(1)} %collective-permute-done.2.refs_3_, ...), custom_call_target="tpu_custom_call" | custom-call | flops 1610612736 | bytes 9961472 | tf_op jit(solution)/shard_map/product/pallas_call | solution.py:158
  28.9 0.0 collective-permute-done.11
  28.9 1.6 %collective-permute-start.12 = (f32[128,512]{1,0:T(8,128)S(1)}, f32[128,512]{1,0:T(8,128)S(1)}, u32[]{:S(2)}, u32[]{:S(2)}) collective-permute-start(f32[128,512]{1,0:T(8,128)S(1)} %add.35), channel_id=1, source_target_pairs={{0,2},{1,5},{4,0},{5,9},{8,4},{9,13},{12,8},{13,15},{14,12},{15,11... | collective-permute-start | bytes 786440 | tf_op jit(solution)/shard_map/ppermute | solution.py:295
  30.5 0.0 collective-permute-done.8
  30.5 0.6 %collective-permute-start.9 = (f32[128,512]{1,0:T(8,128)S(1)}, f32[128,512]{1,0:T(8,128)S(1)}, u32[]{:S(2)}, u32[]{:S(2)}) collective-permute-start(f32[128,512]{1,0:T(8,128)S(1)} %add.33), channel_id=1, source_target_pairs={{0,4},{1,3},{4,8},{5,1},{8,12},{9,5},{12,14},{13,9},{14,10},{15,13... | collective-permute-start | bytes 786440 | tf_op jit(solution)/shard_map/ppermute | solution.py:295
  31.1 0.0 collective-permute-done.4
  31.1 1.6 %collective-permute-start.6 = (f32[128,512]{1,0:T(8,128)S(1)}, f32[128,512]{1,0:T(8,128)S(1)}, u32[]{:S(2)}, u32[]{:S(2)}) collective-permute-start(f32[128,512]{1,0:T(8,128)S(1)} %add.31), channel_id=1, source_target_pairs={{0,2},{1,5},{4,0},{5,9},{8,4},{9,13},{12,8},{13,15},{14,12},{15,11... | collective-permute-start | bytes 786440 | tf_op jit(solution)/shard_map/ppermute | solution.py:295
  32.7 0.0 collective-permute-done.15
  32.7 0.6 %collective-permute-start.16 = (f32[128,512]{1,0:T(8,128)S(1)}, f32[128,512]{1,0:T(8,128)S(1)}, u32[]{:S(2)}, u32[]{:S(2)}) collective-permute-start(f32[128,512]{1,0:T(8,128)S(1)} %add.38), channel_id=1, source_target_pairs={{0,4},{1,3},{4,8},{5,1},{8,12},{9,5},{12,14},{13,9},{14,10},{15,13... | collective-permute-start | bytes 786440 | tf_op jit(solution)/shard_map/ppermute | solution.py:295
  33.3 2.7 %product.19 = (f32[128,512]{1,0:T(8,128)S(1)}, f32[128,512]{1,0:T(8,128)S(1)}, bf16[256,2048]{1,0:T(8,128)(2,1)}) custom-call(f32[128,2048]{1,0:T(8,128)S(1)} %pick.2.refs_0_, f32[128,2048]{1,0:T(8,128)S(1)} %collective-permute-done.refs_1_, f32[128,2048]{1,0:T(8,128)S(1)} %get-tuple-element.31.refs_2_, f32[128,2048]{1,0:T(8,128)S(1)} %collective-permute-done.2.refs_3_, ...), custom_call_target="tpu_custom_call" | custom-call | flops 1610612736 | bytes 9961472 | tf_op jit(solution)/shard_map/product/pallas_call | solution.py:158
  36.0 3.0 %product.20 = (f32[128,512]{1,0:T(8,128)S(1)}, f32[128,512]{1,0:T(8,128)S(1)}, bf16[256,2048]{1,0:T(8,128)(2,1)}) custom-call(f32[128,2048]{1,0:T(8,128)S(1)} %pick.2.refs_0_, f32[128,2048]{1,0:T(8,128)S(1)} %collective-permute-done.refs_1_, f32[128,2048]{1,0:T(8,128)S(1)} %get-tuple-element.31.refs_2_, f32[128,2048]{1,0:T(8,128)S(1)} %collective-permute-done.2.refs_3_, ...), custom_call_target="tpu_custom_call" | custom-call | flops 1610612736 | bytes 9961472 | tf_op jit(solution)/shard_map/product/pallas_call | solution.py:158
  39.0 0.0 collective-permute-done.12
  39.0 1.6 %collective-permute-start.13 = (f32[128,512]{1,0:T(8,128)S(1)}, f32[128,512]{1,0:T(8,128)S(1)}, u32[]{:S(2)}, u32[]{:S(2)}) collective-permute-start(f32[128,512]{1,0:T(8,128)S(1)} %add.36), channel_id=1, source_target_pairs={{0,2},{1,5},{4,0},{5,9},{8,4},{9,13},{12,8},{13,15},{14,12},{15,11... | collective-permute-start | bytes 786440 | tf_op jit(solution)/shard_map/ppermute | solution.py:295
  40.6 0.0 collective-permute-done.9
  40.7 0.6 %collective-permute-start.10 = (f32[128,512]{1,0:T(8,128)S(1)}, f32[128,512]{1,0:T(8,128)S(1)}, u32[]{:S(2)}, u32[]{:S(2)}) collective-permute-start(f32[128,512]{1,0:T(8,128)S(1)} %add.34), channel_id=1, source_target_pairs={{0,4},{1,3},{4,8},{5,1},{8,12},{9,5},{12,14},{13,9},{14,10},{15,13... | collective-permute-start | bytes 786440 | tf_op jit(solution)/shard_map/ppermute | solution.py:295
  41.2 1.7 %collective-permute-done.6 = f32[128,512]{1,0:T(8,128)S(1)} collective-permute-done((f32[128,512]{1,0:T(8,128)S(1)}, f32[128,512]{1,0:T(8,128)S(1)}, u32[]{:S(2)}, u32[]{:S(2)}) %collective-permute-start.6) | collective-permute-done | bytes 262176 | tf_op jit(solution)/shard_map/ppermute | solution.py:295
  43.0 0.5 collective-permute-start.7
  43.5 0.1 collective-permute-done.16
  43.6 1.6 %collective-permute-start.17 = (f32[128,512]{1,0:T(8,128)S(1)}, f32[128,512]{1,0:T(8,128)S(1)}, u32[]{:S(2)}, u32[]{:S(2)}) collective-permute-start(f32[128,512]{1,0:T(8,128)S(1)} %add.39), channel_id=1, source_target_pairs={{0,4},{1,3},{4,8},{5,1},{8,12},{9,5},{12,14},{13,9},{14,10},{15,13... | collective-permute-start | bytes 786440 | tf_op jit(solution)/shard_map/ppermute | solution.py:295
  45.2 2.7 %product.21 = (f32[128,512]{1,0:T(8,128)S(1)}, f32[128,512]{1,0:T(8,128)S(1)}, bf16[256,2048]{1,0:T(8,128)(2,1)}) custom-call(f32[128,2048]{1,0:T(8,128)S(1)} %pick.2.refs_0_, f32[128,2048]{1,0:T(8,128)S(1)} %collective-permute-done.refs_1_, f32[128,2048]{1,0:T(8,128)S(1)} %get-tuple-element.31.refs_2_, f32[128,2048]{1,0:T(8,128)S(1)} %collective-permute-done.2.refs_3_, ...), custom_call_target="tpu_custom_call" | custom-call | flops 1610612736 | bytes 9961472 | tf_op jit(solution)/shard_map/product/pallas_call | solution.py:158
  47.9 0.7 %collective-permute-done.13.refs_3_ = f32[128,512]{1,0:T(8,128)S(1)} collective-permute-done((f32[128,512]{1,0:T(8,128)S(1)}, f32[128,512]{1,0:T(8,128)S(1)}, u32[]{:S(2)}, u32[]{:S(2)}) %collective-permute-start.13) | collective-permute-done | bytes 262176 | tf_op jit(solution)/shard_map/ppermute | solution.py:295
  48.6 0.7 %collective-permute-done.10.refs_1_ = f32[128,512]{1,0:T(8,128)S(1)} collective-permute-done((f32[128,512]{1,0:T(8,128)S(1)}, f32[128,512]{1,0:T(8,128)S(1)}, u32[]{:S(2)}, u32[]{:S(2)}) %collective-permute-start.10) | collective-permute-done | bytes 262176 | tf_op jit(solution)/shard_map/ppermute | solution.py:295
  49.3 2.7 %collective-permute-done.7.refs_0_ = f32[128,512]{1,0:T(8,128)S(1)} collective-permute-done((f32[128,512]{1,0:T(8,128)S(1)}, f32[128,512]{1,0:T(8,128)S(1)}, u32[]{:S(2)}, u32[]{:S(2)}) %collective-permute-start.7) | collective-permute-done | bytes 262176 | tf_op jit(solution)/shard_map/ppermute | solution.py:295
  52.0 0.1 collective-permute-done.17.refs_4_
  52.1 0.9 %finish.1 = f32[128,1024]{1,0:T(8,128)} custom-call(f32[128,512]{1,0:T(8,128)S(1)} %collective-permute-done.7.refs_0_, f32[128,512]{1,0:T(8,128)S(1)} %collective-permute-done.10.refs_1_, f32[128,512]{1,0:T(8,128)S(1)} %get-tuple-element.45.refs_2_, f32[128,512]{1,0:T(8,128)S(1)} %collective-permute-done.13.refs_3_, ...), custom_call_target="tpu_custom_call" | custom-call | tf_op jit(solution)/shard_map/finish/pallas_call | solution.py:195
  (10 shorter events, 0.4 us)
Async XLA Ops:
  0.0 5.0 %copy-start = (f32[2048,1024]{1,0:T(8,128)S(1)}, f32[2048,1024]{1,0:T(8,128)}, u32[]{:S(2)}) copy-start(f32[2048,1024]{1,0:T(8,128)} %value_ref.3) | copy-start | bytes 25165828
  1.4 4.5 %collective-permute-start = (f32[128,2048]{1,0:T(8,128)S(1)}, f32[128,2048]{1,0:T(8,128)S(1)}, u32[]{:S(2)}, u32[]{:S(2)}) collective-permute-start(f32[128,2048]{1,0:T(8,128)S(1)} %pick.2.refs_0_), channel_id=1, source_target_pairs={{0,1},{1,0},{2,3},{3,2},{4,5},{5,4},{6,7},{7,6},{8,9},{9,8},{10,11... | collective-permute-start | bytes 3145736 | tf_op jit(solution)/shard_map/ppermute | solution.py:261
  4.3 7.9 %collective-permute-start.2 = (f32[128,2048]{1,0:T(8,128)S(1)}, f32[128,2048]{1,0:T(8,128)S(1)}, u32[]{:S(2)}, u32[]{:S(2)}) collective-permute-start(f32[128,2048]{1,0:T(8,128)S(1)} %get-tuple-element.31.refs_2_), channel_id=1, source_target_pairs={{0,1},{1,0},{2,3},{3,2},{4,5},{5,4},{6,7},{7,6},{8,9},{9,8},{10,11... | collective-permute-start | bytes 3145736 | tf_op jit(solution)/shard_map/ppermute | solution.py:261
  4.4 10.8 %collective-permute-start.3 = (f32[128,2048]{1,0:T(8,128)S(1)}, f32[128,2048]{1,0:T(8,128)S(1)}, u32[]{:S(2)}, u32[]{:S(2)}) collective-permute-start(f32[128,2048]{1,0:T(8,128)S(1)} %get-tuple-element.32.refs_4_), channel_id=1, source_target_pairs={{0,1},{1,0},{2,3},{3,2},{4,5},{5,4},{6,7},{7,6},{8,9},{9,8},{10,11... | collective-permute-start | bytes 3145736 | tf_op jit(solution)/shard_map/ppermute | solution.py:261
  4.9 18.4 %collective-permute-start.5 = (f32[128,2048]{1,0:T(8,128)S(1)}, f32[128,2048]{1,0:T(8,128)S(1)}, u32[]{:S(2)}, u32[]{:S(2)}) collective-permute-start(f32[128,2048]{1,0:T(8,128)S(1)} %get-tuple-element.39.refs_6_), channel_id=1, source_target_pairs={{0,1},{1,0},{2,3},{3,2},{4,5},{5,4},{6,7},{7,6},{8,9},{9,8},{10,11... | collective-permute-start | bytes 3145736 | tf_op jit(solution)/shard_map/ppermute | solution.py:261
  7.0 14.2 %collective-permute-start.1 = (f32[128,512]{1,0:T(8,128)S(1)}, f32[128,512]{1,0:T(8,128)S(1)}, u32[]{:S(2)}, u32[]{:S(2)}) collective-permute-start(f32[128,512]{1,0:T(8,128)S(1)} %get-tuple-element.30.refs_0_.refs_3_), channel_id=1, source_target_pairs={{0,2},{1,5},{4,0},{5,9},{8,4},{9,13},{12,8},{13,15},{14,12},{15,11... | collective-permute-start | bytes 786440 | tf_op jit(solution)/shard_map/ppermute | solution.py:295
  12.0 9.1 %collective-permute-start.14 = (f32[128,512]{1,0:T(8,128)S(1)}, f32[128,512]{1,0:T(8,128)S(1)}, u32[]{:S(2)}, u32[]{:S(2)}) collective-permute-start(f32[128,512]{1,0:T(8,128)S(1)} %product.12.refs_7_), channel_id=1, source_target_pairs={{0,4},{1,3},{4,8},{5,1},{8,12},{9,5},{12,14},{13,9},{14,10},{15,13... | collective-permute-start | bytes 786440 | tf_op jit(solution)/shard_map/ppermute | solution.py:295
  13.2 15.6 %collective-permute-start.11 = (f32[128,512]{1,0:T(8,128)S(1)}, f32[128,512]{1,0:T(8,128)S(1)}, u32[]{:S(2)}, u32[]{:S(2)}) collective-permute-start(f32[128,512]{1,0:T(8,128)S(1)} %get-tuple-element.37.refs_8_), channel_id=1, source_target_pairs={{0,2},{1,5},{4,0},{5,9},{8,4},{9,13},{12,8},{13,15},{14,12},{15,11... | collective-permute-start | bytes 786440 | tf_op jit(solution)/shard_map/ppermute | solution.py:295
  16.3 14.2 %collective-permute-start.8 = (f32[128,512]{1,0:T(8,128)S(1)}, f32[128,512]{1,0:T(8,128)S(1)}, u32[]{:S(2)}, u32[]{:S(2)}) collective-permute-start(f32[128,512]{1,0:T(8,128)S(1)} %get-tuple-element.38.refs_3_), channel_id=1, source_target_pairs={{0,4},{1,3},{4,8},{5,1},{8,12},{9,5},{12,14},{13,9},{14,10},{15,13... | collective-permute-start | bytes 786440 | tf_op jit(solution)/shard_map/ppermute | solution.py:295
  21.2 11.6 %collective-permute-start.15 = (f32[128,512]{1,0:T(8,128)S(1)}, f32[128,512]{1,0:T(8,128)S(1)}, u32[]{:S(2)}, u32[]{:S(2)}) collective-permute-start(f32[128,512]{1,0:T(8,128)S(1)} %add.37), channel_id=1, source_target_pairs={{0,4},{1,3},{4,8},{5,1},{8,12},{9,5},{12,14},{13,9},{14,10},{15,13... | collective-permute-start | bytes 786440 | tf_op jit(solution)/shard_map/ppermute | solution.py:295
  21.3 9.8 %collective-permute-start.4 = (f32[128,512]{1,0:T(8,128)S(1)}, f32[128,512]{1,0:T(8,128)S(1)}, u32[]{:S(2)}, u32[]{:S(2)}) collective-permute-start(f32[128,512]{1,0:T(8,128)S(1)} %add.30), channel_id=1, source_target_pairs={{0,2},{1,5},{4,0},{5,9},{8,4},{9,13},{12,8},{13,15},{14,12},{15,11... | collective-permute-start | bytes 786440 | tf_op jit(solution)/shard_map/ppermute | solution.py:295
  28.9 10.1 %collective-permute-start.12 = (f32[128,512]{1,0:T(8,128)S(1)}, f32[128,512]{1,0:T(8,128)S(1)}, u32[]{:S(2)}, u32[]{:S(2)}) collective-permute-start(f32[128,512]{1,0:T(8,128)S(1)} %add.35), channel_id=1, source_target_pairs={{0,2},{1,5},{4,0},{5,9},{8,4},{9,13},{12,8},{13,15},{14,12},{15,11... | collective-permute-start | bytes 786440 | tf_op jit(solution)/shard_map/ppermute | solution.py:295
  30.5 10.1 %collective-permute-start.9 = (f32[128,512]{1,0:T(8,128)S(1)}, f32[128,512]{1,0:T(8,128)S(1)}, u32[]{:S(2)}, u32[]{:S(2)}) collective-permute-start(f32[128,512]{1,0:T(8,128)S(1)} %add.33), channel_id=1, source_target_pairs={{0,4},{1,3},{4,8},{5,1},{8,12},{9,5},{12,14},{13,9},{14,10},{15,13... | collective-permute-start | bytes 786440 | tf_op jit(solution)/shard_map/ppermute | solution.py:295
  31.1 11.8 %collective-permute-start.6 = (f32[128,512]{1,0:T(8,128)S(1)}, f32[128,512]{1,0:T(8,128)S(1)}, u32[]{:S(2)}, u32[]{:S(2)}) collective-permute-start(f32[128,512]{1,0:T(8,128)S(1)} %add.31), channel_id=1, source_target_pairs={{0,2},{1,5},{4,0},{5,9},{8,4},{9,13},{12,8},{13,15},{14,12},{15,11... | collective-permute-start | bytes 786440 | tf_op jit(solution)/shard_map/ppermute | solution.py:295
  32.7 10.8 %collective-permute-start.16 = (f32[128,512]{1,0:T(8,128)S(1)}, f32[128,512]{1,0:T(8,128)S(1)}, u32[]{:S(2)}, u32[]{:S(2)}) collective-permute-start(f32[128,512]{1,0:T(8,128)S(1)} %add.38), channel_id=1, source_target_pairs={{0,4},{1,3},{4,8},{5,1},{8,12},{9,5},{12,14},{13,9},{14,10},{15,13... | collective-permute-start | bytes 786440 | tf_op jit(solution)/shard_map/ppermute | solution.py:295
  39.0 9.5 %collective-permute-start.13 = (f32[128,512]{1,0:T(8,128)S(1)}, f32[128,512]{1,0:T(8,128)S(1)}, u32[]{:S(2)}, u32[]{:S(2)}) collective-permute-start(f32[128,512]{1,0:T(8,128)S(1)} %add.36), channel_id=1, source_target_pairs={{0,2},{1,5},{4,0},{5,9},{8,4},{9,13},{12,8},{13,15},{14,12},{15,11... | collective-permute-start | bytes 786440 | tf_op jit(solution)/shard_map/ppermute | solution.py:295
  40.7 8.7 %collective-permute-start.10 = (f32[128,512]{1,0:T(8,128)S(1)}, f32[128,512]{1,0:T(8,128)S(1)}, u32[]{:S(2)}, u32[]{:S(2)}) collective-permute-start(f32[128,512]{1,0:T(8,128)S(1)} %add.34), channel_id=1, source_target_pairs={{0,4},{1,3},{4,8},{5,1},{8,12},{9,5},{12,14},{13,9},{14,10},{15,13... | collective-permute-start | bytes 786440 | tf_op jit(solution)/shard_map/ppermute | solution.py:295
  43.0 9.0 %collective-permute-start.7 = (f32[128,512]{1,0:T(8,128)S(1)}, f32[128,512]{1,0:T(8,128)S(1)}, u32[]{:S(2)}, u32[]{:S(2)}) collective-permute-start(f32[128,512]{1,0:T(8,128)S(1)} %add.32), channel_id=1, source_target_pairs={{0,2},{1,5},{4,0},{5,9},{8,4},{9,13},{12,8},{13,15},{14,12},{15,11... | collective-permute-start | bytes 786440 | tf_op jit(solution)/shard_map/ppermute | solution.py:295
  43.6 8.5 %collective-permute-start.17 = (f32[128,512]{1,0:T(8,128)S(1)}, f32[128,512]{1,0:T(8,128)S(1)}, u32[]{:S(2)}, u32[]{:S(2)}) collective-permute-start(f32[128,512]{1,0:T(8,128)S(1)} %add.39), channel_id=1, source_target_pairs={{0,4},{1,3},{4,8},{5,1},{8,12},{9,5},{12,14},{13,9},{14,10},{15,13... | collective-permute-start | bytes 786440 | tf_op jit(solution)/shard_map/ppermute | solution.py:295

commit v9 on v7

--- a/solution.py
+++ b/solution.py
@@ -87,33 +87,14 @@
     return high, (value - high.astype(jnp.float32)).astype(jnp.bfloat16)
 
 
-def split_kernel(value_ref, *refs):
-    high_ref, low_ref = refs[-2:]
-    high_ref[...], low_ref[...] = halves(value_ref[...])
-
-
-def split(current_rates, part, *after):
-    depth, width = current_rates.shape
-    width //= 2
-    tile = min(512, depth)
-    return pl.pallas_call(
-        split_kernel,
-        grid=(depth // tile,),
-        out_shape=[jax.ShapeDtypeStruct((depth, width), jnp.bfloat16)] * 2,
-        in_specs=[pl.BlockSpec((tile, width), lambda k: (k, side(part)))]
-        + [pl.BlockSpec(memory_space=pl.ANY)] * len(after),
-        out_specs=[pl.BlockSpec((tile, width), lambda k: (k, 0))] * 2,
-        compiler_params=pltpu.CompilerParams(vmem_limit_bytes=8 * MIB),
-        cost_estimate=pl.CostEstimate(flops=4 * depth * width, bytes_accessed=8 * depth * width, transcendentals=0),
-        name="split",
-    )(current_rates, *after)
-
-
-def product_kernel(starts, size, bounds, parts, *refs):
-    count = len(bounds)
-    sources, pairs = refs[:count], refs[count : count + 2 * parts]
-    outs, (raw, stack, sems) = refs[-3 - parts : -3], refs[-3:]
-    depth = raw.shape[0]
+def times(stack, high, low):
+    depth = stack.shape[0] // 2
+    both = jnp.dot(stack[...], high, preferred_element_type=jnp.float32)
+    rest = jnp.dot(stack[:depth], low, preferred_element_type=jnp.float32)
+    return both[:depth] + (both[depth:] + rest)
+
+
+def fetch_rows(starts, size, bounds, sources, stack, raw, sems):
     for index in range(starts.shape[-1]):
         start = looked_up(starts[..., index])
         first = 0
@@ -132,32 +113,57 @@
         pltpu.make_async_copy(
             sources[0].at[pl.ds(0, size)], raw.at[pl.ds(index * size, size)], sems.at[index]
         ).wait()
+    depth = raw.shape[0]
     stack[:depth], stack[depth:] = halves(raw[...])
-    for part, out_ref in enumerate(outs):
-        high_ref, low_ref = pairs[2 * part : 2 * part + 2]
-        width = out_ref.shape[1]
+
+
+def product_kernel(starts, size, bounds, parts, split, *refs):
+    count = len(bounds)
+    sources, refs = refs[:count], refs[count:]
+    columns, refs = refs[: 1 if split else 2 * parts], refs[1 if split else 2 * parts :]
+    if starts is None:
+        (stack,) = sources
+    else:
+        *refs, stack, raw, sems = refs
+        fetch_rows(starts, size, bounds, sources, stack, raw, sems)
+    outs = refs[-parts - (2 if split else 0) :]
+    for part in range(parts):
+        width = outs[part].shape[1]
         tile = min(LANES, width)
         for at in range(0, width, tile):
-            both = jnp.dot(stack[...], high_ref[:, at : at + tile], preferred_element_type=jnp.float32)
-            rest = jnp.dot(stack[:depth], low_ref[:, at : at + tile], preferred_element_type=jnp.float32)
-            out_ref[:, at : at + tile] = both[:depth] + (both[depth:] + rest)
-
-
-def product(sources, starts, size, pairs, *after):
-    depth = starts.shape[-1] * size
-    inner, width = pairs[0].shape
-    parts = len(pairs) // 2
+            here = slice(at, at + tile)
+            if split:
+                first = pl.multiple_of(side(split - 1) * width + at, tile)
+                high, low = halves(columns[0][:, pl.ds(first, tile)])
+                outs[1][:, here], outs[2][:, here] = high, low
+            else:
+                high, low = (ref[:, here] for ref in columns[2 * part : 2 * part + 2])
+            outs[part][:, here] = times(stack, high, low)
+
+
+def product(sources, starts, size, columns, split, keep, *after):
+    again = starts is None
+    depth = sources[0].shape[0] // 2 if again else starts.shape[-1] * size
+    inner, width = columns[0].shape
+    parts = max(len(columns) // 2, 1)
+    width = width // 2 if split else width
     anywhere, whole = pl.BlockSpec(memory_space=pl.ANY), pl.BlockSpec(memory_space=pltpu.VMEM)
+    outs = [jax.ShapeDtypeStruct((depth, width), jnp.float32)] * parts
+    outs += [jax.ShapeDtypeStruct((inner, width), jnp.bfloat16)] * (2 if split else 0)
+    scratch = []
+    if not again:
+        scratch = [pltpu.VMEM((depth, inner), jnp.float32), pltpu.SemaphoreType.DMA((starts.shape[-1],))]
+        if keep:
+            outs += [jax.ShapeDtypeStruct((2 * depth, inner), jnp.bfloat16)]
+        else:
+            scratch.insert(0, pltpu.VMEM((2 * depth, inner), jnp.bfloat16))
+    bounds = list(np.cumsum([s.shape[0] for s in sources]))
     return pl.pallas_call(
-        functools.partial(product_kernel, starts, size, list(np.cumsum([s.shape[0] for s in sources])), parts),
-        out_shape=[jax.ShapeDtypeStruct((depth, width), jnp.float32)] * parts,
-        in_specs=[anywhere] * len(sources) + [whole] * len(pairs) + [anywhere] * len(after),
-        out_specs=[whole] * parts,
-        scratch_shapes=[
-            pltpu.VMEM((depth, inner), jnp.float32),
-            pltpu.VMEM((2 * depth, inner), jnp.bfloat16),
-            pltpu.SemaphoreType.DMA((starts.shape[-1],)),
-        ],
+        functools.partial(product_kernel, starts, size, bounds, parts, split),
+        out_shape=outs,
+        in_specs=[whole if again else anywhere] * len(sources) + [whole] * len(columns) + [anywhere] * len(after),
+        out_specs=[whole] * len(outs),
+        scratch_shapes=scratch,
         compiler_params=pltpu.CompilerParams(vmem_limit_bytes=16 * MIB),
         cost_estimate=pl.CostEstimate(
             flops=6 * depth * inner * width * parts,
@@ -165,7 +171,7 @@
             transcendentals=0,
         ),
         name="product",
-    )(*sources, *pairs, *after)
+    )(*sources, *columns, *after)
 
 
 def finish_kernel(*refs):
@@ -236,26 +242,36 @@
         spare = int(group > 1)
         chunks = [group + spare] + [group] * (rows // cols // group - 2) + [group - spare]
         taken, given = plan(order, rows, cols, size, chunks)
-        own = pick(inductance, given[..., : chunks[0]], size, chunks[:1], 52)
-        own += pick(inductance, given[..., chunks[0] :], size, chunks[1:], 48, *own)
-        received = [lax.ppermute(each, "col", swap) for each in own]
-        sources = [rows for pair in zip(own, received) for rows in pair]
-        firsts = np.cumsum([0] + [each.shape[0] for each in sources])
-        pairs, calls, made = {}, {}, []
+        sources, pairs, calls, stacks, made = [], {}, {}, {}, []
+
+        def fetch(first, last, room, *after):
+            wanted = slice(sum(chunks[:first]), sum(chunks[:last]))
+            for own in pick(inductance, given[..., wanted], size, chunks[first:last], room, *after):
+                sources.extend([own, lax.ppermute(own, "col", swap)])
 
         def term(index, part):
             call, at = divmod(index, group)
             if (call, part) not in calls:
                 parts = [part] if call < 3 else [0, 1]
-                for each in parts:
-                    if each not in pairs:
-                        pairs[each] = split(current_rates, each, *made)
                 starts = taken[..., call * group : (call + 1) * group]
+                firsts = np.cumsum([0] + [each.shape[0] for each in sources])
                 have = sources[: int(np.searchsorted(firsts, starts.max(), "right"))]
-                got = product(have, starts, size, [half for each in parts for half in pairs[each]], *made[-1:])
+                if call in stacks:
+                    have, starts = [stacks[call]], None
+                keep = call < 3 and call not in stacks
+                split = 0 if part in pairs else 1 + part
+                columns = [current_rates] if split else [half for each in parts for half in pairs[each]]
+                got = product(have, starts, size, columns, split, keep, *made[-1:])
+                if split:
+                    pairs[part] = got[1:3]
+                if keep:
+                    stacks[call] = got[-1]
                 calls.update({(call, each): value for each, value in zip(parts, got)})
                 made.append(got[0])
             return calls[call, part][at * size : (at + 1) * size]
+
+        fetch(0, 1, 52)
+        fetch(1, len(chunks), 48, sources[0])
 
         sums = [[None, None], [None, None]]
         for step in range(half):

time: 53.2 us -> 51.9 us (0.976)
  Pallas kernels: 22.8 us -> 21.2 us
    pallas_call x13 -> x11, Pallas kernels: 18.2 us -> 16.6 us  [product(): pl.pallas_call(functools.partial(product_kernel, starts, size, bounds, pa...]
  transfers between devices with their start and end apart: 18 -> 18, of which waited for: 8 -> 7; matrix products, arithmetic and copies ran while one was open for 1% -> 1% of each run, Pallas kernels for 39% -> 37%
where the time goes in v9:
time: 51.9 us; the launch traced here: 51.8 us
  Pallas kernels  21.2 us (41%)
  starting transfers between devices  17 us (33%)
  waiting for transfers between devices  12.9 us (25%)
    pallas_call x11, Pallas kernels, product(): pl.pallas_call(functools.partial(product_kernel, starts, size, bounds, pa...  16.6 us
    ppermute x14, starting transfers between devices, shards(): sums[way][part] = lax.ppermute(value, ('row', 'col'), ways[way])  15.9 us
    ppermute x14, waiting for transfers between devices, shards(): sums[way][part] = lax.ppermute(value, ('row', 'col'), ways[way])  12.9 us
    pallas_call x2, Pallas kernels, pick(): pl.pallas_call(functools.partial(pick_kernel, starts, size, chunks), out_...  3.77 us
    ppermute x4, starting transfers between devices, fetch(): sources.extend([own, lax.ppermute(own, 'col', swap)])  1.16 us
  transfers between devices with their start and end apart: 18, of which 7 were waited for; matrix products, arithmetic and copies ran while one was open for 1% of the time, Pallas kernels for 37%

profile of v9, /device:TPU:0, one launch (start us, length us, event | category | flops | bytes accessed | tf_op | source)
XLA Modules:
  0.0 51.8 jit_solution(3809018231696537303)
XLA Ops:
  0.0 0.0 copy-start
  0.0 1.4 %pick.2.refs_0_ = f32[128,2048]{1,0:T(8,128)S(1)} custom-call(f32[512,2048]{1,0:T(8,128)} %a_ref.3), custom_call_target="tpu_custom_call" | custom-call | bytes 2097152 | tf_op jit(solution)/shard_map/pick/pallas_call | solution.py:69
  1.4 0.5 %collective-permute-start = (f32[128,2048]{1,0:T(8,128)S(1)}, f32[128,2048]{1,0:T(8,128)S(1)}, u32[]{:S(2)}, u32[]{:S(2)}) collective-permute-start(f32[128,2048]{1,0:T(8,128)S(1)} %pick.2.refs_0_), channel_id=1, source_target_pairs={{0,1},{1,0},{2,3},{3,2},{4,5},{5,4},{6,7},{7,6},{8,9},{9,8},{10,11... | collective-permute-start | bytes 3145736 | tf_op jit(solution)/shard_map/ppermute | solution.py:250
  2.0 2.3 %pick.3 = (f32[128,2048]{1,0:T(8,128)S(1)}, f32[128,2048]{1,0:T(8,128)S(1)}, f32[128,2048]{1,0:T(8,128)S(1)}) custom-call(f32[512,2048]{1,0:T(8,128)} %a_ref.3, f32[128,2048]{1,0:T(8,128)S(1)} %pick.2.refs_0_), custom_call_target="tpu_custom_call" | custom-call | bytes 6291456 | tf_op jit(solution)/shard_map/pick/pallas_call | solution.py:69
  4.3 0.1 collective-permute-start.2
  4.4 0.5 collective-permute-start.3
  4.9 0.1 collective-permute-start.5
  5.0 0.0 collective-permute-done.refs_1_
  5.0 0.0 copy-done
  5.0 1.5 %product.11 = (f32[128,512]{1,0:T(8,128)S(1)}, bf16[2048,512]{1,0:T(8,128)(2,1)S(1)}, bf16[2048,512]{1,0:T(8,128)(2,1)S(1)}, bf16[256,2048]{1,0:T(8,128)(2,1)S(1)}) custom-call(f32[128,2048]{1,0:T(8,128)S(1)} %pick.2.refs_0_, f32[128,2048]{1,0:T(8,128)S(1)} %collective-permute-done.refs_1_, f32[2048,1024]{1,0:T(8,128)S(1)} %copy-done), custom_call_target="tpu_custom_call" | custom-call | flops 805306368 | bytes 5505024 | tf_op jit(solution)/shard_map/product/pallas_call | solution.py:161
  6.4 3.0 %collective-permute-start.1 = (f32[128,512]{1,0:T(8,128)S(1)}, f32[128,512]{1,0:T(8,128)S(1)}, u32[]{:S(2)}, u32[]{:S(2)}) collective-permute-start(f32[128,512]{1,0:T(8,128)S(1)} %get-tuple-element.29.refs_2_), channel_id=1, source_target_pairs={{0,2},{1,5},{4,0},{5,9},{8,4},{9,13},{12,8},{13,15},{14,12},{15,11... | collective-permute-start | bytes 786440 | tf_op jit(solution)/shard_map/ppermute | solution.py:286
  9.5 1.3 %product.12 = (f32[128,512]{1,0:T(8,128)S(1)}, bf16[2048,512]{1,0:T(8,128)(2,1)S(1)}, bf16[2048,512]{1,0:T(8,128)(2,1)S(1)}) custom-call(bf16[256,2048]{1,0:T(8,128)(2,1)S(1)} %get-tuple-element.32.refs_0_, f32[2048,1024]{1,0:T(8,128)S(1)} %copy-done, f32[128,512]{1,0:T(8,128)S(1)} %get-tuple-element.29.refs_2_), custom_call_target="tpu_custom_call" | custom-call | flops 805306368 | bytes 5505024 | tf_op jit(solution)/shard_map/product/pallas_call | solution.py:161
  10.8 0.2 collective-permute-start.14
  10.9 0.0 collective-permute-done.2.refs_3_
  10.9 1.1 %product.13 = (f32[128,512]{1,0:T(8,128)S(1)}, bf16[256,2048]{1,0:T(8,128)(2,1)S(1)}) custom-call(f32[128,2048]{1,0:T(8,128)S(1)} %pick.2.refs_0_, f32[128,2048]{1,0:T(8,128)S(1)} %collective-permute-done.refs_1_, f32[128,2048]{1,0:T(8,128)S(1)} %get-tuple-element.30.refs_2_, f32[128,2048]{1,0:T(8,128)S(1)} %collective-permute-done.2.refs_3_, ...), custom_call_target="tpu_custom_call" | custom-call | flops 805306368 | bytes 5505024 | tf_op jit(solution)/shard_map/product/pallas_call | solution.py:161
  12.0 2.0 %collective-permute-start.11 = (f32[128,512]{1,0:T(8,128)S(1)}, f32[128,512]{1,0:T(8,128)S(1)}, u32[]{:S(2)}, u32[]{:S(2)}) collective-permute-start(f32[128,512]{1,0:T(8,128)S(1)} %get-tuple-element.39.refs_8_), channel_id=1, source_target_pairs={{0,2},{1,5},{4,0},{5,9},{8,4},{9,13},{12,8},{13,15},{14,12},{15,11... | collective-permute-start | bytes 786440 | tf_op jit(solution)/shard_map/ppermute | solution.py:286
  14.0 0.0 collective-permute-done.3.refs_5_
  14.0 1.1 %product.14 = (f32[128,512]{1,0:T(8,128)S(1)}, bf16[256,2048]{1,0:T(8,128)(2,1)S(1)}) custom-call(f32[128,2048]{1,0:T(8,128)S(1)} %pick.2.refs_0_, f32[128,2048]{1,0:T(8,128)S(1)} %collective-permute-done.refs_1_, f32[128,2048]{1,0:T(8,128)S(1)} %get-tuple-element.30.refs_2_, f32[128,2048]{1,0:T(8,128)S(1)} %collective-permute-done.2.refs_3_, ...), custom_call_target="tpu_custom_call" | custom-call | flops 805306368 | bytes 5505024 | tf_op jit(solution)/shard_map/product/pallas_call | solution.py:161
  15.0 0.2 collective-permute-start.8
  15.3 1.0 %product.15.refs_3_ = f32[128,512]{1,0:T(8,128)S(1)} custom-call(bf16[256,2048]{1,0:T(8,128)(2,1)S(1)} %get-tuple-element.36.refs_0_, bf16[2048,512]{1,0:T(8,128)(2,1)S(1)} %get-tuple-element.37.refs_6_.refs_1_.refs_8_, bf16[2048,512]{1,0:T(8,128)(2,1)S(1)} %get-tuple-element.38.refs_7_.refs_2_.refs_9_, f32[128,512]{1,0:T(8,128)S(1)} %get-tuple-element.40.refs_3_), custom_call_target="tpu_custom_call" | custom-call | flops 805306368 | bytes 5505024 | tf_op jit(solution)/shard_map/product/pallas_call | solution.py:161
  16.2 1.0 %product.16.refs_12_ = f32[128,512]{1,0:T(8,128)S(1)} custom-call(bf16[256,2048]{1,0:T(8,128)(2,1)S(1)} %get-tuple-element.42.refs_0_, bf16[2048,512]{1,0:T(8,128)(2,1)S(1)} %get-tuple-element.33.refs_5_.refs_1_.refs_10_, bf16[2048,512]{1,0:T(8,128)(2,1)S(1)} %get-tuple-element.34.refs_6_.refs_2_.refs_11_, f32[128,512]{1,0:T(8,128)S(1)} %product.15.refs_3_), custom_call_target="tpu_custom_call" | custom-call | flops 805306368 | bytes 5505024 | tf_op jit(solution)/shard_map/product/pallas_call | solution.py:161
  17.2 0.0 collective-permute-done.1
  17.3 1.9 %collective-permute-start.4 = (f32[128,512]{1,0:T(8,128)S(1)}, f32[128,512]{1,0:T(8,128)S(1)}, u32[]{:S(2)}, u32[]{:S(2)}) collective-permute-start(f32[128,512]{1,0:T(8,128)S(1)} %add.30), channel_id=1, source_target_pairs={{0,2},{1,5},{4,0},{5,9},{8,4},{9,13},{12,8},{13,15},{14,12},{15,11... | collective-permute-start | bytes 786440 | tf_op jit(solution)/shard_map/ppermute | solution.py:286
  19.2 0.7 %collective-permute-done.14 = f32[128,512]{1,0:T(8,128)S(1)} collective-permute-done((f32[128,512]{1,0:T(8,128)S(1)}, f32[128,512]{1,0:T(8,128)S(1)}, u32[]{:S(2)}, u32[]{:S(2)}) %collective-permute-start.14) | collective-permute-done | bytes 262176 | tf_op jit(solution)/shard_map/ppermute | solution.py:286
  19.9 0.1 collective-permute-start.15
  20.0 0.0 collective-permute-done.5.refs_7_
  20.0 1.9 %product.17 = (f32[128,512]{1,0:T(8,128)S(1)}, f32[128,512]{1,0:T(8,128)S(1)}) custom-call(f32[128,2048]{1,0:T(8,128)S(1)} %pick.2.refs_0_, f32[128,2048]{1,0:T(8,128)S(1)} %collective-permute-done.refs_1_, f32[128,2048]{1,0:T(8,128)S(1)} %get-tuple-element.30.refs_2_, f32[128,2048]{1,0:T(8,128)S(1)} %collective-permute-done.2.refs_3_, ...), custom_call_target="tpu_custom_call" | custom-call | flops 1610612736 | bytes 9961472 | tf_op jit(solution)/shard_map/product/pallas_call | solution.py:161
  21.9 1.9 %product.18 = (f32[128,512]{1,0:T(8,128)S(1)}, f32[128,512]{1,0:T(8,128)S(1)}) custom-call(f32[128,2048]{1,0:T(8,128)S(1)} %pick.2.refs_0_, f32[128,2048]{1,0:T(8,128)S(1)} %collective-permute-done.refs_1_, f32[128,2048]{1,0:T(8,128)S(1)} %get-tuple-element.30.refs_2_, f32[128,2048]{1,0:T(8,128)S(1)} %collective-permute-done.2.refs_3_, ...), custom_call_target="tpu_custom_call" | custom-call | flops 1610612736 | bytes 9961472 | tf_op jit(solution)/shard_map/product/pallas_call | solution.py:161
  23.9 1.6 %collective-permute-done.8 = f32[128,512]{1,0:T(8,128)S(1)} collective-permute-done((f32[128,512]{1,0:T(8,128)S(1)}, f32[128,512]{1,0:T(8,128)S(1)}, u32[]{:S(2)}, u32[]{:S(2)}) %collective-permute-start.8) | collective-permute-done | bytes 262176 | tf_op jit(solution)/shard_map/ppermute | solution.py:286
  25.5 0.1 collective-permute-start.9
  25.6 0.0 collective-permute-done.11
  25.7 2.1 %collective-permute-start.12 = (f32[128,512]{1,0:T(8,128)S(1)}, f32[128,512]{1,0:T(8,128)S(1)}, u32[]{:S(2)}, u32[]{:S(2)}) collective-permute-start(f32[128,512]{1,0:T(8,128)S(1)} %add.35), channel_id=1, source_target_pairs={{0,2},{1,5},{4,0},{5,9},{8,4},{9,13},{12,8},{13,15},{14,12},{15,11... | collective-permute-start | bytes 786440 | tf_op jit(solution)/shard_map/ppermute | solution.py:286
  27.7 0.0 collective-permute-done.4
  27.8 1.8 %collective-permute-start.6 = (f32[128,512]{1,0:T(8,128)S(1)}, f32[128,512]{1,0:T(8,128)S(1)}, u32[]{:S(2)}, u32[]{:S(2)}) collective-permute-start(f32[128,512]{1,0:T(8,128)S(1)} %add.31), channel_id=1, source_target_pairs={{0,2},{1,5},{4,0},{5,9},{8,4},{9,13},{12,8},{13,15},{14,12},{15,11... | collective-permute-start | bytes 786440 | tf_op jit(solution)/shard_map/ppermute | solution.py:286
  29.5 0.0 collective-permute-done.15
  29.6 0.4 collective-permute-start.16
  29.9 1.9 %product.19 = (f32[128,512]{1,0:T(8,128)S(1)}, f32[128,512]{1,0:T(8,128)S(1)}) custom-call(f32[128,2048]{1,0:T(8,128)S(1)} %pick.2.refs_0_, f32[128,2048]{1,0:T(8,128)S(1)} %collective-permute-done.refs_1_, f32[128,2048]{1,0:T(8,128)S(1)} %get-tuple-element.30.refs_2_, f32[128,2048]{1,0:T(8,128)S(1)} %collective-permute-done.2.refs_3_, ...), custom_call_target="tpu_custom_call" | custom-call | flops 1610612736 | bytes 9961472 | tf_op jit(solution)/shard_map/product/pallas_call | solution.py:161
  31.8 2.1 %product.20 = (f32[128,512]{1,0:T(8,128)S(1)}, f32[128,512]{1,0:T(8,128)S(1)}) custom-call(f32[128,2048]{1,0:T(8,128)S(1)} %pick.2.refs_0_, f32[128,2048]{1,0:T(8,128)S(1)} %collective-permute-done.refs_1_, f32[128,2048]{1,0:T(8,128)S(1)} %get-tuple-element.30.refs_2_, f32[128,2048]{1,0:T(8,128)S(1)} %collective-permute-done.2.refs_3_, ...), custom_call_target="tpu_custom_call" | custom-call | flops 1610612736 | bytes 9961472 | tf_op jit(solution)/shard_map/product/pallas_call | solution.py:161
  34.0 1.1 %collective-permute-done.9 = f32[128,512]{1,0:T(8,128)S(1)} collective-permute-done((f32[128,512]{1,0:T(8,128)S(1)}, f32[128,512]{1,0:T(8,128)S(1)}, u32[]{:S(2)}, u32[]{:S(2)}) %collective-permute-start.9) | collective-permute-done | bytes 262176 | tf_op jit(solution)/shard_map/ppermute | solution.py:286
  35.1 0.4 collective-permute-start.10
  35.5 0.0 collective-permute-done.12
  35.5 1.7 %collective-permute-start.13 = (f32[128,512]{1,0:T(8,128)S(1)}, f32[128,512]{1,0:T(8,128)S(1)}, u32[]{:S(2)}, u32[]{:S(2)}) collective-permute-start(f32[128,512]{1,0:T(8,128)S(1)} %add.36), channel_id=1, source_target_pairs={{0,2},{1,5},{4,0},{5,9},{8,4},{9,13},{12,8},{13,15},{14,12},{15,11... | collective-permute-start | bytes 786440 | tf_op jit(solution)/shard_map/ppermute | solution.py:286
  37.2 3.3 %collective-permute-done.6 = f32[128,512]{1,0:T(8,128)S(1)} collective-permute-done((f32[128,512]{1,0:T(8,128)S(1)}, f32[128,512]{1,0:T(8,128)S(1)}, u32[]{:S(2)}, u32[]{:S(2)}) %collective-permute-start.6) | collective-permute-done | bytes 262176 | tf_op jit(solution)/shard_map/ppermute | solution.py:286
  40.6 2.1 %collective-permute-start.7 = (f32[128,512]{1,0:T(8,128)S(1)}, f32[128,512]{1,0:T(8,128)S(1)}, u32[]{:S(2)}, u32[]{:S(2)}) collective-permute-start(f32[128,512]{1,0:T(8,128)S(1)} %add.32), channel_id=1, source_target_pairs={{0,2},{1,5},{4,0},{5,9},{8,4},{9,13},{12,8},{13,15},{14,12},{15,11... | collective-permute-start | bytes 786440 | tf_op jit(solution)/shard_map/ppermute | solution.py:286
  42.7 0.0 collective-permute-done.16
  42.7 0.1 collective-permute-start.17
  42.8 1.9 %product.21 = (f32[128,512]{1,0:T(8,128)S(1)}, f32[128,512]{1,0:T(8,128)S(1)}) custom-call(f32[128,2048]{1,0:T(8,128)S(1)} %pick.2.refs_0_, f32[128,2048]{1,0:T(8,128)S(1)} %collective-permute-done.refs_1_, f32[128,2048]{1,0:T(8,128)S(1)} %get-tuple-element.30.refs_2_, f32[128,2048]{1,0:T(8,128)S(1)} %collective-permute-done.2.refs_3_, ...), custom_call_target="tpu_custom_call" | custom-call | flops 1610612736 | bytes 9961472 | tf_op jit(solution)/shard_map/product/pallas_call | solution.py:161
  44.7 1.5 %collective-permute-done.10.refs_1_ = f32[128,512]{1,0:T(8,128)S(1)} collective-permute-done((f32[128,512]{1,0:T(8,128)S(1)}, f32[128,512]{1,0:T(8,128)S(1)}, u32[]{:S(2)}, u32[]{:S(2)}) %collective-permute-start.10) | collective-permute-done | bytes 262176 | tf_op jit(solution)/shard_map/ppermute | solution.py:286
  46.3 0.0 collective-permute-done.13.refs_3_
  46.3 4.2 %collective-permute-done.7.refs_0_ = f32[128,512]{1,0:T(8,128)S(1)} collective-permute-done((f32[128,512]{1,0:T(8,128)S(1)}, f32[128,512]{1,0:T(8,128)S(1)}, u32[]{:S(2)}, u32[]{:S(2)}) %collective-permute-start.7) | collective-permute-done | bytes 262176 | tf_op jit(solution)/shard_map/ppermute | solution.py:286
  50.4 0.4 collective-permute-done.17.refs_4_
  50.9 0.9 %finish.1 = f32[128,1024]{1,0:T(8,128)} custom-call(f32[128,512]{1,0:T(8,128)S(1)} %collective-permute-done.7.refs_0_, f32[128,512]{1,0:T(8,128)S(1)} %collective-permute-done.10.refs_1_, f32[128,512]{1,0:T(8,128)S(1)} %get-tuple-element.47.refs_2_, f32[128,512]{1,0:T(8,128)S(1)} %collective-permute-done.13.refs_3_, ...), custom_call_target="tpu_custom_call" | custom-call | tf_op jit(solution)/shard_map/finish/pallas_call | solution.py:188
  (10 shorter events, 0.4 us)
Async XLA Ops:
  0.0 5.0 %copy-start = (f32[2048,1024]{1,0:T(8,128)S(1)}, f32[2048,1024]{1,0:T(8,128)}, u32[]{:S(2)}) copy-start(f32[2048,1024]{1,0:T(8,128)} %refs_1_.1) | copy-start | bytes 25165828
  1.4 3.5 %collective-permute-start = (f32[128,2048]{1,0:T(8,128)S(1)}, f32[128,2048]{1,0:T(8,128)S(1)}, u32[]{:S(2)}, u32[]{:S(2)}) collective-permute-start(f32[128,2048]{1,0:T(8,128)S(1)} %pick.2.refs_0_), channel_id=1, source_target_pairs={{0,1},{1,0},{2,3},{3,2},{4,5},{5,4},{6,7},{7,6},{8,9},{9,8},{10,11... | collective-permute-start | bytes 3145736 | tf_op jit(solution)/shard_map/ppermute | solution.py:250
  4.3 6.6 %collective-permute-start.2 = (f32[128,2048]{1,0:T(8,128)S(1)}, f32[128,2048]{1,0:T(8,128)S(1)}, u32[]{:S(2)}, u32[]{:S(2)}) collective-permute-start(f32[128,2048]{1,0:T(8,128)S(1)} %get-tuple-element.30.refs_2_), channel_id=1, source_target_pairs={{0,1},{1,0},{2,3},{3,2},{4,5},{5,4},{6,7},{7,6},{8,9},{9,8},{10,11... | collective-permute-start | bytes 3145736 | tf_op jit(solution)/shard_map/ppermute | solution.py:250
  4.4 9.6 %collective-permute-start.3 = (f32[128,2048]{1,0:T(8,128)S(1)}, f32[128,2048]{1,0:T(8,128)S(1)}, u32[]{:S(2)}, u32[]{:S(2)}) collective-permute-start(f32[128,2048]{1,0:T(8,128)S(1)} %get-tuple-element.31.refs_4_), channel_id=1, source_target_pairs={{0,1},{1,0},{2,3},{3,2},{4,5},{5,4},{6,7},{7,6},{8,9},{9,8},{10,11... | collective-permute-start | bytes 3145736 | tf_op jit(solution)/shard_map/ppermute | solution.py:250
  4.9 15.1 %collective-permute-start.5 = (f32[128,2048]{1,0:T(8,128)S(1)}, f32[128,2048]{1,0:T(8,128)S(1)}, u32[]{:S(2)}, u32[]{:S(2)}) collective-permute-start(f32[128,2048]{1,0:T(8,128)S(1)} %get-tuple-element.41.refs_6_), channel_id=1, source_target_pairs={{0,1},{1,0},{2,3},{3,2},{4,5},{5,4},{6,7},{7,6},{8,9},{9,8},{10,11... | collective-permute-start | bytes 3145736 | tf_op jit(solution)/shard_map/ppermute | solution.py:250
  6.4 10.8 %collective-permute-start.1 = (f32[128,512]{1,0:T(8,128)S(1)}, f32[128,512]{1,0:T(8,128)S(1)}, u32[]{:S(2)}, u32[]{:S(2)}) collective-permute-start(f32[128,512]{1,0:T(8,128)S(1)} %get-tuple-element.29.refs_2_), channel_id=1, source_target_pairs={{0,2},{1,5},{4,0},{5,9},{8,4},{9,13},{12,8},{13,15},{14,12},{15,11... | collective-permute-start | bytes 786440 | tf_op jit(solution)/shard_map/ppermute | solution.py:286
  10.8 9.1 %collective-permute-start.14 = (f32[128,512]{1,0:T(8,128)S(1)}, f32[128,512]{1,0:T(8,128)S(1)}, u32[]{:S(2)}, u32[]{:S(2)}) collective-permute-start(f32[128,512]{1,0:T(8,128)S(1)} %get-tuple-element.35.refs_7_), channel_id=1, source_target_pairs={{0,4},{1,3},{4,8},{5,1},{8,12},{9,5},{12,14},{13,9},{14,10},{15,13... | collective-permute-start | bytes 786440 | tf_op jit(solution)/shard_map/ppermute | solution.py:286
  12.0 13.6 %collective-permute-start.11 = (f32[128,512]{1,0:T(8,128)S(1)}, f32[128,512]{1,0:T(8,128)S(1)}, u32[]{:S(2)}, u32[]{:S(2)}) collective-permute-start(f32[128,512]{1,0:T(8,128)S(1)} %get-tuple-element.39.refs_8_), channel_id=1, source_target_pairs={{0,2},{1,5},{4,0},{5,9},{8,4},{9,13},{12,8},{13,15},{14,12},{15,11... | collective-permute-start | bytes 786440 | tf_op jit(solution)/shard_map/ppermute | solution.py:286
  15.0 10.5 %collective-permute-start.8 = (f32[128,512]{1,0:T(8,128)S(1)}, f32[128,512]{1,0:T(8,128)S(1)}, u32[]{:S(2)}, u32[]{:S(2)}) collective-permute-start(f32[128,512]{1,0:T(8,128)S(1)} %get-tuple-element.40.refs_3_), channel_id=1, source_target_pairs={{0,4},{1,3},{4,8},{5,1},{8,12},{9,5},{12,14},{13,9},{14,10},{15,13... | collective-permute-start | bytes 786440 | tf_op jit(solution)/shard_map/ppermute | solution.py:286
  17.3 10.4 %collective-permute-start.4 = (f32[128,512]{1,0:T(8,128)S(1)}, f32[128,512]{1,0:T(8,128)S(1)}, u32[]{:S(2)}, u32[]{:S(2)}) collective-permute-start(f32[128,512]{1,0:T(8,128)S(1)} %add.30), channel_id=1, source_target_pairs={{0,2},{1,5},{4,0},{5,9},{8,4},{9,13},{12,8},{13,15},{14,12},{15,11... | collective-permute-start | bytes 786440 | tf_op jit(solution)/shard_map/ppermute | solution.py:286
  19.9 9.6 %collective-permute-start.15 = (f32[128,512]{1,0:T(8,128)S(1)}, f32[128,512]{1,0:T(8,128)S(1)}, u32[]{:S(2)}, u32[]{:S(2)}) collective-permute-start(f32[128,512]{1,0:T(8,128)S(1)} %add.37), channel_id=1, source_target_pairs={{0,4},{1,3},{4,8},{5,1},{8,12},{9,5},{12,14},{13,9},{14,10},{15,13... | collective-permute-start | bytes 786440 | tf_op jit(solution)/shard_map/ppermute | solution.py:286
  25.5 9.5 %collective-permute-start.9 = (f32[128,512]{1,0:T(8,128)S(1)}, f32[128,512]{1,0:T(8,128)S(1)}, u32[]{:S(2)}, u32[]{:S(2)}) collective-permute-start(f32[128,512]{1,0:T(8,128)S(1)} %add.33), channel_id=1, source_target_pairs={{0,4},{1,3},{4,8},{5,1},{8,12},{9,5},{12,14},{13,9},{14,10},{15,13... | collective-permute-start | bytes 786440 | tf_op jit(solution)/shard_map/ppermute | solution.py:286
  25.7 9.8 %collective-permute-start.12 = (f32[128,512]{1,0:T(8,128)S(1)}, f32[128,512]{1,0:T(8,128)S(1)}, u32[]{:S(2)}, u32[]{:S(2)}) collective-permute-start(f32[128,512]{1,0:T(8,128)S(1)} %add.35), channel_id=1, source_target_pairs={{0,2},{1,5},{4,0},{5,9},{8,4},{9,13},{12,8},{13,15},{14,12},{15,11... | collective-permute-start | bytes 786440 | tf_op jit(solution)/shard_map/ppermute | solution.py:286
  27.8 12.8 %collective-permute-start.6 = (f32[128,512]{1,0:T(8,128)S(1)}, f32[128,512]{1,0:T(8,128)S(1)}, u32[]{:S(2)}, u32[]{:S(2)}) collective-permute-start(f32[128,512]{1,0:T(8,128)S(1)} %add.31), channel_id=1, source_target_pairs={{0,2},{1,5},{4,0},{5,9},{8,4},{9,13},{12,8},{13,15},{14,12},{15,11... | collective-permute-start | bytes 786440 | tf_op jit(solution)/shard_map/ppermute | solution.py:286
  29.6 13.1 %collective-permute-start.16 = (f32[128,512]{1,0:T(8,128)S(1)}, f32[128,512]{1,0:T(8,128)S(1)}, u32[]{:S(2)}, u32[]{:S(2)}) collective-permute-start(f32[128,512]{1,0:T(8,128)S(1)} %add.38), channel_id=1, source_target_pairs={{0,4},{1,3},{4,8},{5,1},{8,12},{9,5},{12,14},{13,9},{14,10},{15,13... | collective-permute-start | bytes 786440 | tf_op jit(solution)/shard_map/ppermute | solution.py:286
  35.1 11.2 %collective-permute-start.10 = (f32[128,512]{1,0:T(8,128)S(1)}, f32[128,512]{1,0:T(8,128)S(1)}, u32[]{:S(2)}, u32[]{:S(2)}) collective-permute-start(f32[128,512]{1,0:T(8,128)S(1)} %add.34), channel_id=1, source_target_pairs={{0,4},{1,3},{4,8},{5,1},{8,12},{9,5},{12,14},{13,9},{14,10},{15,13... | collective-permute-start | bytes 786440 | tf_op jit(solution)/shard_map/ppermute | solution.py:286
  35.5 10.8 %collective-permute-start.13 = (f32[128,512]{1,0:T(8,128)S(1)}, f32[128,512]{1,0:T(8,128)S(1)}, u32[]{:S(2)}, u32[]{:S(2)}) collective-permute-start(f32[128,512]{1,0:T(8,128)S(1)} %add.36), channel_id=1, source_target_pairs={{0,2},{1,5},{4,0},{5,9},{8,4},{9,13},{12,8},{13,15},{14,12},{15,11... | collective-permute-start | bytes 786440 | tf_op jit(solution)/shard_map/ppermute | solution.py:286
  40.6 9.8 %collective-permute-start.7 = (f32[128,512]{1,0:T(8,128)S(1)}, f32[128,512]{1,0:T(8,128)S(1)}, u32[]{:S(2)}, u32[]{:S(2)}) collective-permute-start(f32[128,512]{1,0:T(8,128)S(1)} %add.32), channel_id=1, source_target_pairs={{0,2},{1,5},{4,0},{5,9},{8,4},{9,13},{12,8},{13,15},{14,12},{15,11... | collective-permute-start | bytes 786440 | tf_op jit(solution)/shard_map/ppermute | solution.py:286
  42.7 8.2 %collective-permute-start.17 = (f32[128,512]{1,0:T(8,128)S(1)}, f32[128,512]{1,0:T(8,128)S(1)}, u32[]{:S(2)}, u32[]{:S(2)}) collective-permute-start(f32[128,512]{1,0:T(8,128)S(1)} %add.39), channel_id=1, source_target_pairs={{0,4},{1,3},{4,8},{5,1},{8,12},{9,5},{12,14},{13,9},{14,10},{15,13... | collective-permute-start | bytes 786440 | tf_op jit(solution)/shard_map/ppermute | solution.py:286

commit v10 on v9

--- a/solution.py
+++ b/solution.py
@@ -117,6 +117,21 @@
     stack[:depth], stack[depth:] = halves(raw[...])
 
 
+def split_rows(starts, size, bounds, sources, stack):
+    depth = stack.shape[0] // 2
+    for index in range(starts.shape[-1]):
+        start = looked_up(starts[..., index])
+        at, first = index * size, 0
+        for source, last in zip(sources, bounds):
+
+            @pl.when((start >= first) & (start < last))
+            def _(source=source, first=first, start=start, at=at):
+                rows = source[...] if source.shape[0] == size else source[pl.ds(pl.multiple_of(start - first, size), size)]
+                stack[at : at + size], stack[depth + at : depth + at + size] = halves(rows)
+
+            first = last
+
+
 def product_kernel(starts, size, bounds, parts, split, *refs):
     count = len(bounds)
     sources, refs = refs[:count], refs[count:]
@@ -125,7 +140,10 @@
         (stack,) = sources
     else:
         *refs, stack, raw, sems = refs
-        fetch_rows(starts, size, bounds, sources, stack, raw, sems)
+        if split:
+            split_rows(starts, size, bounds, sources, stack)
+        else:
+            fetch_rows(starts, size, bounds, sources, stack, raw, sems)
     outs = refs[-parts - (2 if split else 0) :]
     for part in range(parts):
         width = outs[part].shape[1]
@@ -161,7 +179,7 @@
     return pl.pallas_call(
         functools.partial(product_kernel, starts, size, bounds, parts, split),
         out_shape=outs,
-        in_specs=[whole if again else anywhere] * len(sources) + [whole] * len(columns) + [anywhere] * len(after),
+        in_specs=[whole if again or split else anywhere] * len(sources) + [whole] * len(columns) + [anywhere] * len(after),
         out_specs=[whole] * len(outs),
         scratch_shapes=scratch,
         compiler_params=pltpu.CompilerParams(vmem_limit_bytes=16 * MIB),

time: 51.9 us -> 51.9 us (level)
  no operation moved by 1% of the time
where the time goes in v10:
time: 51.9 us; the launch traced here: 51.7 us
  Pallas kernels  21.2 us (41%)
  starting transfers between devices  17.1 us (33%)
  waiting for transfers between devices  12.9 us (25%)
    pallas_call x11, Pallas kernels, product(): pl.pallas_call(functools.partial(product_kernel, starts, size, bounds, pa...  16.5 us
    ppermute x14, starting transfers between devices, shards(): sums[way][part] = lax.ppermute(value, ('row', 'col'), ways[way])  15.9 us
    ppermute x14, waiting for transfers between devices, shards(): sums[way][part] = lax.ppermute(value, ('row', 'col'), ways[way])  12.9 us
    pallas_call x2, Pallas kernels, pick(): pl.pallas_call(functools.partial(pick_kernel, starts, size, chunks), out_...  3.77 us
    ppermute x4, starting transfers between devices, fetch(): sources.extend([own, lax.ppermute(own, 'col', swap)])  1.16 us
  transfers between devices with their start and end apart: 18, of which 7 were waited for; matrix products, arithmetic and copies ran while one was open for 1% of the time, Pallas kernels for 37%

profile of v10, /device:TPU:0, one launch (start us, length us, event | category | flops | bytes accessed | tf_op | source)
XLA Modules:
  0.0 51.7 jit_solution(9708620334596203197)
XLA Ops:
  0.0 0.0 copy-start
  0.0 1.4 %pick.2.refs_0_ = f32[128,2048]{1,0:T(8,128)S(1)} custom-call(f32[512,2048]{1,0:T(8,128)} %a_ref.3), custom_call_target="tpu_custom_call" | custom-call | bytes 2097152 | tf_op jit(solution)/shard_map/pick/pallas_call | solution.py:69
  1.4 0.5 %collective-permute-start = (f32[128,2048]{1,0:T(8,128)S(1)}, f32[128,2048]{1,0:T(8,128)S(1)}, u32[]{:S(2)}, u32[]{:S(2)}) collective-permute-start(f32[128,2048]{1,0:T(8,128)S(1)} %pick.2.refs_0_), channel_id=1, source_target_pairs={{0,1},{1,0},{2,3},{3,2},{4,5},{5,4},{6,7},{7,6},{8,9},{9,8},{10,11... | collective-permute-start | bytes 3145736 | tf_op jit(solution)/shard_map/ppermute | solution.py:268
  2.0 2.3 %pick.3 = (f32[128,2048]{1,0:T(8,128)S(1)}, f32[128,2048]{1,0:T(8,128)S(1)}, f32[128,2048]{1,0:T(8,128)S(1)}) custom-call(f32[512,2048]{1,0:T(8,128)} %a_ref.3, f32[128,2048]{1,0:T(8,128)S(1)} %pick.2.refs_0_), custom_call_target="tpu_custom_call" | custom-call | bytes 6291456 | tf_op jit(solution)/shard_map/pick/pallas_call | solution.py:69
  4.3 0.1 collective-permute-start.2
  4.4 0.5 collective-permute-start.3
  4.9 0.1 collective-permute-start.5
  5.0 0.0 collective-permute-done.refs_1_
  5.0 0.0 copy-done
  5.0 1.4 %product.11 = (f32[128,512]{1,0:T(8,128)S(1)}, bf16[2048,512]{1,0:T(8,128)(2,1)S(1)}, bf16[2048,512]{1,0:T(8,128)(2,1)S(1)}, bf16[256,2048]{1,0:T(8,128)(2,1)S(1)}) custom-call(f32[128,2048]{1,0:T(8,128)S(1)} %pick.2.refs_0_, f32[128,2048]{1,0:T(8,128)S(1)} %collective-permute-done.refs_1_, f32[2048,1024]{1,0:T(8,128)S(1)} %copy-done), custom_call_target="tpu_custom_call" | custom-call | flops 805306368 | bytes 5505024 | tf_op jit(solution)/shard_map/product/pallas_call | solution.py:179
  6.4 3.1 %collective-permute-start.1 = (f32[128,512]{1,0:T(8,128)S(1)}, f32[128,512]{1,0:T(8,128)S(1)}, u32[]{:S(2)}, u32[]{:S(2)}) collective-permute-start(f32[128,512]{1,0:T(8,128)S(1)} %get-tuple-element.29.refs_2_), channel_id=1, source_target_pairs={{0,2},{1,5},{4,0},{5,9},{8,4},{9,13},{12,8},{13,15},{14,12},{15,11... | collective-permute-start | bytes 786440 | tf_op jit(solution)/shard_map/ppermute | solution.py:304
  9.5 1.3 %product.12 = (f32[128,512]{1,0:T(8,128)S(1)}, bf16[2048,512]{1,0:T(8,128)(2,1)S(1)}, bf16[2048,512]{1,0:T(8,128)(2,1)S(1)}) custom-call(bf16[256,2048]{1,0:T(8,128)(2,1)S(1)} %get-tuple-element.32.refs_0_, f32[2048,1024]{1,0:T(8,128)S(1)} %copy-done, f32[128,512]{1,0:T(8,128)S(1)} %get-tuple-element.29.refs_2_), custom_call_target="tpu_custom_call" | custom-call | flops 805306368 | bytes 5505024 | tf_op jit(solution)/shard_map/product/pallas_call | solution.py:179
  10.7 0.2 collective-permute-start.14
  10.9 0.0 collective-permute-done.2.refs_3_
  10.9 1.1 %product.13 = (f32[128,512]{1,0:T(8,128)S(1)}, bf16[256,2048]{1,0:T(8,128)(2,1)S(1)}) custom-call(f32[128,2048]{1,0:T(8,128)S(1)} %pick.2.refs_0_, f32[128,2048]{1,0:T(8,128)S(1)} %collective-permute-done.refs_1_, f32[128,2048]{1,0:T(8,128)S(1)} %get-tuple-element.30.refs_2_, f32[128,2048]{1,0:T(8,128)S(1)} %collective-permute-done.2.refs_3_, ...), custom_call_target="tpu_custom_call" | custom-call | flops 805306368 | bytes 5505024 | tf_op jit(solution)/shard_map/product/pallas_call | solution.py:179
  12.0 2.0 %collective-permute-start.11 = (f32[128,512]{1,0:T(8,128)S(1)}, f32[128,512]{1,0:T(8,128)S(1)}, u32[]{:S(2)}, u32[]{:S(2)}) collective-permute-start(f32[128,512]{1,0:T(8,128)S(1)} %get-tuple-element.39.refs_8_), channel_id=1, source_target_pairs={{0,2},{1,5},{4,0},{5,9},{8,4},{9,13},{12,8},{13,15},{14,12},{15,11... | collective-permute-start | bytes 786440 | tf_op jit(solution)/shard_map/ppermute | solution.py:304
  13.9 0.0 collective-permute-done.3.refs_5_
  13.9 1.1 %product.14 = (f32[128,512]{1,0:T(8,128)S(1)}, bf16[256,2048]{1,0:T(8,128)(2,1)S(1)}) custom-call(f32[128,2048]{1,0:T(8,128)S(1)} %pick.2.refs_0_, f32[128,2048]{1,0:T(8,128)S(1)} %collective-permute-done.refs_1_, f32[128,2048]{1,0:T(8,128)S(1)} %get-tuple-element.30.refs_2_, f32[128,2048]{1,0:T(8,128)S(1)} %collective-permute-done.2.refs_3_, ...), custom_call_target="tpu_custom_call" | custom-call | flops 805306368 | bytes 5505024 | tf_op jit(solution)/shard_map/product/pallas_call | solution.py:179
  15.0 0.2 collective-permute-start.8
  15.2 1.0 %product.15.refs_3_ = f32[128,512]{1,0:T(8,128)S(1)} custom-call(bf16[256,2048]{1,0:T(8,128)(2,1)S(1)} %get-tuple-element.36.refs_0_, bf16[2048,512]{1,0:T(8,128)(2,1)S(1)} %get-tuple-element.37.refs_6_.refs_1_.refs_8_, bf16[2048,512]{1,0:T(8,128)(2,1)S(1)} %get-tuple-element.38.refs_7_.refs_2_.refs_9_, f32[128,512]{1,0:T(8,128)S(1)} %get-tuple-element.40.refs_3_), custom_call_target="tpu_custom_call" | custom-call | flops 805306368 | bytes 5505024 | tf_op jit(solution)/shard_map/product/pallas_call | solution.py:179
  16.2 1.0 %product.16.refs_12_ = f32[128,512]{1,0:T(8,128)S(1)} custom-call(bf16[256,2048]{1,0:T(8,128)(2,1)S(1)} %get-tuple-element.42.refs_0_, bf16[2048,512]{1,0:T(8,128)(2,1)S(1)} %get-tuple-element.33.refs_5_.refs_1_.refs_10_, bf16[2048,512]{1,0:T(8,128)(2,1)S(1)} %get-tuple-element.34.refs_6_.refs_2_.refs_11_, f32[128,512]{1,0:T(8,128)S(1)} %product.15.refs_3_), custom_call_target="tpu_custom_call" | custom-call | flops 805306368 | bytes 5505024 | tf_op jit(solution)/shard_map/product/pallas_call | solution.py:179
  17.2 0.0 collective-permute-done.1
  17.2 1.9 %collective-permute-start.4 = (f32[128,512]{1,0:T(8,128)S(1)}, f32[128,512]{1,0:T(8,128)S(1)}, u32[]{:S(2)}, u32[]{:S(2)}) collective-permute-start(f32[128,512]{1,0:T(8,128)S(1)} %add.30), channel_id=1, source_target_pairs={{0,2},{1,5},{4,0},{5,9},{8,4},{9,13},{12,8},{13,15},{14,12},{15,11... | collective-permute-start | bytes 786440 | tf_op jit(solution)/shard_map/ppermute | solution.py:304
  19.1 0.7 %collective-permute-done.14 = f32[128,512]{1,0:T(8,128)S(1)} collective-permute-done((f32[128,512]{1,0:T(8,128)S(1)}, f32[128,512]{1,0:T(8,128)S(1)}, u32[]{:S(2)}, u32[]{:S(2)}) %collective-permute-start.14) | collective-permute-done | bytes 262176 | tf_op jit(solution)/shard_map/ppermute | solution.py:304
  19.9 0.1 collective-permute-start.15
  20.0 0.0 collective-permute-done.5.refs_7_
  20.0 1.9 %product.17 = (f32[128,512]{1,0:T(8,128)S(1)}, f32[128,512]{1,0:T(8,128)S(1)}) custom-call(f32[128,2048]{1,0:T(8,128)S(1)} %pick.2.refs_0_, f32[128,2048]{1,0:T(8,128)S(1)} %collective-permute-done.refs_1_, f32[128,2048]{1,0:T(8,128)S(1)} %get-tuple-element.30.refs_2_, f32[128,2048]{1,0:T(8,128)S(1)} %collective-permute-done.2.refs_3_, ...), custom_call_target="tpu_custom_call" | custom-call | flops 1610612736 | bytes 9961472 | tf_op jit(solution)/shard_map/product/pallas_call | solution.py:179
  21.9 1.9 %product.18 = (f32[128,512]{1,0:T(8,128)S(1)}, f32[128,512]{1,0:T(8,128)S(1)}) custom-call(f32[128,2048]{1,0:T(8,128)S(1)} %pick.2.refs_0_, f32[128,2048]{1,0:T(8,128)S(1)} %collective-permute-done.refs_1_, f32[128,2048]{1,0:T(8,128)S(1)} %get-tuple-element.30.refs_2_, f32[128,2048]{1,0:T(8,128)S(1)} %collective-permute-done.2.refs_3_, ...), custom_call_target="tpu_custom_call" | custom-call | flops 1610612736 | bytes 9961472 | tf_op jit(solution)/shard_map/product/pallas_call | solution.py:179
  23.8 1.6 %collective-permute-done.8 = f32[128,512]{1,0:T(8,128)S(1)} collective-permute-done((f32[128,512]{1,0:T(8,128)S(1)}, f32[128,512]{1,0:T(8,128)S(1)}, u32[]{:S(2)}, u32[]{:S(2)}) %collective-permute-start.8) | collective-permute-done | bytes 262176 | tf_op jit(solution)/shard_map/ppermute | solution.py:304
  25.5 0.1 collective-permute-start.9
  25.6 0.0 collective-permute-done.11
  25.6 2.1 %collective-permute-start.12 = (f32[128,512]{1,0:T(8,128)S(1)}, f32[128,512]{1,0:T(8,128)S(1)}, u32[]{:S(2)}, u32[]{:S(2)}) collective-permute-start(f32[128,512]{1,0:T(8,128)S(1)} %add.35), channel_id=1, source_target_pairs={{0,2},{1,5},{4,0},{5,9},{8,4},{9,13},{12,8},{13,15},{14,12},{15,11... | collective-permute-start | bytes 786440 | tf_op jit(solution)/shard_map/ppermute | solution.py:304
  27.7 0.0 collective-permute-done.4
  27.7 1.8 %collective-permute-start.6 = (f32[128,512]{1,0:T(8,128)S(1)}, f32[128,512]{1,0:T(8,128)S(1)}, u32[]{:S(2)}, u32[]{:S(2)}) collective-permute-start(f32[128,512]{1,0:T(8,128)S(1)} %add.31), channel_id=1, source_target_pairs={{0,2},{1,5},{4,0},{5,9},{8,4},{9,13},{12,8},{13,15},{14,12},{15,11... | collective-permute-start | bytes 786440 | tf_op jit(solution)/shard_map/ppermute | solution.py:304
  29.5 0.0 collective-permute-done.15
  29.5 0.4 collective-permute-start.16
  29.9 1.9 %product.19 = (f32[128,512]{1,0:T(8,128)S(1)}, f32[128,512]{1,0:T(8,128)S(1)}) custom-call(f32[128,2048]{1,0:T(8,128)S(1)} %pick.2.refs_0_, f32[128,2048]{1,0:T(8,128)S(1)} %collective-permute-done.refs_1_, f32[128,2048]{1,0:T(8,128)S(1)} %get-tuple-element.30.refs_2_, f32[128,2048]{1,0:T(8,128)S(1)} %collective-permute-done.2.refs_3_, ...), custom_call_target="tpu_custom_call" | custom-call | flops 1610612736 | bytes 9961472 | tf_op jit(solution)/shard_map/product/pallas_call | solution.py:179
  31.8 2.1 %product.20 = (f32[128,512]{1,0:T(8,128)S(1)}, f32[128,512]{1,0:T(8,128)S(1)}) custom-call(f32[128,2048]{1,0:T(8,128)S(1)} %pick.2.refs_0_, f32[128,2048]{1,0:T(8,128)S(1)} %collective-permute-done.refs_1_, f32[128,2048]{1,0:T(8,128)S(1)} %get-tuple-element.30.refs_2_, f32[128,2048]{1,0:T(8,128)S(1)} %collective-permute-done.2.refs_3_, ...), custom_call_target="tpu_custom_call" | custom-call | flops 1610612736 | bytes 9961472 | tf_op jit(solution)/shard_map/product/pallas_call | solution.py:179
  33.9 1.1 %collective-permute-done.9 = f32[128,512]{1,0:T(8,128)S(1)} collective-permute-done((f32[128,512]{1,0:T(8,128)S(1)}, f32[128,512]{1,0:T(8,128)S(1)}, u32[]{:S(2)}, u32[]{:S(2)}) %collective-permute-start.9) | collective-permute-done | bytes 262176 | tf_op jit(solution)/shard_map/ppermute | solution.py:304
  35.0 0.4 collective-permute-start.10
  35.4 0.0 collective-permute-done.12
  35.5 1.7 %collective-permute-start.13 = (f32[128,512]{1,0:T(8,128)S(1)}, f32[128,512]{1,0:T(8,128)S(1)}, u32[]{:S(2)}, u32[]{:S(2)}) collective-permute-start(f32[128,512]{1,0:T(8,128)S(1)} %add.36), channel_id=1, source_target_pairs={{0,2},{1,5},{4,0},{5,9},{8,4},{9,13},{12,8},{13,15},{14,12},{15,11... | collective-permute-start | bytes 786440 | tf_op jit(solution)/shard_map/ppermute | solution.py:304
  37.2 3.3 %collective-permute-done.6 = f32[128,512]{1,0:T(8,128)S(1)} collective-permute-done((f32[128,512]{1,0:T(8,128)S(1)}, f32[128,512]{1,0:T(8,128)S(1)}, u32[]{:S(2)}, u32[]{:S(2)}) %collective-permute-start.6) | collective-permute-done | bytes 262176 | tf_op jit(solution)/shard_map/ppermute | solution.py:304
  40.6 2.1 %collective-permute-start.7 = (f32[128,512]{1,0:T(8,128)S(1)}, f32[128,512]{1,0:T(8,128)S(1)}, u32[]{:S(2)}, u32[]{:S(2)}) collective-permute-start(f32[128,512]{1,0:T(8,128)S(1)} %add.32), channel_id=1, source_target_pairs={{0,2},{1,5},{4,0},{5,9},{8,4},{9,13},{12,8},{13,15},{14,12},{15,11... | collective-permute-start | bytes 786440 | tf_op jit(solution)/shard_map/ppermute | solution.py:304
  42.6 0.0 collective-permute-done.16
  42.7 0.1 collective-permute-start.17
  42.7 1.9 %product.21 = (f32[128,512]{1,0:T(8,128)S(1)}, f32[128,512]{1,0:T(8,128)S(1)}) custom-call(f32[128,2048]{1,0:T(8,128)S(1)} %pick.2.refs_0_, f32[128,2048]{1,0:T(8,128)S(1)} %collective-permute-done.refs_1_, f32[128,2048]{1,0:T(8,128)S(1)} %get-tuple-element.30.refs_2_, f32[128,2048]{1,0:T(8,128)S(1)} %collective-permute-done.2.refs_3_, ...), custom_call_target="tpu_custom_call" | custom-call | flops 1610612736 | bytes 9961472 | tf_op jit(solution)/shard_map/product/pallas_call | solution.py:179
  44.7 1.5 %collective-permute-done.10.refs_1_ = f32[128,512]{1,0:T(8,128)S(1)} collective-permute-done((f32[128,512]{1,0:T(8,128)S(1)}, f32[128,512]{1,0:T(8,128)S(1)}, u32[]{:S(2)}, u32[]{:S(2)}) %collective-permute-start.10) | collective-permute-done | bytes 262176 | tf_op jit(solution)/shard_map/ppermute | solution.py:304
  46.2 0.0 collective-permute-done.13.refs_3_
  46.2 4.2 %collective-permute-done.7.refs_0_ = f32[128,512]{1,0:T(8,128)S(1)} collective-permute-done((f32[128,512]{1,0:T(8,128)S(1)}, f32[128,512]{1,0:T(8,128)S(1)}, u32[]{:S(2)}, u32[]{:S(2)}) %collective-permute-start.7) | collective-permute-done | bytes 262176 | tf_op jit(solution)/shard_map/ppermute | solution.py:304
  50.4 0.4 collective-permute-done.17.refs_4_
  50.9 0.9 %finish.1 = f32[128,1024]{1,0:T(8,128)} custom-call(f32[128,512]{1,0:T(8,128)S(1)} %collective-permute-done.7.refs_0_, f32[128,512]{1,0:T(8,128)S(1)} %collective-permute-done.10.refs_1_, f32[128,512]{1,0:T(8,128)S(1)} %get-tuple-element.47.refs_2_, f32[128,512]{1,0:T(8,128)S(1)} %collective-permute-done.13.refs_3_, ...), custom_call_target="tpu_custom_call" | custom-call | tf_op jit(solution)/shard_map/finish/pallas_call | solution.py:206
  (10 shorter events, 0.4 us)
Async XLA Ops:
  0.0 5.0 %copy-start = (f32[2048,1024]{1,0:T(8,128)S(1)}, f32[2048,1024]{1,0:T(8,128)}, u32[]{:S(2)}) copy-start(f32[2048,1024]{1,0:T(8,128)} %refs_1_.1) | copy-start | bytes 25165828
  1.4 3.5 %collective-permute-start = (f32[128,2048]{1,0:T(8,128)S(1)}, f32[128,2048]{1,0:T(8,128)S(1)}, u32[]{:S(2)}, u32[]{:S(2)}) collective-permute-start(f32[128,2048]{1,0:T(8,128)S(1)} %pick.2.refs_0_), channel_id=1, source_target_pairs={{0,1},{1,0},{2,3},{3,2},{4,5},{5,4},{6,7},{7,6},{8,9},{9,8},{10,11... | collective-permute-start | bytes 3145736 | tf_op jit(solution)/shard_map/ppermute | solution.py:268
  4.3 6.6 %collective-permute-start.2 = (f32[128,2048]{1,0:T(8,128)S(1)}, f32[128,2048]{1,0:T(8,128)S(1)}, u32[]{:S(2)}, u32[]{:S(2)}) collective-permute-start(f32[128,2048]{1,0:T(8,128)S(1)} %get-tuple-element.30.refs_2_), channel_id=1, source_target_pairs={{0,1},{1,0},{2,3},{3,2},{4,5},{5,4},{6,7},{7,6},{8,9},{9,8},{10,11... | collective-permute-start | bytes 3145736 | tf_op jit(solution)/shard_map/ppermute | solution.py:268
  4.4 9.5 %collective-permute-start.3 = (f32[128,2048]{1,0:T(8,128)S(1)}, f32[128,2048]{1,0:T(8,128)S(1)}, u32[]{:S(2)}, u32[]{:S(2)}) collective-permute-start(f32[128,2048]{1,0:T(8,128)S(1)} %get-tuple-element.31.refs_4_), channel_id=1, source_target_pairs={{0,1},{1,0},{2,3},{3,2},{4,5},{5,4},{6,7},{7,6},{8,9},{9,8},{10,11... | collective-permute-start | bytes 3145736 | tf_op jit(solution)/shard_map/ppermute | solution.py:268
  4.9 15.1 %collective-permute-start.5 = (f32[128,2048]{1,0:T(8,128)S(1)}, f32[128,2048]{1,0:T(8,128)S(1)}, u32[]{:S(2)}, u32[]{:S(2)}) collective-permute-start(f32[128,2048]{1,0:T(8,128)S(1)} %get-tuple-element.41.refs_6_), channel_id=1, source_target_pairs={{0,1},{1,0},{2,3},{3,2},{4,5},{5,4},{6,7},{7,6},{8,9},{9,8},{10,11... | collective-permute-start | bytes 3145736 | tf_op jit(solution)/shard_map/ppermute | solution.py:268
  6.4 10.8 %collective-permute-start.1 = (f32[128,512]{1,0:T(8,128)S(1)}, f32[128,512]{1,0:T(8,128)S(1)}, u32[]{:S(2)}, u32[]{:S(2)}) collective-permute-start(f32[128,512]{1,0:T(8,128)S(1)} %get-tuple-element.29.refs_2_), channel_id=1, source_target_pairs={{0,2},{1,5},{4,0},{5,9},{8,4},{9,13},{12,8},{13,15},{14,12},{15,11... | collective-permute-start | bytes 786440 | tf_op jit(solution)/shard_map/ppermute | solution.py:304
  10.7 9.1 %collective-permute-start.14 = (f32[128,512]{1,0:T(8,128)S(1)}, f32[128,512]{1,0:T(8,128)S(1)}, u32[]{:S(2)}, u32[]{:S(2)}) collective-permute-start(f32[128,512]{1,0:T(8,128)S(1)} %get-tuple-element.35.refs_7_), channel_id=1, source_target_pairs={{0,4},{1,3},{4,8},{5,1},{8,12},{9,5},{12,14},{13,9},{14,10},{15,13... | collective-permute-start | bytes 786440 | tf_op jit(solution)/shard_map/ppermute | solution.py:304
  12.0 13.6 %collective-permute-start.11 = (f32[128,512]{1,0:T(8,128)S(1)}, f32[128,512]{1,0:T(8,128)S(1)}, u32[]{:S(2)}, u32[]{:S(2)}) collective-permute-start(f32[128,512]{1,0:T(8,128)S(1)} %get-tuple-element.39.refs_8_), channel_id=1, source_target_pairs={{0,2},{1,5},{4,0},{5,9},{8,4},{9,13},{12,8},{13,15},{14,12},{15,11... | collective-permute-start | bytes 786440 | tf_op jit(solution)/shard_map/ppermute | solution.py:304
  15.0 10.5 %collective-permute-start.8 = (f32[128,512]{1,0:T(8,128)S(1)}, f32[128,512]{1,0:T(8,128)S(1)}, u32[]{:S(2)}, u32[]{:S(2)}) collective-permute-start(f32[128,512]{1,0:T(8,128)S(1)} %get-tuple-element.40.refs_3_), channel_id=1, source_target_pairs={{0,4},{1,3},{4,8},{5,1},{8,12},{9,5},{12,14},{13,9},{14,10},{15,13... | collective-permute-start | bytes 786440 | tf_op jit(solution)/shard_map/ppermute | solution.py:304
  17.2 10.4 %collective-permute-start.4 = (f32[128,512]{1,0:T(8,128)S(1)}, f32[128,512]{1,0:T(8,128)S(1)}, u32[]{:S(2)}, u32[]{:S(2)}) collective-permute-start(f32[128,512]{1,0:T(8,128)S(1)} %add.30), channel_id=1, source_target_pairs={{0,2},{1,5},{4,0},{5,9},{8,4},{9,13},{12,8},{13,15},{14,12},{15,11... | collective-permute-start | bytes 786440 | tf_op jit(solution)/shard_map/ppermute | solution.py:304
  19.9 9.6 %collective-permute-start.15 = (f32[128,512]{1,0:T(8,128)S(1)}, f32[128,512]{1,0:T(8,128)S(1)}, u32[]{:S(2)}, u32[]{:S(2)}) collective-permute-start(f32[128,512]{1,0:T(8,128)S(1)} %add.37), channel_id=1, source_target_pairs={{0,4},{1,3},{4,8},{5,1},{8,12},{9,5},{12,14},{13,9},{14,10},{15,13... | collective-permute-start | bytes 786440 | tf_op jit(solution)/shard_map/ppermute | solution.py:304
  25.5 9.5 %collective-permute-start.9 = (f32[128,512]{1,0:T(8,128)S(1)}, f32[128,512]{1,0:T(8,128)S(1)}, u32[]{:S(2)}, u32[]{:S(2)}) collective-permute-start(f32[128,512]{1,0:T(8,128)S(1)} %add.33), channel_id=1, source_target_pairs={{0,4},{1,3},{4,8},{5,1},{8,12},{9,5},{12,14},{13,9},{14,10},{15,13... | collective-permute-start | bytes 786440 | tf_op jit(solution)/shard_map/ppermute | solution.py:304
  25.6 9.8 %collective-permute-start.12 = (f32[128,512]{1,0:T(8,128)S(1)}, f32[128,512]{1,0:T(8,128)S(1)}, u32[]{:S(2)}, u32[]{:S(2)}) collective-permute-start(f32[128,512]{1,0:T(8,128)S(1)} %add.35), channel_id=1, source_target_pairs={{0,2},{1,5},{4,0},{5,9},{8,4},{9,13},{12,8},{13,15},{14,12},{15,11... | collective-permute-start | bytes 786440 | tf_op jit(solution)/shard_map/ppermute | solution.py:304
  27.7 12.8 %collective-permute-start.6 = (f32[128,512]{1,0:T(8,128)S(1)}, f32[128,512]{1,0:T(8,128)S(1)}, u32[]{:S(2)}, u32[]{:S(2)}) collective-permute-start(f32[128,512]{1,0:T(8,128)S(1)} %add.31), channel_id=1, source_target_pairs={{0,2},{1,5},{4,0},{5,9},{8,4},{9,13},{12,8},{13,15},{14,12},{15,11... | collective-permute-start | bytes 786440 | tf_op jit(solution)/shard_map/ppermute | solution.py:304
  29.5 13.1 %collective-permute-start.16 = (f32[128,512]{1,0:T(8,128)S(1)}, f32[128,512]{1,0:T(8,128)S(1)}, u32[]{:S(2)}, u32[]{:S(2)}) collective-permute-start(f32[128,512]{1,0:T(8,128)S(1)} %add.38), channel_id=1, source_target_pairs={{0,4},{1,3},{4,8},{5,1},{8,12},{9,5},{12,14},{13,9},{14,10},{15,13... | collective-permute-start | bytes 786440 | tf_op jit(solution)/shard_map/ppermute | solution.py:304
  35.0 11.2 %collective-permute-start.10 = (f32[128,512]{1,0:T(8,128)S(1)}, f32[128,512]{1,0:T(8,128)S(1)}, u32[]{:S(2)}, u32[]{:S(2)}) collective-permute-start(f32[128,512]{1,0:T(8,128)S(1)} %add.34), channel_id=1, source_target_pairs={{0,4},{1,3},{4,8},{5,1},{8,12},{9,5},{12,14},{13,9},{14,10},{15,13... | collective-permute-start | bytes 786440 | tf_op jit(solution)/shard_map/ppermute | solution.py:304
  35.5 10.8 %collective-permute-start.13 = (f32[128,512]{1,0:T(8,128)S(1)}, f32[128,512]{1,0:T(8,128)S(1)}, u32[]{:S(2)}, u32[]{:S(2)}) collective-permute-start(f32[128,512]{1,0:T(8,128)S(1)} %add.36), channel_id=1, source_target_pairs={{0,2},{1,5},{4,0},{5,9},{8,4},{9,13},{12,8},{13,15},{14,12},{15,11... | collective-permute-start | bytes 786440 | tf_op jit(solution)/shard_map/ppermute | solution.py:304
  40.6 9.8 %collective-permute-start.7 = (f32[128,512]{1,0:T(8,128)S(1)}, f32[128,512]{1,0:T(8,128)S(1)}, u32[]{:S(2)}, u32[]{:S(2)}) collective-permute-start(f32[128,512]{1,0:T(8,128)S(1)} %add.32), channel_id=1, source_target_pairs={{0,2},{1,5},{4,0},{5,9},{8,4},{9,13},{12,8},{13,15},{14,12},{15,11... | collective-permute-start | bytes 786440 | tf_op jit(solution)/shard_map/ppermute | solution.py:304
  42.7 8.2 %collective-permute-start.17 = (f32[128,512]{1,0:T(8,128)S(1)}, f32[128,512]{1,0:T(8,128)S(1)}, u32[]{:S(2)}, u32[]{:S(2)}) collective-permute-start(f32[128,512]{1,0:T(8,128)S(1)} %add.39), channel_id=1, source_target_pairs={{0,4},{1,3},{4,8},{5,1},{8,12},{9,5},{12,14},{13,9},{14,10},{15,13... | collective-permute-start | bytes 786440 | tf_op jit(solution)/shard_map/ppermute | solution.py:304

commit v11 on v10

--- a/solution.py
+++ b/solution.py
@@ -288,8 +288,8 @@
                 made.append(got[0])
             return calls[call, part][at * size : (at + 1) * size]
 
-        fetch(0, 1, 52)
-        fetch(1, len(chunks), 48, sources[0])
+        fetch(0, 2, 50)
+        fetch(2, len(chunks), 48, sources[0])
 
         sums = [[None, None], [None, None]]
         for step in range(half):

time: 51.9 us -> 51.8 us (level)
  transfers between devices with their start and end apart: 18 -> 18, of which waited for: 7 -> 7; matrix products, arithmetic and copies ran while one was open for 1% -> 1% of each run, Pallas kernels for 37% -> 36%
where the time goes in v11:
time: 51.8 us; the launch traced here: 51.7 us
  Pallas kernels  21.2 us (41%)
  starting transfers between devices  17.1 us (33%)
  waiting for transfers between devices  12.8 us (25%)
    pallas_call x11, Pallas kernels, product(): pl.pallas_call(functools.partial(product_kernel, starts, size, bounds, pa...  16.5 us
    ppermute x14, starting transfers between devices, shards(): sums[way][part] = lax.ppermute(value, ('row', 'col'), ways[way])  15.9 us
    ppermute x14, waiting for transfers between devices, shards(): sums[way][part] = lax.ppermute(value, ('row', 'col'), ways[way])  12.8 us
    pallas_call x2, Pallas kernels, pick(): pl.pallas_call(functools.partial(pick_kernel, starts, size, chunks), out_...  3.81 us
    ppermute x4, starting transfers between devices, fetch(): sources.extend([own, lax.ppermute(own, 'col', swap)])  1.17 us
  transfers between devices with their start and end apart: 18, of which 7 were waited for; matrix products, arithmetic and copies ran while one was open for 1% of the time, Pallas kernels for 36%

profile of v11, /device:TPU:0, one launch (start us, length us, event | category | flops | bytes accessed | tf_op | source)
XLA Modules:
  0.0 51.7 jit_solution(14775360077434783279)
XLA Ops:
  0.0 0.0 copy-start
  0.0 1.7 %pick.2 = (f32[128,2048]{1,0:T(8,128)S(1)}, f32[128,2048]{1,0:T(8,128)S(1)}) custom-call(f32[512,2048]{1,0:T(8,128)} %a_ref.3), custom_call_target="tpu_custom_call" | custom-call | bytes 4194304 | tf_op jit(solution)/shard_map/pick/pallas_call | solution.py:69
  1.8 0.5 %collective-permute-start = (f32[128,2048]{1,0:T(8,128)S(1)}, f32[128,2048]{1,0:T(8,128)S(1)}, u32[]{:S(2)}, u32[]{:S(2)}) collective-permute-start(f32[128,2048]{1,0:T(8,128)S(1)} %get-tuple-element.30.refs_0_), channel_id=1, source_target_pairs={{0,1},{1,0},{2,3},{3,2},{4,5},{5,4},{6,7},{7,6},{8,9},{9,8},{10,11... | collective-permute-start | bytes 3145736 | tf_op jit(solution)/shard_map/ppermute | solution.py:268
  2.3 0.1 collective-permute-start.2
  2.4 2.1 %pick.3 = (f32[128,2048]{1,0:T(8,128)S(1)}, f32[128,2048]{1,0:T(8,128)S(1)}) custom-call(f32[512,2048]{1,0:T(8,128)} %a_ref.3, f32[128,2048]{1,0:T(8,128)S(1)} %get-tuple-element.30.refs_0_), custom_call_target="tpu_custom_call" | custom-call | bytes 4194304 | tf_op jit(solution)/shard_map/pick/pallas_call | solution.py:69
  4.4 0.5 collective-permute-start.3
  4.9 0.1 collective-permute-start.5
  5.0 0.0 collective-permute-done.refs_1_
  5.0 0.0 copy-done
  5.0 1.4 %product.11 = (f32[128,512]{1,0:T(8,128)S(1)}, bf16[2048,512]{1,0:T(8,128)(2,1)S(1)}, bf16[2048,512]{1,0:T(8,128)(2,1)S(1)}, bf16[256,2048]{1,0:T(8,128)(2,1)S(1)}) custom-call(f32[128,2048]{1,0:T(8,128)S(1)} %get-tuple-element.30.refs_0_, f32[128,2048]{1,0:T(8,128)S(1)} %collective-permute-done.refs_1_, f32[2048,1024]{1,0:T(8,128)S(1)} %copy-done), custom_call_target="tpu_custom_call" | custom-call | flops 805306368 | bytes 5505024 | tf_op jit(solution)/shard_map/product/pallas_call | solution.py:179
  6.4 3.0 %collective-permute-start.1 = (f32[128,512]{1,0:T(8,128)S(1)}, f32[128,512]{1,0:T(8,128)S(1)}, u32[]{:S(2)}, u32[]{:S(2)}) collective-permute-start(f32[128,512]{1,0:T(8,128)S(1)} %get-tuple-element.31.refs_2_), channel_id=1, source_target_pairs={{0,2},{1,5},{4,0},{5,9},{8,4},{9,13},{12,8},{13,15},{14,12},{15,11... | collective-permute-start | bytes 786440 | tf_op jit(solution)/shard_map/ppermute | solution.py:304
  9.4 1.3 %product.12 = (f32[128,512]{1,0:T(8,128)S(1)}, bf16[2048,512]{1,0:T(8,128)(2,1)S(1)}, bf16[2048,512]{1,0:T(8,128)(2,1)S(1)}) custom-call(bf16[256,2048]{1,0:T(8,128)(2,1)S(1)} %get-tuple-element.34.refs_0_, f32[2048,1024]{1,0:T(8,128)S(1)} %copy-done, f32[128,512]{1,0:T(8,128)S(1)} %get-tuple-element.31.refs_2_), custom_call_target="tpu_custom_call" | custom-call | flops 805306368 | bytes 5505024 | tf_op jit(solution)/shard_map/product/pallas_call | solution.py:179
  10.7 0.2 collective-permute-start.14
  10.8 0.0 collective-permute-done.2.refs_3_
  10.8 1.1 %product.13 = (f32[128,512]{1,0:T(8,128)S(1)}, bf16[256,2048]{1,0:T(8,128)(2,1)S(1)}) custom-call(f32[128,2048]{1,0:T(8,128)S(1)} %get-tuple-element.30.refs_0_, f32[128,2048]{1,0:T(8,128)S(1)} %collective-permute-done.refs_1_, f32[128,2048]{1,0:T(8,128)S(1)} %get-tuple-element.32.refs_2_, f32[128,2048]{1,0:T(8,128)S(1)} %collective-permute-done.2.refs_3_, ...), custom_call_target="tpu_custom_call" | custom-call | flops 805306368 | bytes 5505024 | tf_op jit(solution)/shard_map/product/pallas_call | solution.py:179
  11.9 2.0 %collective-permute-start.11 = (f32[128,512]{1,0:T(8,128)S(1)}, f32[128,512]{1,0:T(8,128)S(1)}, u32[]{:S(2)}, u32[]{:S(2)}) collective-permute-start(f32[128,512]{1,0:T(8,128)S(1)} %get-tuple-element.41.refs_8_), channel_id=1, source_target_pairs={{0,2},{1,5},{4,0},{5,9},{8,4},{9,13},{12,8},{13,15},{14,12},{15,11... | collective-permute-start | bytes 786440 | tf_op jit(solution)/shard_map/ppermute | solution.py:304
  13.9 0.0 collective-permute-done.3.refs_5_
  13.9 1.1 %product.14 = (f32[128,512]{1,0:T(8,128)S(1)}, bf16[256,2048]{1,0:T(8,128)(2,1)S(1)}) custom-call(f32[128,2048]{1,0:T(8,128)S(1)} %get-tuple-element.30.refs_0_, f32[128,2048]{1,0:T(8,128)S(1)} %collective-permute-done.refs_1_, f32[128,2048]{1,0:T(8,128)S(1)} %get-tuple-element.32.refs_2_, f32[128,2048]{1,0:T(8,128)S(1)} %collective-permute-done.2.refs_3_, ...), custom_call_target="tpu_custom_call" | custom-call | flops 805306368 | bytes 5505024 | tf_op jit(solution)/shard_map/product/pallas_call | solution.py:179
  14.9 0.2 collective-permute-start.8
  15.2 1.0 %product.15.refs_3_ = f32[128,512]{1,0:T(8,128)S(1)} custom-call(bf16[256,2048]{1,0:T(8,128)(2,1)S(1)} %get-tuple-element.38.refs_0_, bf16[2048,512]{1,0:T(8,128)(2,1)S(1)} %get-tuple-element.39.refs_6_.refs_1_.refs_8_, bf16[2048,512]{1,0:T(8,128)(2,1)S(1)} %get-tuple-element.40.refs_7_.refs_2_.refs_9_, f32[128,512]{1,0:T(8,128)S(1)} %get-tuple-element.42.refs_3_), custom_call_target="tpu_custom_call" | custom-call | flops 805306368 | bytes 5505024 | tf_op jit(solution)/shard_map/product/pallas_call | solution.py:179
  16.1 1.0 %product.16.refs_12_ = f32[128,512]{1,0:T(8,128)S(1)} custom-call(bf16[256,2048]{1,0:T(8,128)(2,1)S(1)} %get-tuple-element.44.refs_0_, bf16[2048,512]{1,0:T(8,128)(2,1)S(1)} %get-tuple-element.35.refs_5_.refs_1_.refs_10_, bf16[2048,512]{1,0:T(8,128)(2,1)S(1)} %get-tuple-element.36.refs_6_.refs_2_.refs_11_, f32[128,512]{1,0:T(8,128)S(1)} %product.15.refs_3_), custom_call_target="tpu_custom_call" | custom-call | flops 805306368 | bytes 5505024 | tf_op jit(solution)/shard_map/product/pallas_call | solution.py:179
  17.1 0.0 collective-permute-done.1
  17.2 1.9 %collective-permute-start.4 = (f32[128,512]{1,0:T(8,128)S(1)}, f32[128,512]{1,0:T(8,128)S(1)}, u32[]{:S(2)}, u32[]{:S(2)}) collective-permute-start(f32[128,512]{1,0:T(8,128)S(1)} %add.30), channel_id=1, source_target_pairs={{0,2},{1,5},{4,0},{5,9},{8,4},{9,13},{12,8},{13,15},{14,12},{15,11... | collective-permute-start | bytes 786440 | tf_op jit(solution)/shard_map/ppermute | solution.py:304
  19.1 0.6 %collective-permute-done.14 = f32[128,512]{1,0:T(8,128)S(1)} collective-permute-done((f32[128,512]{1,0:T(8,128)S(1)}, f32[128,512]{1,0:T(8,128)S(1)}, u32[]{:S(2)}, u32[]{:S(2)}) %collective-permute-start.14) | collective-permute-done | bytes 262176 | tf_op jit(solution)/shard_map/ppermute | solution.py:304
  19.8 0.1 collective-permute-start.15
  19.8 0.0 collective-permute-done.5.refs_7_
  19.8 1.9 %product.17 = (f32[128,512]{1,0:T(8,128)S(1)}, f32[128,512]{1,0:T(8,128)S(1)}) custom-call(f32[128,2048]{1,0:T(8,128)S(1)} %get-tuple-element.30.refs_0_, f32[128,2048]{1,0:T(8,128)S(1)} %collective-permute-done.refs_1_, f32[128,2048]{1,0:T(8,128)S(1)} %get-tuple-element.32.refs_2_, f32[128,2048]{1,0:T(8,128)S(1)} %collective-permute-done.2.refs_3_, ...), custom_call_target="tpu_custom_call" | custom-call | flops 1610612736 | bytes 9961472 | tf_op jit(solution)/shard_map/product/pallas_call | solution.py:179
  21.8 1.9 %product.18 = (f32[128,512]{1,0:T(8,128)S(1)}, f32[128,512]{1,0:T(8,128)S(1)}) custom-call(f32[128,2048]{1,0:T(8,128)S(1)} %get-tuple-element.30.refs_0_, f32[128,2048]{1,0:T(8,128)S(1)} %collective-permute-done.refs_1_, f32[128,2048]{1,0:T(8,128)S(1)} %get-tuple-element.32.refs_2_, f32[128,2048]{1,0:T(8,128)S(1)} %collective-permute-done.2.refs_3_, ...), custom_call_target="tpu_custom_call" | custom-call | flops 1610612736 | bytes 9961472 | tf_op jit(solution)/shard_map/product/pallas_call | solution.py:179
  23.7 1.6 %collective-permute-done.8 = f32[128,512]{1,0:T(8,128)S(1)} collective-permute-done((f32[128,512]{1,0:T(8,128)S(1)}, f32[128,512]{1,0:T(8,128)S(1)}, u32[]{:S(2)}, u32[]{:S(2)}) %collective-permute-start.8) | collective-permute-done | bytes 262176 | tf_op jit(solution)/shard_map/ppermute | solution.py:304
  25.4 0.1 collective-permute-start.9
  25.4 0.0 collective-permute-done.11
  25.5 2.1 %collective-permute-start.12 = (f32[128,512]{1,0:T(8,128)S(1)}, f32[128,512]{1,0:T(8,128)S(1)}, u32[]{:S(2)}, u32[]{:S(2)}) collective-permute-start(f32[128,512]{1,0:T(8,128)S(1)} %add.35), channel_id=1, source_target_pairs={{0,2},{1,5},{4,0},{5,9},{8,4},{9,13},{12,8},{13,15},{14,12},{15,11... | collective-permute-start | bytes 786440 | tf_op jit(solution)/shard_map/ppermute | solution.py:304
  27.6 0.0 collective-permute-done.4
  27.6 1.8 %collective-permute-start.6 = (f32[128,512]{1,0:T(8,128)S(1)}, f32[128,512]{1,0:T(8,128)S(1)}, u32[]{:S(2)}, u32[]{:S(2)}) collective-permute-start(f32[128,512]{1,0:T(8,128)S(1)} %add.31), channel_id=1, source_target_pairs={{0,2},{1,5},{4,0},{5,9},{8,4},{9,13},{12,8},{13,15},{14,12},{15,11... | collective-permute-start | bytes 786440 | tf_op jit(solution)/shard_map/ppermute | solution.py:304
  29.4 0.0 collective-permute-done.15
  29.4 0.5 collective-permute-start.16
  29.9 1.9 %product.19 = (f32[128,512]{1,0:T(8,128)S(1)}, f32[128,512]{1,0:T(8,128)S(1)}) custom-call(f32[128,2048]{1,0:T(8,128)S(1)} %get-tuple-element.30.refs_0_, f32[128,2048]{1,0:T(8,128)S(1)} %collective-permute-done.refs_1_, f32[128,2048]{1,0:T(8,128)S(1)} %get-tuple-element.32.refs_2_, f32[128,2048]{1,0:T(8,128)S(1)} %collective-permute-done.2.refs_3_, ...), custom_call_target="tpu_custom_call" | custom-call | flops 1610612736 | bytes 9961472 | tf_op jit(solution)/shard_map/product/pallas_call | solution.py:179
  31.8 2.1 %product.20 = (f32[128,512]{1,0:T(8,128)S(1)}, f32[128,512]{1,0:T(8,128)S(1)}) custom-call(f32[128,2048]{1,0:T(8,128)S(1)} %get-tuple-element.30.refs_0_, f32[128,2048]{1,0:T(8,128)S(1)} %collective-permute-done.refs_1_, f32[128,2048]{1,0:T(8,128)S(1)} %get-tuple-element.32.refs_2_, f32[128,2048]{1,0:T(8,128)S(1)} %collective-permute-done.2.refs_3_, ...), custom_call_target="tpu_custom_call" | custom-call | flops 1610612736 | bytes 9961472 | tf_op jit(solution)/shard_map/product/pallas_call | solution.py:179
  33.9 1.0 %collective-permute-done.9 = f32[128,512]{1,0:T(8,128)S(1)} collective-permute-done((f32[128,512]{1,0:T(8,128)S(1)}, f32[128,512]{1,0:T(8,128)S(1)}, u32[]{:S(2)}, u32[]{:S(2)}) %collective-permute-start.9) | collective-permute-done | bytes 262176 | tf_op jit(solution)/shard_map/ppermute | solution.py:304
  34.9 0.6 %collective-permute-start.10 = (f32[128,512]{1,0:T(8,128)S(1)}, f32[128,512]{1,0:T(8,128)S(1)}, u32[]{:S(2)}, u32[]{:S(2)}) collective-permute-start(f32[128,512]{1,0:T(8,128)S(1)} %add.34), channel_id=1, source_target_pairs={{0,4},{1,3},{4,8},{5,1},{8,12},{9,5},{12,14},{13,9},{14,10},{15,13... | collective-permute-start | bytes 786440 | tf_op jit(solution)/shard_map/ppermute | solution.py:304
  35.5 0.0 collective-permute-done.12
  35.6 1.5 %collective-permute-start.13 = (f32[128,512]{1,0:T(8,128)S(1)}, f32[128,512]{1,0:T(8,128)S(1)}, u32[]{:S(2)}, u32[]{:S(2)}) collective-permute-start(f32[128,512]{1,0:T(8,128)S(1)} %add.36), channel_id=1, source_target_pairs={{0,2},{1,5},{4,0},{5,9},{8,4},{9,13},{12,8},{13,15},{14,12},{15,11... | collective-permute-start | bytes 786440 | tf_op jit(solution)/shard_map/ppermute | solution.py:304
  37.1 3.3 %collective-permute-done.6 = f32[128,512]{1,0:T(8,128)S(1)} collective-permute-done((f32[128,512]{1,0:T(8,128)S(1)}, f32[128,512]{1,0:T(8,128)S(1)}, u32[]{:S(2)}, u32[]{:S(2)}) %collective-permute-start.6) | collective-permute-done | bytes 262176 | tf_op jit(solution)/shard_map/ppermute | solution.py:304
  40.5 2.1 %collective-permute-start.7 = (f32[128,512]{1,0:T(8,128)S(1)}, f32[128,512]{1,0:T(8,128)S(1)}, u32[]{:S(2)}, u32[]{:S(2)}) collective-permute-start(f32[128,512]{1,0:T(8,128)S(1)} %add.32), channel_id=1, source_target_pairs={{0,2},{1,5},{4,0},{5,9},{8,4},{9,13},{12,8},{13,15},{14,12},{15,11... | collective-permute-start | bytes 786440 | tf_op jit(solution)/shard_map/ppermute | solution.py:304
  42.5 0.0 collective-permute-done.16
  42.5 0.1 collective-permute-start.17
  42.6 1.9 %product.21 = (f32[128,512]{1,0:T(8,128)S(1)}, f32[128,512]{1,0:T(8,128)S(1)}) custom-call(f32[128,2048]{1,0:T(8,128)S(1)} %get-tuple-element.30.refs_0_, f32[128,2048]{1,0:T(8,128)S(1)} %collective-permute-done.refs_1_, f32[128,2048]{1,0:T(8,128)S(1)} %get-tuple-element.32.refs_2_, f32[128,2048]{1,0:T(8,128)S(1)} %collective-permute-done.2.refs_3_, ...), custom_call_target="tpu_custom_call" | custom-call | flops 1610612736 | bytes 9961472 | tf_op jit(solution)/shard_map/product/pallas_call | solution.py:179
  44.6 1.5 %collective-permute-done.10.refs_1_ = f32[128,512]{1,0:T(8,128)S(1)} collective-permute-done((f32[128,512]{1,0:T(8,128)S(1)}, f32[128,512]{1,0:T(8,128)S(1)}, u32[]{:S(2)}, u32[]{:S(2)}) %collective-permute-start.10) | collective-permute-done | bytes 262176 | tf_op jit(solution)/shard_map/ppermute | solution.py:304
  46.1 0.0 collective-permute-done.13.refs_3_
  46.1 4.3 %collective-permute-done.7.refs_0_ = f32[128,512]{1,0:T(8,128)S(1)} collective-permute-done((f32[128,512]{1,0:T(8,128)S(1)}, f32[128,512]{1,0:T(8,128)S(1)}, u32[]{:S(2)}, u32[]{:S(2)}) %collective-permute-start.7) | collective-permute-done | bytes 262176 | tf_op jit(solution)/shard_map/ppermute | solution.py:304
  50.4 0.4 collective-permute-done.17.refs_4_
  50.8 0.9 %finish.1 = f32[128,1024]{1,0:T(8,128)} custom-call(f32[128,512]{1,0:T(8,128)S(1)} %collective-permute-done.7.refs_0_, f32[128,512]{1,0:T(8,128)S(1)} %collective-permute-done.10.refs_1_, f32[128,512]{1,0:T(8,128)S(1)} %get-tuple-element.49.refs_2_, f32[128,512]{1,0:T(8,128)S(1)} %collective-permute-done.13.refs_3_, ...), custom_call_target="tpu_custom_call" | custom-call | tf_op jit(solution)/shard_map/finish/pallas_call | solution.py:206
  (10 shorter events, 0.4 us)
Async XLA Ops:
  0.0 5.0 %copy-start = (f32[2048,1024]{1,0:T(8,128)S(1)}, f32[2048,1024]{1,0:T(8,128)}, u32[]{:S(2)}) copy-start(f32[2048,1024]{1,0:T(8,128)} %refs_1_.1) | copy-start | bytes 25165828
  1.8 3.2 %collective-permute-start = (f32[128,2048]{1,0:T(8,128)S(1)}, f32[128,2048]{1,0:T(8,128)S(1)}, u32[]{:S(2)}, u32[]{:S(2)}) collective-permute-start(f32[128,2048]{1,0:T(8,128)S(1)} %get-tuple-element.30.refs_0_), channel_id=1, source_target_pairs={{0,1},{1,0},{2,3},{3,2},{4,5},{5,4},{6,7},{7,6},{8,9},{9,8},{10,11... | collective-permute-start | bytes 3145736 | tf_op jit(solution)/shard_map/ppermute | solution.py:268
  2.3 8.6 %collective-permute-start.2 = (f32[128,2048]{1,0:T(8,128)S(1)}, f32[128,2048]{1,0:T(8,128)S(1)}, u32[]{:S(2)}, u32[]{:S(2)}) collective-permute-start(f32[128,2048]{1,0:T(8,128)S(1)} %get-tuple-element.32.refs_2_), channel_id=1, source_target_pairs={{0,1},{1,0},{2,3},{3,2},{4,5},{5,4},{6,7},{7,6},{8,9},{9,8},{10,11... | collective-permute-start | bytes 3145736 | tf_op jit(solution)/shard_map/ppermute | solution.py:268
  4.4 9.4 %collective-permute-start.3 = (f32[128,2048]{1,0:T(8,128)S(1)}, f32[128,2048]{1,0:T(8,128)S(1)}, u32[]{:S(2)}, u32[]{:S(2)}) collective-permute-start(f32[128,2048]{1,0:T(8,128)S(1)} %get-tuple-element.33.refs_4_), channel_id=1, source_target_pairs={{0,1},{1,0},{2,3},{3,2},{4,5},{5,4},{6,7},{7,6},{8,9},{9,8},{10,11... | collective-permute-start | bytes 3145736 | tf_op jit(solution)/shard_map/ppermute | solution.py:268
  4.9 14.9 %collective-permute-start.5 = (f32[128,2048]{1,0:T(8,128)S(1)}, f32[128,2048]{1,0:T(8,128)S(1)}, u32[]{:S(2)}, u32[]{:S(2)}) collective-permute-start(f32[128,2048]{1,0:T(8,128)S(1)} %get-tuple-element.43.refs_6_), channel_id=1, source_target_pairs={{0,1},{1,0},{2,3},{3,2},{4,5},{5,4},{6,7},{7,6},{8,9},{9,8},{10,11... | collective-permute-start | bytes 3145736 | tf_op jit(solution)/shard_map/ppermute | solution.py:268
  6.4 10.7 %collective-permute-start.1 = (f32[128,512]{1,0:T(8,128)S(1)}, f32[128,512]{1,0:T(8,128)S(1)}, u32[]{:S(2)}, u32[]{:S(2)}) collective-permute-start(f32[128,512]{1,0:T(8,128)S(1)} %get-tuple-element.31.refs_2_), channel_id=1, source_target_pairs={{0,2},{1,5},{4,0},{5,9},{8,4},{9,13},{12,8},{13,15},{14,12},{15,11... | collective-permute-start | bytes 786440 | tf_op jit(solution)/shard_map/ppermute | solution.py:304
  10.7 9.1 %collective-permute-start.14 = (f32[128,512]{1,0:T(8,128)S(1)}, f32[128,512]{1,0:T(8,128)S(1)}, u32[]{:S(2)}, u32[]{:S(2)}) collective-permute-start(f32[128,512]{1,0:T(8,128)S(1)} %get-tuple-element.37.refs_7_), channel_id=1, source_target_pairs={{0,4},{1,3},{4,8},{5,1},{8,12},{9,5},{12,14},{13,9},{14,10},{15,13... | collective-permute-start | bytes 786440 | tf_op jit(solution)/shard_map/ppermute | solution.py:304
  11.9 13.5 %collective-permute-start.11 = (f32[128,512]{1,0:T(8,128)S(1)}, f32[128,512]{1,0:T(8,128)S(1)}, u32[]{:S(2)}, u32[]{:S(2)}) collective-permute-start(f32[128,512]{1,0:T(8,128)S(1)} %get-tuple-element.41.refs_8_), channel_id=1, source_target_pairs={{0,2},{1,5},{4,0},{5,9},{8,4},{9,13},{12,8},{13,15},{14,12},{15,11... | collective-permute-start | bytes 786440 | tf_op jit(solution)/shard_map/ppermute | solution.py:304
  14.9 10.4 %collective-permute-start.8 = (f32[128,512]{1,0:T(8,128)S(1)}, f32[128,512]{1,0:T(8,128)S(1)}, u32[]{:S(2)}, u32[]{:S(2)}) collective-permute-start(f32[128,512]{1,0:T(8,128)S(1)} %get-tuple-element.42.refs_3_), channel_id=1, source_target_pairs={{0,4},{1,3},{4,8},{5,1},{8,12},{9,5},{12,14},{13,9},{14,10},{15,13... | collective-permute-start | bytes 786440 | tf_op jit(solution)/shard_map/ppermute | solution.py:304
  17.2 10.4 %collective-permute-start.4 = (f32[128,512]{1,0:T(8,128)S(1)}, f32[128,512]{1,0:T(8,128)S(1)}, u32[]{:S(2)}, u32[]{:S(2)}) collective-permute-start(f32[128,512]{1,0:T(8,128)S(1)} %add.30), channel_id=1, source_target_pairs={{0,2},{1,5},{4,0},{5,9},{8,4},{9,13},{12,8},{13,15},{14,12},{15,11... | collective-permute-start | bytes 786440 | tf_op jit(solution)/shard_map/ppermute | solution.py:304
  19.8 9.6 %collective-permute-start.15 = (f32[128,512]{1,0:T(8,128)S(1)}, f32[128,512]{1,0:T(8,128)S(1)}, u32[]{:S(2)}, u32[]{:S(2)}) collective-permute-start(f32[128,512]{1,0:T(8,128)S(1)} %add.37), channel_id=1, source_target_pairs={{0,4},{1,3},{4,8},{5,1},{8,12},{9,5},{12,14},{13,9},{14,10},{15,13... | collective-permute-start | bytes 786440 | tf_op jit(solution)/shard_map/ppermute | solution.py:304
  25.4 9.5 %collective-permute-start.9 = (f32[128,512]{1,0:T(8,128)S(1)}, f32[128,512]{1,0:T(8,128)S(1)}, u32[]{:S(2)}, u32[]{:S(2)}) collective-permute-start(f32[128,512]{1,0:T(8,128)S(1)} %add.33), channel_id=1, source_target_pairs={{0,4},{1,3},{4,8},{5,1},{8,12},{9,5},{12,14},{13,9},{14,10},{15,13... | collective-permute-start | bytes 786440 | tf_op jit(solution)/shard_map/ppermute | solution.py:304
  25.5 10.0 %collective-permute-start.12 = (f32[128,512]{1,0:T(8,128)S(1)}, f32[128,512]{1,0:T(8,128)S(1)}, u32[]{:S(2)}, u32[]{:S(2)}) collective-permute-start(f32[128,512]{1,0:T(8,128)S(1)} %add.35), channel_id=1, source_target_pairs={{0,2},{1,5},{4,0},{5,9},{8,4},{9,13},{12,8},{13,15},{14,12},{15,11... | collective-permute-start | bytes 786440 | tf_op jit(solution)/shard_map/ppermute | solution.py:304
  27.6 12.8 %collective-permute-start.6 = (f32[128,512]{1,0:T(8,128)S(1)}, f32[128,512]{1,0:T(8,128)S(1)}, u32[]{:S(2)}, u32[]{:S(2)}) collective-permute-start(f32[128,512]{1,0:T(8,128)S(1)} %add.31), channel_id=1, source_target_pairs={{0,2},{1,5},{4,0},{5,9},{8,4},{9,13},{12,8},{13,15},{14,12},{15,11... | collective-permute-start | bytes 786440 | tf_op jit(solution)/shard_map/ppermute | solution.py:304
  29.4 13.1 %collective-permute-start.16 = (f32[128,512]{1,0:T(8,128)S(1)}, f32[128,512]{1,0:T(8,128)S(1)}, u32[]{:S(2)}, u32[]{:S(2)}) collective-permute-start(f32[128,512]{1,0:T(8,128)S(1)} %add.38), channel_id=1, source_target_pairs={{0,4},{1,3},{4,8},{5,1},{8,12},{9,5},{12,14},{13,9},{14,10},{15,13... | collective-permute-start | bytes 786440 | tf_op jit(solution)/shard_map/ppermute | solution.py:304
  34.9 11.2 %collective-permute-start.10 = (f32[128,512]{1,0:T(8,128)S(1)}, f32[128,512]{1,0:T(8,128)S(1)}, u32[]{:S(2)}, u32[]{:S(2)}) collective-permute-start(f32[128,512]{1,0:T(8,128)S(1)} %add.34), channel_id=1, source_target_pairs={{0,4},{1,3},{4,8},{5,1},{8,12},{9,5},{12,14},{13,9},{14,10},{15,13... | collective-permute-start | bytes 786440 | tf_op jit(solution)/shard_map/ppermute | solution.py:304
  35.6 10.5 %collective-permute-start.13 = (f32[128,512]{1,0:T(8,128)S(1)}, f32[128,512]{1,0:T(8,128)S(1)}, u32[]{:S(2)}, u32[]{:S(2)}) collective-permute-start(f32[128,512]{1,0:T(8,128)S(1)} %add.36), channel_id=1, source_target_pairs={{0,2},{1,5},{4,0},{5,9},{8,4},{9,13},{12,8},{13,15},{14,12},{15,11... | collective-permute-start | bytes 786440 | tf_op jit(solution)/shard_map/ppermute | solution.py:304
  40.5 9.9 %collective-permute-start.7 = (f32[128,512]{1,0:T(8,128)S(1)}, f32[128,512]{1,0:T(8,128)S(1)}, u32[]{:S(2)}, u32[]{:S(2)}) collective-permute-start(f32[128,512]{1,0:T(8,128)S(1)} %add.32), channel_id=1, source_target_pairs={{0,2},{1,5},{4,0},{5,9},{8,4},{9,13},{12,8},{13,15},{14,12},{15,11... | collective-permute-start | bytes 786440 | tf_op jit(solution)/shard_map/ppermute | solution.py:304
  42.5 8.2 %collective-permute-start.17 = (f32[128,512]{1,0:T(8,128)S(1)}, f32[128,512]{1,0:T(8,128)S(1)}, u32[]{:S(2)}, u32[]{:S(2)}) collective-permute-start(f32[128,512]{1,0:T(8,128)S(1)} %add.39), channel_id=1, source_target_pairs={{0,4},{1,3},{4,8},{5,1},{8,12},{9,5},{12,14},{13,9},{14,10},{15,13... | collective-permute-start | bytes 786440 | tf_op jit(solution)/shard_map/ppermute | solution.py:304

commit v12 on v10

--- a/solution.py
+++ b/solution.py
@@ -10,6 +10,7 @@
 
 CALLS = 8
 LANES = 256
+SLAB = 512
 PIECE = 16
 MIB = 2**20
 
@@ -89,7 +90,7 @@
 
 def times(stack, high, low):
     depth = stack.shape[0] // 2
-    both = jnp.dot(stack[...], high, preferred_element_type=jnp.float32)
+    both = jnp.dot(stack, high, preferred_element_type=jnp.float32)
     rest = jnp.dot(stack[:depth], low, preferred_element_type=jnp.float32)
     return both[:depth] + (both[depth:] + rest)
 
@@ -152,11 +153,18 @@
             here = slice(at, at + tile)
             if split:
                 first = pl.multiple_of(side(split - 1) * width + at, tile)
-                high, low = halves(columns[0][:, pl.ds(first, tile)])
-                outs[1][:, here], outs[2][:, here] = high, low
+                depth, inner = stack.shape[0] // 2, stack.shape[1]
+                slab = min(SLAB, inner)
+                total = jnp.zeros((depth, tile), jnp.float32)
+                for top in range(0, inner, slab):
+                    deep = slice(top, top + slab)
+                    high, low = halves(columns[0][deep, pl.ds(first, tile)])
+                    outs[1][deep, here], outs[2][deep, here] = high, low
+                    total += times(stack[:, deep], high, low)
+                outs[part][:, here] = total
             else:
                 high, low = (ref[:, here] for ref in columns[2 * part : 2 * part + 2])
-            outs[part][:, here] = times(stack, high, low)
+                outs[part][:, here] = times(stack[...], high, low)
 
 
 def product(sources, starts, size, columns, split, keep, *after):

time: 51.9 us -> 52.3 us (level)
  no operation moved by 1% of the time
where the time goes in v12:
time: 52.3 us; the launch traced here: 52.1 us
  Pallas kernels  21.6 us (41%)
  starting transfers between devices  17 us (33%)
  waiting for transfers between devices  13 us (25%)
    pallas_call x11, Pallas kernels, product(): pl.pallas_call(functools.partial(product_kernel, starts, size, bounds, pa...  16.9 us
    ppermute x14, starting transfers between devices, shards(): sums[way][part] = lax.ppermute(value, ('row', 'col'), ways[way])  15.9 us
    ppermute x14, waiting for transfers between devices, shards(): sums[way][part] = lax.ppermute(value, ('row', 'col'), ways[way])  12.9 us
    pallas_call x2, Pallas kernels, pick(): pl.pallas_call(functools.partial(pick_kernel, starts, size, chunks), out_...  3.77 us
    ppermute x4, starting transfers between devices, fetch(): sources.extend([own, lax.ppermute(own, 'col', swap)])  1.16 us
  transfers between devices with their start and end apart: 18, of which 7 were waited for; matrix products, arithmetic and copies ran while one was open for 1% of the time, Pallas kernels for 37%

profile of v12, /device:TPU:0, one launch (start us, length us, event | category | flops | bytes accessed | tf_op | source)
XLA Modules:
  0.0 52.1 jit_solution(8000820593941908111)
XLA Ops:
  0.0 0.0 copy-start
  0.0 1.4 %pick.2.refs_0_ = f32[128,2048]{1,0:T(8,128)S(1)} custom-call(f32[512,2048]{1,0:T(8,128)} %a_ref.3), custom_call_target="tpu_custom_call" | custom-call | bytes 2097152 | tf_op jit(solution)/shard_map/pick/pallas_call | solution.py:70
  1.4 0.5 collective-permute-start
  2.0 2.3 %pick.3 = (f32[128,2048]{1,0:T(8,128)S(1)}, f32[128,2048]{1,0:T(8,128)S(1)}, f32[128,2048]{1,0:T(8,128)S(1)}) custom-call(f32[512,2048]{1,0:T(8,128)} %a_ref.3, f32[128,2048]{1,0:T(8,128)S(1)} %pick.2.refs_0_), custom_call_target="tpu_custom_call" | custom-call | bytes 6291456 | tf_op jit(solution)/shard_map/pick/pallas_call | solution.py:70
  4.3 0.1 collective-permute-start.2
  4.4 0.5 collective-permute-start.3
  4.9 0.1 collective-permute-start.5
  5.0 0.0 collective-permute-done.refs_1_
  5.0 0.0 copy-done
  5.0 1.6 %product.11 = (f32[128,512]{1,0:T(8,128)S(1)}, bf16[2048,512]{1,0:T(8,128)(2,1)S(1)}, bf16[2048,512]{1,0:T(8,128)(2,1)S(1)}, bf16[256,2048]{1,0:T(8,128)(2,1)S(1)}) custom-call(f32[128,2048]{1,0:T(8,128)S(1)} %pick.2.refs_0_, f32[128,2048]{1,0:T(8,128)S(1)} %collective-permute-done.refs_1_, f32[2048,1024]{1,0:T(8,128)S(1)} %copy-done), custom_call_target="tpu_custom_call" | custom-call | flops 805306368 | bytes 5505024 | tf_op jit(solution)/shard_map/product/pallas_call | solution.py:187
  6.6 3.1 %collective-permute-start.1 = (f32[128,512]{1,0:T(8,128)S(1)}, f32[128,512]{1,0:T(8,128)S(1)}, u32[]{:S(2)}, u32[]{:S(2)}) collective-permute-start(f32[128,512]{1,0:T(8,128)S(1)} %get-tuple-element.29.refs_2_), channel_id=1, source_target_pairs={{0,2},{1,5},{4,0},{5,9},{8,4},{9,13},{12,8},{13,15},{14,12},{15,11... | collective-permute-start | bytes 786440 | tf_op jit(solution)/shard_map/ppermute | solution.py:312
  9.7 1.5 %product.12 = (f32[128,512]{1,0:T(8,128)S(1)}, bf16[2048,512]{1,0:T(8,128)(2,1)S(1)}, bf16[2048,512]{1,0:T(8,128)(2,1)S(1)}) custom-call(bf16[256,2048]{1,0:T(8,128)(2,1)S(1)} %get-tuple-element.32.refs_0_, f32[2048,1024]{1,0:T(8,128)S(1)} %copy-done, f32[128,512]{1,0:T(8,128)S(1)} %get-tuple-element.29.refs_2_), custom_call_target="tpu_custom_call" | custom-call | flops 805306368 | bytes 5505024 | tf_op jit(solution)/shard_map/product/pallas_call | solution.py:187
  11.2 0.2 collective-permute-start.14
  11.3 0.0 collective-permute-done.2.refs_3_
  11.3 1.1 %product.13 = (f32[128,512]{1,0:T(8,128)S(1)}, bf16[256,2048]{1,0:T(8,128)(2,1)S(1)}) custom-call(f32[128,2048]{1,0:T(8,128)S(1)} %pick.2.refs_0_, f32[128,2048]{1,0:T(8,128)S(1)} %collective-permute-done.refs_1_, f32[128,2048]{1,0:T(8,128)S(1)} %get-tuple-element.30.refs_2_, f32[128,2048]{1,0:T(8,128)S(1)} %collective-permute-done.2.refs_3_, ...), custom_call_target="tpu_custom_call" | custom-call | flops 805306368 | bytes 5505024 | tf_op jit(solution)/shard_map/product/pallas_call | solution.py:187
  12.4 2.0 %collective-permute-start.11 = (f32[128,512]{1,0:T(8,128)S(1)}, f32[128,512]{1,0:T(8,128)S(1)}, u32[]{:S(2)}, u32[]{:S(2)}) collective-permute-start(f32[128,512]{1,0:T(8,128)S(1)} %get-tuple-element.39.refs_8_), channel_id=1, source_target_pairs={{0,2},{1,5},{4,0},{5,9},{8,4},{9,13},{12,8},{13,15},{14,12},{15,11... | collective-permute-start | bytes 786440 | tf_op jit(solution)/shard_map/ppermute | solution.py:312
  14.4 0.0 collective-permute-done.3.refs_5_
  14.4 1.1 %product.14 = (f32[128,512]{1,0:T(8,128)S(1)}, bf16[256,2048]{1,0:T(8,128)(2,1)S(1)}) custom-call(f32[128,2048]{1,0:T(8,128)S(1)} %pick.2.refs_0_, f32[128,2048]{1,0:T(8,128)S(1)} %collective-permute-done.refs_1_, f32[128,2048]{1,0:T(8,128)S(1)} %get-tuple-element.30.refs_2_, f32[128,2048]{1,0:T(8,128)S(1)} %collective-permute-done.2.refs_3_, ...), custom_call_target="tpu_custom_call" | custom-call | flops 805306368 | bytes 5505024 | tf_op jit(solution)/shard_map/product/pallas_call | solution.py:187
  15.4 0.2 collective-permute-start.8
  15.7 1.0 %product.15.refs_3_ = f32[128,512]{1,0:T(8,128)S(1)} custom-call(bf16[256,2048]{1,0:T(8,128)(2,1)S(1)} %get-tuple-element.36.refs_0_, bf16[2048,512]{1,0:T(8,128)(2,1)S(1)} %get-tuple-element.37.refs_6_.refs_1_.refs_8_, bf16[2048,512]{1,0:T(8,128)(2,1)S(1)} %get-tuple-element.38.refs_7_.refs_2_.refs_9_, f32[128,512]{1,0:T(8,128)S(1)} %get-tuple-element.40.refs_3_), custom_call_target="tpu_custom_call" | custom-call | flops 805306368 | bytes 5505024 | tf_op jit(solution)/shard_map/product/pallas_call | solution.py:187
  16.6 1.0 %product.16.refs_12_ = f32[128,512]{1,0:T(8,128)S(1)} custom-call(bf16[256,2048]{1,0:T(8,128)(2,1)S(1)} %get-tuple-element.42.refs_0_, bf16[2048,512]{1,0:T(8,128)(2,1)S(1)} %get-tuple-element.33.refs_5_.refs_1_.refs_10_, bf16[2048,512]{1,0:T(8,128)(2,1)S(1)} %get-tuple-element.34.refs_6_.refs_2_.refs_11_, f32[128,512]{1,0:T(8,128)S(1)} %product.15.refs_3_), custom_call_target="tpu_custom_call" | custom-call | flops 805306368 | bytes 5505024 | tf_op jit(solution)/shard_map/product/pallas_call | solution.py:187
  17.6 0.0 collective-permute-done.1
  17.7 1.9 %collective-permute-start.4 = (f32[128,512]{1,0:T(8,128)S(1)}, f32[128,512]{1,0:T(8,128)S(1)}, u32[]{:S(2)}, u32[]{:S(2)}) collective-permute-start(f32[128,512]{1,0:T(8,128)S(1)} %add.30), channel_id=1, source_target_pairs={{0,2},{1,5},{4,0},{5,9},{8,4},{9,13},{12,8},{13,15},{14,12},{15,11... | collective-permute-start | bytes 786440 | tf_op jit(solution)/shard_map/ppermute | solution.py:312
  19.6 0.7 %collective-permute-done.14 = f32[128,512]{1,0:T(8,128)S(1)} collective-permute-done((f32[128,512]{1,0:T(8,128)S(1)}, f32[128,512]{1,0:T(8,128)S(1)}, u32[]{:S(2)}, u32[]{:S(2)}) %collective-permute-start.14) | collective-permute-done | bytes 262176 | tf_op jit(solution)/shard_map/ppermute | solution.py:312
  20.3 0.1 collective-permute-start.15
  20.4 0.0 collective-permute-done.5.refs_7_
  20.4 1.9 %product.17 = (f32[128,512]{1,0:T(8,128)S(1)}, f32[128,512]{1,0:T(8,128)S(1)}) custom-call(f32[128,2048]{1,0:T(8,128)S(1)} %pick.2.refs_0_, f32[128,2048]{1,0:T(8,128)S(1)} %collective-permute-done.refs_1_, f32[128,2048]{1,0:T(8,128)S(1)} %get-tuple-element.30.refs_2_, f32[128,2048]{1,0:T(8,128)S(1)} %collective-permute-done.2.refs_3_, ...), custom_call_target="tpu_custom_call" | custom-call | flops 1610612736 | bytes 9961472 | tf_op jit(solution)/shard_map/product/pallas_call | solution.py:187
  22.3 1.9 %product.18 = (f32[128,512]{1,0:T(8,128)S(1)}, f32[128,512]{1,0:T(8,128)S(1)}) custom-call(f32[128,2048]{1,0:T(8,128)S(1)} %pick.2.refs_0_, f32[128,2048]{1,0:T(8,128)S(1)} %collective-permute-done.refs_1_, f32[128,2048]{1,0:T(8,128)S(1)} %get-tuple-element.30.refs_2_, f32[128,2048]{1,0:T(8,128)S(1)} %collective-permute-done.2.refs_3_, ...), custom_call_target="tpu_custom_call" | custom-call | flops 1610612736 | bytes 9961472 | tf_op jit(solution)/shard_map/product/pallas_call | solution.py:187
  24.3 1.6 %collective-permute-done.8 = f32[128,512]{1,0:T(8,128)S(1)} collective-permute-done((f32[128,512]{1,0:T(8,128)S(1)}, f32[128,512]{1,0:T(8,128)S(1)}, u32[]{:S(2)}, u32[]{:S(2)}) %collective-permute-start.8) | collective-permute-done | bytes 262176 | tf_op jit(solution)/shard_map/ppermute | solution.py:312
  25.9 0.1 collective-permute-start.9
  26.0 0.0 collective-permute-done.11
  26.1 2.1 %collective-permute-start.12 = (f32[128,512]{1,0:T(8,128)S(1)}, f32[128,512]{1,0:T(8,128)S(1)}, u32[]{:S(2)}, u32[]{:S(2)}) collective-permute-start(f32[128,512]{1,0:T(8,128)S(1)} %add.35), channel_id=1, source_target_pairs={{0,2},{1,5},{4,0},{5,9},{8,4},{9,13},{12,8},{13,15},{14,12},{15,11... | collective-permute-start | bytes 786440 | tf_op jit(solution)/shard_map/ppermute | solution.py:312
  28.1 0.0 collective-permute-done.4
  28.2 1.6 %collective-permute-start.6 = (f32[128,512]{1,0:T(8,128)S(1)}, f32[128,512]{1,0:T(8,128)S(1)}, u32[]{:S(2)}, u32[]{:S(2)}) collective-permute-start(f32[128,512]{1,0:T(8,128)S(1)} %add.31), channel_id=1, source_target_pairs={{0,2},{1,5},{4,0},{5,9},{8,4},{9,13},{12,8},{13,15},{14,12},{15,11... | collective-permute-start | bytes 786440 | tf_op jit(solution)/shard_map/ppermute | solution.py:312
  29.8 0.0 collective-permute-done.15
  29.8 0.5 collective-permute-start.16
  30.3 1.9 %product.19 = (f32[128,512]{1,0:T(8,128)S(1)}, f32[128,512]{1,0:T(8,128)S(1)}) custom-call(f32[128,2048]{1,0:T(8,128)S(1)} %pick.2.refs_0_, f32[128,2048]{1,0:T(8,128)S(1)} %collective-permute-done.refs_1_, f32[128,2048]{1,0:T(8,128)S(1)} %get-tuple-element.30.refs_2_, f32[128,2048]{1,0:T(8,128)S(1)} %collective-permute-done.2.refs_3_, ...), custom_call_target="tpu_custom_call" | custom-call | flops 1610612736 | bytes 9961472 | tf_op jit(solution)/shard_map/product/pallas_call | solution.py:187
  32.2 2.1 %product.20 = (f32[128,512]{1,0:T(8,128)S(1)}, f32[128,512]{1,0:T(8,128)S(1)}) custom-call(f32[128,2048]{1,0:T(8,128)S(1)} %pick.2.refs_0_, f32[128,2048]{1,0:T(8,128)S(1)} %collective-permute-done.refs_1_, f32[128,2048]{1,0:T(8,128)S(1)} %get-tuple-element.30.refs_2_, f32[128,2048]{1,0:T(8,128)S(1)} %collective-permute-done.2.refs_3_, ...), custom_call_target="tpu_custom_call" | custom-call | flops 1610612736 | bytes 9961472 | tf_op jit(solution)/shard_map/product/pallas_call | solution.py:187
  34.3 1.1 %collective-permute-done.9 = f32[128,512]{1,0:T(8,128)S(1)} collective-permute-done((f32[128,512]{1,0:T(8,128)S(1)}, f32[128,512]{1,0:T(8,128)S(1)}, u32[]{:S(2)}, u32[]{:S(2)}) %collective-permute-start.9) | collective-permute-done | bytes 262176 | tf_op jit(solution)/shard_map/ppermute | solution.py:312
  35.4 0.5 collective-permute-start.10
  35.9 0.0 collective-permute-done.12
  36.0 1.6 %collective-permute-start.13 = (f32[128,512]{1,0:T(8,128)S(1)}, f32[128,512]{1,0:T(8,128)S(1)}, u32[]{:S(2)}, u32[]{:S(2)}) collective-permute-start(f32[128,512]{1,0:T(8,128)S(1)} %add.36), channel_id=1, source_target_pairs={{0,2},{1,5},{4,0},{5,9},{8,4},{9,13},{12,8},{13,15},{14,12},{15,11... | collective-permute-start | bytes 786440 | tf_op jit(solution)/shard_map/ppermute | solution.py:312
  37.6 3.4 %collective-permute-done.6 = f32[128,512]{1,0:T(8,128)S(1)} collective-permute-done((f32[128,512]{1,0:T(8,128)S(1)}, f32[128,512]{1,0:T(8,128)S(1)}, u32[]{:S(2)}, u32[]{:S(2)}) %collective-permute-start.6) | collective-permute-done | bytes 262176 | tf_op jit(solution)/shard_map/ppermute | solution.py:312
  41.0 2.1 %collective-permute-start.7 = (f32[128,512]{1,0:T(8,128)S(1)}, f32[128,512]{1,0:T(8,128)S(1)}, u32[]{:S(2)}, u32[]{:S(2)}) collective-permute-start(f32[128,512]{1,0:T(8,128)S(1)} %add.32), channel_id=1, source_target_pairs={{0,2},{1,5},{4,0},{5,9},{8,4},{9,13},{12,8},{13,15},{14,12},{15,11... | collective-permute-start | bytes 786440 | tf_op jit(solution)/shard_map/ppermute | solution.py:312
  43.1 0.0 collective-permute-done.16
  43.1 0.1 collective-permute-start.17
  43.2 1.9 %product.21 = (f32[128,512]{1,0:T(8,128)S(1)}, f32[128,512]{1,0:T(8,128)S(1)}) custom-call(f32[128,2048]{1,0:T(8,128)S(1)} %pick.2.refs_0_, f32[128,2048]{1,0:T(8,128)S(1)} %collective-permute-done.refs_1_, f32[128,2048]{1,0:T(8,128)S(1)} %get-tuple-element.30.refs_2_, f32[128,2048]{1,0:T(8,128)S(1)} %collective-permute-done.2.refs_3_, ...), custom_call_target="tpu_custom_call" | custom-call | flops 1610612736 | bytes 9961472 | tf_op jit(solution)/shard_map/product/pallas_call | solution.py:187
  45.1 1.5 %collective-permute-done.10.refs_1_ = f32[128,512]{1,0:T(8,128)S(1)} collective-permute-done((f32[128,512]{1,0:T(8,128)S(1)}, f32[128,512]{1,0:T(8,128)S(1)}, u32[]{:S(2)}, u32[]{:S(2)}) %collective-permute-start.10) | collective-permute-done | bytes 262176 | tf_op jit(solution)/shard_map/ppermute | solution.py:312
  46.6 0.0 collective-permute-done.13.refs_3_
  46.6 4.0 %collective-permute-done.7.refs_0_ = f32[128,512]{1,0:T(8,128)S(1)} collective-permute-done((f32[128,512]{1,0:T(8,128)S(1)}, f32[128,512]{1,0:T(8,128)S(1)}, u32[]{:S(2)}, u32[]{:S(2)}) %collective-permute-start.7) | collective-permute-done | bytes 262176 | tf_op jit(solution)/shard_map/ppermute | solution.py:312
  50.6 0.7 %collective-permute-done.17.refs_4_ = f32[128,512]{1,0:T(8,128)S(1)} collective-permute-done((f32[128,512]{1,0:T(8,128)S(1)}, f32[128,512]{1,0:T(8,128)S(1)}, u32[]{:S(2)}, u32[]{:S(2)}) %collective-permute-start.17) | collective-permute-done | bytes 262176 | tf_op jit(solution)/shard_map/ppermute | solution.py:312
  51.3 0.9 %finish.1 = f32[128,1024]{1,0:T(8,128)} custom-call(f32[128,512]{1,0:T(8,128)S(1)} %collective-permute-done.7.refs_0_, f32[128,512]{1,0:T(8,128)S(1)} %collective-permute-done.10.refs_1_, f32[128,512]{1,0:T(8,128)S(1)} %get-tuple-element.47.refs_2_, f32[128,512]{1,0:T(8,128)S(1)} %collective-permute-done.13.refs_3_, ...), custom_call_target="tpu_custom_call" | custom-call | tf_op jit(solution)/shard_map/finish/pallas_call | solution.py:214
  (10 shorter events, 0.4 us)
Async XLA Ops:
  0.0 5.0 %copy-start = (f32[2048,1024]{1,0:T(8,128)S(1)}, f32[2048,1024]{1,0:T(8,128)}, u32[]{:S(2)}) copy-start(f32[2048,1024]{1,0:T(8,128)} %refs_1_.1) | copy-start | bytes 25165828
  1.4 3.5 %collective-permute-start = (f32[128,2048]{1,0:T(8,128)S(1)}, f32[128,2048]{1,0:T(8,128)S(1)}, u32[]{:S(2)}, u32[]{:S(2)}) collective-permute-start(f32[128,2048]{1,0:T(8,128)S(1)} %pick.2.refs_0_), channel_id=1, source_target_pairs={{0,1},{1,0},{2,3},{3,2},{4,5},{5,4},{6,7},{7,6},{8,9},{9,8},{10,11... | collective-permute-start | bytes 3145736 | tf_op jit(solution)/shard_map/ppermute | solution.py:276
  4.3 7.0 %collective-permute-start.2 = (f32[128,2048]{1,0:T(8,128)S(1)}, f32[128,2048]{1,0:T(8,128)S(1)}, u32[]{:S(2)}, u32[]{:S(2)}) collective-permute-start(f32[128,2048]{1,0:T(8,128)S(1)} %get-tuple-element.30.refs_2_), channel_id=1, source_target_pairs={{0,1},{1,0},{2,3},{3,2},{4,5},{5,4},{6,7},{7,6},{8,9},{9,8},{10,11... | collective-permute-start | bytes 3145736 | tf_op jit(solution)/shard_map/ppermute | solution.py:276
  4.4 10.0 %collective-permute-start.3 = (f32[128,2048]{1,0:T(8,128)S(1)}, f32[128,2048]{1,0:T(8,128)S(1)}, u32[]{:S(2)}, u32[]{:S(2)}) collective-permute-start(f32[128,2048]{1,0:T(8,128)S(1)} %get-tuple-element.31.refs_4_), channel_id=1, source_target_pairs={{0,1},{1,0},{2,3},{3,2},{4,5},{5,4},{6,7},{7,6},{8,9},{9,8},{10,11... | collective-permute-start | bytes 3145736 | tf_op jit(solution)/shard_map/ppermute | solution.py:276
  4.9 15.5 %collective-permute-start.5 = (f32[128,2048]{1,0:T(8,128)S(1)}, f32[128,2048]{1,0:T(8,128)S(1)}, u32[]{:S(2)}, u32[]{:S(2)}) collective-permute-start(f32[128,2048]{1,0:T(8,128)S(1)} %get-tuple-element.41.refs_6_), channel_id=1, source_target_pairs={{0,1},{1,0},{2,3},{3,2},{4,5},{5,4},{6,7},{7,6},{8,9},{9,8},{10,11... | collective-permute-start | bytes 3145736 | tf_op jit(solution)/shard_map/ppermute | solution.py:276
  6.6 11.0 %collective-permute-start.1 = (f32[128,512]{1,0:T(8,128)S(1)}, f32[128,512]{1,0:T(8,128)S(1)}, u32[]{:S(2)}, u32[]{:S(2)}) collective-permute-start(f32[128,512]{1,0:T(8,128)S(1)} %get-tuple-element.29.refs_2_), channel_id=1, source_target_pairs={{0,2},{1,5},{4,0},{5,9},{8,4},{9,13},{12,8},{13,15},{14,12},{15,11... | collective-permute-start | bytes 786440 | tf_op jit(solution)/shard_map/ppermute | solution.py:312
  11.2 9.1 %collective-permute-start.14 = (f32[128,512]{1,0:T(8,128)S(1)}, f32[128,512]{1,0:T(8,128)S(1)}, u32[]{:S(2)}, u32[]{:S(2)}) collective-permute-start(f32[128,512]{1,0:T(8,128)S(1)} %get-tuple-element.35.refs_7_), channel_id=1, source_target_pairs={{0,4},{1,3},{4,8},{5,1},{8,12},{9,5},{12,14},{13,9},{14,10},{15,13... | collective-permute-start | bytes 786440 | tf_op jit(solution)/shard_map/ppermute | solution.py:312
  12.4 13.6 %collective-permute-start.11 = (f32[128,512]{1,0:T(8,128)S(1)}, f32[128,512]{1,0:T(8,128)S(1)}, u32[]{:S(2)}, u32[]{:S(2)}) collective-permute-start(f32[128,512]{1,0:T(8,128)S(1)} %get-tuple-element.39.refs_8_), channel_id=1, source_target_pairs={{0,2},{1,5},{4,0},{5,9},{8,4},{9,13},{12,8},{13,15},{14,12},{15,11... | collective-permute-start | bytes 786440 | tf_op jit(solution)/shard_map/ppermute | solution.py:312
  15.4 10.5 %collective-permute-start.8 = (f32[128,512]{1,0:T(8,128)S(1)}, f32[128,512]{1,0:T(8,128)S(1)}, u32[]{:S(2)}, u32[]{:S(2)}) collective-permute-start(f32[128,512]{1,0:T(8,128)S(1)} %get-tuple-element.40.refs_3_), channel_id=1, source_target_pairs={{0,4},{1,3},{4,8},{5,1},{8,12},{9,5},{12,14},{13,9},{14,10},{15,13... | collective-permute-start | bytes 786440 | tf_op jit(solution)/shard_map/ppermute | solution.py:312
  17.7 10.5 %collective-permute-start.4 = (f32[128,512]{1,0:T(8,128)S(1)}, f32[128,512]{1,0:T(8,128)S(1)}, u32[]{:S(2)}, u32[]{:S(2)}) collective-permute-start(f32[128,512]{1,0:T(8,128)S(1)} %add.30), channel_id=1, source_target_pairs={{0,2},{1,5},{4,0},{5,9},{8,4},{9,13},{12,8},{13,15},{14,12},{15,11... | collective-permute-start | bytes 786440 | tf_op jit(solution)/shard_map/ppermute | solution.py:312
  20.3 9.5 %collective-permute-start.15 = (f32[128,512]{1,0:T(8,128)S(1)}, f32[128,512]{1,0:T(8,128)S(1)}, u32[]{:S(2)}, u32[]{:S(2)}) collective-permute-start(f32[128,512]{1,0:T(8,128)S(1)} %add.37), channel_id=1, source_target_pairs={{0,4},{1,3},{4,8},{5,1},{8,12},{9,5},{12,14},{13,9},{14,10},{15,13... | collective-permute-start | bytes 786440 | tf_op jit(solution)/shard_map/ppermute | solution.py:312
  25.9 9.5 %collective-permute-start.9 = (f32[128,512]{1,0:T(8,128)S(1)}, f32[128,512]{1,0:T(8,128)S(1)}, u32[]{:S(2)}, u32[]{:S(2)}) collective-permute-start(f32[128,512]{1,0:T(8,128)S(1)} %add.33), channel_id=1, source_target_pairs={{0,4},{1,3},{4,8},{5,1},{8,12},{9,5},{12,14},{13,9},{14,10},{15,13... | collective-permute-start | bytes 786440 | tf_op jit(solution)/shard_map/ppermute | solution.py:312
  26.1 9.9 %collective-permute-start.12 = (f32[128,512]{1,0:T(8,128)S(1)}, f32[128,512]{1,0:T(8,128)S(1)}, u32[]{:S(2)}, u32[]{:S(2)}) collective-permute-start(f32[128,512]{1,0:T(8,128)S(1)} %add.35), channel_id=1, source_target_pairs={{0,2},{1,5},{4,0},{5,9},{8,4},{9,13},{12,8},{13,15},{14,12},{15,11... | collective-permute-start | bytes 786440 | tf_op jit(solution)/shard_map/ppermute | solution.py:312
  28.2 12.8 %collective-permute-start.6 = (f32[128,512]{1,0:T(8,128)S(1)}, f32[128,512]{1,0:T(8,128)S(1)}, u32[]{:S(2)}, u32[]{:S(2)}) collective-permute-start(f32[128,512]{1,0:T(8,128)S(1)} %add.31), channel_id=1, source_target_pairs={{0,2},{1,5},{4,0},{5,9},{8,4},{9,13},{12,8},{13,15},{14,12},{15,11... | collective-permute-start | bytes 786440 | tf_op jit(solution)/shard_map/ppermute | solution.py:312
  29.8 13.2 %collective-permute-start.16 = (f32[128,512]{1,0:T(8,128)S(1)}, f32[128,512]{1,0:T(8,128)S(1)}, u32[]{:S(2)}, u32[]{:S(2)}) collective-permute-start(f32[128,512]{1,0:T(8,128)S(1)} %add.38), channel_id=1, source_target_pairs={{0,4},{1,3},{4,8},{5,1},{8,12},{9,5},{12,14},{13,9},{14,10},{15,13... | collective-permute-start | bytes 786440 | tf_op jit(solution)/shard_map/ppermute | solution.py:312
  35.4 11.2 %collective-permute-start.10 = (f32[128,512]{1,0:T(8,128)S(1)}, f32[128,512]{1,0:T(8,128)S(1)}, u32[]{:S(2)}, u32[]{:S(2)}) collective-permute-start(f32[128,512]{1,0:T(8,128)S(1)} %add.34), channel_id=1, source_target_pairs={{0,4},{1,3},{4,8},{5,1},{8,12},{9,5},{12,14},{13,9},{14,10},{15,13... | collective-permute-start | bytes 786440 | tf_op jit(solution)/shard_map/ppermute | solution.py:312
  36.0 10.7 %collective-permute-start.13 = (f32[128,512]{1,0:T(8,128)S(1)}, f32[128,512]{1,0:T(8,128)S(1)}, u32[]{:S(2)}, u32[]{:S(2)}) collective-permute-start(f32[128,512]{1,0:T(8,128)S(1)} %add.36), channel_id=1, source_target_pairs={{0,2},{1,5},{4,0},{5,9},{8,4},{9,13},{12,8},{13,15},{14,12},{15,11... | collective-permute-start | bytes 786440 | tf_op jit(solution)/shard_map/ppermute | solution.py:312
  41.0 9.6 %collective-permute-start.7 = (f32[128,512]{1,0:T(8,128)S(1)}, f32[128,512]{1,0:T(8,128)S(1)}, u32[]{:S(2)}, u32[]{:S(2)}) collective-permute-start(f32[128,512]{1,0:T(8,128)S(1)} %add.32), channel_id=1, source_target_pairs={{0,2},{1,5},{4,0},{5,9},{8,4},{9,13},{12,8},{13,15},{14,12},{15,11... | collective-permute-start | bytes 786440 | tf_op jit(solution)/shard_map/ppermute | solution.py:312
  43.1 8.2 %collective-permute-start.17 = (f32[128,512]{1,0:T(8,128)S(1)}, f32[128,512]{1,0:T(8,128)S(1)}, u32[]{:S(2)}, u32[]{:S(2)}) collective-permute-start(f32[128,512]{1,0:T(8,128)S(1)} %add.39), channel_id=1, source_target_pairs={{0,4},{1,3},{4,8},{5,1},{8,12},{9,5},{12,14},{13,9},{14,10},{15,13... | collective-permute-start | bytes 786440 | tf_op jit(solution)/shard_map/ppermute | solution.py:312

commit v13 on v10

--- a/solution.py
+++ b/solution.py
@@ -9,7 +9,7 @@
 from jax.sharding import PartitionSpec as P
 
 CALLS = 8
-LANES = 256
+LANES = 512
 PIECE = 16
 MIB = 2**20
 

time: 51.9 us -> 51.6 us (level)
  transfers between devices with their start and end apart: 18 -> 18, of which waited for: 7 -> 7; matrix products, arithmetic and copies ran while one was open for 1% -> 1% of each run, Pallas kernels for 37% -> 36%
where the time goes in v13:
time: 51.6 us; the launch traced here: 51.5 us
  Pallas kernels  20.9 us (41%)
  starting transfers between devices  17 us (33%)
  waiting for transfers between devices  12.9 us (25%)
    pallas_call x11, Pallas kernels, product(): pl.pallas_call(functools.partial(product_kernel, starts, size, bounds, pa...  16.3 us
    ppermute x14, starting transfers between devices, shards(): sums[way][part] = lax.ppermute(value, ('row', 'col'), ways[way])  15.9 us
    ppermute x14, waiting for transfers between devices, shards(): sums[way][part] = lax.ppermute(value, ('row', 'col'), ways[way])  12.9 us
    pallas_call x2, Pallas kernels, pick(): pl.pallas_call(functools.partial(pick_kernel, starts, size, chunks), out_...  3.77 us
    ppermute x4, starting transfers between devices, fetch(): sources.extend([own, lax.ppermute(own, 'col', swap)])  1.16 us
  transfers between devices with their start and end apart: 18, of which 7 were waited for; matrix products, arithmetic and copies ran while one was open for 1% of the time, Pallas kernels for 36%

profile of v13, /device:TPU:0, one launch (start us, length us, event | category | flops | bytes accessed | tf_op | source)
XLA Modules:
  0.0 51.5 jit_solution(17707458943980752519)
XLA Ops:
  0.0 0.0 copy-start
  0.0 1.4 %pick.2.refs_0_ = f32[128,2048]{1,0:T(8,128)S(1)} custom-call(f32[512,2048]{1,0:T(8,128)} %a_ref.3), custom_call_target="tpu_custom_call" | custom-call | bytes 2097152 | tf_op jit(solution)/shard_map/pick/pallas_call | solution.py:69
  1.4 0.5 %collective-permute-start = (f32[128,2048]{1,0:T(8,128)S(1)}, f32[128,2048]{1,0:T(8,128)S(1)}, u32[]{:S(2)}, u32[]{:S(2)}) collective-permute-start(f32[128,2048]{1,0:T(8,128)S(1)} %pick.2.refs_0_), channel_id=1, source_target_pairs={{0,1},{1,0},{2,3},{3,2},{4,5},{5,4},{6,7},{7,6},{8,9},{9,8},{10,11... | collective-permute-start | bytes 3145736 | tf_op jit(solution)/shard_map/ppermute | solution.py:268
  2.0 2.3 %pick.3 = (f32[128,2048]{1,0:T(8,128)S(1)}, f32[128,2048]{1,0:T(8,128)S(1)}, f32[128,2048]{1,0:T(8,128)S(1)}) custom-call(f32[512,2048]{1,0:T(8,128)} %a_ref.3, f32[128,2048]{1,0:T(8,128)S(1)} %pick.2.refs_0_), custom_call_target="tpu_custom_call" | custom-call | bytes 6291456 | tf_op jit(solution)/shard_map/pick/pallas_call | solution.py:69
  4.3 0.1 collective-permute-start.2
  4.4 0.5 collective-permute-start.3
  4.9 0.1 collective-permute-start.5
  5.0 0.0 collective-permute-done.refs_1_
  5.0 0.0 copy-done
  5.0 1.3 %product.11 = (f32[128,512]{1,0:T(8,128)S(1)}, bf16[2048,512]{1,0:T(8,128)(2,1)S(1)}, bf16[2048,512]{1,0:T(8,128)(2,1)S(1)}, bf16[256,2048]{1,0:T(8,128)(2,1)S(1)}) custom-call(f32[128,2048]{1,0:T(8,128)S(1)} %pick.2.refs_0_, f32[128,2048]{1,0:T(8,128)S(1)} %collective-permute-done.refs_1_, f32[2048,1024]{1,0:T(8,128)S(1)} %copy-done), custom_call_target="tpu_custom_call" | custom-call | flops 805306368 | bytes 5505024 | tf_op jit(solution)/shard_map/product/pallas_call | solution.py:179
  6.3 3.0 %collective-permute-start.1 = (f32[128,512]{1,0:T(8,128)S(1)}, f32[128,512]{1,0:T(8,128)S(1)}, u32[]{:S(2)}, u32[]{:S(2)}) collective-permute-start(f32[128,512]{1,0:T(8,128)S(1)} %get-tuple-element.29.refs_2_), channel_id=1, source_target_pairs={{0,2},{1,5},{4,0},{5,9},{8,4},{9,13},{12,8},{13,15},{14,12},{15,11... | collective-permute-start | bytes 786440 | tf_op jit(solution)/shard_map/ppermute | solution.py:304
  9.3 1.2 %product.12 = (f32[128,512]{1,0:T(8,128)S(1)}, bf16[2048,512]{1,0:T(8,128)(2,1)S(1)}, bf16[2048,512]{1,0:T(8,128)(2,1)S(1)}) custom-call(bf16[256,2048]{1,0:T(8,128)(2,1)S(1)} %get-tuple-element.32.refs_0_, f32[2048,1024]{1,0:T(8,128)S(1)} %copy-done, f32[128,512]{1,0:T(8,128)S(1)} %get-tuple-element.29.refs_2_), custom_call_target="tpu_custom_call" | custom-call | flops 805306368 | bytes 5505024 | tf_op jit(solution)/shard_map/product/pallas_call | solution.py:179
  10.5 0.2 collective-permute-start.14
  10.7 0.0 collective-permute-done.2.refs_3_
  10.7 1.1 %product.13 = (f32[128,512]{1,0:T(8,128)S(1)}, bf16[256,2048]{1,0:T(8,128)(2,1)S(1)}) custom-call(f32[128,2048]{1,0:T(8,128)S(1)} %pick.2.refs_0_, f32[128,2048]{1,0:T(8,128)S(1)} %collective-permute-done.refs_1_, f32[128,2048]{1,0:T(8,128)S(1)} %get-tuple-element.30.refs_2_, f32[128,2048]{1,0:T(8,128)S(1)} %collective-permute-done.2.refs_3_, ...), custom_call_target="tpu_custom_call" | custom-call | flops 805306368 | bytes 5505024 | tf_op jit(solution)/shard_map/product/pallas_call | solution.py:179
  11.7 2.0 %collective-permute-start.11 = (f32[128,512]{1,0:T(8,128)S(1)}, f32[128,512]{1,0:T(8,128)S(1)}, u32[]{:S(2)}, u32[]{:S(2)}) collective-permute-start(f32[128,512]{1,0:T(8,128)S(1)} %get-tuple-element.39.refs_8_), channel_id=1, source_target_pairs={{0,2},{1,5},{4,0},{5,9},{8,4},{9,13},{12,8},{13,15},{14,12},{15,11... | collective-permute-start | bytes 786440 | tf_op jit(solution)/shard_map/ppermute | solution.py:304
  13.7 0.0 collective-permute-done.3.refs_5_
  13.7 1.1 %product.14 = (f32[128,512]{1,0:T(8,128)S(1)}, bf16[256,2048]{1,0:T(8,128)(2,1)S(1)}) custom-call(f32[128,2048]{1,0:T(8,128)S(1)} %pick.2.refs_0_, f32[128,2048]{1,0:T(8,128)S(1)} %collective-permute-done.refs_1_, f32[128,2048]{1,0:T(8,128)S(1)} %get-tuple-element.30.refs_2_, f32[128,2048]{1,0:T(8,128)S(1)} %collective-permute-done.2.refs_3_, ...), custom_call_target="tpu_custom_call" | custom-call | flops 805306368 | bytes 5505024 | tf_op jit(solution)/shard_map/product/pallas_call | solution.py:179
  14.8 0.2 collective-permute-start.8
  15.0 1.0 %product.15.refs_3_ = f32[128,512]{1,0:T(8,128)S(1)} custom-call(bf16[256,2048]{1,0:T(8,128)(2,1)S(1)} %get-tuple-element.36.refs_0_, bf16[2048,512]{1,0:T(8,128)(2,1)S(1)} %get-tuple-element.37.refs_6_.refs_1_.refs_8_, bf16[2048,512]{1,0:T(8,128)(2,1)S(1)} %get-tuple-element.38.refs_7_.refs_2_.refs_9_, f32[128,512]{1,0:T(8,128)S(1)} %get-tuple-element.40.refs_3_), custom_call_target="tpu_custom_call" | custom-call | flops 805306368 | bytes 5505024 | tf_op jit(solution)/shard_map/product/pallas_call | solution.py:179
  16.0 1.0 %product.16.refs_12_ = f32[128,512]{1,0:T(8,128)S(1)} custom-call(bf16[256,2048]{1,0:T(8,128)(2,1)S(1)} %get-tuple-element.42.refs_0_, bf16[2048,512]{1,0:T(8,128)(2,1)S(1)} %get-tuple-element.33.refs_5_.refs_1_.refs_10_, bf16[2048,512]{1,0:T(8,128)(2,1)S(1)} %get-tuple-element.34.refs_6_.refs_2_.refs_11_, f32[128,512]{1,0:T(8,128)S(1)} %product.15.refs_3_), custom_call_target="tpu_custom_call" | custom-call | flops 805306368 | bytes 5505024 | tf_op jit(solution)/shard_map/product/pallas_call | solution.py:179
  17.0 0.0 collective-permute-done.1
  17.0 1.9 %collective-permute-start.4 = (f32[128,512]{1,0:T(8,128)S(1)}, f32[128,512]{1,0:T(8,128)S(1)}, u32[]{:S(2)}, u32[]{:S(2)}) collective-permute-start(f32[128,512]{1,0:T(8,128)S(1)} %add.30), channel_id=1, source_target_pairs={{0,2},{1,5},{4,0},{5,9},{8,4},{9,13},{12,8},{13,15},{14,12},{15,11... | collective-permute-start | bytes 786440 | tf_op jit(solution)/shard_map/ppermute | solution.py:304
  18.9 0.7 %collective-permute-done.14 = f32[128,512]{1,0:T(8,128)S(1)} collective-permute-done((f32[128,512]{1,0:T(8,128)S(1)}, f32[128,512]{1,0:T(8,128)S(1)}, u32[]{:S(2)}, u32[]{:S(2)}) %collective-permute-start.14) | collective-permute-done | bytes 262176 | tf_op jit(solution)/shard_map/ppermute | solution.py:304
  19.7 0.1 collective-permute-start.15
  19.7 0.0 collective-permute-done.5.refs_7_
  19.7 1.9 %product.17 = (f32[128,512]{1,0:T(8,128)S(1)}, f32[128,512]{1,0:T(8,128)S(1)}) custom-call(f32[128,2048]{1,0:T(8,128)S(1)} %pick.2.refs_0_, f32[128,2048]{1,0:T(8,128)S(1)} %collective-permute-done.refs_1_, f32[128,2048]{1,0:T(8,128)S(1)} %get-tuple-element.30.refs_2_, f32[128,2048]{1,0:T(8,128)S(1)} %collective-permute-done.2.refs_3_, ...), custom_call_target="tpu_custom_call" | custom-call | flops 1610612736 | bytes 9961472 | tf_op jit(solution)/shard_map/product/pallas_call | solution.py:179
  21.7 1.9 %product.18 = (f32[128,512]{1,0:T(8,128)S(1)}, f32[128,512]{1,0:T(8,128)S(1)}) custom-call(f32[128,2048]{1,0:T(8,128)S(1)} %pick.2.refs_0_, f32[128,2048]{1,0:T(8,128)S(1)} %collective-permute-done.refs_1_, f32[128,2048]{1,0:T(8,128)S(1)} %get-tuple-element.30.refs_2_, f32[128,2048]{1,0:T(8,128)S(1)} %collective-permute-done.2.refs_3_, ...), custom_call_target="tpu_custom_call" | custom-call | flops 1610612736 | bytes 9961472 | tf_op jit(solution)/shard_map/product/pallas_call | solution.py:179
  23.6 1.6 %collective-permute-done.8 = f32[128,512]{1,0:T(8,128)S(1)} collective-permute-done((f32[128,512]{1,0:T(8,128)S(1)}, f32[128,512]{1,0:T(8,128)S(1)}, u32[]{:S(2)}, u32[]{:S(2)}) %collective-permute-start.8) | collective-permute-done | bytes 262176 | tf_op jit(solution)/shard_map/ppermute | solution.py:304
  25.3 0.1 collective-permute-start.9
  25.3 0.0 collective-permute-done.11
  25.4 2.1 %collective-permute-start.12 = (f32[128,512]{1,0:T(8,128)S(1)}, f32[128,512]{1,0:T(8,128)S(1)}, u32[]{:S(2)}, u32[]{:S(2)}) collective-permute-start(f32[128,512]{1,0:T(8,128)S(1)} %add.35), channel_id=1, source_target_pairs={{0,2},{1,5},{4,0},{5,9},{8,4},{9,13},{12,8},{13,15},{14,12},{15,11... | collective-permute-start | bytes 786440 | tf_op jit(solution)/shard_map/ppermute | solution.py:304
  27.4 0.0 collective-permute-done.4
  27.5 2.0 %collective-permute-start.6 = (f32[128,512]{1,0:T(8,128)S(1)}, f32[128,512]{1,0:T(8,128)S(1)}, u32[]{:S(2)}, u32[]{:S(2)}) collective-permute-start(f32[128,512]{1,0:T(8,128)S(1)} %add.31), channel_id=1, source_target_pairs={{0,2},{1,5},{4,0},{5,9},{8,4},{9,13},{12,8},{13,15},{14,12},{15,11... | collective-permute-start | bytes 786440 | tf_op jit(solution)/shard_map/ppermute | solution.py:304
  29.5 0.0 collective-permute-done.15
  29.5 0.1 collective-permute-start.16
  29.7 1.9 %product.19 = (f32[128,512]{1,0:T(8,128)S(1)}, f32[128,512]{1,0:T(8,128)S(1)}) custom-call(f32[128,2048]{1,0:T(8,128)S(1)} %pick.2.refs_0_, f32[128,2048]{1,0:T(8,128)S(1)} %collective-permute-done.refs_1_, f32[128,2048]{1,0:T(8,128)S(1)} %get-tuple-element.30.refs_2_, f32[128,2048]{1,0:T(8,128)S(1)} %collective-permute-done.2.refs_3_, ...), custom_call_target="tpu_custom_call" | custom-call | flops 1610612736 | bytes 9961472 | tf_op jit(solution)/shard_map/product/pallas_call | solution.py:179
  31.6 2.1 %product.20 = (f32[128,512]{1,0:T(8,128)S(1)}, f32[128,512]{1,0:T(8,128)S(1)}) custom-call(f32[128,2048]{1,0:T(8,128)S(1)} %pick.2.refs_0_, f32[128,2048]{1,0:T(8,128)S(1)} %collective-permute-done.refs_1_, f32[128,2048]{1,0:T(8,128)S(1)} %get-tuple-element.30.refs_2_, f32[128,2048]{1,0:T(8,128)S(1)} %collective-permute-done.2.refs_3_, ...), custom_call_target="tpu_custom_call" | custom-call | flops 1610612736 | bytes 9961472 | tf_op jit(solution)/shard_map/product/pallas_call | solution.py:179
  33.7 1.1 %collective-permute-done.9 = f32[128,512]{1,0:T(8,128)S(1)} collective-permute-done((f32[128,512]{1,0:T(8,128)S(1)}, f32[128,512]{1,0:T(8,128)S(1)}, u32[]{:S(2)}, u32[]{:S(2)}) %collective-permute-start.9) | collective-permute-done | bytes 262176 | tf_op jit(solution)/shard_map/ppermute | solution.py:304
  34.8 0.4 collective-permute-start.10
  35.2 0.0 collective-permute-done.12
  35.3 1.7 %collective-permute-start.13 = (f32[128,512]{1,0:T(8,128)S(1)}, f32[128,512]{1,0:T(8,128)S(1)}, u32[]{:S(2)}, u32[]{:S(2)}) collective-permute-start(f32[128,512]{1,0:T(8,128)S(1)} %add.36), channel_id=1, source_target_pairs={{0,2},{1,5},{4,0},{5,9},{8,4},{9,13},{12,8},{13,15},{14,12},{15,11... | collective-permute-start | bytes 786440 | tf_op jit(solution)/shard_map/ppermute | solution.py:304
  37.0 3.3 %collective-permute-done.6 = f32[128,512]{1,0:T(8,128)S(1)} collective-permute-done((f32[128,512]{1,0:T(8,128)S(1)}, f32[128,512]{1,0:T(8,128)S(1)}, u32[]{:S(2)}, u32[]{:S(2)}) %collective-permute-start.6) | collective-permute-done | bytes 262176 | tf_op jit(solution)/shard_map/ppermute | solution.py:304
  40.4 2.1 %collective-permute-start.7 = (f32[128,512]{1,0:T(8,128)S(1)}, f32[128,512]{1,0:T(8,128)S(1)}, u32[]{:S(2)}, u32[]{:S(2)}) collective-permute-start(f32[128,512]{1,0:T(8,128)S(1)} %add.32), channel_id=1, source_target_pairs={{0,2},{1,5},{4,0},{5,9},{8,4},{9,13},{12,8},{13,15},{14,12},{15,11... | collective-permute-start | bytes 786440 | tf_op jit(solution)/shard_map/ppermute | solution.py:304
  42.4 0.0 collective-permute-done.16
  42.4 0.1 collective-permute-start.17
  42.5 1.9 %product.21 = (f32[128,512]{1,0:T(8,128)S(1)}, f32[128,512]{1,0:T(8,128)S(1)}) custom-call(f32[128,2048]{1,0:T(8,128)S(1)} %pick.2.refs_0_, f32[128,2048]{1,0:T(8,128)S(1)} %collective-permute-done.refs_1_, f32[128,2048]{1,0:T(8,128)S(1)} %get-tuple-element.30.refs_2_, f32[128,2048]{1,0:T(8,128)S(1)} %collective-permute-done.2.refs_3_, ...), custom_call_target="tpu_custom_call" | custom-call | flops 1610612736 | bytes 9961472 | tf_op jit(solution)/shard_map/product/pallas_call | solution.py:179
  44.5 1.6 %collective-permute-done.10.refs_1_ = f32[128,512]{1,0:T(8,128)S(1)} collective-permute-done((f32[128,512]{1,0:T(8,128)S(1)}, f32[128,512]{1,0:T(8,128)S(1)}, u32[]{:S(2)}, u32[]{:S(2)}) %collective-permute-start.10) | collective-permute-done | bytes 262176 | tf_op jit(solution)/shard_map/ppermute | solution.py:304
  46.0 0.0 collective-permute-done.13.refs_3_
  46.0 4.3 %collective-permute-done.7.refs_0_ = f32[128,512]{1,0:T(8,128)S(1)} collective-permute-done((f32[128,512]{1,0:T(8,128)S(1)}, f32[128,512]{1,0:T(8,128)S(1)}, u32[]{:S(2)}, u32[]{:S(2)}) %collective-permute-start.7) | collective-permute-done | bytes 262176 | tf_op jit(solution)/shard_map/ppermute | solution.py:304
  50.3 0.3 collective-permute-done.17.refs_4_
  50.6 0.9 %finish.1 = f32[128,1024]{1,0:T(8,128)} custom-call(f32[128,512]{1,0:T(8,128)S(1)} %collective-permute-done.7.refs_0_, f32[128,512]{1,0:T(8,128)S(1)} %collective-permute-done.10.refs_1_, f32[128,512]{1,0:T(8,128)S(1)} %get-tuple-element.47.refs_2_, f32[128,512]{1,0:T(8,128)S(1)} %collective-permute-done.13.refs_3_, ...), custom_call_target="tpu_custom_call" | custom-call | tf_op jit(solution)/shard_map/finish/pallas_call | solution.py:206
  (10 shorter events, 0.4 us)
Async XLA Ops:
  0.0 5.0 %copy-start = (f32[2048,1024]{1,0:T(8,128)S(1)}, f32[2048,1024]{1,0:T(8,128)}, u32[]{:S(2)}) copy-start(f32[2048,1024]{1,0:T(8,128)} %refs_1_.1) | copy-start | bytes 25165828
  1.4 3.5 %collective-permute-start = (f32[128,2048]{1,0:T(8,128)S(1)}, f32[128,2048]{1,0:T(8,128)S(1)}, u32[]{:S(2)}, u32[]{:S(2)}) collective-permute-start(f32[128,2048]{1,0:T(8,128)S(1)} %pick.2.refs_0_), channel_id=1, source_target_pairs={{0,1},{1,0},{2,3},{3,2},{4,5},{5,4},{6,7},{7,6},{8,9},{9,8},{10,11... | collective-permute-start | bytes 3145736 | tf_op jit(solution)/shard_map/ppermute | solution.py:268
  4.3 6.4 %collective-permute-start.2 = (f32[128,2048]{1,0:T(8,128)S(1)}, f32[128,2048]{1,0:T(8,128)S(1)}, u32[]{:S(2)}, u32[]{:S(2)}) collective-permute-start(f32[128,2048]{1,0:T(8,128)S(1)} %get-tuple-element.30.refs_2_), channel_id=1, source_target_pairs={{0,1},{1,0},{2,3},{3,2},{4,5},{5,4},{6,7},{7,6},{8,9},{9,8},{10,11... | collective-permute-start | bytes 3145736 | tf_op jit(solution)/shard_map/ppermute | solution.py:268
  4.4 9.3 %collective-permute-start.3 = (f32[128,2048]{1,0:T(8,128)S(1)}, f32[128,2048]{1,0:T(8,128)S(1)}, u32[]{:S(2)}, u32[]{:S(2)}) collective-permute-start(f32[128,2048]{1,0:T(8,128)S(1)} %get-tuple-element.31.refs_4_), channel_id=1, source_target_pairs={{0,1},{1,0},{2,3},{3,2},{4,5},{5,4},{6,7},{7,6},{8,9},{9,8},{10,11... | collective-permute-start | bytes 3145736 | tf_op jit(solution)/shard_map/ppermute | solution.py:268
  4.9 14.8 %collective-permute-start.5 = (f32[128,2048]{1,0:T(8,128)S(1)}, f32[128,2048]{1,0:T(8,128)S(1)}, u32[]{:S(2)}, u32[]{:S(2)}) collective-permute-start(f32[128,2048]{1,0:T(8,128)S(1)} %get-tuple-element.41.refs_6_), channel_id=1, source_target_pairs={{0,1},{1,0},{2,3},{3,2},{4,5},{5,4},{6,7},{7,6},{8,9},{9,8},{10,11... | collective-permute-start | bytes 3145736 | tf_op jit(solution)/shard_map/ppermute | solution.py:268
  6.3 10.7 %collective-permute-start.1 = (f32[128,512]{1,0:T(8,128)S(1)}, f32[128,512]{1,0:T(8,128)S(1)}, u32[]{:S(2)}, u32[]{:S(2)}) collective-permute-start(f32[128,512]{1,0:T(8,128)S(1)} %get-tuple-element.29.refs_2_), channel_id=1, source_target_pairs={{0,2},{1,5},{4,0},{5,9},{8,4},{9,13},{12,8},{13,15},{14,12},{15,11... | collective-permute-start | bytes 786440 | tf_op jit(solution)/shard_map/ppermute | solution.py:304
  10.5 9.1 %collective-permute-start.14 = (f32[128,512]{1,0:T(8,128)S(1)}, f32[128,512]{1,0:T(8,128)S(1)}, u32[]{:S(2)}, u32[]{:S(2)}) collective-permute-start(f32[128,512]{1,0:T(8,128)S(1)} %get-tuple-element.35.refs_7_), channel_id=1, source_target_pairs={{0,4},{1,3},{4,8},{5,1},{8,12},{9,5},{12,14},{13,9},{14,10},{15,13... | collective-permute-start | bytes 786440 | tf_op jit(solution)/shard_map/ppermute | solution.py:304
  11.7 13.6 %collective-permute-start.11 = (f32[128,512]{1,0:T(8,128)S(1)}, f32[128,512]{1,0:T(8,128)S(1)}, u32[]{:S(2)}, u32[]{:S(2)}) collective-permute-start(f32[128,512]{1,0:T(8,128)S(1)} %get-tuple-element.39.refs_8_), channel_id=1, source_target_pairs={{0,2},{1,5},{4,0},{5,9},{8,4},{9,13},{12,8},{13,15},{14,12},{15,11... | collective-permute-start | bytes 786440 | tf_op jit(solution)/shard_map/ppermute | solution.py:304
  14.8 10.5 %collective-permute-start.8 = (f32[128,512]{1,0:T(8,128)S(1)}, f32[128,512]{1,0:T(8,128)S(1)}, u32[]{:S(2)}, u32[]{:S(2)}) collective-permute-start(f32[128,512]{1,0:T(8,128)S(1)} %get-tuple-element.40.refs_3_), channel_id=1, source_target_pairs={{0,4},{1,3},{4,8},{5,1},{8,12},{9,5},{12,14},{13,9},{14,10},{15,13... | collective-permute-start | bytes 786440 | tf_op jit(solution)/shard_map/ppermute | solution.py:304
  17.0 10.4 %collective-permute-start.4 = (f32[128,512]{1,0:T(8,128)S(1)}, f32[128,512]{1,0:T(8,128)S(1)}, u32[]{:S(2)}, u32[]{:S(2)}) collective-permute-start(f32[128,512]{1,0:T(8,128)S(1)} %add.30), channel_id=1, source_target_pairs={{0,2},{1,5},{4,0},{5,9},{8,4},{9,13},{12,8},{13,15},{14,12},{15,11... | collective-permute-start | bytes 786440 | tf_op jit(solution)/shard_map/ppermute | solution.py:304
  19.7 9.8 %collective-permute-start.15 = (f32[128,512]{1,0:T(8,128)S(1)}, f32[128,512]{1,0:T(8,128)S(1)}, u32[]{:S(2)}, u32[]{:S(2)}) collective-permute-start(f32[128,512]{1,0:T(8,128)S(1)} %add.37), channel_id=1, source_target_pairs={{0,4},{1,3},{4,8},{5,1},{8,12},{9,5},{12,14},{13,9},{14,10},{15,13... | collective-permute-start | bytes 786440 | tf_op jit(solution)/shard_map/ppermute | solution.py:304
  25.3 9.5 %collective-permute-start.9 = (f32[128,512]{1,0:T(8,128)S(1)}, f32[128,512]{1,0:T(8,128)S(1)}, u32[]{:S(2)}, u32[]{:S(2)}) collective-permute-start(f32[128,512]{1,0:T(8,128)S(1)} %add.33), channel_id=1, source_target_pairs={{0,4},{1,3},{4,8},{5,1},{8,12},{9,5},{12,14},{13,9},{14,10},{15,13... | collective-permute-start | bytes 786440 | tf_op jit(solution)/shard_map/ppermute | solution.py:304
  25.4 9.8 %collective-permute-start.12 = (f32[128,512]{1,0:T(8,128)S(1)}, f32[128,512]{1,0:T(8,128)S(1)}, u32[]{:S(2)}, u32[]{:S(2)}) collective-permute-start(f32[128,512]{1,0:T(8,128)S(1)} %add.35), channel_id=1, source_target_pairs={{0,2},{1,5},{4,0},{5,9},{8,4},{9,13},{12,8},{13,15},{14,12},{15,11... | collective-permute-start | bytes 786440 | tf_op jit(solution)/shard_map/ppermute | solution.py:304
  27.5 12.8 %collective-permute-start.6 = (f32[128,512]{1,0:T(8,128)S(1)}, f32[128,512]{1,0:T(8,128)S(1)}, u32[]{:S(2)}, u32[]{:S(2)}) collective-permute-start(f32[128,512]{1,0:T(8,128)S(1)} %add.31), channel_id=1, source_target_pairs={{0,2},{1,5},{4,0},{5,9},{8,4},{9,13},{12,8},{13,15},{14,12},{15,11... | collective-permute-start | bytes 786440 | tf_op jit(solution)/shard_map/ppermute | solution.py:304
  29.5 12.9 %collective-permute-start.16 = (f32[128,512]{1,0:T(8,128)S(1)}, f32[128,512]{1,0:T(8,128)S(1)}, u32[]{:S(2)}, u32[]{:S(2)}) collective-permute-start(f32[128,512]{1,0:T(8,128)S(1)} %add.38), channel_id=1, source_target_pairs={{0,4},{1,3},{4,8},{5,1},{8,12},{9,5},{12,14},{13,9},{14,10},{15,13... | collective-permute-start | bytes 786440 | tf_op jit(solution)/shard_map/ppermute | solution.py:304
  34.8 11.2 %collective-permute-start.10 = (f32[128,512]{1,0:T(8,128)S(1)}, f32[128,512]{1,0:T(8,128)S(1)}, u32[]{:S(2)}, u32[]{:S(2)}) collective-permute-start(f32[128,512]{1,0:T(8,128)S(1)} %add.34), channel_id=1, source_target_pairs={{0,4},{1,3},{4,8},{5,1},{8,12},{9,5},{12,14},{13,9},{14,10},{15,13... | collective-permute-start | bytes 786440 | tf_op jit(solution)/shard_map/ppermute | solution.py:304
  35.3 10.8 %collective-permute-start.13 = (f32[128,512]{1,0:T(8,128)S(1)}, f32[128,512]{1,0:T(8,128)S(1)}, u32[]{:S(2)}, u32[]{:S(2)}) collective-permute-start(f32[128,512]{1,0:T(8,128)S(1)} %add.36), channel_id=1, source_target_pairs={{0,2},{1,5},{4,0},{5,9},{8,4},{9,13},{12,8},{13,15},{14,12},{15,11... | collective-permute-start | bytes 786440 | tf_op jit(solution)/shard_map/ppermute | solution.py:304
  40.4 10.0 %collective-permute-start.7 = (f32[128,512]{1,0:T(8,128)S(1)}, f32[128,512]{1,0:T(8,128)S(1)}, u32[]{:S(2)}, u32[]{:S(2)}) collective-permute-start(f32[128,512]{1,0:T(8,128)S(1)} %add.32), channel_id=1, source_target_pairs={{0,2},{1,5},{4,0},{5,9},{8,4},{9,13},{12,8},{13,15},{14,12},{15,11... | collective-permute-start | bytes 786440 | tf_op jit(solution)/shard_map/ppermute | solution.py:304
  42.4 8.2 %collective-permute-start.17 = (f32[128,512]{1,0:T(8,128)S(1)}, f32[128,512]{1,0:T(8,128)S(1)}, u32[]{:S(2)}, u32[]{:S(2)}) collective-permute-start(f32[128,512]{1,0:T(8,128)S(1)} %add.39), channel_id=1, source_target_pairs={{0,4},{1,3},{4,8},{5,1},{8,12},{9,5},{12,14},{13,9},{14,10},{15,13... | collective-permute-start | bytes 786440 | tf_op jit(solution)/shard_map/ppermute | solution.py:304

commit v14 on v13

--- a/solution.py
+++ b/solution.py
@@ -10,7 +10,7 @@
 
 CALLS = 8
 LANES = 512
-PIECE = 16
+PIECE = 128
 MIB = 2**20
 
 

time: 51.6 us -> 51.6 us (level)
  no operation moved by 1% of the time
where the time goes in v14:
time: 51.6 us; the launch traced here: 51.4 us
  Pallas kernels  20.9 us (41%)
  starting transfers between devices  17 us (33%)
  waiting for transfers between devices  12.9 us (25%)
    pallas_call x11, Pallas kernels, product(): pl.pallas_call(functools.partial(product_kernel, starts, size, bounds, pa...  16.3 us
    ppermute x14, starting transfers between devices, shards(): sums[way][part] = lax.ppermute(value, ('row', 'col'), ways[way])  15.9 us
    ppermute x14, waiting for transfers between devices, shards(): sums[way][part] = lax.ppermute(value, ('row', 'col'), ways[way])  12.9 us
    pallas_call x2, Pallas kernels, pick(): pl.pallas_call(functools.partial(pick_kernel, starts, size, chunks), out_...  3.7 us
    ppermute x4, starting transfers between devices, fetch(): sources.extend([own, lax.ppermute(own, 'col', swap)])  1.16 us
  transfers between devices with their start and end apart: 18, of which 7 were waited for; matrix products, arithmetic and copies ran while one was open for 1% of the time, Pallas kernels for 36%

profile of v14, /device:TPU:0, one launch (start us, length us, event | category | flops | bytes accessed | tf_op | source)
XLA Modules:
  0.0 51.4 jit_solution(2692922025931102179)
XLA Ops:
  0.0 0.0 copy-start
  0.0 1.4 %pick.2.refs_0_ = f32[128,2048]{1,0:T(8,128)S(1)} custom-call(f32[512,2048]{1,0:T(8,128)} %a_ref.3), custom_call_target="tpu_custom_call" | custom-call | bytes 2097152 | tf_op jit(solution)/shard_map/pick/pallas_call | solution.py:69
  1.4 0.5 %collective-permute-start = (f32[128,2048]{1,0:T(8,128)S(1)}, f32[128,2048]{1,0:T(8,128)S(1)}, u32[]{:S(2)}, u32[]{:S(2)}) collective-permute-start(f32[128,2048]{1,0:T(8,128)S(1)} %pick.2.refs_0_), channel_id=1, source_target_pairs={{0,1},{1,0},{2,3},{3,2},{4,5},{5,4},{6,7},{7,6},{8,9},{9,8},{10,11... | collective-permute-start | bytes 3145736 | tf_op jit(solution)/shard_map/ppermute | solution.py:268
  1.9 2.3 %pick.3 = (f32[128,2048]{1,0:T(8,128)S(1)}, f32[128,2048]{1,0:T(8,128)S(1)}, f32[128,2048]{1,0:T(8,128)S(1)}) custom-call(f32[512,2048]{1,0:T(8,128)} %a_ref.3, f32[128,2048]{1,0:T(8,128)S(1)} %pick.2.refs_0_), custom_call_target="tpu_custom_call" | custom-call | bytes 6291456 | tf_op jit(solution)/shard_map/pick/pallas_call | solution.py:69
  4.2 0.1 collective-permute-start.2
  4.3 0.5 collective-permute-start.3
  4.8 0.1 collective-permute-start.5
  4.9 0.0 collective-permute-done.refs_1_
  4.9 0.0 copy-done
  4.9 1.3 %product.11 = (f32[128,512]{1,0:T(8,128)S(1)}, bf16[2048,512]{1,0:T(8,128)(2,1)S(1)}, bf16[2048,512]{1,0:T(8,128)(2,1)S(1)}, bf16[256,2048]{1,0:T(8,128)(2,1)S(1)}) custom-call(f32[128,2048]{1,0:T(8,128)S(1)} %pick.2.refs_0_, f32[128,2048]{1,0:T(8,128)S(1)} %collective-permute-done.refs_1_, f32[2048,1024]{1,0:T(8,128)S(1)} %copy-done), custom_call_target="tpu_custom_call" | custom-call | flops 805306368 | bytes 5505024 | tf_op jit(solution)/shard_map/product/pallas_call | solution.py:179
  6.2 3.0 %collective-permute-start.1 = (f32[128,512]{1,0:T(8,128)S(1)}, f32[128,512]{1,0:T(8,128)S(1)}, u32[]{:S(2)}, u32[]{:S(2)}) collective-permute-start(f32[128,512]{1,0:T(8,128)S(1)} %get-tuple-element.29.refs_2_), channel_id=1, source_target_pairs={{0,2},{1,5},{4,0},{5,9},{8,4},{9,13},{12,8},{13,15},{14,12},{15,11... | collective-permute-start | bytes 786440 | tf_op jit(solution)/shard_map/ppermute | solution.py:304
  9.3 1.2 %product.12 = (f32[128,512]{1,0:T(8,128)S(1)}, bf16[2048,512]{1,0:T(8,128)(2,1)S(1)}, bf16[2048,512]{1,0:T(8,128)(2,1)S(1)}) custom-call(bf16[256,2048]{1,0:T(8,128)(2,1)S(1)} %get-tuple-element.32.refs_0_, f32[2048,1024]{1,0:T(8,128)S(1)} %copy-done, f32[128,512]{1,0:T(8,128)S(1)} %get-tuple-element.29.refs_2_), custom_call_target="tpu_custom_call" | custom-call | flops 805306368 | bytes 5505024 | tf_op jit(solution)/shard_map/product/pallas_call | solution.py:179
  10.4 0.2 collective-permute-start.14
  10.6 0.0 collective-permute-done.2.refs_3_
  10.6 1.1 %product.13 = (f32[128,512]{1,0:T(8,128)S(1)}, bf16[256,2048]{1,0:T(8,128)(2,1)S(1)}) custom-call(f32[128,2048]{1,0:T(8,128)S(1)} %pick.2.refs_0_, f32[128,2048]{1,0:T(8,128)S(1)} %collective-permute-done.refs_1_, f32[128,2048]{1,0:T(8,128)S(1)} %get-tuple-element.30.refs_2_, f32[128,2048]{1,0:T(8,128)S(1)} %collective-permute-done.2.refs_3_, ...), custom_call_target="tpu_custom_call" | custom-call | flops 805306368 | bytes 5505024 | tf_op jit(solution)/shard_map/product/pallas_call | solution.py:179
  11.7 2.0 %collective-permute-start.11 = (f32[128,512]{1,0:T(8,128)S(1)}, f32[128,512]{1,0:T(8,128)S(1)}, u32[]{:S(2)}, u32[]{:S(2)}) collective-permute-start(f32[128,512]{1,0:T(8,128)S(1)} %get-tuple-element.39.refs_8_), channel_id=1, source_target_pairs={{0,2},{1,5},{4,0},{5,9},{8,4},{9,13},{12,8},{13,15},{14,12},{15,11... | collective-permute-start | bytes 786440 | tf_op jit(solution)/shard_map/ppermute | solution.py:304
  13.6 0.0 collective-permute-done.3.refs_5_
  13.6 1.1 %product.14 = (f32[128,512]{1,0:T(8,128)S(1)}, bf16[256,2048]{1,0:T(8,128)(2,1)S(1)}) custom-call(f32[128,2048]{1,0:T(8,128)S(1)} %pick.2.refs_0_, f32[128,2048]{1,0:T(8,128)S(1)} %collective-permute-done.refs_1_, f32[128,2048]{1,0:T(8,128)S(1)} %get-tuple-element.30.refs_2_, f32[128,2048]{1,0:T(8,128)S(1)} %collective-permute-done.2.refs_3_, ...), custom_call_target="tpu_custom_call" | custom-call | flops 805306368 | bytes 5505024 | tf_op jit(solution)/shard_map/product/pallas_call | solution.py:179
  14.7 0.2 collective-permute-start.8
  14.9 1.0 %product.15.refs_3_ = f32[128,512]{1,0:T(8,128)S(1)} custom-call(bf16[256,2048]{1,0:T(8,128)(2,1)S(1)} %get-tuple-element.36.refs_0_, bf16[2048,512]{1,0:T(8,128)(2,1)S(1)} %get-tuple-element.37.refs_6_.refs_1_.refs_8_, bf16[2048,512]{1,0:T(8,128)(2,1)S(1)} %get-tuple-element.38.refs_7_.refs_2_.refs_9_, f32[128,512]{1,0:T(8,128)S(1)} %get-tuple-element.40.refs_3_), custom_call_target="tpu_custom_call" | custom-call | flops 805306368 | bytes 5505024 | tf_op jit(solution)/shard_map/product/pallas_call | solution.py:179
  15.9 1.0 %product.16.refs_12_ = f32[128,512]{1,0:T(8,128)S(1)} custom-call(bf16[256,2048]{1,0:T(8,128)(2,1)S(1)} %get-tuple-element.42.refs_0_, bf16[2048,512]{1,0:T(8,128)(2,1)S(1)} %get-tuple-element.33.refs_5_.refs_1_.refs_10_, bf16[2048,512]{1,0:T(8,128)(2,1)S(1)} %get-tuple-element.34.refs_6_.refs_2_.refs_11_, f32[128,512]{1,0:T(8,128)S(1)} %product.15.refs_3_), custom_call_target="tpu_custom_call" | custom-call | flops 805306368 | bytes 5505024 | tf_op jit(solution)/shard_map/product/pallas_call | solution.py:179
  16.9 0.0 collective-permute-done.1
  16.9 1.9 %collective-permute-start.4 = (f32[128,512]{1,0:T(8,128)S(1)}, f32[128,512]{1,0:T(8,128)S(1)}, u32[]{:S(2)}, u32[]{:S(2)}) collective-permute-start(f32[128,512]{1,0:T(8,128)S(1)} %add.30), channel_id=1, source_target_pairs={{0,2},{1,5},{4,0},{5,9},{8,4},{9,13},{12,8},{13,15},{14,12},{15,11... | collective-permute-start | bytes 786440 | tf_op jit(solution)/shard_map/ppermute | solution.py:304
  18.8 0.7 %collective-permute-done.14 = f32[128,512]{1,0:T(8,128)S(1)} collective-permute-done((f32[128,512]{1,0:T(8,128)S(1)}, f32[128,512]{1,0:T(8,128)S(1)}, u32[]{:S(2)}, u32[]{:S(2)}) %collective-permute-start.14) | collective-permute-done | bytes 262176 | tf_op jit(solution)/shard_map/ppermute | solution.py:304
  19.6 0.1 collective-permute-start.15
  19.7 0.0 collective-permute-done.5.refs_7_
  19.7 1.9 %product.17 = (f32[128,512]{1,0:T(8,128)S(1)}, f32[128,512]{1,0:T(8,128)S(1)}) custom-call(f32[128,2048]{1,0:T(8,128)S(1)} %pick.2.refs_0_, f32[128,2048]{1,0:T(8,128)S(1)} %collective-permute-done.refs_1_, f32[128,2048]{1,0:T(8,128)S(1)} %get-tuple-element.30.refs_2_, f32[128,2048]{1,0:T(8,128)S(1)} %collective-permute-done.2.refs_3_, ...), custom_call_target="tpu_custom_call" | custom-call | flops 1610612736 | bytes 9961472 | tf_op jit(solution)/shard_map/product/pallas_call | solution.py:179
  21.6 1.9 %product.18 = (f32[128,512]{1,0:T(8,128)S(1)}, f32[128,512]{1,0:T(8,128)S(1)}) custom-call(f32[128,2048]{1,0:T(8,128)S(1)} %pick.2.refs_0_, f32[128,2048]{1,0:T(8,128)S(1)} %collective-permute-done.refs_1_, f32[128,2048]{1,0:T(8,128)S(1)} %get-tuple-element.30.refs_2_, f32[128,2048]{1,0:T(8,128)S(1)} %collective-permute-done.2.refs_3_, ...), custom_call_target="tpu_custom_call" | custom-call | flops 1610612736 | bytes 9961472 | tf_op jit(solution)/shard_map/product/pallas_call | solution.py:179
  23.6 1.6 %collective-permute-done.8 = f32[128,512]{1,0:T(8,128)S(1)} collective-permute-done((f32[128,512]{1,0:T(8,128)S(1)}, f32[128,512]{1,0:T(8,128)S(1)}, u32[]{:S(2)}, u32[]{:S(2)}) %collective-permute-start.8) | collective-permute-done | bytes 262176 | tf_op jit(solution)/shard_map/ppermute | solution.py:304
  25.2 0.1 collective-permute-start.9
  25.3 0.0 collective-permute-done.11
  25.3 2.1 %collective-permute-start.12 = (f32[128,512]{1,0:T(8,128)S(1)}, f32[128,512]{1,0:T(8,128)S(1)}, u32[]{:S(2)}, u32[]{:S(2)}) collective-permute-start(f32[128,512]{1,0:T(8,128)S(1)} %add.35), channel_id=1, source_target_pairs={{0,2},{1,5},{4,0},{5,9},{8,4},{9,13},{12,8},{13,15},{14,12},{15,11... | collective-permute-start | bytes 786440 | tf_op jit(solution)/shard_map/ppermute | solution.py:304
  27.4 0.0 collective-permute-done.4
  27.4 2.0 %collective-permute-start.6 = (f32[128,512]{1,0:T(8,128)S(1)}, f32[128,512]{1,0:T(8,128)S(1)}, u32[]{:S(2)}, u32[]{:S(2)}) collective-permute-start(f32[128,512]{1,0:T(8,128)S(1)} %add.31), channel_id=1, source_target_pairs={{0,2},{1,5},{4,0},{5,9},{8,4},{9,13},{12,8},{13,15},{14,12},{15,11... | collective-permute-start | bytes 786440 | tf_op jit(solution)/shard_map/ppermute | solution.py:304
  29.4 0.0 collective-permute-done.15
  29.5 0.1 collective-permute-start.16
  29.6 1.9 %product.19 = (f32[128,512]{1,0:T(8,128)S(1)}, f32[128,512]{1,0:T(8,128)S(1)}) custom-call(f32[128,2048]{1,0:T(8,128)S(1)} %pick.2.refs_0_, f32[128,2048]{1,0:T(8,128)S(1)} %collective-permute-done.refs_1_, f32[128,2048]{1,0:T(8,128)S(1)} %get-tuple-element.30.refs_2_, f32[128,2048]{1,0:T(8,128)S(1)} %collective-permute-done.2.refs_3_, ...), custom_call_target="tpu_custom_call" | custom-call | flops 1610612736 | bytes 9961472 | tf_op jit(solution)/shard_map/product/pallas_call | solution.py:179
  31.5 2.1 %product.20 = (f32[128,512]{1,0:T(8,128)S(1)}, f32[128,512]{1,0:T(8,128)S(1)}) custom-call(f32[128,2048]{1,0:T(8,128)S(1)} %pick.2.refs_0_, f32[128,2048]{1,0:T(8,128)S(1)} %collective-permute-done.refs_1_, f32[128,2048]{1,0:T(8,128)S(1)} %get-tuple-element.30.refs_2_, f32[128,2048]{1,0:T(8,128)S(1)} %collective-permute-done.2.refs_3_, ...), custom_call_target="tpu_custom_call" | custom-call | flops 1610612736 | bytes 9961472 | tf_op jit(solution)/shard_map/product/pallas_call | solution.py:179
  33.6 1.1 %collective-permute-done.9 = f32[128,512]{1,0:T(8,128)S(1)} collective-permute-done((f32[128,512]{1,0:T(8,128)S(1)}, f32[128,512]{1,0:T(8,128)S(1)}, u32[]{:S(2)}, u32[]{:S(2)}) %collective-permute-start.9) | collective-permute-done | bytes 262176 | tf_op jit(solution)/shard_map/ppermute | solution.py:304
  34.8 0.4 collective-permute-start.10
  35.2 0.0 collective-permute-done.12
  35.2 1.7 %collective-permute-start.13 = (f32[128,512]{1,0:T(8,128)S(1)}, f32[128,512]{1,0:T(8,128)S(1)}, u32[]{:S(2)}, u32[]{:S(2)}) collective-permute-start(f32[128,512]{1,0:T(8,128)S(1)} %add.36), channel_id=1, source_target_pairs={{0,2},{1,5},{4,0},{5,9},{8,4},{9,13},{12,8},{13,15},{14,12},{15,11... | collective-permute-start | bytes 786440 | tf_op jit(solution)/shard_map/ppermute | solution.py:304
  36.9 3.3 %collective-permute-done.6 = f32[128,512]{1,0:T(8,128)S(1)} collective-permute-done((f32[128,512]{1,0:T(8,128)S(1)}, f32[128,512]{1,0:T(8,128)S(1)}, u32[]{:S(2)}, u32[]{:S(2)}) %collective-permute-start.6) | collective-permute-done | bytes 262176 | tf_op jit(solution)/shard_map/ppermute | solution.py:304
  40.3 2.1 %collective-permute-start.7 = (f32[128,512]{1,0:T(8,128)S(1)}, f32[128,512]{1,0:T(8,128)S(1)}, u32[]{:S(2)}, u32[]{:S(2)}) collective-permute-start(f32[128,512]{1,0:T(8,128)S(1)} %add.32), channel_id=1, source_target_pairs={{0,2},{1,5},{4,0},{5,9},{8,4},{9,13},{12,8},{13,15},{14,12},{15,11... | collective-permute-start | bytes 786440 | tf_op jit(solution)/shard_map/ppermute | solution.py:304
  42.3 0.0 collective-permute-done.16
  42.4 0.1 collective-permute-start.17
  42.5 1.9 %product.21 = (f32[128,512]{1,0:T(8,128)S(1)}, f32[128,512]{1,0:T(8,128)S(1)}) custom-call(f32[128,2048]{1,0:T(8,128)S(1)} %pick.2.refs_0_, f32[128,2048]{1,0:T(8,128)S(1)} %collective-permute-done.refs_1_, f32[128,2048]{1,0:T(8,128)S(1)} %get-tuple-element.30.refs_2_, f32[128,2048]{1,0:T(8,128)S(1)} %collective-permute-done.2.refs_3_, ...), custom_call_target="tpu_custom_call" | custom-call | flops 1610612736 | bytes 9961472 | tf_op jit(solution)/shard_map/product/pallas_call | solution.py:179
  44.4 1.6 %collective-permute-done.10.refs_1_ = f32[128,512]{1,0:T(8,128)S(1)} collective-permute-done((f32[128,512]{1,0:T(8,128)S(1)}, f32[128,512]{1,0:T(8,128)S(1)}, u32[]{:S(2)}, u32[]{:S(2)}) %collective-permute-start.10) | collective-permute-done | bytes 262176 | tf_op jit(solution)/shard_map/ppermute | solution.py:304
  46.0 0.0 collective-permute-done.13.refs_3_
  46.0 4.3 %collective-permute-done.7.refs_0_ = f32[128,512]{1,0:T(8,128)S(1)} collective-permute-done((f32[128,512]{1,0:T(8,128)S(1)}, f32[128,512]{1,0:T(8,128)S(1)}, u32[]{:S(2)}, u32[]{:S(2)}) %collective-permute-start.7) | collective-permute-done | bytes 262176 | tf_op jit(solution)/shard_map/ppermute | solution.py:304
  50.2 0.3 collective-permute-done.17.refs_4_
  50.6 0.9 %finish.1 = f32[128,1024]{1,0:T(8,128)} custom-call(f32[128,512]{1,0:T(8,128)S(1)} %collective-permute-done.7.refs_0_, f32[128,512]{1,0:T(8,128)S(1)} %collective-permute-done.10.refs_1_, f32[128,512]{1,0:T(8,128)S(1)} %get-tuple-element.47.refs_2_, f32[128,512]{1,0:T(8,128)S(1)} %collective-permute-done.13.refs_3_, ...), custom_call_target="tpu_custom_call" | custom-call | tf_op jit(solution)/shard_map/finish/pallas_call | solution.py:206
  (10 shorter events, 0.4 us)
Async XLA Ops:
  0.0 4.9 %copy-start = (f32[2048,1024]{1,0:T(8,128)S(1)}, f32[2048,1024]{1,0:T(8,128)}, u32[]{:S(2)}) copy-start(f32[2048,1024]{1,0:T(8,128)} %refs_1_.1) | copy-start | bytes 25165828
  1.4 3.5 %collective-permute-start = (f32[128,2048]{1,0:T(8,128)S(1)}, f32[128,2048]{1,0:T(8,128)S(1)}, u32[]{:S(2)}, u32[]{:S(2)}) collective-permute-start(f32[128,2048]{1,0:T(8,128)S(1)} %pick.2.refs_0_), channel_id=1, source_target_pairs={{0,1},{1,0},{2,3},{3,2},{4,5},{5,4},{6,7},{7,6},{8,9},{9,8},{10,11... | collective-permute-start | bytes 3145736 | tf_op jit(solution)/shard_map/ppermute | solution.py:268
  4.2 6.4 %collective-permute-start.2 = (f32[128,2048]{1,0:T(8,128)S(1)}, f32[128,2048]{1,0:T(8,128)S(1)}, u32[]{:S(2)}, u32[]{:S(2)}) collective-permute-start(f32[128,2048]{1,0:T(8,128)S(1)} %get-tuple-element.30.refs_2_), channel_id=1, source_target_pairs={{0,1},{1,0},{2,3},{3,2},{4,5},{5,4},{6,7},{7,6},{8,9},{9,8},{10,11... | collective-permute-start | bytes 3145736 | tf_op jit(solution)/shard_map/ppermute | solution.py:268
  4.3 9.3 %collective-permute-start.3 = (f32[128,2048]{1,0:T(8,128)S(1)}, f32[128,2048]{1,0:T(8,128)S(1)}, u32[]{:S(2)}, u32[]{:S(2)}) collective-permute-start(f32[128,2048]{1,0:T(8,128)S(1)} %get-tuple-element.31.refs_4_), channel_id=1, source_target_pairs={{0,1},{1,0},{2,3},{3,2},{4,5},{5,4},{6,7},{7,6},{8,9},{9,8},{10,11... | collective-permute-start | bytes 3145736 | tf_op jit(solution)/shard_map/ppermute | solution.py:268
  4.8 14.8 %collective-permute-start.5 = (f32[128,2048]{1,0:T(8,128)S(1)}, f32[128,2048]{1,0:T(8,128)S(1)}, u32[]{:S(2)}, u32[]{:S(2)}) collective-permute-start(f32[128,2048]{1,0:T(8,128)S(1)} %get-tuple-element.41.refs_6_), channel_id=1, source_target_pairs={{0,1},{1,0},{2,3},{3,2},{4,5},{5,4},{6,7},{7,6},{8,9},{9,8},{10,11... | collective-permute-start | bytes 3145736 | tf_op jit(solution)/shard_map/ppermute | solution.py:268
  6.2 10.7 %collective-permute-start.1 = (f32[128,512]{1,0:T(8,128)S(1)}, f32[128,512]{1,0:T(8,128)S(1)}, u32[]{:S(2)}, u32[]{:S(2)}) collective-permute-start(f32[128,512]{1,0:T(8,128)S(1)} %get-tuple-element.29.refs_2_), channel_id=1, source_target_pairs={{0,2},{1,5},{4,0},{5,9},{8,4},{9,13},{12,8},{13,15},{14,12},{15,11... | collective-permute-start | bytes 786440 | tf_op jit(solution)/shard_map/ppermute | solution.py:304
  10.4 9.1 %collective-permute-start.14 = (f32[128,512]{1,0:T(8,128)S(1)}, f32[128,512]{1,0:T(8,128)S(1)}, u32[]{:S(2)}, u32[]{:S(2)}) collective-permute-start(f32[128,512]{1,0:T(8,128)S(1)} %get-tuple-element.35.refs_7_), channel_id=1, source_target_pairs={{0,4},{1,3},{4,8},{5,1},{8,12},{9,5},{12,14},{13,9},{14,10},{15,13... | collective-permute-start | bytes 786440 | tf_op jit(solution)/shard_map/ppermute | solution.py:304
  11.7 13.6 %collective-permute-start.11 = (f32[128,512]{1,0:T(8,128)S(1)}, f32[128,512]{1,0:T(8,128)S(1)}, u32[]{:S(2)}, u32[]{:S(2)}) collective-permute-start(f32[128,512]{1,0:T(8,128)S(1)} %get-tuple-element.39.refs_8_), channel_id=1, source_target_pairs={{0,2},{1,5},{4,0},{5,9},{8,4},{9,13},{12,8},{13,15},{14,12},{15,11... | collective-permute-start | bytes 786440 | tf_op jit(solution)/shard_map/ppermute | solution.py:304
  14.7 10.5 %collective-permute-start.8 = (f32[128,512]{1,0:T(8,128)S(1)}, f32[128,512]{1,0:T(8,128)S(1)}, u32[]{:S(2)}, u32[]{:S(2)}) collective-permute-start(f32[128,512]{1,0:T(8,128)S(1)} %get-tuple-element.40.refs_3_), channel_id=1, source_target_pairs={{0,4},{1,3},{4,8},{5,1},{8,12},{9,5},{12,14},{13,9},{14,10},{15,13... | collective-permute-start | bytes 786440 | tf_op jit(solution)/shard_map/ppermute | solution.py:304
  16.9 10.4 %collective-permute-start.4 = (f32[128,512]{1,0:T(8,128)S(1)}, f32[128,512]{1,0:T(8,128)S(1)}, u32[]{:S(2)}, u32[]{:S(2)}) collective-permute-start(f32[128,512]{1,0:T(8,128)S(1)} %add.30), channel_id=1, source_target_pairs={{0,2},{1,5},{4,0},{5,9},{8,4},{9,13},{12,8},{13,15},{14,12},{15,11... | collective-permute-start | bytes 786440 | tf_op jit(solution)/shard_map/ppermute | solution.py:304
  19.6 9.8 %collective-permute-start.15 = (f32[128,512]{1,0:T(8,128)S(1)}, f32[128,512]{1,0:T(8,128)S(1)}, u32[]{:S(2)}, u32[]{:S(2)}) collective-permute-start(f32[128,512]{1,0:T(8,128)S(1)} %add.37), channel_id=1, source_target_pairs={{0,4},{1,3},{4,8},{5,1},{8,12},{9,5},{12,14},{13,9},{14,10},{15,13... | collective-permute-start | bytes 786440 | tf_op jit(solution)/shard_map/ppermute | solution.py:304
  25.2 9.5 %collective-permute-start.9 = (f32[128,512]{1,0:T(8,128)S(1)}, f32[128,512]{1,0:T(8,128)S(1)}, u32[]{:S(2)}, u32[]{:S(2)}) collective-permute-start(f32[128,512]{1,0:T(8,128)S(1)} %add.33), channel_id=1, source_target_pairs={{0,4},{1,3},{4,8},{5,1},{8,12},{9,5},{12,14},{13,9},{14,10},{15,13... | collective-permute-start | bytes 786440 | tf_op jit(solution)/shard_map/ppermute | solution.py:304
  25.3 9.8 %collective-permute-start.12 = (f32[128,512]{1,0:T(8,128)S(1)}, f32[128,512]{1,0:T(8,128)S(1)}, u32[]{:S(2)}, u32[]{:S(2)}) collective-permute-start(f32[128,512]{1,0:T(8,128)S(1)} %add.35), channel_id=1, source_target_pairs={{0,2},{1,5},{4,0},{5,9},{8,4},{9,13},{12,8},{13,15},{14,12},{15,11... | collective-permute-start | bytes 786440 | tf_op jit(solution)/shard_map/ppermute | solution.py:304
  27.4 12.8 %collective-permute-start.6 = (f32[128,512]{1,0:T(8,128)S(1)}, f32[128,512]{1,0:T(8,128)S(1)}, u32[]{:S(2)}, u32[]{:S(2)}) collective-permute-start(f32[128,512]{1,0:T(8,128)S(1)} %add.31), channel_id=1, source_target_pairs={{0,2},{1,5},{4,0},{5,9},{8,4},{9,13},{12,8},{13,15},{14,12},{15,11... | collective-permute-start | bytes 786440 | tf_op jit(solution)/shard_map/ppermute | solution.py:304
  29.5 12.9 %collective-permute-start.16 = (f32[128,512]{1,0:T(8,128)S(1)}, f32[128,512]{1,0:T(8,128)S(1)}, u32[]{:S(2)}, u32[]{:S(2)}) collective-permute-start(f32[128,512]{1,0:T(8,128)S(1)} %add.38), channel_id=1, source_target_pairs={{0,4},{1,3},{4,8},{5,1},{8,12},{9,5},{12,14},{13,9},{14,10},{15,13... | collective-permute-start | bytes 786440 | tf_op jit(solution)/shard_map/ppermute | solution.py:304
  34.8 11.2 %collective-permute-start.10 = (f32[128,512]{1,0:T(8,128)S(1)}, f32[128,512]{1,0:T(8,128)S(1)}, u32[]{:S(2)}, u32[]{:S(2)}) collective-permute-start(f32[128,512]{1,0:T(8,128)S(1)} %add.34), channel_id=1, source_target_pairs={{0,4},{1,3},{4,8},{5,1},{8,12},{9,5},{12,14},{13,9},{14,10},{15,13... | collective-permute-start | bytes 786440 | tf_op jit(solution)/shard_map/ppermute | solution.py:304
  35.2 10.8 %collective-permute-start.13 = (f32[128,512]{1,0:T(8,128)S(1)}, f32[128,512]{1,0:T(8,128)S(1)}, u32[]{:S(2)}, u32[]{:S(2)}) collective-permute-start(f32[128,512]{1,0:T(8,128)S(1)} %add.36), channel_id=1, source_target_pairs={{0,2},{1,5},{4,0},{5,9},{8,4},{9,13},{12,8},{13,15},{14,12},{15,11... | collective-permute-start | bytes 786440 | tf_op jit(solution)/shard_map/ppermute | solution.py:304
  40.3 10.0 %collective-permute-start.7 = (f32[128,512]{1,0:T(8,128)S(1)}, f32[128,512]{1,0:T(8,128)S(1)}, u32[]{:S(2)}, u32[]{:S(2)}) collective-permute-start(f32[128,512]{1,0:T(8,128)S(1)} %add.32), channel_id=1, source_target_pairs={{0,2},{1,5},{4,0},{5,9},{8,4},{9,13},{12,8},{13,15},{14,12},{15,11... | collective-permute-start | bytes 786440 | tf_op jit(solution)/shard_map/ppermute | solution.py:304
  42.4 8.2 %collective-permute-start.17 = (f32[128,512]{1,0:T(8,128)S(1)}, f32[128,512]{1,0:T(8,128)S(1)}, u32[]{:S(2)}, u32[]{:S(2)}) collective-permute-start(f32[128,512]{1,0:T(8,128)S(1)} %add.39), channel_id=1, source_target_pairs={{0,4},{1,3},{4,8},{5,1},{8,12},{9,5},{12,14},{13,9},{14,10},{15,13... | collective-permute-start | bytes 786440 | tf_op jit(solution)/shard_map/ppermute | solution.py:304
